TPU v7x, 256 devices: a whole 4x4x8 slice. The times are simulated.
256 devices in a mesh: grp: 8 (over y_lo, x), seq: 32 (over z, y_hi, core).
Axes of the slice: x: 4, y: 4 (y_hi: 2, y_lo: 2; y = y_hi * 2 + y_lo), z: 8, core: 2. Of those that a mesh axis runs over, the one named last changes fastest.
Arguments:
- fake_tokens: bfloat16 [8, 6144, 1536], P('grp', 'seq'), may hold values from -16 to 16
- real_tokens: bfloat16 [8, 6144, 1536], P('grp', 'seq'), may hold values from -6 to 6
- proj_weight: bfloat16 [1536, 2048], P('seq'), may hold values from -0.15625 to 0.15625
- score_vector: float32 [2048], replicated, may hold values from -0.25 to 0.25
Outputs:
- grad_weight: float32 [1536, 2048], P('seq')
All inputs are finite; a program needn't handle non-finite values.
Results may differ from a plain program's by a relative error of at most 0.0003.
Values may be sent and summed in bfloat16 or wider, within the bound.
No kernel may reach another device: no remote copies, remote signals or barrier semaphores. Data moves between devices by JAX's collectives and lax.ppermute only.
A program may use at most 64 MiB of HBM per device.

v0:
```python
import math

import jax
import jax.numpy as jnp
from jax import lax
from jax.sharding import PartitionSpec as P

R1_WEIGHT = 40.0


def per_device(fake_tokens, real_tokens, proj_weight, score_vector):
    fake_rows = fake_tokens[0]
    real_rows = real_tokens[0]
    tok_count = fake_rows.shape[0]
    hid_width = proj_weight.shape[1]
    loss_scale = math.sqrt(hid_width / (lax.axis_size("grp") * lax.axis_size("seq") * tok_count))
    joined = jnp.concatenate([fake_rows, real_rows], 0)
    shard_rows = lax.all_gather(proj_weight, "seq", axis=0, tiled=True)
    partial_pre = jnp.dot(joined, shard_rows, preferred_element_type=jnp.float32)
    full_weight = shard_rows
    preact, full_weight = (partial_pre, full_weight)
    squash = jax.nn.sigmoid(preact)
    slopes = squash * (1.0 + preact * (1.0 - squash))
    curves = squash * (1.0 - squash) * (2.0 + preact * (1.0 - 2.0 * squash))
    logits = jnp.dot(preact * squash, score_vector, precision=lax.Precision.HIGHEST)
    slopes_real = slopes[tok_count:]
    lifted = (slopes_real * score_vector).astype(jnp.bfloat16)
    input_grad = lax.dot_general(
        lifted, full_weight, (((1,), (1,)), ((), ())), preferred_element_type=jnp.float32
    )
    r1_cot = (loss_scale * R1_WEIGHT * input_grad).astype(jnp.bfloat16)
    back_grad = jnp.dot(r1_cot, full_weight, preferred_element_type=jnp.float32)
    fake_cot = (
        loss_scale * jax.nn.sigmoid(logits[:tok_count])[:, None] * slopes[:tok_count] * score_vector
    ).astype(jnp.bfloat16)
    real_cot = (
        -loss_scale * jax.nn.sigmoid(-logits[tok_count:])[:, None] * slopes_real * score_vector
        + back_grad * score_vector * curves[tok_count:]
    ).astype(jnp.bfloat16)
    left_rows = jnp.concatenate([fake_rows, real_rows, r1_cot], 0)
    right_rows = jnp.concatenate([fake_cot, real_cot, lifted], 0)
    grad_term = lax.dot_general(
        left_rows, right_rows, (((0,), (0,)), ((), ())), preferred_element_type=jnp.float32
    )
    grad_shard = lax.psum_scatter(grad_term, "seq", scatter_dimension=0, tiled=True)
    return lax.psum(grad_shard, "grp")


def solution(mesh):
    in_specs = (P("grp", "seq", None), P("grp", "seq", None), P("seq", None), P())
    out_specs = P("seq", None)
    return jax.shard_map(
        per_device, mesh=mesh, in_specs=in_specs, out_specs=out_specs, check_vma=False
    )
```

profile of v0, /device:TPU:1, one launch (start us, length us, event | category | flops | bytes accessed | tf_op | source)
XLA Modules:
  0.0 384.0 jit_solution(6854587875983400413)
XLA Ops:
  6.5 0.0 all-gather.2.cloned.1.call-start
  6.5 0.7 all-gather.2.cloned.1.call-update
  7.3 0.0 reduce-scatter.2.cloned.1.call-start
  7.3 101.6 %all-gather.2.cloned.1.call-done = bf16[1536,2048]{1,0:T(8,128)(2,1)} async-done(((bf16[48,2048]{1,0:T(8,128)(2,1)}), bf16[1536,2048]{1,0:T(8,128)(2,1)}) %all-gather.2.cloned.1.call-update) | async-done | bytes 6291472 | tf_op jit(solution)/shard_map/all_gather | solution.py:18
  108.9 0.0 copy-start
  108.9 5.6 %add_divide_fusion = (f32[384,2048]{1,0:T(8,128)S(1)}, f32[384,2048]{1,0:T(8,128)S(1)}, f32[384,2048]{1,0:T(8,128)S(1)}, f32[384,2048]{1,0:T(8,128)S(1)}) fusion(bf16[1536,2048]{1,0:T(8,128)(2,1)} %all-gather.2.cloned.1.call-done, bf16[192,1536]{1,0:T(8,128)(2,1)} %bitcast.12, bf16[192,1536]{1,0:T(8,128)(2,1)} %bitcast.14), kind=kOutput, calls=%fused_computation.3 | convolution fusion | flops 2423783424 | bytes 20054016 | tf_op jit(solution)/shard_map/dot_general | solution.py:19
  114.6 0.0 slice-start
  114.6 0.0 copy-done
  114.6 0.0 slice-start.1
  114.6 3.3 fusion.25
  117.9 0.1 divide_multiply_fusion.1
  117.9 0.3 fusion.20
  118.3 0.0 slice-done
  118.3 0.0 slice-done.1
  118.3 2.2 fusion.5
  120.5 0.0 copy-start.1
  120.6 0.0 copy-start.2
  120.6 1.8 fusion.4
  122.4 0.0 copy-done.1
  122.4 0.0 copy-done.2
  122.4 8.0 %fusion.6 = f32[1536,2048]{1,0:T(8,128)} fusion(bf16[192,2048]{1,0:T(8,128)(2,1)S(1)} %get-tuple-element.6, bf16[192,2048]{1,0:T(8,128)(2,1)S(1)} %fusion.4, bf16[192,2048]{1,0:T(8,128)(2,1)S(1)} %get-tuple-element.5, bf16[192,1536]{1,0:T(8,128)(2,1)S(1)} %fusion.5, bf16[192,1536]{1,0:T(8,128)(2,1)S(1)} %bitcast.13, bf16[192,1536]{1,0:T(8,128)(2,1)S(1)} %bitcast.15), kind=kOutput, calls=%fused_computation.10 | convolution fusion | flops 3636264960 | bytes 16711680 | tf_op jit(solution)/shard_map/dot_general | solution.py:42
  130.4 0.0 reduce-scatter.2.cloned.1.call-update
  130.4 0.0 all-reduce.2.cloned.1.call-start
  130.5 166.0 %reduce-scatter.2.cloned.1.call-done = f32[48,2048]{1,0:T(8,128)} async-done(((f32[1536,2048]{1,0:T(8,128)}), f32[48,2048]{1,0:T(8,128)}) %reduce-scatter.2.cloned.1.call-update) | async-done | bytes 393232 | tf_op jit(solution)/shard_map/reduce_scatter | solution.py:45
  296.5 0.0 all-reduce.2.cloned.1.call-update
  296.5 79.2 %all-reduce.2.cloned.1.call-done = f32[48,2048]{1,0:T(8,128)} async-done(((f32[48,2048]{1,0:T(8,128)}), f32[48,2048]{1,0:T(8,128)}) %all-reduce.2.cloned.1.call-update) | async-done | bytes 393232 | tf_op jit(solution)/shard_map/psum | solution.py:46
  375.7 1.8 copy.6
  (1 shorter events, 0.0 us)
Async XLA Ops:
  6.5 102.4 %all-gather.2.cloned.1.call-start = ((), (), s32[]{:S(2)}) async-start(), calls=%async_computation.1 | async-start | bytes 6488064 | tf_op jit(solution)/shard_map/all_gather | solution.py:18
  7.3 289.3 %reduce-scatter.2.cloned.1.call-start = ((), (), s32[]{:S(2)}) async-start(), calls=%async_computation.2 | async-start | bytes 12976128 | tf_op jit(solution)/shard_map/reduce_scatter | solution.py:45
  108.9 5.6 %copy-start = (f32[2048]{0:T(1024)S(1)}, f32[2048]{0:T(1024)}, u32[]{:S(2)}) copy-start(f32[2048]{0:T(1024)} %param.7) | copy-start | bytes 24580
  114.6 3.7 slice-start
  114.6 3.7 slice-start.1
  120.5 1.9 copy-start.1
  120.6 1.9 copy-start.2
  130.4 245.3 %all-reduce.2.cloned.1.call-start = ((), (), s32[]{:S(2)}) async-start(), calls=%async_computation.3 | async-start | bytes 786432 | tf_op jit(solution)/shard_map/psum | solution.py:46
Sparse Core Ops, SparseCore 0:
  10.1 98.7 all-gather.1
  130.6 165.9 reduce-scatter.1
  299.1 76.5 all-reduce.1
where the time goes:
time: 388 us; the launch traced here: 384 us
  waiting for transfers between devices  348 us (90%)
  matrix products  20.9 us (5%)
  between operations  13.2 us (3%)
    reduce_scatter x1, waiting for transfers between devices, per_device(): lax.psum_scatter(grad_term, 'seq', scatter_dimension=0, tiled=True)  166 us
    all_gather x1, waiting for transfers between devices, per_device(): shard_rows = lax.all_gather(proj_weight, 'seq', axis=0, tiled=True)  102 us
    psum x1, waiting for transfers between devices, per_device(): return lax.psum(grad_shard, 'grp')  79.2 us
    dot_general x1, matrix products, per_device(): lax.dot_general(left_rows, right_rows, (((0,), (0,)), ((), ())), preferre...  8.01 us
  transfers between devices with their start and end apart: 3, of which 3 were waited for; matrix products, arithmetic and copies ran while one was open for 0% of the time, Pallas kernels for 0%

commit v1 on v0

v1 whole, which is shorter than its diff:
```python
import functools
import math

import jax
import jax.numpy as jnp
from jax import lax
from jax.experimental import pallas as pl
from jax.experimental.pallas import tpu as pltpu
from jax.sharding import Mesh
from jax.sharding import PartitionSpec as P

R1_WEIGHT = 40.0
NX, NY, NZ = 4, 4, 8
AXES = ("ylo", "x", "z", "yhi", "c")
BF16, F16, F32 = jnp.bfloat16, jnp.float16, jnp.float32
VMEM_BYTES = 20 * 1024 * 1024


def flat_index(x, y, z, c):
    return ((y % 2) * NX + x) * (NZ * 4) + z * 4 + (y // 2) * 2 + c


def send(array, to):
    pairs = []
    for x in range(NX):
        for y in range(NY):
            for z in range(NZ):
                for c in range(2):
                    tx, ty, tc = to(x, y, c)
                    pairs.append((flat_index(x, y, z, c), flat_index(tx % NX, ty % NY, z, tc)))
    return lax.ppermute(array, AXES, pairs)


def to_core(array):
    return send(array, lambda x, y, c: (x, y, 1 - c))


def together(arrays, routes):
    arrays = lax.optimization_barrier(tuple(arrays))
    return lax.optimization_barrier(tuple(send(a, to) for a, to in zip(arrays, routes, strict=True)))


RING = (
    lambda x, y, c: (x + 1, y, c),
    lambda x, y, c: (x - 1, y, c),
    lambda x, y, c: (x, y + 1, c),
    lambda x, y, c: (x, y - 1, c),
)


def ordered(first_is_mine, mine, theirs, axis):
    return jnp.concatenate(
        [jnp.where(first_is_mine, mine, theirs), jnp.where(first_is_mine, theirs, mine)], axis
    )


def packed(piece, exponent):
    scaled = (piece * jnp.exp2(-exponent)).astype(F16)
    return jnp.concatenate([scaled, jnp.broadcast_to(exponent.astype(F16), (16, piece.shape[1]))], 0)


def unpacked(message):
    exponent = message[-16:-15].astype(F32)
    return message[:-16].astype(F32) * jnp.exp2(exponent), exponent


def column_tiles(width):
    return [(start, min(256, width - start)) for start in range(0, width, 256)]


def nt(a, b):
    return lax.dot_general(a, b, (((1,), (1,)), ((), ())), preferred_element_type=F32)


def forward_tiles(tokens_ref, w_ref, score_ref, slope_ref, curve_ref, lifted_ref, logit_ref, first):
    n = tokens_ref.shape[0] // 2
    for kind in (0, 1):
        rows = slice(kind * n, kind * n + n)
        total = jnp.zeros((n, 128), F32) if first is None else first[rows, :]
        for start, width in column_tiles(w_ref.shape[1]):
            cols = slice(start, start + width)
            preact = jnp.dot(tokens_ref[rows, :], w_ref[:, cols], preferred_element_type=F32)
            score = score_ref[:, cols]
            squash = jax.nn.sigmoid(preact)
            rest = 1.0 - squash
            act = preact * squash * score
            for lane in range(0, width, 128):
                total = total + act[:, lane : lane + 128]
            slope = squash * (1.0 + preact * rest) * score
            slope_ref[rows, cols] = slope
            if kind == 1:
                lifted_ref[:, cols] = slope.astype(BF16)
                curve_ref[:, cols] = squash * rest * (2.0 + preact * (1.0 - 2.0 * squash)) * score
        logit_ref[rows, :] = total


def pull_back(w_ref, lifted_ref, part_ref, so_far):
    for start in range(0, w_ref.shape[0], 512):
        rows = slice(start, start + 512)
        value = nt(w_ref[rows, :], lifted_ref[...])
        part_ref[rows, :] = value if so_far is None else so_far[rows, :] + value


def place_pair(w_ref, column, low_ref, high_ref, swap):
    width = low_ref.shape[1]
    turn = w_ref.shape[0] // (2 * NZ)
    for z in range(NZ):
        rows = slice(z * turn, z * turn + turn)
        low, high = low_ref[rows, :], high_ref[rows, :]
        w_ref[2 * z * turn : 2 * z * turn + turn, column : column + width] = jnp.where(swap, high, low)
        w_ref[2 * z * turn + turn : 2 * z * turn + 2 * turn, column : column + width] = jnp.where(swap, low, high)


def first_kernel(flag_ref, tokens_ref, own_ref, left_ref, right_ref, low_ref, high_ref, score_ref,
                 w_ref, slope_ref, curve_ref, lifted_ref, logit_ref, part_ref):
    w_ref[:, 0:128] = own_ref[...]
    w_ref[:, 128:256] = left_ref[...]
    w_ref[:, 256:384] = right_ref[...]
    place_pair(w_ref, 384, low_ref, high_ref, flag_ref[0] == 1)
    forward_tiles(tokens_ref, w_ref, score_ref, slope_ref, curve_ref, lifted_ref, logit_ref, None)
    pull_back(w_ref, lifted_ref, part_ref, None)


def tokens_kernel(flag_ref, fake_ref, real_ref, other_ref, tokens_ref, tokens_t_ref, peak_ref):
    tok = fake_ref.shape[0]
    first = flag_ref[0] == 0
    for kind, own in enumerate((fake_ref, real_ref)):
        mine, theirs = own[...], other_ref[kind * tok : kind * tok + tok, :]
        start = 2 * kind * tok
        tokens_ref[start : start + tok, :] = jnp.where(first, mine, theirs)
        tokens_ref[start + tok : start + 2 * tok, :] = jnp.where(first, theirs, mine)
        peak = peak_of(tokens_ref[start : start + 2 * tok, :])
        peak_ref[8 * kind : 8 * kind + 8, :] = jnp.broadcast_to(peak, (8, 128))
    tokens_t_ref[...] = tokens_ref[...].T


def second_kernel(flag_ref, tokens_ref, low_ref, high_top_ref, high_bottom_ref, across_top_ref, across_bottom_ref,
                  score_ref, logit_in_ref, part_in_ref,
                  w_ref, slope_ref, curve_ref, lifted_ref, logit_ref, part_ref, high_ref):
    top = high_top_ref.shape[0]
    high_ref[0:top, :] = high_top_ref[...]
    high_ref[top : 2 * top, :] = high_bottom_ref[...]
    place_pair(w_ref, 0, low_ref, high_ref, flag_ref[0] == 1)
    top = across_top_ref.shape[0]
    w_ref[0:top, 256:384] = across_top_ref[...]
    w_ref[top : 2 * top, 256:384] = across_bottom_ref[...]
    forward_tiles(tokens_ref, w_ref, score_ref, slope_ref, curve_ref, lifted_ref, logit_ref, logit_in_ref)
    pull_back(w_ref, lifted_ref, part_ref, part_in_ref)


def peak_of(array):
    flat = jnp.max(jnp.abs(array).astype(F32), axis=0, keepdims=True)
    return jnp.max(flat, axis=1, keepdims=True)


def term_tiles(scale, tokens_t_ref, r1_t_ref, r1_ref, logits, w_ref, slope_ref, curve_ref, lifted_ref, peak_ref,
               outs, exp_ref, fake_ref, real_ref):
    n = lifted_ref.shape[0]
    fake_gain = scale * jax.nn.sigmoid(logits[:n])
    real_gain = -scale * jax.nn.sigmoid(-logits[n:])
    fake_ref[...] = (fake_gain * slope_ref[0:n, :]).astype(BF16)
    for start, width in column_tiles(w_ref.shape[1]):
        cols = slice(start, start + width)
        back = jnp.dot(r1_ref[...], w_ref[:, cols], preferred_element_type=F32)
        real_ref[:, cols] = (real_gain * slope_ref[n : 2 * n, cols] + back * curve_ref[:, cols]).astype(BF16)
    bound = n * (
        peak_ref[0:1, 0:1] * peak_of(fake_ref[...])
        + peak_ref[8:9, 0:1] * peak_of(real_ref[...])
        + peak_of(r1_t_ref[...]) * peak_of(lifted_ref[...])
    )
    bound = jnp.broadcast_to(bound, (16, 128))
    exp_ref[...] = jnp.ceil(jnp.log(jnp.maximum(bound, 1e-30)) * (1.0 / math.log(2.0)) + 0.01) - 15.0
    d_in = tokens_t_ref.shape[0]
    turn = d_in // (2 * NZ)
    height = 4 * turn
    for start, width, parts in outs:
        cols = slice(start, start + width)
        for row in range(0, d_in, height):
            rows = slice(row, row + height)
            value = (
                jnp.dot(tokens_t_ref[rows, 0:n], fake_ref[:, cols], preferred_element_type=F32)
                + jnp.dot(tokens_t_ref[rows, n : 2 * n], real_ref[:, cols], preferred_element_type=F32)
                + jnp.dot(r1_t_ref[rows, :], lifted_ref[:, cols], preferred_element_type=F32)
            )
            for column, turns, out in parts:
                piece = value[:, column : column + out.shape[1]]
                if turns is None:
                    out[rows, :] = piece
                else:
                    for k in range(2):
                        at = row // 2 + k * turn
                        out[at : at + turn, :] = piece[(2 * k + turns) * turn : (2 * k + turns + 1) * turn, :]


def third_kernel(scale, tokens_t_ref, part_ref, part_in_ref, logit_ref, logit_in_ref, w_ref, slope_ref, curve_ref,
                 lifted_ref, peak_ref, low_ref, high_ref, across_ref, exp_ref, r1_t_ref, r1_ref, logits_ref,
                 fake_ref, real_ref):
    r1_t_ref[...] = (scale * R1_WEIGHT * (part_ref[...] + part_in_ref[...])).astype(BF16)
    r1_ref[...] = r1_t_ref[...].T
    logits = jnp.sum(logit_ref[...] + logit_in_ref[...], axis=1, keepdims=True)
    logits_ref[...] = jnp.broadcast_to(logits, logits_ref.shape)
    outs = [(0, 256, [(0, 0, low_ref), (0, 1, high_ref)]), (256, 128, [(0, None, across_ref)])]
    term_tiles(scale, tokens_t_ref, r1_t_ref, r1_ref, logits, w_ref, slope_ref, curve_ref, lifted_ref, peak_ref,
               outs, exp_ref, fake_ref, real_ref)


def fourth_kernel(scale, tokens_t_ref, r1_t_ref, r1_ref, logits_ref, w_ref, slope_ref, curve_ref, lifted_ref, peak_ref,
                  own_ref, left_ref, right_ref, low_ref, high_ref, exp_ref, fake_ref, real_ref):
    outs = [
        (0, 256, [(0, None, own_ref), (128, None, left_ref)]),
        (256, 128, [(0, None, right_ref)]),
        (384, 256, [(0, 0, low_ref), (0, 1, high_ref)]),
    ]
    term_tiles(scale, tokens_t_ref, r1_t_ref, r1_ref, logits_ref[:, 0:1], w_ref, slope_ref, curve_ref, lifted_ref,
               peak_ref, outs, exp_ref, fake_ref, real_ref)


def call(kernel, flops, outs, scratch, *args, flags=None):
    vmem = pl.BlockSpec(memory_space=pltpu.VMEM)
    specs = [vmem] * len(args)
    if flags is not None:
        args, specs = (flags, *args), [pl.BlockSpec(memory_space=pltpu.SMEM), *specs]
    return pl.pallas_call(
        kernel,
        out_shape=[jax.ShapeDtypeStruct(shape, dtype) for shape, dtype in outs],
        in_specs=specs,
        out_specs=[vmem] * len(outs),
        scratch_shapes=[pltpu.VMEM(shape, dtype) for shape, dtype in scratch],
        compiler_params=pltpu.CompilerParams(vmem_limit_bytes=VMEM_BYTES),
        cost_estimate=pl.CostEstimate(flops=flops, bytes_accessed=8_000_000, transcendentals=0),
    )(*args)


def per_device(fake_tokens, real_tokens, proj_weight, score_vector):
    ylo, x, z, yhi, c = (lax.axis_index(a) for a in AXES)
    y = yhi * 2 + ylo
    gray_x, gray_y = ((v == 1) | (v == 2) for v in (x, y))
    core0 = c == 0
    tok = fake_tokens.shape[1]
    rows, hid = proj_weight.shape
    half = hid // 2
    d_in = rows * NZ * 4
    n = 2 * tok
    scale = math.sqrt(hid / (8 * 32 * tok))

    def slices_of(side):
        mine = lax.dynamic_slice_in_dim(proj_weight, side * half, half, 1)
        first = lax.dynamic_slice_in_dim(mine, x * 128, 128, 1)
        second = lax.dynamic_slice_in_dim(mine, 512 + ylo * 256 + gray_x * 128, 128, 1)
        return jnp.concatenate([first, second], 1)

    block = ordered(core0, slices_of(c), to_core(slices_of(1 - c)), 0)
    over_z = lax.all_to_all(jnp.broadcast_to(block[None], (NZ, *block.shape)), "z", 0, 0)
    piece_a, piece_b = over_z[:, :, :128], over_z[:, :, 128:].reshape(d_in // 2, 128)
    far_a, far_b = together(
        (piece_a.reshape(d_in // 2, 128), piece_b), (lambda x, y, c: (x, 3 - y, c), lambda x, y, c: (x ^ 1, y, c))
    )
    far_a = far_a.reshape(piece_a.shape)
    own_a = ordered(yhi == 0, piece_a[:, None], far_a[:, None], 1).reshape(d_in, 128)
    own_b = ordered(~gray_x, piece_b, far_b, 1)

    own_tokens = jnp.concatenate([fake_tokens[0], real_tokens[0]], 0)
    tokens, tokens_t, peak = call(
        tokens_kernel, 2 * n * d_in * 128, [((2 * n, d_in), BF16), ((d_in, 2 * n), BF16), ((16, 128), F32)], [],
        fake_tokens[0], real_tokens[0], to_core(own_tokens),
        flags=c[None].astype(jnp.int32),
    )

    left_a, right_a, left_b, right_b = together((own_a, own_a, own_b, own_b), RING)
    mid_a, mid_b = d_in // 2, d_in // 4
    across = together((left_a[:mid_a], right_a[mid_a:], left_b[:mid_b], right_b[mid_b:]), RING)
    across_a, across_b = across[:2], across[2:]

    def score_at(start, width):
        return lax.dynamic_slice_in_dim(score_vector, c * half + start, width, 0)

    score_1 = jnp.concatenate(
        [score_at((x + k) % 4 * 128, 128) for k in (0, 3, 1)] + [score_at(512 + (1 - ylo) * 256, 256)]
    )[None]
    score_2 = jnp.concatenate([score_at(512 + ylo * 256, 256), score_at((x + 2) % 4 * 128, 128)])[None]
    yhi_left, yhi_right = (y + 3) % 4 // 2, (y + 1) % 4 // 2

    def states(width):
        return [
            ((d_in, width), BF16),
            ((2 * n, width), F32),
            ((n, width), F32),
            ((n, width), BF16),
            ((2 * n, 128), F32),
            ((d_in, n), F32),
        ]

    wide, narrow = 640, 384
    w_1, slope_1, curve_1, lifted_1, logit_1, part_1 = call(
        first_kernel, 6 * n * d_in * wide, states(wide), [],
        tokens, own_a, left_a, right_a, left_b, right_b, score_1,
        flags=yhi_left[None].astype(jnp.int32),
    )
    w_2, slope_2, curve_2, lifted_2, logit, part = call(
        second_kernel, 6 * n * d_in * narrow, states(narrow), [((d_in // 2, 256), BF16)],
        tokens, own_b, *across_b, *across_a, score_2, logit_1, part_1,
        flags=yhi[None].astype(jnp.int32),
    )
    part_in, logit_in = to_core(part), to_core(logit)

    def works(width):
        return [((n, width), BF16)] * 2

    side = [((d_in // 2, 256), F32)] * 2
    strip = ((d_in, 128), F32)
    low_2, high_2, far_a, exp_2, r1_t, r1, logits = call(
        functools.partial(third_kernel, scale), 8 * n * d_in * narrow,
        [*side, strip, ((16, 128), F32), ((d_in, n), BF16), ((n, d_in), BF16), ((2 * n, 128), F32)],
        works(narrow),
        tokens_t, part, part_in, logit, logit_in, w_2, slope_2, curve_2, lifted_2, peak,
    )
    own_1, left_1, right_1, low_1, high_1, exp_1 = call(
        functools.partial(fourth_kernel, scale), 8 * n * d_in * wide,
        [strip, strip, strip, *side, ((16, 128), F32)], works(wide),
        tokens_t, r1_t, r1, logits, w_1, slope_1, curve_1, lifted_1, peak,
    )
    exp_1, exp_2 = exp_1[:1], exp_2[:1]
    twice = lambda row: jnp.concatenate([row, row], 1)

    own_2 = jnp.where(yhi == 0, low_2, high_2)
    far_b = jnp.where(yhi == 0, high_2, low_2)
    a_up, a_down, b_up, b_down = together(
        (
            packed(far_a[:mid_a], exp_2),
            packed(far_a[mid_a:], exp_2),
            packed(far_b[:mid_b], twice(exp_2)),
            packed(far_b[mid_b:], twice(exp_2)),
        ),
        RING,
    )

    def joined(piece, exponent, top=None, bottom=None):
        middle = piece.shape[0] // 2
        values, theirs = unpacked(bottom if top is None else top)
        exponent = jnp.maximum(exponent, theirs) + 1.0
        upper, lower = piece[:middle], piece[middle:]
        upper, lower = (upper, lower + values) if top is None else (upper + values, lower)
        return packed(jnp.concatenate([upper, lower], 0), exponent)

    right_b = jnp.where(yhi_right == 0, low_1, high_1)
    left_b = jnp.where(yhi_left == 0, low_1, high_1)
    from_left_a, from_right_a, from_left_b, from_right_b = together(
        (
            joined(right_1, exp_1, top=a_up),
            joined(left_1, exp_1, bottom=a_down),
            joined(right_b, twice(exp_1), top=b_up),
            joined(left_b, twice(exp_1), bottom=b_down),
        ),
        RING,
    )

    def three(own, exponent, one, two):
        (one, exp_one), (two, exp_two) = unpacked(one), unpacked(two)
        return own + one + two, jnp.maximum(exponent, jnp.maximum(exp_one, exp_two)) + 2.0

    top = jnp.maximum(exp_1, exp_2)
    sum_a, exp_a = three(own_1, top, from_left_a, from_right_a)
    sum_b, exp_b = three(own_2, twice(top), from_left_b, from_right_b)

    turns = sum_a.reshape(NZ, 2, 2 * rows, 128)
    keep_a = jnp.where(yhi == 0, turns[:, 0], turns[:, 1]).reshape(d_in // 2, 128)
    give_a = jnp.where(yhi == 0, turns[:, 1], turns[:, 0]).reshape(d_in // 2, 128)
    keep_b = jnp.where(gray_x, sum_b[:, 128:], sum_b[:, :128])
    give_b = jnp.where(gray_x, sum_b[:, :128], sum_b[:, 128:])
    got_a, got_b = together(
        (packed(give_a, exp_a), packed(give_b, exp_b[:, :128])),
        (lambda x, y, c: (x, 3 - y, c), lambda x, y, c: (x ^ 1, y, c)),
    )
    turns_a = (keep_a + unpacked(got_a)[0]).reshape(NZ, 2, rows, 128)
    turns_b = (keep_b + unpacked(got_b)[0]).reshape(NZ, 2, rows, 128)

    def split_rows(turns, second):
        return jnp.where(second, turns[:, 1], turns[:, 0]), jnp.where(second, turns[:, 0], turns[:, 1])

    keep_a, give_a = split_rows(turns_a, gray_y)
    keep_b, give_b = split_rows(turns_b, x >= 2)
    got_a, got_b = together(
        (give_a, give_b), (lambda x, y, c: (x, y ^ 1, c), lambda x, y, c: (3 - x, y, c))
    )
    both = jnp.concatenate([keep_a + got_a, keep_b + got_b], 2)
    both = jnp.sum(lax.all_to_all(both, "z", 0, 0), 0)

    spread = lax.all_to_all(jnp.broadcast_to(both[None], (8, *both.shape)), ("ylo", "x"), 0, 0)
    spread = spread.reshape(2, 4, rows, 256)

    def row_group(r):
        pick = jnp.where(yhi == r, spread[0, :, :, :128], spread[1, :, :, :128])
        order = (0, 1) if r == 0 else (3, 2)
        return jnp.concatenate(
            [pick[k] for k in range(4)] + [spread[v, k, :, 128:] for v in (0, 1) for k in order], 1
        )

    zero, one = row_group(0), row_group(1)
    theirs = to_core(jnp.where(core0, one, zero))
    return ordered(core0, jnp.where(core0, zero, one), theirs, 1)


def solution(mesh):
    split = Mesh(mesh.devices.reshape(2, NX, NZ, 2, 2), AXES)
    tokens = P(("ylo", "x"), ("z", "yhi", "c"), None)
    shard = P(("z", "yhi", "c"), None)
    return jax.shard_map(
        per_device, mesh=split, in_specs=(tokens, tokens, shard, P()), out_specs=shard, check_vma=False
    )
```

time: 388 us -> 165 us (0.43)
  waiting for transfers between devices: 348 us -> 32 us
  starting transfers between devices: 0.08 us -> 52.9 us
  blocking collectives: 0 us -> 33.5 us
  Pallas kernels: 0 us -> 22.8 us
  matrix products: 20.9 us -> 0 us
  local copies, waits for them, and re-layouts: 1.79 us -> 16.2 us
  between operations: 13.2 us -> 0.77 us
  other arithmetic: 0.42 us -> 6.5 us
    reduce_scatter x1 -> x0, waiting for transfers between devices: 166 us -> none  [per_device(): lax.psum_scatter(grad_term, 'seq', scatter_dimension=0, tiled=True)]
    all_gather x1 -> x0, waiting for transfers between devices: 102 us -> none  [per_device(): shard_rows = lax.all_gather(proj_weight, 'seq', axis=0, tiled=True)]
    psum x1 -> x0, waiting for transfers between devices: 79.2 us -> none  [per_device(): return lax.psum(grad_shard, 'grp')]
    ppermute x0 -> x27, starting transfers between devices: none -> 48.1 us  [send(): return lax.ppermute(array, AXES, pairs)]
    all_to_all x0 -> x2, blocking collectives: none -> 33.5 us  [the longest x1 20.2 us: per_device(): lax.all_to_all(jnp.broadcast_to(block[None], (NZ, *block.shape)), 'z', 0, 0)]
    ppermute x0 -> x27, waiting for transfers between devices: none -> 25.2 us  [send(): return lax.ppermute(array, AXES, pairs)]
    pallas_call x0 -> x5, Pallas kernels: none -> 22.8 us  [call(): pl.pallas_call(kernel, out_shape=[jax.ShapeDtypeStruct(shape, dtype) for...]
    dot_general x5 -> x0, matrix products: 20.9 us -> none  [the longest x1 8.01 us: per_device(): lax.dot_general(left_rows, right_rows, (((0,), (0,)), ((), ())), preferre...]
  transfers between devices with their start and end apart: 3 -> 28, of which waited for: 3 -> 10; matrix products, arithmetic and copies ran while one was open for 0% -> 2% of each run, Pallas kernels for 0% -> 7%
where the time goes in v1:
time: 165 us
  starting transfers between devices  52.9 us (32%)
  blocking collectives  33.5 us (20%)
  waiting for transfers between devices  32 us (19%)
  Pallas kernels  22.8 us (14%)
  local copies, waits for them, and re-layouts  16.2 us (10%)
  other arithmetic  6.5 us (4%)
    ppermute x27, starting transfers between devices, send(): return lax.ppermute(array, AXES, pairs)  48.1 us
    ppermute x27, waiting for transfers between devices, send(): return lax.ppermute(array, AXES, pairs)  25.2 us
    pallas_call x5, Pallas kernels, call(): pl.pallas_call(kernel, out_shape=[jax.ShapeDtypeStruct(shape, dtype) for...  22.8 us
    all_to_all x1, blocking collectives, per_device(): lax.all_to_all(jnp.broadcast_to(block[None], (NZ, *block.shape)), 'z', 0, 0)  20.2 us
    all_to_all x1, blocking collectives, per_device(): both = jnp.sum(lax.all_to_all(both, 'z', 0, 0), 0)  13.2 us
    unnamed x49, local copies, waits for them, and re-layouts  10.4 us
    all_to_all x1, waiting for transfers between devices, per_device(): lax.all_to_all(jnp.broadcast_to(both[None], (8, *both.shape)), ('ylo', 'x...  6.84 us
    all_to_all x1, starting transfers between devices, per_device(): lax.all_to_all(jnp.broadcast_to(both[None], (8, *both.shape)), ('ylo', 'x...  4.73 us
  transfers between devices with their start and end apart: 28, of which 10 were waited for; matrix products, arithmetic and copies ran while one was open for 2% of the time, Pallas kernels for 7%

profile of v1, /device:TPU:1, one launch (start us, length us, event | category | flops | bytes accessed | tf_op | source)
XLA Modules:
  0.0 164.6 jit_solution(333315640484350471)
XLA Ops:
  1.0 3.3 %collective-permute-start.1 = (bf16[48,256]{1,0:T(8,128)(2,1)S(1)}, bf16[48,256]{1,0:T(8,128)(2,1)S(1)}, u32[]{:S(2)}, u32[]{:S(2)}) collective-permute-start(bf16[48,256]{1,0:T(8,128)(2,1)S(1)} %pad_maximum_fusion.17), channel_id=1, source_target_pairs={{0,1},{1,0},{4,5},{5,4},{8,9},{9,8},{12,13},{13,12},{16,17},{17,16... | collective-permute-start | bytes 73736 | tf_op jit(solution)/shard_map/ppermute | solution.py:31
  5.2 20.2 %all_to_all.15 = bf16[8,96,256]{2,1,0:T(8,128)(2,1)S(1)} all-to-all(bf16[8,96,256]{2,1,0:T(8,128)(2,1)S(1)} %broadcast_in_dim.90), channel_id=1, replica_groups=mesh['ylo'=2,'x'=4,'z'=8,'yhi'=2,'c'=2] {'z'}, dimensions={0} | all-to-all | bytes 786432 | tf_op jit(solution)/shard_map/all_to_all | solution.py:253
  25.5 2.8 %collective-permute-start.2 = (bf16[768,128]{1,0:T(8,128)(2,1)S(1)}, bf16[768,128]{1,0:T(8,128)(2,1)S(1)}, u32[]{:S(2)}, u32[]{:S(2)}) collective-permute-start(bf16[768,128]{1,0:T(8,128)(2,1)S(1)} %bitcast.189), channel_id=1, source_target_pairs={{0,130},{1,131},{4,134},{5,135},{8,138},{9,139},{12,142},{13,143},... | collective-permute-start | bytes 589832 | tf_op jit(solution)/shard_map/ppermute | solution.py:31
  30.7 2.2 %collective-permute-start = (bf16[384,1536]{1,0:T(8,128)(2,1)}, bf16[384,1536]{1,0:T(8,128)(2,1)S(1)}, u32[]{:S(2)}, u32[]{:S(2)}) collective-permute-start(bf16[384,1536]{1,0:T(8,128)(2,1)} %pad_maximum_fusion), channel_id=1, source_target_pairs={{0,1},{1,0},{4,5},{5,4},{8,9},{9,8},{12,13},{13,12},{16,17},{17,16... | collective-permute-start | bytes 3538952 | tf_op jit(solution)/shard_map/ppermute | solution.py:31
  36.1 1.5 collective-permute-start.5
  37.5 2.7 %collective-permute-start.7 = (bf16[768,256]{1,0:T(8,128)(2,1)}, bf16[768,256]{1,0:T(8,128)(2,1)}, u32[]{:S(2)}, u32[]{:S(2)}) collective-permute-start(bf16[768,256]{1,0:T(8,128)(2,1)} %pad_maximum_fusion.5.low_ref), channel_id=1, source_target_pairs={{0,130},{1,131},{4,134},{5,135},{8,138},{9,139},{12,142},{13,143},... | collective-permute-start | bytes 1179656 | tf_op jit(solution)/shard_map/ppermute | solution.py:31
  41.5 1.3 copy-done.5
  42.8 1.5 shard_map.46
  44.3 2.0 %collective-permute-done.6.low_ref = bf16[768,256]{1,0:T(8,128)(2,1)} collective-permute-done((bf16[768,256]{1,0:T(8,128)(2,1)}, bf16[768,256]{1,0:T(8,128)(2,1)}, u32[]{:S(2)}, u32[]{:S(2)}) %collective-permute-start.6) | collective-permute-done | bytes 393248 | tf_op jit(solution)/shard_map/ppermute | solution.py:31
  50.2 2.7 %collective-permute-start.11 = (bf16[384,256]{1,0:T(8,128)(2,1)S(1)}, bf16[384,256]{1,0:T(8,128)(2,1)S(1)}, u32[]{:S(2)}, u32[]{:S(2)}) collective-permute-start(bf16[384,256]{1,0:T(8,128)(2,1)S(1)} %slice.224), channel_id=1, source_target_pairs={{0,130},{1,131},{4,134},{5,135},{8,138},{9,139},{12,142},{13,143},... | collective-permute-start | bytes 589832 | tf_op jit(solution)/shard_map/ppermute | solution.py:31
  52.9 2.7 %collective-permute-start.9 = (bf16[768,128]{1,0:T(8,128)(2,1)S(1)}, bf16[768,128]{1,0:T(8,128)(2,1)S(1)}, u32[]{:S(2)}, u32[]{:S(2)}) collective-permute-start(bf16[768,128]{1,0:T(8,128)(2,1)S(1)} %slice.222), channel_id=1, source_target_pairs={{0,96},{1,97},{4,100},{5,101},{8,104},{9,105},{12,108},{13,109},{1... | collective-permute-start | bytes 589832 | tf_op jit(solution)/shard_map/ppermute | solution.py:31
  55.5 5.1 %shard_map.47 = (bf16[1536,640]{1,0:T(8,128)(2,1)S(1)}, f32[768,640]{1,0:T(8,128)S(1)}, f32[384,640]{1,0:T(8,128)S(1)}, bf16[384,640]{1,0:T(8,128)(2,1)S(1)}, f3...) custom-call(s32[1]{0:T(128)} %bitcast.11.flag_ref, bf16[768,1536]{1,0:T(8,128)(2,1)S(1)} %get-tuple-element.78.tokens_ref, ...), custom_call_target="tpu_custom_call" | custom-call | flops 2264924160 | bytes 8000000 | tf_op jit(solution)/shard_map/pallas_call | solution.py:223
  60.7 1.3 copy-done.10
  62.8 5.1 %shard_map.48 = (bf16[1536,384]{1,0:T(8,128)(2,1)S(1)}, f32[768,384]{1,0:T(8,128)S(1)}, f32[384,384]{1,0:T(8,128)S(1)}, bf16[384,384]{1,0:T(8,128)(2,1)S(1)}, f32[768,128]{1,0:T(8,128)}, /*index=5*/f32[1536,384]{1,0:T(8,128)}) custom-call(s32[1]{0:T(128)} %bitcast.3.flag_ref, bf16[768,1536]{1,0:T(8,128)(2,1)S(1)} %get-tuple-element.78.tokens_ref, ...), custom_call_target="tpu_custom_call" | custom-call | flops 1358954496 | bytes 8000000 | tf_op jit(solution)/shard_map/pallas_call | solution.py:223
  70.5 5.4 %collective-permute-start.12 = (f32[1536,384]{1,0:T(8,128)}, f32[1536,384]{1,0:T(8,128)}, u32[]{:S(2)}, u32[]{:S(2)}) collective-permute-start(f32[1536,384]{1,0:T(8,128)} %get-tuple-element.101.part_ref), channel_id=1, source_target_pairs={{0,1},{1,0},{4,5},{5,4},{8,9},{9,8},{12,13},{13,12},{16,17},{17,16... | collective-permute-start | bytes 7077896 | tf_op jit(solution)/shard_map/ppermute | solution.py:31
  75.9 5.1 %collective-permute-done.13.logit_in_ref = f32[768,128]{1,0:T(8,128)} collective-permute-done((f32[768,128]{1,0:T(8,128)}, f32[768,128]{1,0:T(8,128)}, u32[]{:S(2)}, u32[]{:S(2)}) %collective-permute-start.13) | collective-permute-done | bytes 393248 | tf_op jit(solution)/shard_map/ppermute | solution.py:31
  81.0 1.3 copy-done.3
  84.3 6.1 %shard_map.49 = (f32[768,256]{1,0:T(8,128)S(1)}, f32[768,256]{1,0:T(8,128)S(1)}, f32[1536,128]{1,0:T(8,128)S(1)}, f32[16,128]{1,0:T(8,128)S(1)}, bf16[1536,384]{...) custom-call(bf16[1536,768]{1,0:T(8,128)(2,1)S(1)} %get-tuple-element.77.tokens_t_ref, ...), custom_call_target="tpu_custom_call" | custom-call | flops 1811939328 | bytes 8000000 | tf_op jit(solution)/shard_map/pallas_call | solution.py:223
  91.0 2.7 %collective-permute-start.17 = (f16[400,256]{1,0:T(8,128)(2,1)S(1)}, f16[400,256]{1,0:T(8,128)(2,1)S(1)}, u32[]{:S(2)}, u32[]{:S(2)}) collective-permute-start(f16[400,256]{1,0:T(8,128)(2,1)S(1)} %get-tuple-element.124), channel_id=1, source_target_pairs={{0,130},{1,131},{4,134},{5,135},{8,138},{9,139},{12,142},{13,143},... | collective-permute-start | bytes 614408 | tf_op jit(solution)/shard_map/ppermute | solution.py:31
  93.7 2.7 %collective-permute-start.15 = (f16[784,128]{1,0:T(8,128)(2,1)S(1)}, f16[784,128]{1,0:T(8,128)(2,1)S(1)}, u32[]{:S(2)}, u32[]{:S(2)}) collective-permute-start(f16[784,128]{1,0:T(8,128)(2,1)S(1)} %get-tuple-element.122), channel_id=1, source_target_pairs={{0,96},{1,97},{4,100},{5,101},{8,104},{9,105},{12,108},{13,109},{1... | collective-permute-start | bytes 602120 | tf_op jit(solution)/shard_map/ppermute | solution.py:31
  96.4 4.9 %shard_map.50 = (f32[1536,128]{1,0:T(8,128)S(1)}, f32[1536,128]{1,0:T(8,128)S(1)}, f32[1536,128]{1,0:T(8,128)S(1)}, f32[768,256]{1,0:T(8,128)S(1)}, f32[768,256]{1,0:T(8,128)S(1)}, /*index=5*/f32[16,128]{1,0:T(8,128)S(1)}) custom-call(bf16[1536,768]{1,0:T(8,128)(2,1)S(1)} %get-tuple-element.77.tokens_t_ref, ...), custom_call_target="tpu_custom_call" | custom-call | flops 3019898880 | bytes 8000000 | tf_op jit(solution)/shard_map/pallas_call | solution.py:223
  102.9 2.7 %collective-permute-start.21 = (f16[784,256]{1,0:T(8,128)(2,1)S(1)}, f16[784,256]{1,0:T(8,128)(2,1)S(1)}, u32[]{:S(2)}, u32[]{:S(2)}) collective-permute-start(f16[784,256]{1,0:T(8,128)(2,1)S(1)} %pad_maximum_fusion.2), channel_id=1, source_target_pairs={{0,130},{1,131},{4,134},{5,135},{8,138},{9,139},{12,142},{13,143},... | collective-permute-start | bytes 1204232 | tf_op jit(solution)/shard_map/ppermute | solution.py:31
  105.5 2.7 %collective-permute-start.19 = (f16[1552,128]{1,0:T(8,128)(2,1)S(1)}, f16[1552,128]{1,0:T(8,128)(2,1)S(1)}, u32[]{:S(2)}, u32[]{:S(2)}) collective-permute-start(f16[1552,128]{1,0:T(8,128)(2,1)S(1)} %pad_maximum_fusion.4), channel_id=1, source_target_pairs={{0,96},{1,97},{4,100},{5,101},{8,104},{9,105},{12,108},{13,109},{1... | collective-permute-start | bytes 1191944 | tf_op jit(solution)/shard_map/ppermute | solution.py:31
  108.2 7.2 %collective-permute-done.18 = f16[1552,128]{1,0:T(8,128)(2,1)S(1)} collective-permute-done((f16[1552,128]{1,0:T(8,128)(2,1)S(1)}, f16[1552,128]{1,0:T(8,128)(2,1)S(1)}, u32[]{:S(2)}, u32[]{:S(2)}) %collective-permute-start.18) | collective-permute-done | bytes 397344 | tf_op jit(solution)/shard_map/ppermute | solution.py:31
  116.7 5.4 %collective-permute-done.22 = f16[784,128]{1,0:T(8,128)(2,1)S(1)} collective-permute-done((f16[784,128]{1,0:T(8,128)(2,1)S(1)}, f16[784,128]{1,0:T(8,128)(2,1)S(1)}, u32[]{:S(2)}, u32[]{:S(2)}) %collective-permute-start.22) | collective-permute-done | bytes 200736 | tf_op jit(solution)/shard_map/ppermute | solution.py:31
  122.4 2.5 %collective-permute-start.25 = (f32[8,48,128]{2,1,0:T(8,128)S(1)}, f32[8,48,128]{2,1,0:T(8,128)S(1)}, u32[]{:S(2)}, u32[]{:S(2)}) collective-permute-start(f32[8,48,128]{2,1,0:T(8,128)S(1)} %fusion.9), channel_id=1, source_target_pairs={{0,96},{1,97},{4,100},{5,101},{8,104},{9,105},{12,108},{13,109},{1... | collective-permute-start | bytes 589832 | tf_op jit(solution)/shard_map/ppermute | solution.py:31
  124.9 2.0 %collective-permute-done.24 = f32[8,48,128]{2,1,0:T(8,128)S(1)} collective-permute-done((f32[8,48,128]{2,1,0:T(8,128)S(1)}, f32[8,48,128]{2,1,0:T(8,128)S(1)}, u32[]{:S(2)}, u32[]{:S(2)}) %collective-permute-start.24) | collective-permute-done | bytes 196640 | tf_op jit(solution)/shard_map/ppermute | solution.py:31
  126.9 1.3 collective-permute-done.25
  128.4 13.2 %all_to_all.16 = f32[8,48,256]{2,1,0:T(8,128)S(1)} all-to-all(f32[8,48,256]{2,1,0:T(8,128)S(1)} %pad_maximum_fusion.7), channel_id=1, replica_groups=mesh['ylo'=2,'x'=4,'z'=8,'yhi'=2,'c'=2] {'z'}, dimensions={0} | all-to-all | bytes 786432 | tf_op jit(solution)/shard_map/all_to_all | solution.py:386
  142.4 4.7 %all-to-all-start.2 = ((f32[8,48,256]{2,1,0:T(8,128)}), f32[8,48,256]{2,1,0:T(8,128)S(1)}, u32[]{:S(2)}, u32[]{:S(2)}) async-start(f32[8,48,256]{2,1,0:T(8,128)} %broadcast_in_dim.109), calls=%async_computation.2 | async-start | bytes 786432 | tf_op jit(solution)/shard_map/all_to_all | solution.py:388
  147.1 6.8 %all-to-all-done.2 = f32[8,48,256]{2,1,0:T(8,128)S(1)} async-done(((f32[8,48,256]{2,1,0:T(8,128)}), f32[8,48,256]{2,1,0:T(8,128)S(1)}, u32[]{:S(2)}, u32[]{:S(2)}) %all-to-all-start.2) | async-done | bytes 393248 | tf_op jit(solution)/shard_map/all_to_all | solution.py:388
  154.2 8.6 %collective-permute-start.26 = (f32[48,1024]{1,0:T(8,128)S(1)}, f32[48,1024]{1,0:T(8,128)S(1)}, u32[]{:S(2)}, u32[]{:S(2)}) collective-permute-start(f32[48,1024]{1,0:T(8,128)S(1)} %broadcast_select_fusion.7), channel_id=1, source_target_pairs={{0,1},{1,0},{4,5},{5,4},{8,9},{9,8},{12,13},{13,12},{16,17},{17,16... | collective-permute-start | bytes 589832 | tf_op jit(solution)/shard_map/ppermute | solution.py:31
  (161 shorter events, 24.3 us)
Async XLA Ops:
  0.0 29.6 %copy-start = (bf16[1,192,1536]{2,1,0:T(8,128)(2,1)S(1)}, bf16[1,192,1536]{2,1,0:T(8,128)(2,1)}, u32[]{:S(2)}) copy-start(bf16[1,192,1536]{2,1,0:T(8,128)(2,1)} %param.4) | copy-start | bytes 1769476
  0.0 29.6 %copy-start.1 = (bf16[1,192,1536]{2,1,0:T(8,128)(2,1)S(1)}, bf16[1,192,1536]{2,1,0:T(8,128)(2,1)}, u32[]{:S(2)}) copy-start(bf16[1,192,1536]{2,1,0:T(8,128)(2,1)} %param.5) | copy-start | bytes 1769476
  1.0 4.2 %collective-permute-start.1 = (bf16[48,256]{1,0:T(8,128)(2,1)S(1)}, bf16[48,256]{1,0:T(8,128)(2,1)S(1)}, u32[]{:S(2)}, u32[]{:S(2)}) collective-permute-start(bf16[48,256]{1,0:T(8,128)(2,1)S(1)} %pad_maximum_fusion.17), channel_id=1, source_target_pairs={{0,1},{1,0},{4,5},{5,4},{8,9},{9,8},{12,13},{13,12},{16,17},{17,16... | collective-permute-start | bytes 73736 | tf_op jit(solution)/shard_map/ppermute | solution.py:31
  25.5 7.4 %collective-permute-start.2 = (bf16[768,128]{1,0:T(8,128)(2,1)S(1)}, bf16[768,128]{1,0:T(8,128)(2,1)S(1)}, u32[]{:S(2)}, u32[]{:S(2)}) collective-permute-start(bf16[768,128]{1,0:T(8,128)(2,1)S(1)} %bitcast.189), channel_id=1, source_target_pairs={{0,130},{1,131},{4,134},{5,135},{8,138},{9,139},{12,142},{13,143},... | collective-permute-start | bytes 589832 | tf_op jit(solution)/shard_map/ppermute | solution.py:31
  28.4 4.8 %collective-permute-start.3 = (bf16[768,128]{1,0:T(8,128)(2,1)S(1)}, bf16[768,128]{1,0:T(8,128)(2,1)S(1)}, u32[]{:S(2)}, u32[]{:S(2)}) collective-permute-start(bf16[768,128]{1,0:T(8,128)(2,1)S(1)} %bitcast.187), channel_id=1, source_target_pairs={{0,32},{1,33},{4,36},{5,37},{8,40},{9,41},{12,44},{13,45},{16,48},... | collective-permute-start | bytes 589832 | tf_op jit(solution)/shard_map/ppermute | solution.py:31
  30.7 9.5 %copy-start.18 = (f32[2048]{0:T(1024)S(1)}, f32[2048]{0:T(1024)}, u32[]{:S(2)}) copy-start(f32[2048]{0:T(1024)} %param.7) | copy-start | bytes 24580
  30.7 9.8 %collective-permute-start = (bf16[384,1536]{1,0:T(8,128)(2,1)}, bf16[384,1536]{1,0:T(8,128)(2,1)S(1)}, u32[]{:S(2)}, u32[]{:S(2)}) collective-permute-start(bf16[384,1536]{1,0:T(8,128)(2,1)} %pad_maximum_fusion), channel_id=1, source_target_pairs={{0,1},{1,0},{4,5},{5,4},{8,9},{9,8},{12,13},{13,12},{16,17},{17,16... | collective-permute-start | bytes 3538952 | tf_op jit(solution)/shard_map/ppermute | solution.py:31
  34.8 9.5 %collective-permute-start.4 = (bf16[1536,128]{1,0:T(8,128)(2,1)}, bf16[1536,128]{1,0:T(8,128)(2,1)}, u32[]{:S(2)}, u32[]{:S(2)}) collective-permute-start(bf16[1536,128]{1,0:T(8,128)(2,1)} %bitcast.10.own_ref), channel_id=1, source_target_pairs={{0,32},{1,33},{4,36},{5,37},{8,40},{9,41},{12,44},{13,45},{16,48},... | collective-permute-start | bytes 1179656 | tf_op jit(solution)/shard_map/ppermute | solution.py:31
  36.1 8.3 %collective-permute-start.5 = (bf16[1536,128]{1,0:T(8,128)(2,1)}, bf16[1536,128]{1,0:T(8,128)(2,1)}, u32[]{:S(2)}, u32[]{:S(2)}) collective-permute-start(bf16[1536,128]{1,0:T(8,128)(2,1)} %bitcast.10.own_ref), channel_id=1, source_target_pairs={{0,96},{1,97},{4,100},{5,101},{8,104},{9,105},{12,108},{13,109},{1... | collective-permute-start | bytes 1179656 | tf_op jit(solution)/shard_map/ppermute | solution.py:31
  37.5 8.8 %collective-permute-start.6 = (bf16[768,256]{1,0:T(8,128)(2,1)}, bf16[768,256]{1,0:T(8,128)(2,1)}, u32[]{:S(2)}, u32[]{:S(2)}) collective-permute-start(bf16[768,256]{1,0:T(8,128)(2,1)} %pad_maximum_fusion.5.low_ref), channel_id=1, source_target_pairs={{0,128},{1,129},{4,132},{5,133},{8,136},{9,137},{12,140},{13,141},... | collective-permute-start | bytes 1179656 | tf_op jit(solution)/shard_map/ppermute | solution.py:31
  37.5 8.8 %collective-permute-start.7 = (bf16[768,256]{1,0:T(8,128)(2,1)}, bf16[768,256]{1,0:T(8,128)(2,1)}, u32[]{:S(2)}, u32[]{:S(2)}) collective-permute-start(bf16[768,256]{1,0:T(8,128)(2,1)} %pad_maximum_fusion.5.low_ref), channel_id=1, source_target_pairs={{0,130},{1,131},{4,134},{5,135},{8,138},{9,139},{12,142},{13,143},... | collective-permute-start | bytes 1179656 | tf_op jit(solution)/shard_map/ppermute | solution.py:31
  50.1 12.6 %collective-permute-start.10 = (bf16[384,256]{1,0:T(8,128)(2,1)S(1)}, bf16[384,256]{1,0:T(8,128)(2,1)S(1)}, u32[]{:S(2)}, u32[]{:S(2)}) collective-permute-start(bf16[384,256]{1,0:T(8,128)(2,1)S(1)} %slice.223), channel_id=1, source_target_pairs={{0,128},{1,129},{4,132},{5,133},{8,136},{9,137},{12,140},{13,141},... | collective-permute-start | bytes 589832 | tf_op jit(solution)/shard_map/ppermute | solution.py:31
  50.2 12.6 %collective-permute-start.11 = (bf16[384,256]{1,0:T(8,128)(2,1)S(1)}, bf16[384,256]{1,0:T(8,128)(2,1)S(1)}, u32[]{:S(2)}, u32[]{:S(2)}) collective-permute-start(bf16[384,256]{1,0:T(8,128)(2,1)S(1)} %slice.224), channel_id=1, source_target_pairs={{0,130},{1,131},{4,134},{5,135},{8,138},{9,139},{12,142},{13,143},... | collective-permute-start | bytes 589832 | tf_op jit(solution)/shard_map/ppermute | solution.py:31
  52.8 9.9 %collective-permute-start.8 = (bf16[768,128]{1,0:T(8,128)(2,1)S(1)}, bf16[768,128]{1,0:T(8,128)(2,1)S(1)}, u32[]{:S(2)}, u32[]{:S(2)}) collective-permute-start(bf16[768,128]{1,0:T(8,128)(2,1)S(1)} %slice.221), channel_id=1, source_target_pairs={{0,32},{1,33},{4,36},{5,37},{8,40},{9,41},{12,44},{13,45},{16,48},... | collective-permute-start | bytes 589832 | tf_op jit(solution)/shard_map/ppermute | solution.py:31
  52.9 9.9 %collective-permute-start.9 = (bf16[768,128]{1,0:T(8,128)(2,1)S(1)}, bf16[768,128]{1,0:T(8,128)(2,1)S(1)}, u32[]{:S(2)}, u32[]{:S(2)}) collective-permute-start(bf16[768,128]{1,0:T(8,128)(2,1)S(1)} %slice.222), channel_id=1, source_target_pairs={{0,96},{1,97},{4,100},{5,101},{8,104},{9,105},{12,108},{13,109},{1... | collective-permute-start | bytes 589832 | tf_op jit(solution)/shard_map/ppermute | solution.py:31
  70.5 10.5 %collective-permute-start.12 = (f32[1536,384]{1,0:T(8,128)}, f32[1536,384]{1,0:T(8,128)}, u32[]{:S(2)}, u32[]{:S(2)}) collective-permute-start(f32[1536,384]{1,0:T(8,128)} %get-tuple-element.101.part_ref), channel_id=1, source_target_pairs={{0,1},{1,0},{4,5},{5,4},{8,9},{9,8},{12,13},{13,12},{16,17},{17,16... | collective-permute-start | bytes 7077896 | tf_op jit(solution)/shard_map/ppermute | solution.py:31
  75.9 5.1 %collective-permute-start.13 = (f32[768,128]{1,0:T(8,128)}, f32[768,128]{1,0:T(8,128)}, u32[]{:S(2)}, u32[]{:S(2)}) collective-permute-start(f32[768,128]{1,0:T(8,128)} %get-tuple-element.102.logit_ref), channel_id=1, source_target_pairs={{0,1},{1,0},{4,5},{5,4},{8,9},{9,8},{12,13},{13,12},{16,17},{17,16... | collective-permute-start | bytes 1179656 | tf_op jit(solution)/shard_map/ppermute | solution.py:31
  90.4 6.0 %copy-start.15 = (f32[384,640]{1,0:T(8,128)S(1)}, f32[384,640]{1,0:T(8,128)}, u32[]{:S(2)}) copy-start(f32[384,640]{1,0:T(8,128)} %copy-done.14) | copy-start | bytes 2949124
  90.9 10.5 %collective-permute-start.16 = (f16[400,256]{1,0:T(8,128)(2,1)S(1)}, f16[400,256]{1,0:T(8,128)(2,1)S(1)}, u32[]{:S(2)}, u32[]{:S(2)}) collective-permute-start(f16[400,256]{1,0:T(8,128)(2,1)S(1)} %get-tuple-element.123), channel_id=1, source_target_pairs={{0,128},{1,129},{4,132},{5,133},{8,136},{9,137},{12,140},{13,141},... | collective-permute-start | bytes 614408 | tf_op jit(solution)/shard_map/ppermute | solution.py:31
  91.0 10.4 %collective-permute-start.17 = (f16[400,256]{1,0:T(8,128)(2,1)S(1)}, f16[400,256]{1,0:T(8,128)(2,1)S(1)}, u32[]{:S(2)}, u32[]{:S(2)}) collective-permute-start(f16[400,256]{1,0:T(8,128)(2,1)S(1)} %get-tuple-element.124), channel_id=1, source_target_pairs={{0,130},{1,131},{4,134},{5,135},{8,138},{9,139},{12,142},{13,143},... | collective-permute-start | bytes 614408 | tf_op jit(solution)/shard_map/ppermute | solution.py:31
  93.7 7.7 %collective-permute-start.14 = (f16[784,128]{1,0:T(8,128)(2,1)S(1)}, f16[784,128]{1,0:T(8,128)(2,1)S(1)}, u32[]{:S(2)}, u32[]{:S(2)}) collective-permute-start(f16[784,128]{1,0:T(8,128)(2,1)S(1)} %get-tuple-element.121), channel_id=1, source_target_pairs={{0,32},{1,33},{4,36},{5,37},{8,40},{9,41},{12,44},{13,45},{16,48},... | collective-permute-start | bytes 602120 | tf_op jit(solution)/shard_map/ppermute | solution.py:31
  93.7 7.7 %collective-permute-start.15 = (f16[784,128]{1,0:T(8,128)(2,1)S(1)}, f16[784,128]{1,0:T(8,128)(2,1)S(1)}, u32[]{:S(2)}, u32[]{:S(2)}) collective-permute-start(f16[784,128]{1,0:T(8,128)(2,1)S(1)} %get-tuple-element.122), channel_id=1, source_target_pairs={{0,96},{1,97},{4,100},{5,101},{8,104},{9,105},{12,108},{13,109},{1... | collective-permute-start | bytes 602120 | tf_op jit(solution)/shard_map/ppermute | solution.py:31
  102.8 12.6 %collective-permute-start.20 = (f16[784,256]{1,0:T(8,128)(2,1)S(1)}, f16[784,256]{1,0:T(8,128)(2,1)S(1)}, u32[]{:S(2)}, u32[]{:S(2)}) collective-permute-start(f16[784,256]{1,0:T(8,128)(2,1)S(1)} %pad_maximum_fusion.1), channel_id=1, source_target_pairs={{0,128},{1,129},{4,132},{5,133},{8,136},{9,137},{12,140},{13,141},... | collective-permute-start | bytes 1204232 | tf_op jit(solution)/shard_map/ppermute | solution.py:31
  102.9 12.5 %collective-permute-start.21 = (f16[784,256]{1,0:T(8,128)(2,1)S(1)}, f16[784,256]{1,0:T(8,128)(2,1)S(1)}, u32[]{:S(2)}, u32[]{:S(2)}) collective-permute-start(f16[784,256]{1,0:T(8,128)(2,1)S(1)} %pad_maximum_fusion.2), channel_id=1, source_target_pairs={{0,130},{1,131},{4,134},{5,135},{8,138},{9,139},{12,142},{13,143},... | collective-permute-start | bytes 1204232 | tf_op jit(solution)/shard_map/ppermute | solution.py:31
  105.5 9.8 %collective-permute-start.18 = (f16[1552,128]{1,0:T(8,128)(2,1)S(1)}, f16[1552,128]{1,0:T(8,128)(2,1)S(1)}, u32[]{:S(2)}, u32[]{:S(2)}) collective-permute-start(f16[1552,128]{1,0:T(8,128)(2,1)S(1)} %pad_maximum_fusion.3), channel_id=1, source_target_pairs={{0,32},{1,33},{4,36},{5,37},{8,40},{9,41},{12,44},{13,45},{16,48},... | collective-permute-start | bytes 1191944 | tf_op jit(solution)/shard_map/ppermute | solution.py:31
  105.5 9.8 %collective-permute-start.19 = (f16[1552,128]{1,0:T(8,128)(2,1)S(1)}, f16[1552,128]{1,0:T(8,128)(2,1)S(1)}, u32[]{:S(2)}, u32[]{:S(2)}) collective-permute-start(f16[1552,128]{1,0:T(8,128)(2,1)S(1)} %pad_maximum_fusion.4), channel_id=1, source_target_pairs={{0,96},{1,97},{4,100},{5,101},{8,104},{9,105},{12,108},{13,109},{1... | collective-permute-start | bytes 1191944 | tf_op jit(solution)/shard_map/ppermute | solution.py:31
  116.2 5.9 %collective-permute-start.22 = (f16[784,128]{1,0:T(8,128)(2,1)S(1)}, f16[784,128]{1,0:T(8,128)(2,1)S(1)}, u32[]{:S(2)}, u32[]{:S(2)}) collective-permute-start(f16[784,128]{1,0:T(8,128)(2,1)S(1)} %pad_maximum_fusion.13), channel_id=1, source_target_pairs={{0,130},{1,131},{4,134},{5,135},{8,138},{9,139},{12,142},{13,143},... | collective-permute-start | bytes 602120 | tf_op jit(solution)/shard_map/ppermute | solution.py:31
  116.7 5.4 %collective-permute-start.23 = (f16[784,128]{1,0:T(8,128)(2,1)S(1)}, f16[784,128]{1,0:T(8,128)(2,1)S(1)}, u32[]{:S(2)}, u32[]{:S(2)}) collective-permute-start(f16[784,128]{1,0:T(8,128)(2,1)S(1)} %pad_maximum_fusion.14), channel_id=1, source_target_pairs={{0,32},{1,33},{4,36},{5,37},{8,40},{9,41},{12,44},{13,45},{16,48},... | collective-permute-start | bytes 602120 | tf_op jit(solution)/shard_map/ppermute | solution.py:31
  122.3 4.6 %collective-permute-start.24 = (f32[8,48,128]{2,1,0:T(8,128)S(1)}, f32[8,48,128]{2,1,0:T(8,128)S(1)}, u32[]{:S(2)}, u32[]{:S(2)}) collective-permute-start(f32[8,48,128]{2,1,0:T(8,128)S(1)} %select_bitcast_fusion), channel_id=1, source_target_pairs={{0,128},{1,129},{4,132},{5,133},{8,136},{9,137},{12,140},{13,141},... | collective-permute-start | bytes 589832 | tf_op jit(solution)/shard_map/ppermute | solution.py:31
  122.4 5.8 %collective-permute-start.25 = (f32[8,48,128]{2,1,0:T(8,128)S(1)}, f32[8,48,128]{2,1,0:T(8,128)S(1)}, u32[]{:S(2)}, u32[]{:S(2)}) collective-permute-start(f32[8,48,128]{2,1,0:T(8,128)S(1)} %fusion.9), channel_id=1, source_target_pairs={{0,96},{1,97},{4,100},{5,101},{8,104},{9,105},{12,108},{13,109},{1... | collective-permute-start | bytes 589832 | tf_op jit(solution)/shard_map/ppermute | solution.py:31
  142.4 11.6 %all-to-all-start.2 = ((f32[8,48,256]{2,1,0:T(8,128)}), f32[8,48,256]{2,1,0:T(8,128)S(1)}, u32[]{:S(2)}, u32[]{:S(2)}) async-start(f32[8,48,256]{2,1,0:T(8,128)} %broadcast_in_dim.109), calls=%async_computation.2 | async-start | bytes 786432 | tf_op jit(solution)/shard_map/all_to_all | solution.py:388
  154.2 9.6 %collective-permute-start.26 = (f32[48,1024]{1,0:T(8,128)S(1)}, f32[48,1024]{1,0:T(8,128)S(1)}, u32[]{:S(2)}, u32[]{:S(2)}) collective-permute-start(f32[48,1024]{1,0:T(8,128)S(1)} %broadcast_select_fusion.7), channel_id=1, source_target_pairs={{0,1},{1,0},{4,5},{5,4},{8,9},{9,8},{12,13},{13,12},{16,17},{17,16... | collective-permute-start | bytes 589832 | tf_op jit(solution)/shard_map/ppermute | solution.py:31
  (15 other events, 38.4 us)

commit v2 on v1

--- a/solution.py
+++ b/solution.py
@@ -13,7 +13,7 @@
 NX, NY, NZ = 4, 4, 8
 AXES = ("ylo", "x", "z", "yhi", "c")
 BF16, F16, F32 = jnp.bfloat16, jnp.float16, jnp.float32
-VMEM_BYTES = 20 * 1024 * 1024
+VMEM_BYTES = 26 * 1024 * 1024
 
 
 def flat_index(x, y, z, c):
@@ -72,14 +72,30 @@
     return lax.dot_general(a, b, (((1,), (1,)), ((), ())), preferred_element_type=F32)
 
 
+def flat(block):
+    return block.reshape(block.shape[0] * block.shape[1], block.shape[2])
+
+
+def fetched(sems, *pairs):
+    copies = [pltpu.make_async_copy(source, target, sems.at[k]) for k, (source, target) in enumerate(pairs)]
+    for copy in copies:
+        copy.start()
+    return copies
+
+
+def done(copies):
+    for copy in copies:
+        copy.wait()
+
+
 def forward_tiles(tokens_ref, w_ref, score_ref, slope_ref, curve_ref, lifted_ref, logit_ref, first):
     n = tokens_ref.shape[0] // 2
     for kind in (0, 1):
         rows = slice(kind * n, kind * n + n)
         total = jnp.zeros((n, 128), F32) if first is None else first[rows, :]
-        for start, width in column_tiles(w_ref.shape[1]):
+        for start, width in column_tiles(w_ref.shape[2]):
             cols = slice(start, start + width)
-            preact = jnp.dot(tokens_ref[rows, :], w_ref[:, cols], preferred_element_type=F32)
+            preact = jnp.dot(tokens_ref[rows, :], flat(w_ref[:, :, cols]), preferred_element_type=F32)
             score = score_ref[:, cols]
             squash = jax.nn.sigmoid(preact)
             rest = 1.0 - squash
@@ -95,74 +111,107 @@
 
 
 def pull_back(w_ref, lifted_ref, part_ref, so_far):
-    for start in range(0, w_ref.shape[0], 512):
-        rows = slice(start, start + 512)
-        value = nt(w_ref[rows, :], lifted_ref[...])
+    height = 2 * w_ref.shape[1]
+    for k in range(w_ref.shape[0] // 2):
+        rows = slice(k * height, k * height + height)
+        value = nt(flat(w_ref[2 * k : 2 * k + 2]), lifted_ref[...])
         part_ref[rows, :] = value if so_far is None else so_far[rows, :] + value
 
 
-def place_pair(w_ref, column, low_ref, high_ref, swap):
-    width = low_ref.shape[1]
-    turn = w_ref.shape[0] // (2 * NZ)
-    for z in range(NZ):
-        rows = slice(z * turn, z * turn + turn)
-        low, high = low_ref[rows, :], high_ref[rows, :]
-        w_ref[2 * z * turn : 2 * z * turn + turn, column : column + width] = jnp.where(swap, high, low)
-        w_ref[2 * z * turn + turn : 2 * z * turn + 2 * turn, column : column + width] = jnp.where(swap, low, high)
-
-
-def first_kernel(flag_ref, tokens_ref, own_ref, left_ref, right_ref, low_ref, high_ref, score_ref,
-                 w_ref, slope_ref, curve_ref, lifted_ref, logit_ref, part_ref):
-    w_ref[:, 0:128] = own_ref[...]
-    w_ref[:, 128:256] = left_ref[...]
-    w_ref[:, 256:384] = right_ref[...]
-    place_pair(w_ref, 384, low_ref, high_ref, flag_ref[0] == 1)
-    forward_tiles(tokens_ref, w_ref, score_ref, slope_ref, curve_ref, lifted_ref, logit_ref, None)
-    pull_back(w_ref, lifted_ref, part_ref, None)
-
-
-def tokens_kernel(flag_ref, fake_ref, real_ref, other_ref, tokens_ref, tokens_t_ref, peak_ref):
-    tok = fake_ref.shape[0]
+def turn_of(w_ref, which, start, width):
+    height = w_ref.shape[1] // 2
+    return w_ref.at[:, pl.ds(pl.multiple_of(which * height, 16), height), pl.ds(start, width)]
+
+
+def tokens_kernel(flag_ref, fake_hbm, real_hbm, other_hbm, tokens_hbm, tokens_t_hbm, peak_ref,
+                  own_ref, other_ref, tokens_ref, tokens_t_ref, sems):
+    tok = fake_hbm.shape[0]
+    done(
+        fetched(
+            sems,
+            (fake_hbm, own_ref.at[0:tok, :]),
+            (real_hbm, own_ref.at[tok : 2 * tok, :]),
+            (other_hbm, other_ref),
+        )
+    )
     first = flag_ref[0] == 0
-    for kind, own in enumerate((fake_ref, real_ref)):
-        mine, theirs = own[...], other_ref[kind * tok : kind * tok + tok, :]
+    for kind in (0, 1):
+        mine, theirs = (ref[kind * tok : kind * tok + tok, :] for ref in (own_ref, other_ref))
         start = 2 * kind * tok
         tokens_ref[start : start + tok, :] = jnp.where(first, mine, theirs)
         tokens_ref[start + tok : start + 2 * tok, :] = jnp.where(first, theirs, mine)
         peak = peak_of(tokens_ref[start : start + 2 * tok, :])
         peak_ref[8 * kind : 8 * kind + 8, :] = jnp.broadcast_to(peak, (8, 128))
     tokens_t_ref[...] = tokens_ref[...].T
-
-
-def second_kernel(flag_ref, tokens_ref, low_ref, high_top_ref, high_bottom_ref, across_top_ref, across_bottom_ref,
-                  score_ref, logit_in_ref, part_in_ref,
-                  w_ref, slope_ref, curve_ref, lifted_ref, logit_ref, part_ref, high_ref):
-    top = high_top_ref.shape[0]
-    high_ref[0:top, :] = high_top_ref[...]
-    high_ref[top : 2 * top, :] = high_bottom_ref[...]
-    place_pair(w_ref, 0, low_ref, high_ref, flag_ref[0] == 1)
-    top = across_top_ref.shape[0]
-    w_ref[0:top, 256:384] = across_top_ref[...]
-    w_ref[top : 2 * top, 256:384] = across_bottom_ref[...]
+    done(fetched(sems, (tokens_ref, tokens_hbm), (tokens_t_ref, tokens_t_hbm)))
+
+
+def first_kernel(flag_ref, tokens_hbm, own_hbm, left_hbm, right_hbm, low_hbm, high_hbm, score_ref,
+                 w_hbm, slope_hbm, curve_hbm, lifted_hbm, logit_hbm, part_hbm,
+                 w_ref, slope_ref, curve_ref, lifted_ref, logit_ref, part_ref, tokens_ref, sems, out_sems):
+    done(
+        fetched(
+            sems,
+            (tokens_hbm, tokens_ref),
+            (own_hbm, w_ref.at[:, :, pl.ds(0, 128)]),
+            (left_hbm, w_ref.at[:, :, pl.ds(128, 128)]),
+            (right_hbm, w_ref.at[:, :, pl.ds(256, 128)]),
+            (low_hbm, turn_of(w_ref, flag_ref[0], 384, 256)),
+            (high_hbm, turn_of(w_ref, 1 - flag_ref[0], 384, 256)),
+        )
+    )
+    forward_tiles(tokens_ref, w_ref, score_ref, slope_ref, curve_ref, lifted_ref, logit_ref, None)
+    out = fetched(
+        out_sems,
+        (w_ref, w_hbm), (slope_ref, slope_hbm), (curve_ref, curve_hbm), (lifted_ref, lifted_hbm), (logit_ref, logit_hbm),
+    )
+    pull_back(w_ref, lifted_ref, part_ref, None)
+    done(out)
+    done(fetched(sems, (part_ref, part_hbm)))
+
+
+def second_kernel(flag_ref, tokens_hbm, low_hbm, high_hbm, across_hbm, score_ref, logit_in_hbm, part_in_hbm,
+                  w_hbm, slope_hbm, curve_hbm, lifted_hbm, logit_hbm, part_hbm,
+                  w_ref, slope_ref, curve_ref, lifted_ref, logit_ref, part_ref, tokens_ref, logit_in_ref, part_in_ref,
+                  sems, out_sems):
+    copies = fetched(
+        sems,
+        (tokens_hbm, tokens_ref),
+        (low_hbm, turn_of(w_ref, flag_ref[0], 0, 256)),
+        (high_hbm, turn_of(w_ref, 1 - flag_ref[0], 0, 256)),
+        (across_hbm, w_ref.at[:, :, pl.ds(256, 128)]),
+        (logit_in_hbm, logit_in_ref),
+        (part_in_hbm, part_in_ref),
+    )
+    done(copies[:5])
     forward_tiles(tokens_ref, w_ref, score_ref, slope_ref, curve_ref, lifted_ref, logit_ref, logit_in_ref)
+    out = fetched(
+        out_sems,
+        (w_ref, w_hbm), (slope_ref, slope_hbm), (curve_ref, curve_hbm), (lifted_ref, lifted_hbm), (logit_ref, logit_hbm),
+    )
+    done(copies[5:])
     pull_back(w_ref, lifted_ref, part_ref, part_in_ref)
+    done(out)
+    done(fetched(sems, (part_ref, part_hbm)))
 
 
 def peak_of(array):
-    flat = jnp.max(jnp.abs(array).astype(F32), axis=0, keepdims=True)
-    return jnp.max(flat, axis=1, keepdims=True)
-
-
-def term_tiles(scale, tokens_t_ref, r1_t_ref, r1_ref, logits, w_ref, slope_ref, curve_ref, lifted_ref, peak_ref,
+    tall = jnp.max(jnp.abs(array).astype(F32), axis=0, keepdims=True)
+    return jnp.max(tall, axis=1, keepdims=True)
+
+
+def term_tiles(scale, copies, tokens_t_ref, r1_t_ref, r1_ref, logits, w_ref, slope_ref, curve_ref, lifted_ref, peak_ref,
                outs, exp_ref, fake_ref, real_ref):
     n = lifted_ref.shape[0]
     fake_gain = scale * jax.nn.sigmoid(logits[:n])
     real_gain = -scale * jax.nn.sigmoid(-logits[n:])
+    done(copies[:3])
     fake_ref[...] = (fake_gain * slope_ref[0:n, :]).astype(BF16)
-    for start, width in column_tiles(w_ref.shape[1]):
+    for start, width in column_tiles(w_ref.shape[2]):
         cols = slice(start, start + width)
-        back = jnp.dot(r1_ref[...], w_ref[:, cols], preferred_element_type=F32)
+        back = jnp.dot(r1_ref[...], flat(w_ref[:, :, cols]), preferred_element_type=F32)
         real_ref[:, cols] = (real_gain * slope_ref[n : 2 * n, cols] + back * curve_ref[:, cols]).astype(BF16)
+    done(copies[3:])
     bound = n * (
         peak_ref[0:1, 0:1] * peak_of(fake_ref[...])
         + peak_ref[8:9, 0:1] * peak_of(real_ref[...])
@@ -192,40 +241,59 @@
                         out[at : at + turn, :] = piece[(2 * k + turns) * turn : (2 * k + turns + 1) * turn, :]
 
 
-def third_kernel(scale, tokens_t_ref, part_ref, part_in_ref, logit_ref, logit_in_ref, w_ref, slope_ref, curve_ref,
-                 lifted_ref, peak_ref, low_ref, high_ref, across_ref, exp_ref, r1_t_ref, r1_ref, logits_ref,
-                 fake_ref, real_ref):
+def third_kernel(scale, tokens_t_hbm, part_hbm, part_in_hbm, logit_hbm, logit_in_hbm, w_hbm, slope_hbm, curve_hbm,
+                 lifted_hbm, peak_ref, low_ref, high_ref, across_ref, exp_ref, r1_t_hbm, r1_hbm, logits_hbm,
+                 fake_ref, real_ref, tokens_t_ref, part_ref, part_in_ref, logit_ref, logit_in_ref, w_ref, slope_ref,
+                 curve_ref, lifted_ref, r1_t_ref, r1_ref, logits_ref, sems, out_sems):
+    copies = fetched(
+        sems,
+        (part_hbm, part_ref), (part_in_hbm, part_in_ref), (logit_hbm, logit_ref), (logit_in_hbm, logit_in_ref),
+        (w_hbm, w_ref), (slope_hbm, slope_ref), (curve_hbm, curve_ref), (lifted_hbm, lifted_ref),
+        (tokens_t_hbm, tokens_t_ref),
+    )
+    done(copies[:4])
     r1_t_ref[...] = (scale * R1_WEIGHT * (part_ref[...] + part_in_ref[...])).astype(BF16)
     r1_ref[...] = r1_t_ref[...].T
     logits = jnp.sum(logit_ref[...] + logit_in_ref[...], axis=1, keepdims=True)
     logits_ref[...] = jnp.broadcast_to(logits, logits_ref.shape)
+    out = fetched(out_sems, (r1_t_ref, r1_t_hbm), (r1_ref, r1_hbm), (logits_ref, logits_hbm))
     outs = [(0, 256, [(0, 0, low_ref), (0, 1, high_ref)]), (256, 128, [(0, None, across_ref)])]
-    term_tiles(scale, tokens_t_ref, r1_t_ref, r1_ref, logits, w_ref, slope_ref, curve_ref, lifted_ref, peak_ref,
-               outs, exp_ref, fake_ref, real_ref)
-
-
-def fourth_kernel(scale, tokens_t_ref, r1_t_ref, r1_ref, logits_ref, w_ref, slope_ref, curve_ref, lifted_ref, peak_ref,
-                  own_ref, left_ref, right_ref, low_ref, high_ref, exp_ref, fake_ref, real_ref):
+    term_tiles(scale, copies[4:], tokens_t_ref, r1_t_ref, r1_ref, logits, w_ref, slope_ref, curve_ref, lifted_ref,
+               peak_ref, outs, exp_ref, fake_ref, real_ref)
+    done(out)
+
+
+def fourth_kernel(scale, tokens_t_hbm, r1_t_hbm, r1_hbm, logits_hbm, w_hbm, slope_hbm, curve_hbm, lifted_hbm, peak_ref,
+                  own_ref, left_ref, right_ref, low_ref, high_ref, exp_ref,
+                  fake_ref, real_ref, tokens_t_ref, r1_t_ref, r1_ref, logits_ref, w_ref, slope_ref, curve_ref,
+                  lifted_ref, sems):
+    copies = fetched(
+        sems,
+        (logits_hbm, logits_ref), (r1_hbm, r1_ref), (w_hbm, w_ref), (slope_hbm, slope_ref), (curve_hbm, curve_ref),
+        (r1_t_hbm, r1_t_ref), (lifted_hbm, lifted_ref), (tokens_t_hbm, tokens_t_ref),
+    )
+    done(copies[:2])
     outs = [
         (0, 256, [(0, None, own_ref), (128, None, left_ref)]),
         (256, 128, [(0, None, right_ref)]),
         (384, 256, [(0, 0, low_ref), (0, 1, high_ref)]),
     ]
-    term_tiles(scale, tokens_t_ref, r1_t_ref, r1_ref, logits_ref[:, 0:1], w_ref, slope_ref, curve_ref, lifted_ref,
-               peak_ref, outs, exp_ref, fake_ref, real_ref)
-
-
-def call(kernel, flops, outs, scratch, *args, flags=None):
-    vmem = pl.BlockSpec(memory_space=pltpu.VMEM)
-    specs = [vmem] * len(args)
+    term_tiles(scale, copies[2:], tokens_t_ref, r1_t_ref, r1_ref, logits_ref[:, 0:1], w_ref, slope_ref, curve_ref,
+               lifted_ref, peak_ref, outs, exp_ref, fake_ref, real_ref)
+
+
+def call(kernel, flops, outs, scratch, sems, *args, flags=None):
+    vmem, there = pl.BlockSpec(memory_space=pltpu.VMEM), pl.BlockSpec(memory_space=pl.ANY)
+    specs = [vmem if a.size <= 4096 else there for a in args]
     if flags is not None:
         args, specs = (flags, *args), [pl.BlockSpec(memory_space=pltpu.SMEM), *specs]
     return pl.pallas_call(
         kernel,
-        out_shape=[jax.ShapeDtypeStruct(shape, dtype) for shape, dtype in outs],
+        out_shape=[jax.ShapeDtypeStruct(shape, dtype) for shape, dtype, _ in outs],
         in_specs=specs,
-        out_specs=[vmem] * len(outs),
-        scratch_shapes=[pltpu.VMEM(shape, dtype) for shape, dtype in scratch],
+        out_specs=[vmem if inside else pl.BlockSpec(memory_space=pltpu.HBM) for *_, inside in outs],
+        scratch_shapes=[pltpu.VMEM(shape, dtype) for shape, dtype in scratch]
+        + [pltpu.SemaphoreType.DMA((k,)) for k in sems],
         compiler_params=pltpu.CompilerParams(vmem_limit_bytes=VMEM_BYTES),
         cost_estimate=pl.CostEstimate(flops=flops, bytes_accessed=8_000_000, transcendentals=0),
     )(*args)
@@ -261,15 +329,15 @@
 
     own_tokens = jnp.concatenate([fake_tokens[0], real_tokens[0]], 0)
     tokens, tokens_t, peak = call(
-        tokens_kernel, 2 * n * d_in * 128, [((2 * n, d_in), BF16), ((d_in, 2 * n), BF16), ((16, 128), F32)], [],
+        tokens_kernel, 2 * n * d_in * 128,
+        [((2 * n, d_in), BF16, False), ((d_in, 2 * n), BF16, False), ((16, 128), F32, True)],
+        [((n, d_in), BF16), ((n, d_in), BF16), ((2 * n, d_in), BF16), ((d_in, 2 * n), BF16)], [3],
         fake_tokens[0], real_tokens[0], to_core(own_tokens),
         flags=c[None].astype(jnp.int32),
     )
 
     left_a, right_a, left_b, right_b = together((own_a, own_a, own_b, own_b), RING)
-    mid_a, mid_b = d_in // 2, d_in // 4
-    across = together((left_a[:mid_a], right_a[mid_a:], left_b[:mid_b], right_b[mid_b:]), RING)
-    across_a, across_b = across[:2], across[2:]
+    across_a, across_b = together((left_a, left_b), (RING[0], RING[2]))
 
     def score_at(start, width):
         return lax.dynamic_slice_in_dim(score_vector, c * half + start, width, 0)
@@ -280,9 +348,12 @@
     score_2 = jnp.concatenate([score_at(512 + ylo * 256, 256), score_at((x + 2) % 4 * 128, 128)])[None]
     yhi_left, yhi_right = (y + 3) % 4 // 2, (y + 1) % 4 // 2
 
+    turn = d_in // NZ
+    in_turns = lambda array: array.reshape(NZ, array.shape[0] // NZ, array.shape[1])
+
     def states(width):
         return [
-            ((d_in, width), BF16),
+            ((NZ, turn, width), BF16),
             ((2 * n, width), F32),
             ((n, width), F32),
             ((n, width), BF16),
@@ -290,15 +361,19 @@
             ((d_in, n), F32),
         ]
 
+    def kept(shapes):
+        return [(*shape, False) for shape in shapes]
+
     wide, narrow = 640, 384
     w_1, slope_1, curve_1, lifted_1, logit_1, part_1 = call(
-        first_kernel, 6 * n * d_in * wide, states(wide), [],
-        tokens, own_a, left_a, right_a, left_b, right_b, score_1,
+        first_kernel, 6 * n * d_in * wide, kept(states(wide)), [*states(wide), ((2 * n, d_in), BF16)], [6, 5],
+        tokens, *map(in_turns, (own_a, left_a, right_a, left_b, right_b)), score_1,
         flags=yhi_left[None].astype(jnp.int32),
     )
     w_2, slope_2, curve_2, lifted_2, logit, part = call(
-        second_kernel, 6 * n * d_in * narrow, states(narrow), [((d_in // 2, 256), BF16)],
-        tokens, own_b, *across_b, *across_a, score_2, logit_1, part_1,
+        second_kernel, 6 * n * d_in * narrow, kept(states(narrow)),
+        [*states(narrow), ((2 * n, d_in), BF16), *states(narrow)[4:]], [6, 5],
+        tokens, *map(in_turns, (own_b, across_b, across_a)), score_2, logit_1, part_1,
         flags=yhi[None].astype(jnp.int32),
     )
     part_in, logit_in = to_core(part), to_core(logit)
@@ -306,17 +381,19 @@
     def works(width):
         return [((n, width), BF16)] * 2
 
-    side = [((d_in // 2, 256), F32)] * 2
-    strip = ((d_in, 128), F32)
+    side = [((d_in // 2, 256), F32, True)] * 2
+    strip, exps = ((d_in, 128), F32, True), ((16, 128), F32, True)
+    r1s = [((d_in, n), BF16), ((n, d_in), BF16), ((2 * n, 128), F32)]
+    tall = ((d_in, 2 * n), BF16)
+    *_, logit_shape, part_shape = states(narrow)
     low_2, high_2, far_a, exp_2, r1_t, r1, logits = call(
-        functools.partial(third_kernel, scale), 8 * n * d_in * narrow,
-        [*side, strip, ((16, 128), F32), ((d_in, n), BF16), ((n, d_in), BF16), ((2 * n, 128), F32)],
-        works(narrow),
+        functools.partial(third_kernel, scale), 8 * n * d_in * narrow, [*side, strip, exps, *kept(r1s)],
+        [*works(narrow), tall, part_shape, part_shape, logit_shape, logit_shape, *states(narrow)[:4], *r1s], [9, 3],
         tokens_t, part, part_in, logit, logit_in, w_2, slope_2, curve_2, lifted_2, peak,
     )
     own_1, left_1, right_1, low_1, high_1, exp_1 = call(
-        functools.partial(fourth_kernel, scale), 8 * n * d_in * wide,
-        [strip, strip, strip, *side, ((16, 128), F32)], works(wide),
+        functools.partial(fourth_kernel, scale), 8 * n * d_in * wide, [strip, strip, strip, *side, exps],
+        [*works(wide), tall, *r1s, *states(wide)[:4]], [8],
         tokens_t, r1_t, r1, logits, w_1, slope_1, curve_1, lifted_1, peak,
     )
     exp_1, exp_2 = exp_1[:1], exp_2[:1]
@@ -324,32 +401,20 @@
 
     own_2 = jnp.where(yhi == 0, low_2, high_2)
     far_b = jnp.where(yhi == 0, high_2, low_2)
-    a_up, a_down, b_up, b_down = together(
-        (
-            packed(far_a[:mid_a], exp_2),
-            packed(far_a[mid_a:], exp_2),
-            packed(far_b[:mid_b], twice(exp_2)),
-            packed(far_b[mid_b:], twice(exp_2)),
-        ),
-        RING,
-    )
-
-    def joined(piece, exponent, top=None, bottom=None):
-        middle = piece.shape[0] // 2
-        values, theirs = unpacked(bottom if top is None else top)
-        exponent = jnp.maximum(exponent, theirs) + 1.0
-        upper, lower = piece[:middle], piece[middle:]
-        upper, lower = (upper, lower + values) if top is None else (upper + values, lower)
-        return packed(jnp.concatenate([upper, lower], 0), exponent)
+    a_up, b_up = together((packed(far_a, exp_2), packed(far_b, twice(exp_2))), (RING[0], RING[2]))
+
+    def joined(piece, exponent, arrived):
+        values, theirs = unpacked(arrived)
+        return packed(piece + values, jnp.maximum(exponent, theirs) + 1.0)
 
     right_b = jnp.where(yhi_right == 0, low_1, high_1)
     left_b = jnp.where(yhi_left == 0, low_1, high_1)
     from_left_a, from_right_a, from_left_b, from_right_b = together(
         (
-            joined(right_1, exp_1, top=a_up),
-            joined(left_1, exp_1, bottom=a_down),
-            joined(right_b, twice(exp_1), top=b_up),
-            joined(left_b, twice(exp_1), bottom=b_down),
+            joined(right_1, exp_1, a_up),
+            packed(left_1, exp_1),
+            joined(right_b, twice(exp_1), b_up),
+            packed(left_b, twice(exp_1)),
         ),
         RING,
     )

time: 165 us -> 166 us (level)
  starting transfers between devices: 52.9 us -> 45.3 us
  Pallas kernels: 22.8 us -> 28.1 us
  other arithmetic: 6.5 us -> 9.76 us
    ppermute x27 -> x23, starting transfers between devices: 48.1 us -> 41.3 us  [send(): return lax.ppermute(array, AXES, pairs)]
    pallas_call x5, Pallas kernels: 22.8 us -> 28.1 us  [call(): pl.pallas_call(kernel, out_shape=[jax.ShapeDtypeStruct(shape, dtype) for...]
    slice x4 -> x0, local copies, waits for them, and re-layouts: 3.77 us -> none  [the longest x1 0.94 us: per_device(): right_a[mid_a:]]
    unnamed x49 -> x47, local copies, waits for them, and re-layouts: 10.4 us -> 12.7 us
    convert_element_type x8 -> x6, other arithmetic: 0.62 us -> 2.87 us  [packed(): scaled = (piece * jnp.exp2(-exponent)).astype(F16)]
    concatenate x8 -> x7, other arithmetic: 0.74 us -> 2.43 us  [packed(): jnp.concatenate([scaled, jnp.broadcast_to(exponent.astype(F16), (16, piec...]
    ppermute x27 -> x23, waiting for transfers between devices: 25.2 us -> 24.8 us  [send(): return lax.ppermute(array, AXES, pairs)]
  transfers between devices with their start and end apart: 28 -> 24, of which waited for: 10 -> 11; matrix products, arithmetic and copies ran while one was open for 2% -> 2% of each run, Pallas kernels for 7% -> 11%
where the time goes in v2:
time: 166 us; the launch traced here: 165 us
  starting transfers between devices  45.3 us (27%)
  blocking collectives  33.6 us (20%)
  waiting for transfers between devices  31.7 us (19%)
  Pallas kernels  28.1 us (17%)
  local copies, waits for them, and re-layouts  16.4 us (10%)
  other arithmetic  9.76 us (6%)
    ppermute x23, starting transfers between devices, send(): return lax.ppermute(array, AXES, pairs)  41.3 us
    pallas_call x5, Pallas kernels, call(): pl.pallas_call(kernel, out_shape=[jax.ShapeDtypeStruct(shape, dtype) for...  28.1 us
    ppermute x23, waiting for transfers between devices, send(): return lax.ppermute(array, AXES, pairs)  24.8 us
    all_to_all x1, blocking collectives, per_device(): lax.all_to_all(jnp.broadcast_to(block[None], (NZ, *block.shape)), 'z', 0, 0)  20.2 us
    all_to_all x1, blocking collectives, per_device(): both = jnp.sum(lax.all_to_all(both, 'z', 0, 0), 0)  13.3 us
    unnamed x47, local copies, waits for them, and re-layouts  12.7 us
    all_to_all x1, waiting for transfers between devices, per_device(): lax.all_to_all(jnp.broadcast_to(both[None], (8, *both.shape)), ('ylo', 'x...  6.84 us
    all_to_all x1, starting transfers between devices, per_device(): lax.all_to_all(jnp.broadcast_to(both[None], (8, *both.shape)), ('ylo', 'x...  4.02 us
  transfers between devices with their start and end apart: 24, of which 11 were waited for; matrix products, arithmetic and copies ran while one was open for 2% of the time, Pallas kernels for 11%

profile of v2, /device:TPU:1, one launch (start us, length us, event | category | flops | bytes accessed | tf_op | source)
XLA Modules:
  0.0 165.4 jit_solution(10016562915639140122)
XLA Ops:
  1.0 3.3 %collective-permute-start.1 = (bf16[48,256]{1,0:T(8,128)(2,1)S(1)}, bf16[48,256]{1,0:T(8,128)(2,1)S(1)}, u32[]{:S(2)}, u32[]{:S(2)}) collective-permute-start(bf16[48,256]{1,0:T(8,128)(2,1)S(1)} %pad_maximum_fusion.15), channel_id=1, source_target_pairs={{0,1},{1,0},{4,5},{5,4},{8,9},{9,8},{12,13},{13,12},{16,17},{17,16... | collective-permute-start | bytes 73736 | tf_op jit(solution)/shard_map/ppermute | solution.py:31
  5.2 20.2 %all_to_all.15 = bf16[8,96,256]{2,1,0:T(8,128)(2,1)S(1)} all-to-all(bf16[8,96,256]{2,1,0:T(8,128)(2,1)S(1)} %broadcast_in_dim.82), channel_id=1, replica_groups=mesh['ylo'=2,'x'=4,'z'=8,'yhi'=2,'c'=2] {'z'}, dimensions={0} | all-to-all | bytes 786432 | tf_op jit(solution)/shard_map/all_to_all | solution.py:321
  25.5 2.8 %collective-permute-start.2 = (bf16[768,128]{1,0:T(8,128)(2,1)S(1)}, bf16[768,128]{1,0:T(8,128)(2,1)S(1)}, u32[]{:S(2)}, u32[]{:S(2)}) collective-permute-start(bf16[768,128]{1,0:T(8,128)(2,1)S(1)} %bitcast.202), channel_id=1, source_target_pairs={{0,130},{1,131},{4,134},{5,135},{8,138},{9,139},{12,142},{13,143},... | collective-permute-start | bytes 589832 | tf_op jit(solution)/shard_map/ppermute | solution.py:31
  30.7 2.2 %collective-permute-start = (bf16[384,1536]{1,0:T(8,128)(2,1)}, bf16[384,1536]{1,0:T(8,128)(2,1)S(1)}, u32[]{:S(2)}, u32[]{:S(2)}) collective-permute-start(bf16[384,1536]{1,0:T(8,128)(2,1)} %pad_maximum_fusion), channel_id=1, source_target_pairs={{0,1},{1,0},{4,5},{5,4},{8,9},{9,8},{12,13},{13,12},{16,17},{17,16... | collective-permute-start | bytes 3538952 | tf_op jit(solution)/shard_map/ppermute | solution.py:31
  33.4 1.3 collective-permute-start.4
  34.7 1.5 collective-permute-start.5
  36.1 2.7 %collective-permute-start.7 = (bf16[768,256]{1,0:T(8,128)(2,1)S(1)}, bf16[768,256]{1,0:T(8,128)(2,1)}, u32[]{:S(2)}, u32[]{:S(2)}) collective-permute-start(bf16[768,256]{1,0:T(8,128)(2,1)S(1)} %pad_maximum_fusion.7), channel_id=1, source_target_pairs={{0,130},{1,131},{4,134},{5,135},{8,138},{9,139},{12,142},{13,143},... | collective-permute-start | bytes 1179656 | tf_op jit(solution)/shard_map/ppermute | solution.py:31
  40.6 2.0 %collective-permute-done.4 = bf16[1536,128]{1,0:T(8,128)(2,1)} collective-permute-done((bf16[1536,128]{1,0:T(8,128)(2,1)S(1)}, bf16[1536,128]{1,0:T(8,128)(2,1)}, u32[]{:S(2)}, u32[]{:S(2)}) %collective-permute-start.4) | collective-permute-done | bytes 393248 | tf_op jit(solution)/shard_map/ppermute | solution.py:31
  43.4 1.4 collective-permute-done.6
  45.1 2.2 %shard_map.46 = (bf16[768,1536]{1,0:T(8,128)(2,1)S(1)}, bf16[1536,768]{1,0:T(8,128)(2,1)S(1)}, f32[16,128]{1,0:T(8,128)S(1)}) custom-call(s32[1]{0:T(128)} %bitcast.flag_ref, bf16[192,1536]{1,0:T(8,128)(2,1)S(1)} %bitcast.180, bf16[192,1536]{1,0:T(8,128)(2,1)S(1)} %bitcast.182, bf16[384,1536]{1,0:T(8,128)(2,1)S(1)} %collective-permute-done.other_hbm), custom_call_target="tpu_custom_call" | custom-call | flops 150994944 | bytes 8000000 | tf_op jit(solution)/shard_map/pallas_call | solution.py:290
  47.4 7.5 %shard_map.47 = (bf16[8,192,640]{2,1,0:T(8,128)(2,1)S(1)}, f32[768,640]{1,0:T(8,128)S(1)}, f32[384,640]{1,0:T(8,128)S(1)}, bf16[384,640]{1,0:T(8,128)(2,1)S(1)},...) custom-call(s32[1]{0:T(128)} %bitcast.14.flag_ref, bf16[768,1536]{1,0:T(8,128)(2,1)S(1)} %get-tuple-element.70.tokens_hbm, ...), custom_call_target="tpu_custom_call" | custom-call | flops 2264924160 | bytes 8000000 | tf_op jit(solution)/shard_map/pallas_call | solution.py:290
  56.2 1.3 copy-done.12
  58.6 4.4 %shard_map.48 = (bf16[8,192,384]{2,1,0:T(8,128)(2,1)S(1)}, f32[768,384]{1,0:T(8,128)S(1)}, f32[384,384]{1,0:T(8,128)S(1)}, bf16[384,384]{1,0:T(8,128)(2,1)S(1)},...) custom-call(s32[1]{0:T(128)} %bitcast.3.flag_ref, bf16[768,1536]{1,0:T(8,128)(2,1)S(1)} %get-tuple-element.70.tokens_hbm, ...), custom_call_target="tpu_custom_call" | custom-call | flops 1358954496 | bytes 8000000 | tf_op jit(solution)/shard_map/pallas_call | solution.py:290
  63.0 4.3 %collective-permute-start.10 = (f32[1536,384]{1,0:T(8,128)S(1)}, f32[1536,384]{1,0:T(8,128)S(1)}, u32[]{:S(2)}, u32[]{:S(2)}) collective-permute-start(f32[1536,384]{1,0:T(8,128)S(1)} %get-tuple-element.89.part_hbm), channel_id=1, source_target_pairs={{0,1},{1,0},{4,5},{5,4},{8,9},{9,8},{12,13},{13,12},{16,17},{17,16... | collective-permute-start | bytes 7077896 | tf_op jit(solution)/shard_map/ppermute | solution.py:31
  67.7 4.4 %collective-permute-done.11.logit_in_hbm = f32[768,128]{1,0:T(8,128)S(1)} collective-permute-done((f32[768,128]{1,0:T(8,128)S(1)}, f32[768,128]{1,0:T(8,128)S(1)}, u32[]{:S(2)}, u32[]{:S(2)}) %collective-permute-start.11) | collective-permute-done | bytes 393248 | tf_op jit(solution)/shard_map/ppermute | solution.py:31
  72.1 6.3 %shard_map.49 = (f32[768,256]{1,0:T(8,128)S(1)}, f32[768,256]{1,0:T(8,128)S(1)}, f32[1536,128]{1,0:T(8,128)S(1)}, f32[16,128]{1,0:T(8,128)S(1)}, bf16[1536,384]{...) custom-call(bf16[1536,768]{1,0:T(8,128)(2,1)S(1)} %get-tuple-element.69.tokens_t_hbm, ...), custom_call_target="tpu_custom_call" | custom-call | flops 1811939328 | bytes 8000000 | tf_op jit(solution)/shard_map/pallas_call | solution.py:290
  82.8 1.7 %copy-done.3 = bf16[1536,768]{1,0:T(8,128)(2,1)S(1)} copy-done((bf16[1536,768]{1,0:T(8,128)(2,1)S(1)}, bf16[1536,768]{1,0:T(8,128)(2,1)}, u32[]{:S(2)}) %copy-start.3) | copy-done | bytes 2359320
  85.8 1.5 copy-done.11
  87.3 1.5 copy-done.13
  91.1 7.7 %shard_map.50 = (f32[1536,128]{1,0:T(8,128)S(1)}, f32[1536,128]{1,0:T(8,128)S(1)}, f32[1536,128]{1,0:T(8,128)S(1)}, f32[768,256]{1,0:T(8,128)S(1)}, f32[768,256]{1,0:T(8,128)S(1)}, /*index=5*/f32[16,128]{1,0:T(8,128)S(1)}) custom-call(bf16[1536,768]{1,0:T(8,128)(2,1)S(1)} %copy-done.3, bf16[1536,384]{1,0:T(8,128)(2,1)S(1)} %get-tuple-element.96.r1_t_hbm, ...), custom_call_target="tpu_custom_call" | custom-call | flops 3019898880 | bytes 8000000 | tf_op jit(solution)/shard_map/pallas_call | solution.py:290
  101.7 1.3 multiply_convert_fusion
  103.3 2.8 %collective-permute-start.16 = (f16[784,256]{1,0:T(8,128)(2,1)S(1)}, f16[784,256]{1,0:T(8,128)(2,1)S(1)}, u32[]{:S(2)}, u32[]{:S(2)}) collective-permute-start(f16[784,256]{1,0:T(8,128)(2,1)S(1)} %get-tuple-element.119), channel_id=1, source_target_pairs={{0,128},{1,129},{4,132},{5,133},{8,136},{9,137},{12,140},{13,141},... | collective-permute-start | bytes 1204232 | tf_op jit(solution)/shard_map/ppermute | solution.py:31
  107.0 1.8 %collective-permute-start.15 = (f16[1552,128]{1,0:T(8,128)(2,1)S(1)}, f16[1552,128]{1,0:T(8,128)(2,1)S(1)}, u32[]{:S(2)}, u32[]{:S(2)}) collective-permute-start(f16[1552,128]{1,0:T(8,128)(2,1)S(1)} %pad_maximum_fusion.6), channel_id=1, source_target_pairs={{0,96},{1,97},{4,100},{5,101},{8,104},{9,105},{12,108},{13,109},{1... | collective-permute-start | bytes 1191944 | tf_op jit(solution)/shard_map/ppermute | solution.py:31
  108.7 7.7 %collective-permute-done.14 = f16[1552,128]{1,0:T(8,128)(2,1)S(1)} collective-permute-done((f16[1552,128]{1,0:T(8,128)(2,1)S(1)}, f16[1552,128]{1,0:T(8,128)(2,1)S(1)}, u32[]{:S(2)}, u32[]{:S(2)}) %collective-permute-start.14) | collective-permute-done | bytes 397344 | tf_op jit(solution)/shard_map/ppermute | solution.py:31
  117.3 1.3 collective-permute-start.18
  119.5 3.7 %collective-permute-done.18 = f16[784,128]{1,0:T(8,128)(2,1)S(1)} collective-permute-done((f16[784,128]{1,0:T(8,128)(2,1)S(1)}, f16[784,128]{1,0:T(8,128)(2,1)S(1)}, u32[]{:S(2)}, u32[]{:S(2)}) %collective-permute-start.18) | collective-permute-done | bytes 200736 | tf_op jit(solution)/shard_map/ppermute | solution.py:31
  124.4 2.4 %collective-permute-start.21 = (f32[8,48,128]{2,1,0:T(8,128)S(1)}, f32[8,48,128]{2,1,0:T(8,128)S(1)}, u32[]{:S(2)}, u32[]{:S(2)}) collective-permute-start(f32[8,48,128]{2,1,0:T(8,128)S(1)} %fusion.3), channel_id=1, source_target_pairs={{0,96},{1,97},{4,100},{5,101},{8,104},{9,105},{12,108},{13,109},{1... | collective-permute-start | bytes 589832 | tf_op jit(solution)/shard_map/ppermute | solution.py:31
  128.0 2.1 %collective-permute-done.21 = f32[8,48,128]{2,1,0:T(8,128)S(1)} collective-permute-done((f32[8,48,128]{2,1,0:T(8,128)S(1)}, f32[8,48,128]{2,1,0:T(8,128)S(1)}, u32[]{:S(2)}, u32[]{:S(2)}) %collective-permute-start.21) | collective-permute-done | bytes 196640 | tf_op jit(solution)/shard_map/ppermute | solution.py:31
  130.2 13.3 %all_to_all.16 = f32[8,48,256]{2,1,0:T(8,128)S(1)} all-to-all(f32[8,48,256]{2,1,0:T(8,128)S(1)} %pad_maximum_fusion.9), channel_id=1, replica_groups=mesh['ylo'=2,'x'=4,'z'=8,'yhi'=2,'c'=2] {'z'}, dimensions={0} | all-to-all | bytes 786432 | tf_op jit(solution)/shard_map/all_to_all | solution.py:451
  144.4 4.0 %all-to-all-start.2 = ((f32[8,48,256]{2,1,0:T(8,128)}), f32[8,48,256]{2,1,0:T(8,128)S(1)}, u32[]{:S(2)}, u32[]{:S(2)}) async-start(f32[8,48,256]{2,1,0:T(8,128)} %broadcast_in_dim.100), calls=%async_computation.2 | async-start | bytes 786432 | tf_op jit(solution)/shard_map/all_to_all | solution.py:453
  148.4 6.8 %all-to-all-done.2 = f32[8,48,256]{2,1,0:T(8,128)S(1)} async-done(((f32[8,48,256]{2,1,0:T(8,128)}), f32[8,48,256]{2,1,0:T(8,128)S(1)}, u32[]{:S(2)}, u32[]{:S(2)}) %all-to-all-start.2) | async-done | bytes 393248 | tf_op jit(solution)/shard_map/all_to_all | solution.py:453
  155.4 8.1 %collective-permute-start.22 = (f32[48,1024]{1,0:T(8,128)S(1)}, f32[48,1024]{1,0:T(8,128)S(1)}, u32[]{:S(2)}, u32[]{:S(2)}) collective-permute-start(f32[48,1024]{1,0:T(8,128)S(1)} %broadcast_select_fusion.4), channel_id=1, source_target_pairs={{0,1},{1,0},{4,5},{5,4},{8,9},{9,8},{12,13},{13,12},{16,17},{17,16... | collective-permute-start | bytes 589832 | tf_op jit(solution)/shard_map/ppermute | solution.py:31
  (141 shorter events, 29.1 us)
Async XLA Ops:
  0.0 29.6 %copy-start = (bf16[1,192,1536]{2,1,0:T(8,128)(2,1)S(1)}, bf16[1,192,1536]{2,1,0:T(8,128)(2,1)}, u32[]{:S(2)}) copy-start(bf16[1,192,1536]{2,1,0:T(8,128)(2,1)} %param.4) | copy-start | bytes 1769476
  0.0 29.6 %copy-start.1 = (bf16[1,192,1536]{2,1,0:T(8,128)(2,1)S(1)}, bf16[1,192,1536]{2,1,0:T(8,128)(2,1)}, u32[]{:S(2)}) copy-start(bf16[1,192,1536]{2,1,0:T(8,128)(2,1)} %param.5) | copy-start | bytes 1769476
  1.0 4.2 %collective-permute-start.1 = (bf16[48,256]{1,0:T(8,128)(2,1)S(1)}, bf16[48,256]{1,0:T(8,128)(2,1)S(1)}, u32[]{:S(2)}, u32[]{:S(2)}) collective-permute-start(bf16[48,256]{1,0:T(8,128)(2,1)S(1)} %pad_maximum_fusion.15), channel_id=1, source_target_pairs={{0,1},{1,0},{4,5},{5,4},{8,9},{9,8},{12,13},{13,12},{16,17},{17,16... | collective-permute-start | bytes 73736 | tf_op jit(solution)/shard_map/ppermute | solution.py:31
  25.5 7.4 %collective-permute-start.2 = (bf16[768,128]{1,0:T(8,128)(2,1)S(1)}, bf16[768,128]{1,0:T(8,128)(2,1)S(1)}, u32[]{:S(2)}, u32[]{:S(2)}) collective-permute-start(bf16[768,128]{1,0:T(8,128)(2,1)S(1)} %bitcast.202), channel_id=1, source_target_pairs={{0,130},{1,131},{4,134},{5,135},{8,138},{9,139},{12,142},{13,143},... | collective-permute-start | bytes 589832 | tf_op jit(solution)/shard_map/ppermute | solution.py:31
  28.4 4.8 %collective-permute-start.3 = (bf16[768,128]{1,0:T(8,128)(2,1)S(1)}, bf16[768,128]{1,0:T(8,128)(2,1)S(1)}, u32[]{:S(2)}, u32[]{:S(2)}) collective-permute-start(bf16[768,128]{1,0:T(8,128)(2,1)S(1)} %bitcast.200), channel_id=1, source_target_pairs={{0,32},{1,33},{4,36},{5,37},{8,40},{9,41},{12,44},{13,45},{16,48},... | collective-permute-start | bytes 589832 | tf_op jit(solution)/shard_map/ppermute | solution.py:31
  30.7 14.4 %collective-permute-start = (bf16[384,1536]{1,0:T(8,128)(2,1)}, bf16[384,1536]{1,0:T(8,128)(2,1)S(1)}, u32[]{:S(2)}, u32[]{:S(2)}) collective-permute-start(bf16[384,1536]{1,0:T(8,128)(2,1)} %pad_maximum_fusion), channel_id=1, source_target_pairs={{0,1},{1,0},{4,5},{5,4},{8,9},{9,8},{12,13},{13,12},{16,17},{17,16... | collective-permute-start | bytes 3538952 | tf_op jit(solution)/shard_map/ppermute | solution.py:31
  33.3 11.5 %copy-start.4 = (bf16[8,2,96,128]{3,2,1,0:T(8,128)(2,1)}, bf16[8,2,96,128]{3,2,1,0:T(8,128)(2,1)S(1)}, u32[]{:S(2)}) copy-start(bf16[8,2,96,128]{3,2,1,0:T(8,128)(2,1)S(1)} %pad_maximum_fusion.8) | copy-start | bytes 1179652
  33.4 9.2 %collective-permute-start.4 = (bf16[1536,128]{1,0:T(8,128)(2,1)S(1)}, bf16[1536,128]{1,0:T(8,128)(2,1)}, u32[]{:S(2)}, u32[]{:S(2)}) collective-permute-start(bf16[1536,128]{1,0:T(8,128)(2,1)S(1)} %bitcast.186), channel_id=1, source_target_pairs={{0,32},{1,33},{4,36},{5,37},{8,40},{9,41},{12,44},{13,45},{16,48},... | collective-permute-start | bytes 1179656 | tf_op jit(solution)/shard_map/ppermute | solution.py:31
  34.7 7.9 %collective-permute-start.5 = (bf16[1536,128]{1,0:T(8,128)(2,1)S(1)}, bf16[1536,128]{1,0:T(8,128)(2,1)S(1)}, u32[]{:S(2)}, u32[]{:S(2)}) collective-permute-start(bf16[1536,128]{1,0:T(8,128)(2,1)S(1)} %bitcast.187), channel_id=1, source_target_pairs={{0,96},{1,97},{4,100},{5,101},{8,104},{9,105},{12,108},{13,109},{1... | collective-permute-start | bytes 1179656 | tf_op jit(solution)/shard_map/ppermute | solution.py:31
  36.1 8.6 %collective-permute-start.6 = (bf16[768,256]{1,0:T(8,128)(2,1)S(1)}, bf16[768,256]{1,0:T(8,128)(2,1)}, u32[]{:S(2)}, u32[]{:S(2)}) collective-permute-start(bf16[768,256]{1,0:T(8,128)(2,1)S(1)} %pad_maximum_fusion.7), channel_id=1, source_target_pairs={{0,128},{1,129},{4,132},{5,133},{8,136},{9,137},{12,140},{13,141},... | collective-permute-start | bytes 1179656 | tf_op jit(solution)/shard_map/ppermute | solution.py:31
  36.1 8.6 %collective-permute-start.7 = (bf16[768,256]{1,0:T(8,128)(2,1)S(1)}, bf16[768,256]{1,0:T(8,128)(2,1)}, u32[]{:S(2)}, u32[]{:S(2)}) collective-permute-start(bf16[768,256]{1,0:T(8,128)(2,1)S(1)} %pad_maximum_fusion.7), channel_id=1, source_target_pairs={{0,130},{1,131},{4,134},{5,135},{8,138},{9,139},{12,142},{13,143},... | collective-permute-start | bytes 1179656 | tf_op jit(solution)/shard_map/ppermute | solution.py:31
  44.7 13.9 %collective-permute-start.8 = (bf16[1536,128]{1,0:T(8,128)(2,1)}, bf16[1536,128]{1,0:T(8,128)(2,1)S(1)}, u32[]{:S(2)}, u32[]{:S(2)}) collective-permute-start(bf16[1536,128]{1,0:T(8,128)(2,1)} %collective-permute-done.4), channel_id=1, source_target_pairs={{0,32},{1,33},{4,36},{5,37},{8,40},{9,41},{12,44},{13,45},{16,48},... | collective-permute-start | bytes 1179656 | tf_op jit(solution)/shard_map/ppermute | solution.py:31
  44.7 13.9 %collective-permute-start.9 = (bf16[768,256]{1,0:T(8,128)(2,1)}, bf16[768,256]{1,0:T(8,128)(2,1)S(1)}, u32[]{:S(2)}, u32[]{:S(2)}) collective-permute-start(bf16[768,256]{1,0:T(8,128)(2,1)} %collective-permute-done.6), channel_id=1, source_target_pairs={{0,128},{1,129},{4,132},{5,133},{8,136},{9,137},{12,140},{13,141},... | collective-permute-start | bytes 1179656 | tf_op jit(solution)/shard_map/ppermute | solution.py:31
  45.1 2.3 %copy-start.5 = (bf16[8,2,96,128]{3,2,1,0:T(8,128)(2,1)S(1)}, bf16[8,2,96,128]{3,2,1,0:T(8,128)(2,1)}, u32[]{:S(2)}) copy-start(bf16[8,2,96,128]{3,2,1,0:T(8,128)(2,1)} %copy-done.4) | copy-start | bytes 1179652
  45.1 2.3 %copy-start.9 = (bf16[1536,128]{1,0:T(8,128)(2,1)S(1)}, bf16[1536,128]{1,0:T(8,128)(2,1)}, u32[]{:S(2)}) copy-start(bf16[1536,128]{1,0:T(8,128)(2,1)} %copy-done.8) | copy-start | bytes 1179652
  47.4 24.7 %copy-start.2 = (bf16[1536,768]{1,0:T(8,128)(2,1)}, bf16[1536,768]{1,0:T(8,128)(2,1)S(1)}, u32[]{:S(2)}) copy-start(bf16[1536,768]{1,0:T(8,128)(2,1)S(1)} %get-tuple-element.69.tokens_t_hbm) | copy-start | bytes 7077892
  58.6 4.4 %copy-start.16 = (bf16[384,640]{1,0:T(8,128)(2,1)}, bf16[384,640]{1,0:T(8,128)(2,1)S(1)}, u32[]{:S(2)}) copy-start(bf16[384,640]{1,0:T(8,128)(2,1)S(1)} %get-tuple-element.102.lifted_hbm) | copy-start | bytes 1474564
  63.0 9.1 %collective-permute-start.10 = (f32[1536,384]{1,0:T(8,128)S(1)}, f32[1536,384]{1,0:T(8,128)S(1)}, u32[]{:S(2)}, u32[]{:S(2)}) collective-permute-start(f32[1536,384]{1,0:T(8,128)S(1)} %get-tuple-element.89.part_hbm), channel_id=1, source_target_pairs={{0,1},{1,0},{4,5},{5,4},{8,9},{9,8},{12,13},{13,12},{16,17},{17,16... | collective-permute-start | bytes 7077896 | tf_op jit(solution)/shard_map/ppermute | solution.py:31
  67.4 4.7 %collective-permute-start.11 = (f32[768,128]{1,0:T(8,128)S(1)}, f32[768,128]{1,0:T(8,128)S(1)}, u32[]{:S(2)}, u32[]{:S(2)}) collective-permute-start(f32[768,128]{1,0:T(8,128)S(1)} %get-tuple-element.90.logit_hbm), channel_id=1, source_target_pairs={{0,1},{1,0},{4,5},{5,4},{8,9},{9,8},{12,13},{13,12},{16,17},{17,16... | collective-permute-start | bytes 1179656 | tf_op jit(solution)/shard_map/ppermute | solution.py:31
  80.5 18.2 %collective-permute-start.13 = (f16[784,256]{1,0:T(8,128)(2,1)}, f16[784,256]{1,0:T(8,128)(2,1)}, u32[]{:S(2)}, u32[]{:S(2)}) collective-permute-start(f16[784,256]{1,0:T(8,128)(2,1)} %pad_maximum_fusion.1), channel_id=1, source_target_pairs={{0,128},{1,129},{4,132},{5,133},{8,136},{9,137},{12,140},{13,141},... | collective-permute-start | bytes 1204232 | tf_op jit(solution)/shard_map/ppermute | solution.py:31
  81.6 17.1 %collective-permute-start.12 = (f16[1552,128]{1,0:T(8,128)(2,1)}, f16[1552,128]{1,0:T(8,128)(2,1)}, u32[]{:S(2)}, u32[]{:S(2)}) collective-permute-start(f16[1552,128]{1,0:T(8,128)(2,1)} %pad_maximum_fusion.4), channel_id=1, source_target_pairs={{0,32},{1,33},{4,36},{5,37},{8,40},{9,41},{12,44},{13,45},{16,48},... | collective-permute-start | bytes 1191944 | tf_op jit(solution)/shard_map/ppermute | solution.py:31
  82.8 1.7 %copy-start.3 = (bf16[1536,768]{1,0:T(8,128)(2,1)S(1)}, bf16[1536,768]{1,0:T(8,128)(2,1)}, u32[]{:S(2)}) copy-start(bf16[1536,768]{1,0:T(8,128)(2,1)} %copy-done.2) | copy-start | bytes 7077892
  103.3 13.2 %collective-permute-start.16 = (f16[784,256]{1,0:T(8,128)(2,1)S(1)}, f16[784,256]{1,0:T(8,128)(2,1)S(1)}, u32[]{:S(2)}, u32[]{:S(2)}) collective-permute-start(f16[784,256]{1,0:T(8,128)(2,1)S(1)} %get-tuple-element.119), channel_id=1, source_target_pairs={{0,128},{1,129},{4,132},{5,133},{8,136},{9,137},{12,140},{13,141},... | collective-permute-start | bytes 1204232 | tf_op jit(solution)/shard_map/ppermute | solution.py:31
  106.0 10.4 %collective-permute-start.17 = (f16[784,256]{1,0:T(8,128)(2,1)S(1)}, f16[784,256]{1,0:T(8,128)(2,1)S(1)}, u32[]{:S(2)}, u32[]{:S(2)}) collective-permute-start(f16[784,256]{1,0:T(8,128)(2,1)S(1)} %get-tuple-element.120), channel_id=1, source_target_pairs={{0,130},{1,131},{4,134},{5,135},{8,138},{9,139},{12,142},{13,143},... | collective-permute-start | bytes 1204232 | tf_op jit(solution)/shard_map/ppermute | solution.py:31
  106.0 10.4 %collective-permute-start.14 = (f16[1552,128]{1,0:T(8,128)(2,1)S(1)}, f16[1552,128]{1,0:T(8,128)(2,1)S(1)}, u32[]{:S(2)}, u32[]{:S(2)}) collective-permute-start(f16[1552,128]{1,0:T(8,128)(2,1)S(1)} %pad_maximum_fusion.5), channel_id=1, source_target_pairs={{0,32},{1,33},{4,36},{5,37},{8,40},{9,41},{12,44},{13,45},{16,48},... | collective-permute-start | bytes 1191944 | tf_op jit(solution)/shard_map/ppermute | solution.py:31
  107.0 9.5 %collective-permute-start.15 = (f16[1552,128]{1,0:T(8,128)(2,1)S(1)}, f16[1552,128]{1,0:T(8,128)(2,1)S(1)}, u32[]{:S(2)}, u32[]{:S(2)}) collective-permute-start(f16[1552,128]{1,0:T(8,128)(2,1)S(1)} %pad_maximum_fusion.6), channel_id=1, source_target_pairs={{0,96},{1,97},{4,100},{5,101},{8,104},{9,105},{12,108},{13,109},{1... | collective-permute-start | bytes 1191944 | tf_op jit(solution)/shard_map/ppermute | solution.py:31
  117.3 5.9 %collective-permute-start.18 = (f16[784,128]{1,0:T(8,128)(2,1)S(1)}, f16[784,128]{1,0:T(8,128)(2,1)S(1)}, u32[]{:S(2)}, u32[]{:S(2)}) collective-permute-start(f16[784,128]{1,0:T(8,128)(2,1)S(1)} %pad_maximum_fusion.11), channel_id=1, source_target_pairs={{0,130},{1,131},{4,134},{5,135},{8,138},{9,139},{12,142},{13,143},... | collective-permute-start | bytes 602120 | tf_op jit(solution)/shard_map/ppermute | solution.py:31
  118.6 4.6 %collective-permute-start.19 = (f16[784,128]{1,0:T(8,128)(2,1)S(1)}, f16[784,128]{1,0:T(8,128)(2,1)S(1)}, u32[]{:S(2)}, u32[]{:S(2)}) collective-permute-start(f16[784,128]{1,0:T(8,128)(2,1)S(1)} %pad_maximum_fusion.12), channel_id=1, source_target_pairs={{0,32},{1,33},{4,36},{5,37},{8,40},{9,41},{12,44},{13,45},{16,48},... | collective-permute-start | bytes 602120 | tf_op jit(solution)/shard_map/ppermute | solution.py:31
  123.4 4.6 %collective-permute-start.20 = (f32[8,48,128]{2,1,0:T(8,128)S(1)}, f32[8,48,128]{2,1,0:T(8,128)S(1)}, u32[]{:S(2)}, u32[]{:S(2)}) collective-permute-start(f32[8,48,128]{2,1,0:T(8,128)S(1)} %select_bitcast_fusion), channel_id=1, source_target_pairs={{0,128},{1,129},{4,132},{5,133},{8,136},{9,137},{12,140},{13,141},... | collective-permute-start | bytes 589832 | tf_op jit(solution)/shard_map/ppermute | solution.py:31
  124.4 5.7 %collective-permute-start.21 = (f32[8,48,128]{2,1,0:T(8,128)S(1)}, f32[8,48,128]{2,1,0:T(8,128)S(1)}, u32[]{:S(2)}, u32[]{:S(2)}) collective-permute-start(f32[8,48,128]{2,1,0:T(8,128)S(1)} %fusion.3), channel_id=1, source_target_pairs={{0,96},{1,97},{4,100},{5,101},{8,104},{9,105},{12,108},{13,109},{1... | collective-permute-start | bytes 589832 | tf_op jit(solution)/shard_map/ppermute | solution.py:31
  144.4 10.9 %all-to-all-start.2 = ((f32[8,48,256]{2,1,0:T(8,128)}), f32[8,48,256]{2,1,0:T(8,128)S(1)}, u32[]{:S(2)}, u32[]{:S(2)}) async-start(f32[8,48,256]{2,1,0:T(8,128)} %broadcast_in_dim.100), calls=%async_computation.2 | async-start | bytes 786432 | tf_op jit(solution)/shard_map/all_to_all | solution.py:453
  155.4 9.2 %collective-permute-start.22 = (f32[48,1024]{1,0:T(8,128)S(1)}, f32[48,1024]{1,0:T(8,128)S(1)}, u32[]{:S(2)}, u32[]{:S(2)}) collective-permute-start(f32[48,1024]{1,0:T(8,128)S(1)} %broadcast_select_fusion.4), channel_id=1, source_target_pairs={{0,1},{1,0},{4,5},{5,4},{8,9},{9,8},{12,13},{13,12},{16,17},{17,16... | collective-permute-start | bytes 589832 | tf_op jit(solution)/shard_map/ppermute | solution.py:31
  (10 other events, 12.3 us)

commit v3 on v2

--- a/solution.py
+++ b/solution.py
@@ -13,7 +13,7 @@
 NX, NY, NZ = 4, 4, 8
 AXES = ("ylo", "x", "z", "yhi", "c")
 BF16, F16, F32 = jnp.bfloat16, jnp.float16, jnp.float32
-VMEM_BYTES = 26 * 1024 * 1024
+VMEM_BYTES = 56 * 1024 * 1024
 
 
 def flat_index(x, y, z, c):
@@ -35,9 +35,10 @@
     return send(array, lambda x, y, c: (x, y, 1 - c))
 
 
-def together(arrays, routes):
-    arrays = lax.optimization_barrier(tuple(arrays))
-    return lax.optimization_barrier(tuple(send(a, to) for a, to in zip(arrays, routes, strict=True)))
+def together(arrays, routes, beside=None, extra=()):
+    arrays = lax.optimization_barrier((*arrays, *extra))
+    sent = tuple(send(a, to) for a, to in zip(arrays, routes))
+    return lax.optimization_barrier((*sent, *(beside(*arrays[len(sent) :]) if beside else ())))
 
 
 RING = (
@@ -201,7 +202,7 @@
 
 
 def term_tiles(scale, copies, tokens_t_ref, r1_t_ref, r1_ref, logits, w_ref, slope_ref, curve_ref, lifted_ref, peak_ref,
-               outs, exp_ref, fake_ref, real_ref):
+               outs, out_sems, exp_ref, fake_ref, real_ref):
     n = lifted_ref.shape[0]
     fake_gain = scale * jax.nn.sigmoid(logits[:n])
     real_gain = -scale * jax.nn.sigmoid(-logits[n:])
@@ -222,6 +223,7 @@
     d_in = tokens_t_ref.shape[0]
     turn = d_in // (2 * NZ)
     height = 4 * turn
+    leaving = []
     for start, width, parts in outs:
         cols = slice(start, start + width)
         for row in range(0, d_in, height):
@@ -231,20 +233,27 @@
                 + jnp.dot(tokens_t_ref[rows, n : 2 * n], real_ref[:, cols], preferred_element_type=F32)
                 + jnp.dot(r1_t_ref[rows, :], lifted_ref[:, cols], preferred_element_type=F32)
             )
-            for column, turns, out in parts:
+            for column, turns, out, out_hbm in parts:
                 piece = value[:, column : column + out.shape[1]]
                 if turns is None:
+                    there = rows
                     out[rows, :] = piece
                 else:
+                    there = slice(row // 2, row // 2 + 2 * turn)
                     for k in range(2):
                         at = row // 2 + k * turn
                         out[at : at + turn, :] = piece[(2 * k + turns) * turn : (2 * k + turns + 1) * turn, :]
+                leaving.append(
+                    pltpu.make_async_copy(out.at[there, :], out_hbm.at[there, :], out_sems.at[len(leaving)])
+                )
+                leaving[-1].start()
+    done(leaving)
 
 
 def third_kernel(scale, tokens_t_hbm, part_hbm, part_in_hbm, logit_hbm, logit_in_hbm, w_hbm, slope_hbm, curve_hbm,
-                 lifted_hbm, peak_ref, low_ref, high_ref, across_ref, exp_ref, r1_t_hbm, r1_hbm, logits_hbm,
+                 lifted_hbm, peak_ref, low_hbm, high_hbm, across_hbm, exp_ref, r1_t_hbm, r1_hbm, logits_hbm,
                  fake_ref, real_ref, tokens_t_ref, part_ref, part_in_ref, logit_ref, logit_in_ref, w_ref, slope_ref,
-                 curve_ref, lifted_ref, r1_t_ref, r1_ref, logits_ref, sems, out_sems):
+                 curve_ref, lifted_ref, r1_t_ref, r1_ref, logits_ref, low_ref, high_ref, across_ref, sems, r1_sems, out_sems):
     copies = fetched(
         sems,
         (part_hbm, part_ref), (part_in_hbm, part_in_ref), (logit_hbm, logit_ref), (logit_in_hbm, logit_in_ref),
@@ -256,17 +265,20 @@
     r1_ref[...] = r1_t_ref[...].T
     logits = jnp.sum(logit_ref[...] + logit_in_ref[...], axis=1, keepdims=True)
     logits_ref[...] = jnp.broadcast_to(logits, logits_ref.shape)
-    out = fetched(out_sems, (r1_t_ref, r1_t_hbm), (r1_ref, r1_hbm), (logits_ref, logits_hbm))
-    outs = [(0, 256, [(0, 0, low_ref), (0, 1, high_ref)]), (256, 128, [(0, None, across_ref)])]
+    out = fetched(r1_sems, (r1_t_ref, r1_t_hbm), (r1_ref, r1_hbm), (logits_ref, logits_hbm))
+    outs = [
+        (0, 256, [(0, 0, low_ref, low_hbm), (0, 1, high_ref, high_hbm)]),
+        (256, 128, [(0, None, across_ref, across_hbm)]),
+    ]
     term_tiles(scale, copies[4:], tokens_t_ref, r1_t_ref, r1_ref, logits, w_ref, slope_ref, curve_ref, lifted_ref,
-               peak_ref, outs, exp_ref, fake_ref, real_ref)
+               peak_ref, outs, out_sems, exp_ref, fake_ref, real_ref)
     done(out)
 
 
 def fourth_kernel(scale, tokens_t_hbm, r1_t_hbm, r1_hbm, logits_hbm, w_hbm, slope_hbm, curve_hbm, lifted_hbm, peak_ref,
-                  own_ref, left_ref, right_ref, low_ref, high_ref, exp_ref,
+                  own_hbm, left_hbm, right_hbm, low_hbm, high_hbm, exp_ref,
                   fake_ref, real_ref, tokens_t_ref, r1_t_ref, r1_ref, logits_ref, w_ref, slope_ref, curve_ref,
-                  lifted_ref, sems):
+                  lifted_ref, own_ref, left_ref, right_ref, low_ref, high_ref, sems, out_sems):
     copies = fetched(
         sems,
         (logits_hbm, logits_ref), (r1_hbm, r1_ref), (w_hbm, w_ref), (slope_hbm, slope_ref), (curve_hbm, curve_ref),
@@ -274,12 +286,12 @@
     )
     done(copies[:2])
     outs = [
-        (0, 256, [(0, None, own_ref), (128, None, left_ref)]),
-        (256, 128, [(0, None, right_ref)]),
-        (384, 256, [(0, 0, low_ref), (0, 1, high_ref)]),
+        (128, 256, [(0, None, left_ref, left_hbm), (128, None, right_ref, right_hbm)]),
+        (384, 256, [(0, 0, low_ref, low_hbm), (0, 1, high_ref, high_hbm)]),
+        (0, 128, [(0, None, own_ref, own_hbm)]),
     ]
     term_tiles(scale, copies[2:], tokens_t_ref, r1_t_ref, r1_ref, logits_ref[:, 0:1], w_ref, slope_ref, curve_ref,
-               lifted_ref, peak_ref, outs, exp_ref, fake_ref, real_ref)
+               lifted_ref, peak_ref, outs, out_sems, exp_ref, fake_ref, real_ref)
 
 
 def call(kernel, flops, outs, scratch, sems, *args, flags=None):
@@ -328,15 +340,18 @@
     own_b = ordered(~gray_x, piece_b, far_b, 1)
 
     own_tokens = jnp.concatenate([fake_tokens[0], real_tokens[0]], 0)
-    tokens, tokens_t, peak = call(
-        tokens_kernel, 2 * n * d_in * 128,
-        [((2 * n, d_in), BF16, False), ((d_in, 2 * n), BF16, False), ((16, 128), F32, True)],
-        [((n, d_in), BF16), ((n, d_in), BF16), ((2 * n, d_in), BF16), ((d_in, 2 * n), BF16)], [3],
-        fake_tokens[0], real_tokens[0], to_core(own_tokens),
-        flags=c[None].astype(jnp.int32),
-    )
-
-    left_a, right_a, left_b, right_b = together((own_a, own_a, own_b, own_b), RING)
+    def join_tokens(other_tokens):
+        return call(
+            tokens_kernel, 2 * n * d_in * 128,
+            [((2 * n, d_in), BF16, False), ((d_in, 2 * n), BF16, False), ((16, 128), F32, True)],
+            [((n, d_in), BF16), ((n, d_in), BF16), ((2 * n, d_in), BF16), ((d_in, 2 * n), BF16)], [3],
+            fake_tokens[0], real_tokens[0], other_tokens,
+            flags=c[None].astype(jnp.int32),
+        )
+
+    left_a, right_a, left_b, right_b, tokens, tokens_t, peak = together(
+        (own_a, own_a, own_b, own_b), RING, join_tokens, (to_core(own_tokens),)
+    )
     across_a, across_b = together((left_a, left_b), (RING[0], RING[2]))
 
     def score_at(start, width):
@@ -381,51 +396,57 @@
     def works(width):
         return [((n, width), BF16)] * 2
 
-    side = [((d_in // 2, 256), F32, True)] * 2
-    strip, exps = ((d_in, 128), F32, True), ((16, 128), F32, True)
+    side = [((d_in // 2, 256), F32)] * 2
+    strip, exps = ((d_in, 128), F32), ((16, 128), F32, True)
     r1s = [((d_in, n), BF16), ((n, d_in), BF16), ((2 * n, 128), F32)]
     tall = ((d_in, 2 * n), BF16)
     *_, logit_shape, part_shape = states(narrow)
     low_2, high_2, far_a, exp_2, r1_t, r1, logits = call(
-        functools.partial(third_kernel, scale), 8 * n * d_in * narrow, [*side, strip, exps, *kept(r1s)],
-        [*works(narrow), tall, part_shape, part_shape, logit_shape, logit_shape, *states(narrow)[:4], *r1s], [9, 3],
+        functools.partial(third_kernel, scale), 8 * n * d_in * narrow, [*kept([*side, strip]), exps, *kept(r1s)],
+        [*works(narrow), tall, part_shape, part_shape, logit_shape, logit_shape, *states(narrow)[:4], *r1s, *side, strip],
+        [9, 3, 12],
         tokens_t, part, part_in, logit, logit_in, w_2, slope_2, curve_2, lifted_2, peak,
     )
-    own_1, left_1, right_1, low_1, high_1, exp_1 = call(
-        functools.partial(fourth_kernel, scale), 8 * n * d_in * wide, [strip, strip, strip, *side, exps],
-        [*works(wide), tall, *r1s, *states(wide)[:4]], [8],
-        tokens_t, r1_t, r1, logits, w_1, slope_1, curve_1, lifted_1, peak,
-    )
-    exp_1, exp_2 = exp_1[:1], exp_2[:1]
+    exp_2 = exp_2[:1]
     twice = lambda row: jnp.concatenate([row, row], 1)
 
     own_2 = jnp.where(yhi == 0, low_2, high_2)
     far_b = jnp.where(yhi == 0, high_2, low_2)
-    a_up, b_up = together((packed(far_a, exp_2), packed(far_b, twice(exp_2))), (RING[0], RING[2]))
-
-    def joined(piece, exponent, arrived):
-        values, theirs = unpacked(arrived)
-        return packed(piece + values, jnp.maximum(exponent, theirs) + 1.0)
-
+
+    def rest_of_term(r1_t):
+        return call(
+            functools.partial(fourth_kernel, scale), 8 * n * d_in * wide, [*kept([strip] * 3 + side), exps],
+            [*works(wide), tall, *r1s, *states(wide)[:4], *[strip] * 3, *side], [8, 20],
+            tokens_t, r1_t, r1, logits, w_1, slope_1, curve_1, lifted_1, peak,
+        )
+
+    across_a, across_b, own_1, left_1, right_1, low_1, high_1, exp_1 = together(
+        (packed(far_a, exp_2), packed(far_b, twice(exp_2))),
+        (lambda x, y, c: (x + 2, y, c), lambda x, y, c: (x, y + 2, c)),
+        rest_of_term,
+        (r1_t,),
+    )
+    exp_1 = exp_1[:1]
     right_b = jnp.where(yhi_right == 0, low_1, high_1)
     left_b = jnp.where(yhi_left == 0, low_1, high_1)
     from_left_a, from_right_a, from_left_b, from_right_b = together(
         (
-            joined(right_1, exp_1, a_up),
+            packed(right_1, exp_1),
             packed(left_1, exp_1),
-            joined(right_b, twice(exp_1), b_up),
+            packed(right_b, twice(exp_1)),
             packed(left_b, twice(exp_1)),
         ),
         RING,
     )
 
-    def three(own, exponent, one, two):
-        (one, exp_one), (two, exp_two) = unpacked(one), unpacked(two)
-        return own + one + two, jnp.maximum(exponent, jnp.maximum(exp_one, exp_two)) + 2.0
+    def summed(own, exponent, *messages):
+        for values, theirs in map(unpacked, messages):
+            own, exponent = own + values, jnp.maximum(exponent, theirs)
+        return own, exponent + 2.0
 
     top = jnp.maximum(exp_1, exp_2)
-    sum_a, exp_a = three(own_1, top, from_left_a, from_right_a)
-    sum_b, exp_b = three(own_2, twice(top), from_left_b, from_right_b)
+    sum_a, exp_a = summed(own_1, top, from_left_a, from_right_a, across_a)
+    sum_b, exp_b = summed(own_2, twice(top), from_left_b, from_right_b, across_b)
 
     turns = sum_a.reshape(NZ, 2, 2 * rows, 128)
     keep_a = jnp.where(yhi == 0, turns[:, 0], turns[:, 1]).reshape(d_in // 2, 128)

time: 166 us -> 174 us (1.048)
  blocking collectives: 33.6 us -> 13.3 us
  waiting for transfers between devices: 31.7 us -> 49.7 us
  Pallas kernels: 28.1 us -> 41.7 us
  local copies, waits for them, and re-layouts: 16.4 us -> 7.52 us
  starting transfers between devices: 45.3 us -> 52.1 us
    all_to_all x1 -> x0, blocking collectives: 20.2 us -> none  [per_device(): lax.all_to_all(jnp.broadcast_to(block[None], (NZ, *block.shape)), 'z', 0, 0)]
    all_to_all x0 -> x1, waiting for transfers between devices: none -> 14.3 us  [per_device(): lax.all_to_all(jnp.broadcast_to(block[None], (NZ, *block.shape)), 'z', 0, 0)]
    pallas_call x5, Pallas kernels: 28.1 us -> 41.7 us  [call(): pl.pallas_call(kernel, out_shape=[jax.ShapeDtypeStruct(shape, dtype) for...]
    unnamed x47 -> x49, local copies, waits for them, and re-layouts: 12.7 us -> 3.55 us
    all_to_all x0 -> x1, starting transfers between devices: none -> 6.45 us  [per_device(): lax.all_to_all(jnp.broadcast_to(block[None], (NZ, *block.shape)), 'z', 0, 0)]
    ppermute x23, waiting for transfers between devices: 24.8 us -> 28.6 us  [send(): return lax.ppermute(array, AXES, pairs)]
  transfers between devices with their start and end apart: 24 -> 25, of which waited for: 11 -> 12; matrix products, arithmetic and copies ran while one was open for 2% -> 1% of each run, Pallas kernels for 11% -> 14%
where the time goes in v3:
time: 174 us; the launch traced here: 173 us
  starting transfers between devices  52.1 us (30%)
  waiting for transfers between devices  49.7 us (29%)
  Pallas kernels  41.7 us (24%)
  blocking collectives  13.3 us (8%)
  other arithmetic  8.35 us (5%)
  local copies, waits for them, and re-layouts  7.52 us (4%)
    pallas_call x5, Pallas kernels, call(): pl.pallas_call(kernel, out_shape=[jax.ShapeDtypeStruct(shape, dtype) for...  41.7 us
    ppermute x23, starting transfers between devices, send(): return lax.ppermute(array, AXES, pairs)  40.8 us
    ppermute x23, waiting for transfers between devices, send(): return lax.ppermute(array, AXES, pairs)  28.6 us
    all_to_all x1, waiting for transfers between devices, per_device(): lax.all_to_all(jnp.broadcast_to(block[None], (NZ, *block.shape)), 'z', 0, 0)  14.3 us
    all_to_all x1, blocking collectives, per_device(): both = jnp.sum(lax.all_to_all(both, 'z', 0, 0), 0)  13.3 us
    all_to_all x1, waiting for transfers between devices, per_device(): lax.all_to_all(jnp.broadcast_to(both[None], (8, *both.shape)), ('ylo', 'x...  6.84 us
    all_to_all x1, starting transfers between devices, per_device(): lax.all_to_all(jnp.broadcast_to(block[None], (NZ, *block.shape)), 'z', 0, 0)  6.45 us
    all_to_all x1, starting transfers between devices, per_device(): lax.all_to_all(jnp.broadcast_to(both[None], (8, *both.shape)), ('ylo', 'x...  4.82 us
  transfers between devices with their start and end apart: 25, of which 12 were waited for; matrix products, arithmetic and copies ran while one was open for 1% of the time, Pallas kernels for 14%

profile of v3, /device:TPU:1, one launch (start us, length us, event | category | flops | bytes accessed | tf_op | source)
XLA Modules:
  0.0 173.4 jit_solution(17048644568862470079)
XLA Ops:
  1.0 3.3 %collective-permute-start = (bf16[48,256]{1,0:T(8,128)(2,1)S(1)}, bf16[48,256]{1,0:T(8,128)(2,1)S(1)}, u32[]{:S(2)}, u32[]{:S(2)}) collective-permute-start(bf16[48,256]{1,0:T(8,128)(2,1)S(1)} %pad_maximum_fusion.15), channel_id=1, source_target_pairs={{0,1},{1,0},{4,5},{5,4},{8,9},{9,8},{12,13},{13,12},{16,17},{17,16... | collective-permute-start | bytes 73736 | tf_op jit(solution)/shard_map/ppermute | solution.py:31
  6.0 6.5 %all-to-all-start = ((bf16[8,96,256]{2,1,0:T(8,128)(2,1)}), bf16[8,96,256]{2,1,0:T(8,128)(2,1)S(1)}, u32[]{:S(2)}, u32[]{:S(2)}) async-start(bf16[8,96,256]{2,1,0:T(8,128)(2,1)} %broadcast_in_dim.34), calls=%async_computation | async-start | bytes 786432 | tf_op jit(solution)/shard_map/all_to_all | solution.py:333
  13.2 14.3 %all-to-all-done = bf16[8,96,256]{2,1,0:T(8,128)(2,1)S(1)} async-done(((bf16[8,96,256]{2,1,0:T(8,128)(2,1)}), bf16[8,96,256]{2,1,0:T(8,128)(2,1)S(1)}, u32[]{:S(2)}, u32[]{:S(2)}) %all-to-all-start) | async-done | bytes 393248 | tf_op jit(solution)/shard_map/all_to_all | solution.py:333
  27.6 2.8 %collective-permute-start.1 = (bf16[768,128]{1,0:T(8,128)(2,1)S(1)}, bf16[768,128]{1,0:T(8,128)(2,1)S(1)}, u32[]{:S(2)}, u32[]{:S(2)}) collective-permute-start(bf16[768,128]{1,0:T(8,128)(2,1)S(1)} %bitcast.196), channel_id=1, source_target_pairs={{0,130},{1,131},{4,134},{5,135},{8,138},{9,139},{12,142},{13,143},... | collective-permute-start | bytes 589832 | tf_op jit(solution)/shard_map/ppermute | solution.py:31
  30.5 1.2 collective-permute-start.2
  31.7 3.4 %collective-permute-done.1 = bf16[768,128]{1,0:T(8,128)(2,1)S(1)} collective-permute-done((bf16[768,128]{1,0:T(8,128)(2,1)S(1)}, bf16[768,128]{1,0:T(8,128)(2,1)S(1)}, u32[]{:S(2)}, u32[]{:S(2)}) %collective-permute-start.1) | collective-permute-done | bytes 196640 | tf_op jit(solution)/shard_map/ppermute | solution.py:31
  36.3 1.3 collective-permute-start.4
  37.6 1.5 collective-permute-start.5
  39.1 2.7 %collective-permute-start.7 = (bf16[768,256]{1,0:T(8,128)(2,1)S(1)}, bf16[768,256]{1,0:T(8,128)(2,1)}, u32[]{:S(2)}, u32[]{:S(2)}) collective-permute-start(bf16[768,256]{1,0:T(8,128)(2,1)S(1)} %pad_maximum_fusion.8), channel_id=1, source_target_pairs={{0,130},{1,131},{4,134},{5,135},{8,138},{9,139},{12,142},{13,143},... | collective-permute-start | bytes 1179656 | tf_op jit(solution)/shard_map/ppermute | solution.py:31
  41.9 5.1 %shard_map.46 = (bf16[768,1536]{1,0:T(8,128)(2,1)}, bf16[1536,768]{1,0:T(8,128)(2,1)}, f32[16,128]{1,0:T(8,128)}) custom-call(s32[1]{0:T(128)} %bitcast.9.flag_ref, bf16[192,1536]{1,0:T(8,128)(2,1)} %bitcast.179, bf16[192,1536]{1,0:T(8,128)(2,1)} %bitcast.181, bf16[384,1536]{1,0:T(8,128)(2,1)} %copy-done.6), custom_call_target="tpu_custom_call" | custom-call | flops 150994944 | bytes 8000000 | tf_op jit(solution)/shard_map/pallas_call | solution.py:302
  47.1 1.6 collective-permute-done.6
  50.3 8.9 %shard_map.47 = (bf16[8,192,640]{2,1,0:T(8,128)(2,1)}, f32[768,640]{1,0:T(8,128)}, f32[384,640]{1,0:T(8,128)}, bf16[384,640]{1,0:T(8,128)(2,1)}, f32[768,128]{1,0:T(8,128)}, /*index=5*/f32[1536,384]{1,0:T(8,128)}) custom-call(s32[1]{0:T(128)} %bitcast.14.flag_ref, bf16[768,1536]{1,0:T(8,128)(2,1)} %get-tuple-element.93.tokens_hbm, ...), custom_call_target="tpu_custom_call" | custom-call | flops 2264924160 | bytes 8000000 | tf_op jit(solution)/shard_map/pallas_call | solution.py:302
  60.0 7.5 %shard_map.48 = (bf16[8,192,384]{2,1,0:T(8,128)(2,1)}, f32[768,384]{1,0:T(8,128)}, f32[384,384]{1,0:T(8,128)}, bf16[384,384]{1,0:T(8,128)(2,1)}, f32[768,128]{1,0:T(8,128)}, /*index=5*/f32[1536,384]{1,0:T(8,128)}) custom-call(s32[1]{0:T(128)} %bitcast.10.flag_ref, bf16[768,1536]{1,0:T(8,128)(2,1)} %get-tuple-element.93.tokens_hbm, ...), custom_call_target="tpu_custom_call" | custom-call | flops 1358954496 | bytes 8000000 | tf_op jit(solution)/shard_map/pallas_call | solution.py:302
  67.6 3.2 %collective-permute-start.10 = (f32[1536,384]{1,0:T(8,128)}, f32[1536,384]{1,0:T(8,128)S(1)}, u32[]{:S(2)}, u32[]{:S(2)}) collective-permute-start(f32[1536,384]{1,0:T(8,128)} %get-tuple-element.104.part_hbm), channel_id=1, source_target_pairs={{0,1},{1,0},{4,5},{5,4},{8,9},{9,8},{12,13},{13,12},{16,17},{17,16... | collective-permute-start | bytes 7077896 | tf_op jit(solution)/shard_map/ppermute | solution.py:31
  70.9 4.8 %collective-permute-done.11.logit_in_hbm = f32[768,128]{1,0:T(8,128)S(1)} collective-permute-done((f32[768,128]{1,0:T(8,128)}, f32[768,128]{1,0:T(8,128)S(1)}, u32[]{:S(2)}, u32[]{:S(2)}) %collective-permute-start.11) | collective-permute-done | bytes 393248 | tf_op jit(solution)/shard_map/ppermute | solution.py:31
  77.3 9.6 %shard_map.49 = (f32[768,256]{1,0:T(8,128)}, f32[768,256]{1,0:T(8,128)}, f32[1536,128]{1,0:T(8,128)}, f32[16,128]{1,0:T(8,128)}, bf16[1536,384]{1,0:T(8,128)(2,1...) custom-call(bf16[1536,768]{1,0:T(8,128)(2,1)} %get-tuple-element.92.tokens_t_hbm, ...), custom_call_target="tpu_custom_call" | custom-call | flops 1811939328 | bytes 8000000 | tf_op jit(solution)/shard_map/pallas_call | solution.py:302
  87.7 1.3 multiply_convert_fusion.4
  89.3 4.2 %collective-permute-start.13 = (f16[784,256]{1,0:T(8,128)(2,1)S(1)}, f16[784,256]{1,0:T(8,128)(2,1)S(1)}, u32[]{:S(2)}, u32[]{:S(2)}) collective-permute-start(f16[784,256]{1,0:T(8,128)(2,1)S(1)} %pad_maximum_fusion.5), channel_id=1, source_target_pairs={{0,2},{1,3},{4,6},{5,7},{8,10},{9,11},{12,14},{13,15},{16,18},{17,... | collective-permute-start | bytes 1204232 | tf_op jit(solution)/shard_map/ppermute | solution.py:31
  93.6 2.4 %collective-permute-start.12 = (f16[1552,128]{1,0:T(8,128)(2,1)S(1)}, f16[1552,128]{1,0:T(8,128)(2,1)S(1)}, u32[]{:S(2)}, u32[]{:S(2)}) collective-permute-start(f16[1552,128]{1,0:T(8,128)(2,1)S(1)} %pad_maximum_fusion.6), channel_id=1, source_target_pairs={{0,64},{1,65},{4,68},{5,69},{8,72},{9,73},{12,76},{13,77},{16,80},... | collective-permute-start | bytes 1191944 | tf_op jit(solution)/shard_map/ppermute | solution.py:31
  96.0 10.6 %shard_map.50 = (f32[1536,128]{1,0:T(8,128)}, f32[1536,128]{1,0:T(8,128)}, f32[1536,128]{1,0:T(8,128)}, f32[768,256]{1,0:T(8,128)}, f32[768,256]{1,0:T(8,128)}, /*index=5*/f32[16,128]{1,0:T(8,128)}) custom-call(bf16[1536,768]{1,0:T(8,128)(2,1)} %get-tuple-element.92.tokens_t_hbm, bf16[1536,384]{1,0:T(8,128)(2,1)} %get-tuple-element.118.r1_t_hbm, ...), custom_call_target="tpu_custom_call" | custom-call | flops 3019898880 | bytes 8000000 | tf_op jit(solution)/shard_map/pallas_call | solution.py:302
  107.4 1.7 %multiply_convert_fusion = (f16[768,256]{1,0:T(8,128)(2,1)S(1)}, f16[768,256]{1,0:T(8,128)(2,1)S(1)}) fusion(f32[768,256]{1,0:T(8,128)} %get-tuple-element.135, f32[768,256]{1,0:T(8,128)} %get-tuple-element.136, f32[256]{0:T(256)S(1)} %get-tuple-element.207, pred[]{:T(512)S(6)} %eq.46, pred[]{:T(512)S(6)} %eq.45), kind=kLoop, calls=%fused_computation.3 | loop fusion | flops 1179648 | bytes 2360322 | tf_op jit(solution)/shard_map/convert_element_type | solution.py:59
  109.8 2.7 %collective-permute-start.17 = (f16[784,256]{1,0:T(8,128)(2,1)S(1)}, f16[784,256]{1,0:T(8,128)(2,1)S(1)}, u32[]{:S(2)}, u32[]{:S(2)}) collective-permute-start(f16[784,256]{1,0:T(8,128)(2,1)S(1)} %get-tuple-element.140), channel_id=1, source_target_pairs={{0,130},{1,131},{4,134},{5,135},{8,138},{9,139},{12,142},{13,143},... | collective-permute-start | bytes 1204232 | tf_op jit(solution)/shard_map/ppermute | solution.py:31
  113.3 1.9 %collective-permute-start.15 = (f16[1552,128]{1,0:T(8,128)(2,1)S(1)}, f16[1552,128]{1,0:T(8,128)(2,1)S(1)}, u32[]{:S(2)}, u32[]{:S(2)}) collective-permute-start(f16[1552,128]{1,0:T(8,128)(2,1)S(1)} %get-tuple-element.138), channel_id=1, source_target_pairs={{0,96},{1,97},{4,100},{5,101},{8,104},{9,105},{12,108},{13,109},{1... | collective-permute-start | bytes 1191944 | tf_op jit(solution)/shard_map/ppermute | solution.py:31
  115.2 7.7 %collective-permute-done.14 = f16[1552,128]{1,0:T(8,128)(2,1)S(1)} collective-permute-done((f16[1552,128]{1,0:T(8,128)(2,1)S(1)}, f16[1552,128]{1,0:T(8,128)(2,1)S(1)}, u32[]{:S(2)}, u32[]{:S(2)}) %collective-permute-start.14) | collective-permute-done | bytes 397344 | tf_op jit(solution)/shard_map/ppermute | solution.py:31
  126.9 4.6 %collective-permute-done.18 = f16[784,128]{1,0:T(8,128)(2,1)S(1)} collective-permute-done((f16[784,128]{1,0:T(8,128)(2,1)S(1)}, f16[784,128]{1,0:T(8,128)(2,1)S(1)}, u32[]{:S(2)}, u32[]{:S(2)}) %collective-permute-start.18) | collective-permute-done | bytes 200736 | tf_op jit(solution)/shard_map/ppermute | solution.py:31
  131.9 2.5 %collective-permute-start.21 = (f32[8,48,128]{2,1,0:T(8,128)S(1)}, f32[8,48,128]{2,1,0:T(8,128)S(1)}, u32[]{:S(2)}, u32[]{:S(2)}) collective-permute-start(f32[8,48,128]{2,1,0:T(8,128)S(1)} %fusion.3), channel_id=1, source_target_pairs={{0,96},{1,97},{4,100},{5,101},{8,104},{9,105},{12,108},{13,109},{1... | collective-permute-start | bytes 589832 | tf_op jit(solution)/shard_map/ppermute | solution.py:31
  134.4 2.0 %collective-permute-done.20 = f32[8,48,128]{2,1,0:T(8,128)S(1)} collective-permute-done((f32[8,48,128]{2,1,0:T(8,128)S(1)}, f32[8,48,128]{2,1,0:T(8,128)S(1)}, u32[]{:S(2)}, u32[]{:S(2)}) %collective-permute-start.20) | collective-permute-done | bytes 196640 | tf_op jit(solution)/shard_map/ppermute | solution.py:31
  136.4 1.3 collective-permute-done.21
  137.8 13.3 %all_to_all.15 = f32[8,48,256]{2,1,0:T(8,128)S(1)} all-to-all(f32[8,48,256]{2,1,0:T(8,128)S(1)} %pad_maximum_fusion.9), channel_id=1, replica_groups=mesh['ylo'=2,'x'=4,'z'=8,'yhi'=2,'c'=2] {'z'}, dimensions={0} | all-to-all | bytes 786432 | tf_op jit(solution)/shard_map/all_to_all | solution.py:472
  151.9 4.8 %all-to-all-start.2 = ((f32[8,48,256]{2,1,0:T(8,128)}), f32[8,48,256]{2,1,0:T(8,128)S(1)}, u32[]{:S(2)}, u32[]{:S(2)}) async-start(f32[8,48,256]{2,1,0:T(8,128)} %broadcast_in_dim.88), calls=%async_computation.2 | async-start | bytes 786432 | tf_op jit(solution)/shard_map/all_to_all | solution.py:474
  156.7 6.8 %all-to-all-done.2 = f32[8,48,256]{2,1,0:T(8,128)S(1)} async-done(((f32[8,48,256]{2,1,0:T(8,128)}), f32[8,48,256]{2,1,0:T(8,128)S(1)}, u32[]{:S(2)}, u32[]{:S(2)}) %all-to-all-start.2) | async-done | bytes 393248 | tf_op jit(solution)/shard_map/all_to_all | solution.py:474
  163.7 7.7 %collective-permute-start.22 = (f32[48,1024]{1,0:T(8,128)S(1)}, f32[48,1024]{1,0:T(8,128)S(1)}, u32[]{:S(2)}, u32[]{:S(2)}) collective-permute-start(f32[48,1024]{1,0:T(8,128)S(1)} %broadcast_select_fusion.4), channel_id=1, source_target_pairs={{0,1},{1,0},{4,5},{5,4},{8,9},{9,8},{12,13},{13,12},{16,17},{17,16... | collective-permute-start | bytes 589832 | tf_op jit(solution)/shard_map/ppermute | solution.py:31
  (139 shorter events, 19.3 us)
Async XLA Ops:
  0.0 12.4 %copy-start.2 = (bf16[1,192,1536]{2,1,0:T(8,128)(2,1)S(1)}, bf16[1,192,1536]{2,1,0:T(8,128)(2,1)}, u32[]{:S(2)}) copy-start(bf16[1,192,1536]{2,1,0:T(8,128)(2,1)} %param.4) | copy-start | bytes 1769476
  0.0 12.4 %copy-start.3 = (bf16[1,192,1536]{2,1,0:T(8,128)(2,1)S(1)}, bf16[1,192,1536]{2,1,0:T(8,128)(2,1)}, u32[]{:S(2)}) copy-start(bf16[1,192,1536]{2,1,0:T(8,128)(2,1)} %param.5) | copy-start | bytes 1769476
  1.0 4.2 %collective-permute-start = (bf16[48,256]{1,0:T(8,128)(2,1)S(1)}, bf16[48,256]{1,0:T(8,128)(2,1)S(1)}, u32[]{:S(2)}, u32[]{:S(2)}) collective-permute-start(bf16[48,256]{1,0:T(8,128)(2,1)S(1)} %pad_maximum_fusion.15), channel_id=1, source_target_pairs={{0,1},{1,0},{4,5},{5,4},{8,9},{9,8},{12,13},{13,12},{16,17},{17,16... | collective-permute-start | bytes 73736 | tf_op jit(solution)/shard_map/ppermute | solution.py:31
  6.0 21.6 %all-to-all-start = ((bf16[8,96,256]{2,1,0:T(8,128)(2,1)}), bf16[8,96,256]{2,1,0:T(8,128)(2,1)S(1)}, u32[]{:S(2)}, u32[]{:S(2)}) async-start(bf16[8,96,256]{2,1,0:T(8,128)(2,1)} %broadcast_in_dim.34), calls=%async_computation | async-start | bytes 786432 | tf_op jit(solution)/shard_map/all_to_all | solution.py:333
  12.5 29.3 %copy-start.15 = (f32[2048]{0:T(1024)S(1)}, f32[2048]{0:T(1024)}, u32[]{:S(2)}) copy-start(f32[2048]{0:T(1024)} %param.7) | copy-start | bytes 24580
  12.5 23.8 %collective-permute-start.3 = (bf16[384,1536]{1,0:T(8,128)(2,1)S(1)}, bf16[384,1536]{1,0:T(8,128)(2,1)S(1)}, u32[]{:S(2)}, u32[]{:S(2)}) collective-permute-start(bf16[384,1536]{1,0:T(8,128)(2,1)S(1)} %pad_maximum_fusion), channel_id=1, source_target_pairs={{0,1},{1,0},{4,5},{5,4},{8,9},{9,8},{12,13},{13,12},{16,17},{17,16... | collective-permute-start | bytes 3538952 | tf_op jit(solution)/shard_map/ppermute | solution.py:31
  27.6 7.4 %collective-permute-start.1 = (bf16[768,128]{1,0:T(8,128)(2,1)S(1)}, bf16[768,128]{1,0:T(8,128)(2,1)S(1)}, u32[]{:S(2)}, u32[]{:S(2)}) collective-permute-start(bf16[768,128]{1,0:T(8,128)(2,1)S(1)} %bitcast.196), channel_id=1, source_target_pairs={{0,130},{1,131},{4,134},{5,135},{8,138},{9,139},{12,142},{13,143},... | collective-permute-start | bytes 589832 | tf_op jit(solution)/shard_map/ppermute | solution.py:31
  30.5 5.7 %collective-permute-start.2 = (bf16[768,128]{1,0:T(8,128)(2,1)S(1)}, bf16[768,128]{1,0:T(8,128)(2,1)S(1)}, u32[]{:S(2)}, u32[]{:S(2)}) collective-permute-start(bf16[768,128]{1,0:T(8,128)(2,1)S(1)} %bitcast.189), channel_id=1, source_target_pairs={{0,32},{1,33},{4,36},{5,37},{8,40},{9,41},{12,44},{13,45},{16,48},... | collective-permute-start | bytes 589832 | tf_op jit(solution)/shard_map/ppermute | solution.py:31
  36.2 10.8 %copy-start.5 = (bf16[768,256]{1,0:T(8,128)(2,1)}, bf16[768,256]{1,0:T(8,128)(2,1)S(1)}, u32[]{:S(2)}) copy-start(bf16[768,256]{1,0:T(8,128)(2,1)S(1)} %pad_maximum_fusion.8) | copy-start | bytes 1179652
  36.3 14.0 %copy-start.14 = (bf16[8,2,96,128]{3,2,1,0:T(8,128)(2,1)}, bf16[8,2,96,128]{3,2,1,0:T(8,128)(2,1)S(1)}, u32[]{:S(2)}) copy-start(bf16[8,2,96,128]{3,2,1,0:T(8,128)(2,1)S(1)} %pad_maximum_fusion.7) | copy-start | bytes 1179652
  36.3 5.6 %copy-start.6 = (bf16[384,1536]{1,0:T(8,128)(2,1)}, bf16[384,1536]{1,0:T(8,128)(2,1)S(1)}, u32[]{:S(2)}) copy-start(bf16[384,1536]{1,0:T(8,128)(2,1)S(1)} %collective-permute-done.3.other_hbm) | copy-start | bytes 3538948
  36.3 10.7 %collective-permute-start.4 = (bf16[1536,128]{1,0:T(8,128)(2,1)S(1)}, bf16[1536,128]{1,0:T(8,128)(2,1)S(1)}, u32[]{:S(2)}, u32[]{:S(2)}) collective-permute-start(bf16[1536,128]{1,0:T(8,128)(2,1)S(1)} %bitcast.192), channel_id=1, source_target_pairs={{0,32},{1,33},{4,36},{5,37},{8,40},{9,41},{12,44},{13,45},{16,48},... | collective-permute-start | bytes 1179656 | tf_op jit(solution)/shard_map/ppermute | solution.py:31
  37.6 9.4 %collective-permute-start.5 = (bf16[1536,128]{1,0:T(8,128)(2,1)S(1)}, bf16[1536,128]{1,0:T(8,128)(2,1)S(1)}, u32[]{:S(2)}, u32[]{:S(2)}) collective-permute-start(bf16[1536,128]{1,0:T(8,128)(2,1)S(1)} %bitcast.193), channel_id=1, source_target_pairs={{0,96},{1,97},{4,100},{5,101},{8,104},{9,105},{12,108},{13,109},{1... | collective-permute-start | bytes 1179656 | tf_op jit(solution)/shard_map/ppermute | solution.py:31
  39.1 9.6 %collective-permute-start.6 = (bf16[768,256]{1,0:T(8,128)(2,1)S(1)}, bf16[768,256]{1,0:T(8,128)(2,1)S(1)}, u32[]{:S(2)}, u32[]{:S(2)}) collective-permute-start(bf16[768,256]{1,0:T(8,128)(2,1)S(1)} %pad_maximum_fusion.8), channel_id=1, source_target_pairs={{0,128},{1,129},{4,132},{5,133},{8,136},{9,137},{12,140},{13,141},... | collective-permute-start | bytes 1179656 | tf_op jit(solution)/shard_map/ppermute | solution.py:31
  39.1 9.6 %collective-permute-start.7 = (bf16[768,256]{1,0:T(8,128)(2,1)S(1)}, bf16[768,256]{1,0:T(8,128)(2,1)}, u32[]{:S(2)}, u32[]{:S(2)}) collective-permute-start(bf16[768,256]{1,0:T(8,128)(2,1)S(1)} %pad_maximum_fusion.8), channel_id=1, source_target_pairs={{0,130},{1,131},{4,134},{5,135},{8,138},{9,139},{12,142},{13,143},... | collective-permute-start | bytes 1179656 | tf_op jit(solution)/shard_map/ppermute | solution.py:31
  48.7 10.4 %collective-permute-start.8 = (bf16[1536,128]{1,0:T(8,128)(2,1)S(1)}, bf16[1536,128]{1,0:T(8,128)(2,1)S(1)}, u32[]{:S(2)}, u32[]{:S(2)}) collective-permute-start(bf16[1536,128]{1,0:T(8,128)(2,1)S(1)} %collective-permute-done.4), channel_id=1, source_target_pairs={{0,32},{1,33},{4,36},{5,37},{8,40},{9,41},{12,44},{13,45},{16,48},... | collective-permute-start | bytes 1179656 | tf_op jit(solution)/shard_map/ppermute | solution.py:31
  48.8 10.4 %collective-permute-start.9 = (bf16[768,256]{1,0:T(8,128)(2,1)S(1)}, bf16[768,256]{1,0:T(8,128)(2,1)S(1)}, u32[]{:S(2)}, u32[]{:S(2)}) collective-permute-start(bf16[768,256]{1,0:T(8,128)(2,1)S(1)} %collective-permute-done.6), channel_id=1, source_target_pairs={{0,128},{1,129},{4,132},{5,133},{8,136},{9,137},{12,140},{13,141},... | collective-permute-start | bytes 1179656 | tf_op jit(solution)/shard_map/ppermute | solution.py:31
  67.6 8.2 %collective-permute-start.10 = (f32[1536,384]{1,0:T(8,128)}, f32[1536,384]{1,0:T(8,128)S(1)}, u32[]{:S(2)}, u32[]{:S(2)}) collective-permute-start(f32[1536,384]{1,0:T(8,128)} %get-tuple-element.104.part_hbm), channel_id=1, source_target_pairs={{0,1},{1,0},{4,5},{5,4},{8,9},{9,8},{12,13},{13,12},{16,17},{17,16... | collective-permute-start | bytes 7077896 | tf_op jit(solution)/shard_map/ppermute | solution.py:31
  70.8 4.9 %collective-permute-start.11 = (f32[768,128]{1,0:T(8,128)}, f32[768,128]{1,0:T(8,128)S(1)}, u32[]{:S(2)}, u32[]{:S(2)}) collective-permute-start(f32[768,128]{1,0:T(8,128)} %get-tuple-element.105.logit_hbm), channel_id=1, source_target_pairs={{0,1},{1,0},{4,5},{5,4},{8,9},{9,8},{12,13},{13,12},{16,17},{17,16... | collective-permute-start | bytes 1179656 | tf_op jit(solution)/shard_map/ppermute | solution.py:31
  89.3 17.3 %collective-permute-start.13 = (f16[784,256]{1,0:T(8,128)(2,1)S(1)}, f16[784,256]{1,0:T(8,128)(2,1)S(1)}, u32[]{:S(2)}, u32[]{:S(2)}) collective-permute-start(f16[784,256]{1,0:T(8,128)(2,1)S(1)} %pad_maximum_fusion.5), channel_id=1, source_target_pairs={{0,2},{1,3},{4,6},{5,7},{8,10},{9,11},{12,14},{13,15},{16,18},{17,... | collective-permute-start | bytes 1204232 | tf_op jit(solution)/shard_map/ppermute | solution.py:31
  93.6 13.1 %collective-permute-start.12 = (f16[1552,128]{1,0:T(8,128)(2,1)S(1)}, f16[1552,128]{1,0:T(8,128)(2,1)S(1)}, u32[]{:S(2)}, u32[]{:S(2)}) collective-permute-start(f16[1552,128]{1,0:T(8,128)(2,1)S(1)} %pad_maximum_fusion.6), channel_id=1, source_target_pairs={{0,64},{1,65},{4,68},{5,69},{8,72},{9,73},{12,76},{13,77},{16,80},... | collective-permute-start | bytes 1191944 | tf_op jit(solution)/shard_map/ppermute | solution.py:31
  109.4 14.4 %copy-start.10 = (f32[1536,128]{1,0:T(8,128)S(1)}, f32[1536,128]{1,0:T(8,128)}, u32[]{:S(2)}) copy-start(f32[1536,128]{1,0:T(8,128)} %get-tuple-element.131) | copy-start | bytes 2359300
  109.8 13.2 %collective-permute-start.16 = (f16[784,256]{1,0:T(8,128)(2,1)S(1)}, f16[784,256]{1,0:T(8,128)(2,1)S(1)}, u32[]{:S(2)}, u32[]{:S(2)}) collective-permute-start(f16[784,256]{1,0:T(8,128)(2,1)S(1)} %get-tuple-element.139), channel_id=1, source_target_pairs={{0,128},{1,129},{4,132},{5,133},{8,136},{9,137},{12,140},{13,141},... | collective-permute-start | bytes 1204232 | tf_op jit(solution)/shard_map/ppermute | solution.py:31
  109.8 13.1 %collective-permute-start.17 = (f16[784,256]{1,0:T(8,128)(2,1)S(1)}, f16[784,256]{1,0:T(8,128)(2,1)S(1)}, u32[]{:S(2)}, u32[]{:S(2)}) collective-permute-start(f16[784,256]{1,0:T(8,128)(2,1)S(1)} %get-tuple-element.140), channel_id=1, source_target_pairs={{0,130},{1,131},{4,134},{5,135},{8,138},{9,139},{12,142},{13,143},... | collective-permute-start | bytes 1204232 | tf_op jit(solution)/shard_map/ppermute | solution.py:31
  112.5 10.4 %collective-permute-start.14 = (f16[1552,128]{1,0:T(8,128)(2,1)S(1)}, f16[1552,128]{1,0:T(8,128)(2,1)S(1)}, u32[]{:S(2)}, u32[]{:S(2)}) collective-permute-start(f16[1552,128]{1,0:T(8,128)(2,1)S(1)} %get-tuple-element.137), channel_id=1, source_target_pairs={{0,32},{1,33},{4,36},{5,37},{8,40},{9,41},{12,44},{13,45},{16,48},... | collective-permute-start | bytes 1191944 | tf_op jit(solution)/shard_map/ppermute | solution.py:31
  113.3 9.6 %collective-permute-start.15 = (f16[1552,128]{1,0:T(8,128)(2,1)S(1)}, f16[1552,128]{1,0:T(8,128)(2,1)S(1)}, u32[]{:S(2)}, u32[]{:S(2)}) collective-permute-start(f16[1552,128]{1,0:T(8,128)(2,1)S(1)} %get-tuple-element.138), channel_id=1, source_target_pairs={{0,96},{1,97},{4,100},{5,101},{8,104},{9,105},{12,108},{13,109},{1... | collective-permute-start | bytes 1191944 | tf_op jit(solution)/shard_map/ppermute | solution.py:31
  125.7 5.9 %collective-permute-start.18 = (f16[784,128]{1,0:T(8,128)(2,1)S(1)}, f16[784,128]{1,0:T(8,128)(2,1)S(1)}, u32[]{:S(2)}, u32[]{:S(2)}) collective-permute-start(f16[784,128]{1,0:T(8,128)(2,1)S(1)} %pad_maximum_fusion.11), channel_id=1, source_target_pairs={{0,130},{1,131},{4,134},{5,135},{8,138},{9,139},{12,142},{13,143},... | collective-permute-start | bytes 602120 | tf_op jit(solution)/shard_map/ppermute | solution.py:31
  126.1 5.4 %collective-permute-start.19 = (f16[784,128]{1,0:T(8,128)(2,1)S(1)}, f16[784,128]{1,0:T(8,128)(2,1)S(1)}, u32[]{:S(2)}, u32[]{:S(2)}) collective-permute-start(f16[784,128]{1,0:T(8,128)(2,1)S(1)} %pad_maximum_fusion.12), channel_id=1, source_target_pairs={{0,32},{1,33},{4,36},{5,37},{8,40},{9,41},{12,44},{13,45},{16,48},... | collective-permute-start | bytes 602120 | tf_op jit(solution)/shard_map/ppermute | solution.py:31
  131.8 4.6 %collective-permute-start.20 = (f32[8,48,128]{2,1,0:T(8,128)S(1)}, f32[8,48,128]{2,1,0:T(8,128)S(1)}, u32[]{:S(2)}, u32[]{:S(2)}) collective-permute-start(f32[8,48,128]{2,1,0:T(8,128)S(1)} %select_bitcast_fusion), channel_id=1, source_target_pairs={{0,128},{1,129},{4,132},{5,133},{8,136},{9,137},{12,140},{13,141},... | collective-permute-start | bytes 589832 | tf_op jit(solution)/shard_map/ppermute | solution.py:31
  131.9 5.8 %collective-permute-start.21 = (f32[8,48,128]{2,1,0:T(8,128)S(1)}, f32[8,48,128]{2,1,0:T(8,128)S(1)}, u32[]{:S(2)}, u32[]{:S(2)}) collective-permute-start(f32[8,48,128]{2,1,0:T(8,128)S(1)} %fusion.3), channel_id=1, source_target_pairs={{0,96},{1,97},{4,100},{5,101},{8,104},{9,105},{12,108},{13,109},{1... | collective-permute-start | bytes 589832 | tf_op jit(solution)/shard_map/ppermute | solution.py:31
  151.9 11.7 %all-to-all-start.2 = ((f32[8,48,256]{2,1,0:T(8,128)}), f32[8,48,256]{2,1,0:T(8,128)S(1)}, u32[]{:S(2)}, u32[]{:S(2)}) async-start(f32[8,48,256]{2,1,0:T(8,128)} %broadcast_in_dim.88), calls=%async_computation.2 | async-start | bytes 786432 | tf_op jit(solution)/shard_map/all_to_all | solution.py:474
  163.7 8.8 %collective-permute-start.22 = (f32[48,1024]{1,0:T(8,128)S(1)}, f32[48,1024]{1,0:T(8,128)S(1)}, u32[]{:S(2)}, u32[]{:S(2)}) collective-permute-start(f32[48,1024]{1,0:T(8,128)S(1)} %broadcast_select_fusion.4), channel_id=1, source_target_pairs={{0,1},{1,0},{4,5},{5,4},{8,9},{9,8},{12,13},{13,12},{16,17},{17,16... | collective-permute-start | bytes 589832 | tf_op jit(solution)/shard_map/ppermute | solution.py:31
  (12 other events, 19.0 us)

commit v4 on v1

--- a/solution.py
+++ b/solution.py
@@ -13,7 +13,6 @@
 NX, NY, NZ = 4, 4, 8
 AXES = ("ylo", "x", "z", "yhi", "c")
 BF16, F16, F32 = jnp.bfloat16, jnp.float16, jnp.float32
-VMEM_BYTES = 20 * 1024 * 1024
 
 
 def flat_index(x, y, z, c):
@@ -35,9 +34,10 @@
     return send(array, lambda x, y, c: (x, y, 1 - c))
 
 
-def together(arrays, routes):
-    arrays = lax.optimization_barrier(tuple(arrays))
-    return lax.optimization_barrier(tuple(send(a, to) for a, to in zip(arrays, routes, strict=True)))
+def together(arrays, routes, beside=None, extra=()):
+    arrays = lax.optimization_barrier((*arrays, *extra))
+    sent = tuple(send(a, to) for a, to in zip(arrays, routes))
+    return lax.optimization_barrier((*sent, *(beside(*arrays[len(sent) :]) if beside else ())))
 
 
 RING = (
@@ -111,17 +111,34 @@
         w_ref[2 * z * turn + turn : 2 * z * turn + 2 * turn, column : column + width] = jnp.where(swap, low, high)
 
 
+def fetched(sems, *pairs):
+    copies = [pltpu.make_async_copy(source, target, sems.at[k]) for k, (source, target) in enumerate(pairs)]
+    for copy in copies:
+        copy.start()
+    return copies
+
+
+def done(copies):
+    for copy in copies:
+        copy.wait()
+
+
 def first_kernel(flag_ref, tokens_ref, own_ref, left_ref, right_ref, low_ref, high_ref, score_ref,
-                 w_ref, slope_ref, curve_ref, lifted_ref, logit_ref, part_ref):
+                 w_hbm, slope_hbm, curve_hbm, lifted_hbm, logit_ref, part_ref,
+                 w_ref, slope_ref, curve_ref, lifted_ref, sems):
     w_ref[:, 0:128] = own_ref[...]
     w_ref[:, 128:256] = left_ref[...]
     w_ref[:, 256:384] = right_ref[...]
     place_pair(w_ref, 384, low_ref, high_ref, flag_ref[0] == 1)
     forward_tiles(tokens_ref, w_ref, score_ref, slope_ref, curve_ref, lifted_ref, logit_ref, None)
+    copies = fetched(
+        sems, (w_ref, w_hbm), (slope_ref, slope_hbm), (curve_ref, curve_hbm), (lifted_ref, lifted_hbm)
+    )
     pull_back(w_ref, lifted_ref, part_ref, None)
-
-
-def tokens_kernel(flag_ref, fake_ref, real_ref, other_ref, tokens_ref, tokens_t_ref, peak_ref):
+    done(copies)
+
+
+def tokens_kernel(flag_ref, fake_ref, real_ref, other_ref, tokens_ref, tokens_t_hbm, peak_ref, tokens_t_ref, sems):
     tok = fake_ref.shape[0]
     first = flag_ref[0] == 0
     for kind, own in enumerate((fake_ref, real_ref)):
@@ -132,20 +149,20 @@
         peak = peak_of(tokens_ref[start : start + 2 * tok, :])
         peak_ref[8 * kind : 8 * kind + 8, :] = jnp.broadcast_to(peak, (8, 128))
     tokens_t_ref[...] = tokens_ref[...].T
-
-
-def second_kernel(flag_ref, tokens_ref, low_ref, high_top_ref, high_bottom_ref, across_top_ref, across_bottom_ref,
-                  score_ref, logit_in_ref, part_in_ref,
-                  w_ref, slope_ref, curve_ref, lifted_ref, logit_ref, part_ref, high_ref):
-    top = high_top_ref.shape[0]
-    high_ref[0:top, :] = high_top_ref[...]
-    high_ref[top : 2 * top, :] = high_bottom_ref[...]
+    done(fetched(sems, (tokens_t_ref, tokens_t_hbm)))
+
+
+def second_kernel(flag_ref, tokens_ref, low_ref, high_ref, across_ref, score_ref, logit_in_ref, part_in_ref,
+                  w_hbm, slope_hbm, curve_hbm, lifted_hbm, logit_ref, part_ref,
+                  w_ref, slope_ref, curve_ref, lifted_ref, sems):
     place_pair(w_ref, 0, low_ref, high_ref, flag_ref[0] == 1)
-    top = across_top_ref.shape[0]
-    w_ref[0:top, 256:384] = across_top_ref[...]
-    w_ref[top : 2 * top, 256:384] = across_bottom_ref[...]
+    w_ref[:, 256:384] = across_ref[...]
     forward_tiles(tokens_ref, w_ref, score_ref, slope_ref, curve_ref, lifted_ref, logit_ref, logit_in_ref)
+    copies = fetched(
+        sems, (w_ref, w_hbm), (slope_ref, slope_hbm), (curve_ref, curve_hbm), (lifted_ref, lifted_hbm)
+    )
     pull_back(w_ref, lifted_ref, part_ref, part_in_ref)
+    done(copies)
 
 
 def peak_of(array):
@@ -153,27 +170,56 @@
     return jnp.max(flat, axis=1, keepdims=True)
 
 
-def term_tiles(scale, tokens_t_ref, r1_t_ref, r1_ref, logits, w_ref, slope_ref, curve_ref, lifted_ref, peak_ref,
-               outs, exp_ref, fake_ref, real_ref):
-    n = lifted_ref.shape[0]
-    fake_gain = scale * jax.nn.sigmoid(logits[:n])
+def cotangents(scale, logits, r1_ref, w_ref, slope_ref, curve_ref, fake_ref, real_ref):
+    n = r1_ref.shape[0]
+    fake_ref[...] = (scale * jax.nn.sigmoid(logits[:n]) * slope_ref[0:n, :]).astype(BF16)
     real_gain = -scale * jax.nn.sigmoid(-logits[n:])
-    fake_ref[...] = (fake_gain * slope_ref[0:n, :]).astype(BF16)
     for start, width in column_tiles(w_ref.shape[1]):
         cols = slice(start, start + width)
         back = jnp.dot(r1_ref[...], w_ref[:, cols], preferred_element_type=F32)
         real_ref[:, cols] = (real_gain * slope_ref[n : 2 * n, cols] + back * curve_ref[:, cols]).astype(BF16)
+
+
+def third_kernel(scale, part_ref, part_in_ref, logit_ref, logit_in_ref, peak_ref,
+                 w_2_hbm, slope_2_hbm, curve_2_hbm, lifted_2_hbm, tokens_t_hbm, w_1_hbm, slope_1_hbm, curve_1_hbm, lifted_1_hbm,
+                 across_hbm, far_low_hbm, far_high_hbm, left_hbm, right_hbm, low_hbm, high_hbm, own_hbm, exp_ref,
+                 across_ref, far_low_ref, far_high_ref, left_ref, right_ref, low_ref, high_ref, own_ref,
+                 r1_t_ref, r1_ref, fake_1_ref, real_1_ref, fake_2_ref, real_2_ref,
+                 tokens_t_ref, w_1_ref, slope_1_ref, curve_1_ref, lifted_1_ref,
+                 w_2_ref, slope_2_ref, curve_2_ref, lifted_2_ref, sems, out_sems):
+    copies = fetched(
+        sems,
+        (w_2_hbm, w_2_ref), (slope_2_hbm, slope_2_ref), (curve_2_hbm, curve_2_ref), (lifted_2_hbm, lifted_2_ref),
+        (w_1_hbm, w_1_ref), (slope_1_hbm, slope_1_ref), (curve_1_hbm, curve_1_ref), (lifted_1_hbm, lifted_1_ref),
+        (tokens_t_hbm, tokens_t_ref),
+    )
+    r1_t_ref[...] = (scale * R1_WEIGHT * (part_ref[...] + part_in_ref[...])).astype(BF16)
+    r1_ref[...] = r1_t_ref[...].T
+    logits = jnp.sum(logit_ref[...] + logit_in_ref[...], axis=1, keepdims=True)
+    done(copies[:4])
+    cotangents(scale, logits, r1_ref, w_2_ref, slope_2_ref, curve_2_ref, fake_2_ref, real_2_ref)
+    done(copies[4:])
+    cotangents(scale, logits, r1_ref, w_1_ref, slope_1_ref, curve_1_ref, fake_1_ref, real_1_ref)
+    first, second = (fake_1_ref, real_1_ref, lifted_1_ref), (fake_2_ref, real_2_ref, lifted_2_ref)
+    peaks = [jnp.maximum(peak_of(one[...]), peak_of(two[...])) for one, two in zip(first, second)]
+    n = r1_ref.shape[0]
     bound = n * (
-        peak_ref[0:1, 0:1] * peak_of(fake_ref[...])
-        + peak_ref[8:9, 0:1] * peak_of(real_ref[...])
-        + peak_of(r1_t_ref[...]) * peak_of(lifted_ref[...])
+        peak_ref[0:1, 0:1] * peaks[0] + peak_ref[8:9, 0:1] * peaks[1] + peak_of(r1_t_ref[...]) * peaks[2]
     )
     bound = jnp.broadcast_to(bound, (16, 128))
     exp_ref[...] = jnp.ceil(jnp.log(jnp.maximum(bound, 1e-30)) * (1.0 / math.log(2.0)) + 0.01) - 15.0
+    outs = [
+        (second, 256, 128, [(0, None, across_ref, across_hbm)]),
+        (second, 0, 256, [(0, 0, far_low_ref, far_low_hbm), (0, 1, far_high_ref, far_high_hbm)]),
+        (first, 128, 256, [(0, None, left_ref, left_hbm), (128, None, right_ref, right_hbm)]),
+        (first, 384, 256, [(0, 0, low_ref, low_hbm), (0, 1, high_ref, high_hbm)]),
+        (first, 0, 128, [(0, None, own_ref, own_hbm)]),
+    ]
     d_in = tokens_t_ref.shape[0]
     turn = d_in // (2 * NZ)
     height = 4 * turn
-    for start, width, parts in outs:
+    leaving = []
+    for (fake_ref, real_ref, lifted_ref), start, width, parts in outs:
         cols = slice(start, start + width)
         for row in range(0, d_in, height):
             rows = slice(row, row + height)
@@ -182,51 +228,37 @@
                 + jnp.dot(tokens_t_ref[rows, n : 2 * n], real_ref[:, cols], preferred_element_type=F32)
                 + jnp.dot(r1_t_ref[rows, :], lifted_ref[:, cols], preferred_element_type=F32)
             )
-            for column, turns, out in parts:
+            for column, turns, out, out_hbm in parts:
                 piece = value[:, column : column + out.shape[1]]
                 if turns is None:
+                    there = rows
                     out[rows, :] = piece
                 else:
+                    there = slice(row // 2, row // 2 + 2 * turn)
                     for k in range(2):
                         at = row // 2 + k * turn
                         out[at : at + turn, :] = piece[(2 * k + turns) * turn : (2 * k + turns + 1) * turn, :]
-
-
-def third_kernel(scale, tokens_t_ref, part_ref, part_in_ref, logit_ref, logit_in_ref, w_ref, slope_ref, curve_ref,
-                 lifted_ref, peak_ref, low_ref, high_ref, across_ref, exp_ref, r1_t_ref, r1_ref, logits_ref,
-                 fake_ref, real_ref):
-    r1_t_ref[...] = (scale * R1_WEIGHT * (part_ref[...] + part_in_ref[...])).astype(BF16)
-    r1_ref[...] = r1_t_ref[...].T
-    logits = jnp.sum(logit_ref[...] + logit_in_ref[...], axis=1, keepdims=True)
-    logits_ref[...] = jnp.broadcast_to(logits, logits_ref.shape)
-    outs = [(0, 256, [(0, 0, low_ref), (0, 1, high_ref)]), (256, 128, [(0, None, across_ref)])]
-    term_tiles(scale, tokens_t_ref, r1_t_ref, r1_ref, logits, w_ref, slope_ref, curve_ref, lifted_ref, peak_ref,
-               outs, exp_ref, fake_ref, real_ref)
-
-
-def fourth_kernel(scale, tokens_t_ref, r1_t_ref, r1_ref, logits_ref, w_ref, slope_ref, curve_ref, lifted_ref, peak_ref,
-                  own_ref, left_ref, right_ref, low_ref, high_ref, exp_ref, fake_ref, real_ref):
-    outs = [
-        (0, 256, [(0, None, own_ref), (128, None, left_ref)]),
-        (256, 128, [(0, None, right_ref)]),
-        (384, 256, [(0, 0, low_ref), (0, 1, high_ref)]),
-    ]
-    term_tiles(scale, tokens_t_ref, r1_t_ref, r1_ref, logits_ref[:, 0:1], w_ref, slope_ref, curve_ref, lifted_ref,
-               peak_ref, outs, exp_ref, fake_ref, real_ref)
-
-
-def call(kernel, flops, outs, scratch, *args, flags=None):
+                leaving.append(
+                    pltpu.make_async_copy(out.at[there, :], out_hbm.at[there, :], out_sems.at[len(leaving)])
+                )
+                leaving[-1].start()
+    done(leaving)
+
+
+def call(kernel, flops, outs, scratch, *args, flags=None, there=(), sems=(), vmem_mib=20):
     vmem = pl.BlockSpec(memory_space=pltpu.VMEM)
-    specs = [vmem] * len(args)
+    specs = [vmem] * len(args) + [pl.BlockSpec(memory_space=pltpu.HBM)] * len(there)
+    args = (*args, *(pltpu.with_memory_space_constraint(a, pltpu.HBM) for a in there))
     if flags is not None:
         args, specs = (flags, *args), [pl.BlockSpec(memory_space=pltpu.SMEM), *specs]
     return pl.pallas_call(
         kernel,
-        out_shape=[jax.ShapeDtypeStruct(shape, dtype) for shape, dtype in outs],
+        out_shape=[(pltpu.HBM if len(out) == 3 else pltpu.VMEM)(*out[:2]) for out in outs],
         in_specs=specs,
-        out_specs=[vmem] * len(outs),
-        scratch_shapes=[pltpu.VMEM(shape, dtype) for shape, dtype in scratch],
-        compiler_params=pltpu.CompilerParams(vmem_limit_bytes=VMEM_BYTES),
+        out_specs=[pl.BlockSpec(memory_space=pltpu.HBM) if len(out) == 3 else vmem for out in outs],
+        scratch_shapes=[pltpu.VMEM(shape, dtype) for shape, dtype in scratch]
+        + [pltpu.SemaphoreType.DMA((k,)) for k in sems],
+        compiler_params=pltpu.CompilerParams(vmem_limit_bytes=vmem_mib * 1024 * 1024),
         cost_estimate=pl.CostEstimate(flops=flops, bytes_accessed=8_000_000, transcendentals=0),
     )(*args)
 
@@ -260,16 +292,18 @@
     own_b = ordered(~gray_x, piece_b, far_b, 1)
 
     own_tokens = jnp.concatenate([fake_tokens[0], real_tokens[0]], 0)
-    tokens, tokens_t, peak = call(
-        tokens_kernel, 2 * n * d_in * 128, [((2 * n, d_in), BF16), ((d_in, 2 * n), BF16), ((16, 128), F32)], [],
-        fake_tokens[0], real_tokens[0], to_core(own_tokens),
-        flags=c[None].astype(jnp.int32),
-    )
-
-    left_a, right_a, left_b, right_b = together((own_a, own_a, own_b, own_b), RING)
-    mid_a, mid_b = d_in // 2, d_in // 4
-    across = together((left_a[:mid_a], right_a[mid_a:], left_b[:mid_b], right_b[mid_b:]), RING)
-    across_a, across_b = across[:2], across[2:]
+    def join_tokens(other_tokens):
+        return call(
+            tokens_kernel, 2 * n * d_in * 128,
+            [((2 * n, d_in), BF16), ((d_in, 2 * n), BF16, True), ((16, 128), F32)], [((d_in, 2 * n), BF16)],
+            fake_tokens[0], real_tokens[0], other_tokens,
+            flags=c[None].astype(jnp.int32), sems=[1],
+        )
+
+    left_a, right_a, left_b, right_b, tokens, tokens_t, peak = together(
+        (own_a, own_a, own_b, own_b), RING, join_tokens, (to_core(own_tokens),)
+    )
+    across_a, across_b = together((left_a, left_b), (RING[0], RING[2]))
 
     def score_at(start, width):
         return lax.dynamic_slice_in_dim(score_vector, c * half + start, width, 0)
@@ -292,75 +326,58 @@
 
     wide, narrow = 640, 384
     w_1, slope_1, curve_1, lifted_1, logit_1, part_1 = call(
-        first_kernel, 6 * n * d_in * wide, states(wide), [],
+        first_kernel, 6 * n * d_in * wide,
+        [*((*state, True) for state in states(wide)[:4]), *states(wide)[4:]], states(wide)[:4],
         tokens, own_a, left_a, right_a, left_b, right_b, score_1,
-        flags=yhi_left[None].astype(jnp.int32),
+        flags=yhi_left[None].astype(jnp.int32), sems=[4],
     )
     w_2, slope_2, curve_2, lifted_2, logit, part = call(
-        second_kernel, 6 * n * d_in * narrow, states(narrow), [((d_in // 2, 256), BF16)],
-        tokens, own_b, *across_b, *across_a, score_2, logit_1, part_1,
-        flags=yhi[None].astype(jnp.int32),
+        second_kernel, 6 * n * d_in * narrow,
+        [*((*state, True) for state in states(narrow)[:4]), *states(narrow)[4:]], states(narrow)[:4],
+        tokens, own_b, across_b, across_a, score_2, logit_1, part_1,
+        flags=yhi[None].astype(jnp.int32), sems=[4],
     )
     part_in, logit_in = to_core(part), to_core(logit)
 
     def works(width):
         return [((n, width), BF16)] * 2
 
-    side = [((d_in // 2, 256), F32)] * 2
-    strip = ((d_in, 128), F32)
-    low_2, high_2, far_a, exp_2, r1_t, r1, logits = call(
-        functools.partial(third_kernel, scale), 8 * n * d_in * narrow,
-        [*side, strip, ((16, 128), F32), ((d_in, n), BF16), ((n, d_in), BF16), ((2 * n, 128), F32)],
-        works(narrow),
-        tokens_t, part, part_in, logit, logit_in, w_2, slope_2, curve_2, lifted_2, peak,
-    )
-    own_1, left_1, right_1, low_1, high_1, exp_1 = call(
-        functools.partial(fourth_kernel, scale), 8 * n * d_in * wide,
-        [strip, strip, strip, *side, ((16, 128), F32)], works(wide),
-        tokens_t, r1_t, r1, logits, w_1, slope_1, curve_1, lifted_1, peak,
-    )
-    exp_1, exp_2 = exp_1[:1], exp_2[:1]
+    strip, side = ((d_in, 128), F32), [((d_in // 2, 256), F32)] * 2
+    results = [strip, *side, strip, strip, *side, strip]
+    across_a, far_low, far_high, left_a, right_a, low_b, high_b, own_a, exponent = call(
+        functools.partial(third_kernel, scale), 8 * n * d_in * half,
+        [*((*shape, True) for shape in results), ((16, 128), F32)],
+        [*results, ((d_in, n), BF16), ((n, d_in), BF16), *works(wide), *works(narrow), ((d_in, 2 * n), BF16),
+         *states(wide)[:4], *states(narrow)[:4]],
+        part, part_in, logit, logit_in, peak,
+        there=(w_2, slope_2, curve_2, lifted_2, tokens_t, w_1, slope_1, curve_1, lifted_1), sems=[9, 32], vmem_mib=36,
+    )
+    exponent = exponent[:1]
     twice = lambda row: jnp.concatenate([row, row], 1)
 
-    own_2 = jnp.where(yhi == 0, low_2, high_2)
-    far_b = jnp.where(yhi == 0, high_2, low_2)
-    a_up, a_down, b_up, b_down = together(
+    own_b = jnp.where(yhi == 0, far_low, far_high)
+    across_b = jnp.where(yhi == 0, far_high, far_low)
+    right_b = jnp.where(yhi_right == 0, low_b, high_b)
+    left_b = jnp.where(yhi_left == 0, low_b, high_b)
+    arrived = together(
         (
-            packed(far_a[:mid_a], exp_2),
-            packed(far_a[mid_a:], exp_2),
-            packed(far_b[:mid_b], twice(exp_2)),
-            packed(far_b[mid_b:], twice(exp_2)),
+            packed(across_a, exponent),
+            packed(across_b, twice(exponent)),
+            packed(right_a, exponent),
+            packed(left_a, exponent),
+            packed(right_b, twice(exponent)),
+            packed(left_b, twice(exponent)),
         ),
-        RING,
-    )
-
-    def joined(piece, exponent, top=None, bottom=None):
-        middle = piece.shape[0] // 2
-        values, theirs = unpacked(bottom if top is None else top)
-        exponent = jnp.maximum(exponent, theirs) + 1.0
-        upper, lower = piece[:middle], piece[middle:]
-        upper, lower = (upper, lower + values) if top is None else (upper + values, lower)
-        return packed(jnp.concatenate([upper, lower], 0), exponent)
-
-    right_b = jnp.where(yhi_right == 0, low_1, high_1)
-    left_b = jnp.where(yhi_left == 0, low_1, high_1)
-    from_left_a, from_right_a, from_left_b, from_right_b = together(
-        (
-            joined(right_1, exp_1, top=a_up),
-            joined(left_1, exp_1, bottom=a_down),
-            joined(right_b, twice(exp_1), top=b_up),
-            joined(left_b, twice(exp_1), bottom=b_down),
-        ),
-        RING,
-    )
-
-    def three(own, exponent, one, two):
-        (one, exp_one), (two, exp_two) = unpacked(one), unpacked(two)
-        return own + one + two, jnp.maximum(exponent, jnp.maximum(exp_one, exp_two)) + 2.0
-
-    top = jnp.maximum(exp_1, exp_2)
-    sum_a, exp_a = three(own_1, top, from_left_a, from_right_a)
-    sum_b, exp_b = three(own_2, twice(top), from_left_b, from_right_b)
+        (lambda x, y, c: (x + 2, y, c), lambda x, y, c: (x, y + 2, c), *RING),
+    )
+
+    def summed(own, exponent, *messages):
+        for values, theirs in map(unpacked, messages):
+            own, exponent = own + values, jnp.maximum(exponent, theirs)
+        return own, exponent + 2.0
+
+    sum_a, exp_a = summed(own_a, exponent, arrived[2], arrived[3], arrived[0])
+    sum_b, exp_b = summed(own_b, twice(exponent), arrived[4], arrived[5], arrived[1])
 
     turns = sum_a.reshape(NZ, 2, 2 * rows, 128)
     keep_a = jnp.where(yhi == 0, turns[:, 0], turns[:, 1]).reshape(d_in // 2, 128)

time: 165 us -> 168 us (1.018)
  waiting for transfers between devices: 32 us -> 63.1 us
  blocking collectives: 33.5 us -> 14 us
  local copies, waits for them, and re-layouts: 16.2 us -> 7.51 us
  starting transfers between devices: 52.9 us -> 44.4 us
  Pallas kernels: 22.8 us -> 29 us
  other arithmetic: 6.5 us -> 8.6 us
    all_to_all x1 -> x0, blocking collectives: 20.2 us -> none  [per_device(): lax.all_to_all(jnp.broadcast_to(block[None], (NZ, *block.shape)), 'z', 0, 0)]
    ppermute x27 -> x23, waiting for transfers between devices: 25.2 us -> 43 us  [send(): return lax.ppermute(array, AXES, pairs)]
    ppermute x27 -> x23, starting transfers between devices: 48.1 us -> 34.4 us  [send(): return lax.ppermute(array, AXES, pairs)]
    all_to_all x0 -> x1, waiting for transfers between devices: none -> 13.4 us  [per_device(): lax.all_to_all(jnp.broadcast_to(block[None], (NZ, *block.shape)), 'z', 0, 0)]
    all_to_all x0 -> x1, starting transfers between devices: none -> 6.45 us  [per_device(): lax.all_to_all(jnp.broadcast_to(block[None], (NZ, *block.shape)), 'z', 0, 0)]
    pallas_call x5 -> x4, Pallas kernels: 22.8 us -> 29 us  [call(): pl.pallas_call(kernel, out_shape=[(pltpu.HBM if len(out) == 3 else pltpu....]
    unnamed x49 -> x33, local copies, waits for them, and re-layouts: 10.4 us -> 4.72 us
    slice x4 -> x0, local copies, waits for them, and re-layouts: 3.77 us -> none  [the longest x1 0.94 us: per_device(): right_a[mid_a:]]
  transfers between devices with their start and end apart: 28 -> 25, of which waited for: 10 -> 17; matrix products, arithmetic and copies ran while one was open for 2% -> 2% of each run, Pallas kernels for 7% -> 5%
where the time goes in v4:
time: 168 us; the launch traced here: 167 us
  waiting for transfers between devices  63.1 us (38%)
  starting transfers between devices  44.4 us (26%)
  Pallas kernels  29 us (17%)
  blocking collectives  14 us (8%)
  other arithmetic  8.6 us (5%)
  local copies, waits for them, and re-layouts  7.51 us (4%)
    ppermute x23, waiting for transfers between devices, send(): return lax.ppermute(array, AXES, pairs)  43 us
    ppermute x23, starting transfers between devices, send(): return lax.ppermute(array, AXES, pairs)  34.4 us
    pallas_call x4, Pallas kernels, call(): pl.pallas_call(kernel, out_shape=[(pltpu.HBM if len(out) == 3 else pltpu....  29 us
    all_to_all x1, blocking collectives, per_device(): both = jnp.sum(lax.all_to_all(both, 'z', 0, 0), 0)  14 us
    all_to_all x1, waiting for transfers between devices, per_device(): lax.all_to_all(jnp.broadcast_to(block[None], (NZ, *block.shape)), 'z', 0, 0)  13.4 us
    all_to_all x1, waiting for transfers between devices, per_device(): lax.all_to_all(jnp.broadcast_to(both[None], (8, *both.shape)), ('ylo', 'x...  6.77 us
    all_to_all x1, starting transfers between devices, per_device(): lax.all_to_all(jnp.broadcast_to(block[None], (NZ, *block.shape)), 'z', 0, 0)  6.45 us
    unnamed x33, local copies, waits for them, and re-layouts  4.72 us
  transfers between devices with their start and end apart: 25, of which 17 were waited for; matrix products, arithmetic and copies ran while one was open for 2% of the time, Pallas kernels for 5%

profile of v4, /device:TPU:1, one launch (start us, length us, event | category | flops | bytes accessed | tf_op | source)
XLA Modules:
  0.0 167.2 jit_solution(12922421295023536327)
XLA Ops:
  1.0 3.3 %collective-permute-start = (bf16[48,256]{1,0:T(8,128)(2,1)S(1)}, bf16[48,256]{1,0:T(8,128)(2,1)S(1)}, u32[]{:S(2)}, u32[]{:S(2)}) collective-permute-start(bf16[48,256]{1,0:T(8,128)(2,1)S(1)} %pad_maximum_fusion.15), channel_id=1, source_target_pairs={{0,1},{1,0},{4,5},{5,4},{8,9},{9,8},{12,13},{13,12},{16,17},{17,16... | collective-permute-start | bytes 73736 | tf_op jit(solution)/shard_map/ppermute | solution.py:30
  6.0 6.5 %all-to-all-start = ((bf16[8,96,256]{2,1,0:T(8,128)(2,1)}), bf16[8,96,256]{2,1,0:T(8,128)(2,1)S(1)}, u32[]{:S(2)}, u32[]{:S(2)}) async-start(bf16[8,96,256]{2,1,0:T(8,128)(2,1)} %broadcast_in_dim.29), calls=%async_computation | async-start | bytes 786432 | tf_op jit(solution)/shard_map/all_to_all | solution.py:285
  14.2 13.4 %all-to-all-done = bf16[8,96,256]{2,1,0:T(8,128)(2,1)S(1)} async-done(((bf16[8,96,256]{2,1,0:T(8,128)(2,1)}), bf16[8,96,256]{2,1,0:T(8,128)(2,1)S(1)}, u32[]{:S(2)}, u32[]{:S(2)}) %all-to-all-start) | async-done | bytes 393248 | tf_op jit(solution)/shard_map/all_to_all | solution.py:285
  27.6 2.8 %collective-permute-start.1 = (bf16[768,128]{1,0:T(8,128)(2,1)S(1)}, bf16[768,128]{1,0:T(8,128)(2,1)S(1)}, u32[]{:S(2)}, u32[]{:S(2)}) collective-permute-start(bf16[768,128]{1,0:T(8,128)(2,1)S(1)} %bitcast.176), channel_id=1, source_target_pairs={{0,130},{1,131},{4,134},{5,135},{8,138},{9,139},{12,142},{13,143},... | collective-permute-start | bytes 589832 | tf_op jit(solution)/shard_map/ppermute | solution.py:30
  31.7 3.4 %collective-permute-done.1 = bf16[768,128]{1,0:T(8,128)(2,1)S(1)} collective-permute-done((bf16[768,128]{1,0:T(8,128)(2,1)S(1)}, bf16[768,128]{1,0:T(8,128)(2,1)S(1)}, u32[]{:S(2)}, u32[]{:S(2)}) %collective-permute-start.1) | collective-permute-done | bytes 196640 | tf_op jit(solution)/shard_map/ppermute | solution.py:30
  41.1 1.5 collective-permute-start.5
  42.6 2.7 %collective-permute-start.7 = (bf16[768,256]{1,0:T(8,128)(2,1)}, bf16[768,256]{1,0:T(8,128)(2,1)}, u32[]{:S(2)}, u32[]{:S(2)}) collective-permute-start(bf16[768,256]{1,0:T(8,128)(2,1)} %pad_maximum_fusion.8.low_ref), channel_id=1, source_target_pairs={{0,130},{1,131},{4,134},{5,135},{8,138},{9,139},{12,142},{13,143},... | collective-permute-start | bytes 1179656 | tf_op jit(solution)/shard_map/ppermute | solution.py:30
  45.4 1.3 copy-done.3
  46.7 2.9 %shard_map.46 = (bf16[768,1536]{1,0:T(8,128)(2,1)S(1)}, bf16[1536,768]{1,0:T(8,128)(2,1)}, f32[16,128]{1,0:T(8,128)S(1)}) custom-call(s32[1]{0:T(128)} %bitcast.10.flag_ref, bf16[192,1536]{1,0:T(8,128)(2,1)S(1)} %bitcast.161, bf16[192,1536]{1,0:T(8,128)(2,1)S(1)} %bitcast.163, bf16[384,1536]{1,0:T(8,128)(2,1)S(1)} %copy-done.3), custom_call_target="tpu_custom_call" | custom-call | flops 150994944 | bytes 8000000 | tf_op jit(solution)/shard_map/pallas_call | solution.py:254
  50.3 2.1 %collective-permute-done.6.low_ref = bf16[768,256]{1,0:T(8,128)(2,1)} collective-permute-done((bf16[768,256]{1,0:T(8,128)(2,1)}, bf16[768,256]{1,0:T(8,128)(2,1)}, u32[]{:S(2)}, u32[]{:S(2)}) %collective-permute-start.6) | collective-permute-done | bytes 393248 | tf_op jit(solution)/shard_map/ppermute | solution.py:30
  52.5 5.8 %shard_map.47 = (bf16[1536,640]{1,0:T(8,128)(2,1)}, f32[768,640]{1,0:T(8,128)}, f32[384,640]{1,0:T(8,128)}, bf16[384,640]{1,0:T(8,128)(2,1)}, f32[768,128]{1,0:T(8,128)S(1)}, /*index=5*/f32[1536,384]{1,0:T(8,128)S(1)}) custom-call(s32[1]{0:T(128)} %bitcast.11.flag_ref, bf16[768,1536]{1,0:T(8,128)(2,1)S(1)} %get-tuple-element.81.tokens_ref, ...), custom_call_target="tpu_custom_call" | custom-call | flops 2264924160 | bytes 8000000 | tf_op jit(solution)/shard_map/pallas_call | solution.py:254
  58.3 3.0 %collective-permute-done.8.across_ref = bf16[1536,128]{1,0:T(8,128)(2,1)S(1)} collective-permute-done((bf16[1536,128]{1,0:T(8,128)(2,1)}, bf16[1536,128]{1,0:T(8,128)(2,1)S(1)}, u32[]{:S(2)}, u32[]{:S(2)}) %collective-permute-start.8) | collective-permute-done | bytes 393248 | tf_op jit(solution)/shard_map/ppermute | solution.py:30
  61.4 5.5 %shard_map.48 = (bf16[1536,384]{1,0:T(8,128)(2,1)}, f32[768,384]{1,0:T(8,128)}, f32[384,384]{1,0:T(8,128)}, bf16[384,384]{1,0:T(8,128)(2,1)}, f32[768,128]{1,0:T(8,128)S(1)}, /*index=5*/f32[1536,384]{1,0:T(8,128)}) custom-call(s32[1]{0:T(128)} %bitcast.flag_ref, bf16[768,1536]{1,0:T(8,128)(2,1)S(1)} %get-tuple-element.81.tokens_ref, ...), custom_call_target="tpu_custom_call" | custom-call | flops 1358954496 | bytes 8000000 | tf_op jit(solution)/shard_map/pallas_call | solution.py:254
  66.9 4.2 %collective-permute-start.10 = (f32[1536,384]{1,0:T(8,128)}, f32[1536,384]{1,0:T(8,128)S(1)}, u32[]{:S(2)}, u32[]{:S(2)}) collective-permute-start(f32[1536,384]{1,0:T(8,128)} %get-tuple-element.92.part_ref), channel_id=1, source_target_pairs={{0,1},{1,0},{4,5},{5,4},{8,9},{9,8},{12,13},{13,12},{16,17},{17,16... | collective-permute-start | bytes 7077896 | tf_op jit(solution)/shard_map/ppermute | solution.py:30
  71.3 4.4 %collective-permute-done.11.logit_in_ref = f32[768,128]{1,0:T(8,128)S(1)} collective-permute-done((f32[768,128]{1,0:T(8,128)S(1)}, f32[768,128]{1,0:T(8,128)S(1)}, u32[]{:S(2)}, u32[]{:S(2)}) %collective-permute-start.11) | collective-permute-done | bytes 393248 | tf_op jit(solution)/shard_map/ppermute | solution.py:30
  75.7 14.8 %shard_map.49 = (f32[1536,128]{1,0:T(8,128)}, f32[768,256]{1,0:T(8,128)}, f32[768,256]{1,0:T(8,128)}, f32[1536,128]{1,0:T(8,128)}, f32[1536,128]{1,0:T(8,128)}, ...) custom-call(f32[1536,384]{1,0:T(8,128)} %get-tuple-element.92.part_ref, ...), custom_call_target="tpu_custom_call" | custom-call | flops 4831838208 | bytes 8000000 | tf_op jit(solution)/shard_map/pallas_call | solution.py:254
  90.5 1.9 %multiply_convert_fusion = (f16[768,256]{1,0:T(8,128)(2,1)S(1)}, f16[768,256]{1,0:T(8,128)(2,1)S(1)}, f16[768,256]{1,0:T(8,128)(2,1)S(1)}) fusion(f32[768,256]{1,0:T(8,128)} %get-tuple-element.111, f32[768,256]{1,0:T(8,128)} %get-tuple-element.112, f32[256]{0:T(256)S(1)} %get-tuple-element.188, pred[]{:T(512)S(6)} %eq.46, pred[]{:T(512)S(6)} %eq.45, ...), kind=kLoop, calls=%fused_computation.3 | loop fusion | flops 1769472 | bytes 4326403 | tf_op jit(solution)/shard_map/convert_element_type | solution.py:58
  94.6 2.5 %collective-permute-start.12 = (f16[1552,128]{1,0:T(8,128)(2,1)S(1)}, f16[1552,128]{1,0:T(8,128)(2,1)S(1)}, u32[]{:S(2)}, u32[]{:S(2)}) collective-permute-start(f16[1552,128]{1,0:T(8,128)(2,1)S(1)} %get-tuple-element.113), channel_id=1, source_target_pairs={{0,64},{1,65},{4,68},{5,69},{8,72},{9,73},{12,76},{13,77},{16,80},... | collective-permute-start | bytes 1191944 | tf_op jit(solution)/shard_map/ppermute | solution.py:30
  97.7 1.3 collective-permute-start.16
  98.9 1.4 collective-permute-start.17
  101.1 5.6 %collective-permute-done.12 = f16[1552,128]{1,0:T(8,128)(2,1)S(1)} collective-permute-done((f16[1552,128]{1,0:T(8,128)(2,1)S(1)}, f16[1552,128]{1,0:T(8,128)(2,1)S(1)}, u32[]{:S(2)}, u32[]{:S(2)}) %collective-permute-start.12) | collective-permute-done | bytes 397344 | tf_op jit(solution)/shard_map/ppermute | solution.py:30
  106.7 2.6 %collective-permute-start.15 = (f16[1552,128]{1,0:T(8,128)(2,1)S(1)}, f16[1552,128]{1,0:T(8,128)(2,1)S(1)}, u32[]{:S(2)}, u32[]{:S(2)}) collective-permute-start(f16[1552,128]{1,0:T(8,128)(2,1)S(1)} %get-tuple-element.116), channel_id=1, source_target_pairs={{0,96},{1,97},{4,100},{5,101},{8,104},{9,105},{12,108},{13,109},{1... | collective-permute-start | bytes 1191944 | tf_op jit(solution)/shard_map/ppermute | solution.py:30
  109.3 6.6 %collective-permute-done.14 = f16[1552,128]{1,0:T(8,128)(2,1)S(1)} collective-permute-done((f16[1552,128]{1,0:T(8,128)(2,1)S(1)}, f16[1552,128]{1,0:T(8,128)(2,1)S(1)}, u32[]{:S(2)}, u32[]{:S(2)}) %collective-permute-start.14) | collective-permute-done | bytes 397344 | tf_op jit(solution)/shard_map/ppermute | solution.py:30
  116.6 1.9 %collective-permute-done.16 = f16[784,256]{1,0:T(8,128)(2,1)S(1)} collective-permute-done((f16[784,256]{1,0:T(8,128)(2,1)S(1)}, f16[784,256]{1,0:T(8,128)(2,1)S(1)}, u32[]{:S(2)}, u32[]{:S(2)}) %collective-permute-start.16) | collective-permute-done | bytes 401440 | tf_op jit(solution)/shard_map/ppermute | solution.py:30
  120.6 1.3 collective-permute-start.18
  122.7 5.3 %collective-permute-done.18 = f16[784,128]{1,0:T(8,128)(2,1)S(1)} collective-permute-done((f16[784,128]{1,0:T(8,128)(2,1)S(1)}, f16[784,128]{1,0:T(8,128)(2,1)S(1)}, u32[]{:S(2)}, u32[]{:S(2)}) %collective-permute-start.18) | collective-permute-done | bytes 200736 | tf_op jit(solution)/shard_map/ppermute | solution.py:30
  128.4 4.9 %collective-permute-done.20 = f32[8,48,128]{2,1,0:T(8,128)S(1)} collective-permute-done((f32[8,48,128]{2,1,0:T(8,128)S(1)}, f32[8,48,128]{2,1,0:T(8,128)S(1)}, u32[]{:S(2)}, u32[]{:S(2)}) %collective-permute-start.20) | collective-permute-done | bytes 196640 | tf_op jit(solution)/shard_map/ppermute | solution.py:30
  133.3 1.3 collective-permute-done.21
  134.8 14.0 %all_to_all.15 = f32[8,48,256]{2,1,0:T(8,128)S(1)} all-to-all(f32[8,48,256]{2,1,0:T(8,128)S(1)} %pad_maximum_fusion.9), channel_id=1, replica_groups=mesh['ylo'=2,'x'=4,'z'=8,'yhi'=2,'c'=2] {'z'}, dimensions={0} | all-to-all | bytes 786432 | tf_op jit(solution)/shard_map/all_to_all | solution.py:403
  149.6 3.5 %all-to-all-start.2 = ((f32[8,48,256]{2,1,0:T(8,128)}), f32[8,48,256]{2,1,0:T(8,128)S(1)}, u32[]{:S(2)}, u32[]{:S(2)}) async-start(f32[8,48,256]{2,1,0:T(8,128)} %broadcast_in_dim.79), calls=%async_computation.2 | async-start | bytes 786432 | tf_op jit(solution)/shard_map/all_to_all | solution.py:405
  153.1 6.8 %all-to-all-done.2 = f32[8,48,256]{2,1,0:T(8,128)S(1)} async-done(((f32[8,48,256]{2,1,0:T(8,128)}), f32[8,48,256]{2,1,0:T(8,128)S(1)}, u32[]{:S(2)}, u32[]{:S(2)}) %all-to-all-start.2) | async-done | bytes 393248 | tf_op jit(solution)/shard_map/all_to_all | solution.py:405
  160.0 5.2 %collective-permute-start.22 = (f32[48,1024]{1,0:T(8,128)S(1)}, f32[48,1024]{1,0:T(8,128)S(1)}, u32[]{:S(2)}, u32[]{:S(2)}) collective-permute-start(f32[48,1024]{1,0:T(8,128)S(1)} %broadcast_select_fusion.4), channel_id=1, source_target_pairs={{0,1},{1,0},{4,5},{5,4},{8,9},{9,8},{12,13},{13,12},{16,17},{17,16... | collective-permute-start | bytes 589832 | tf_op jit(solution)/shard_map/ppermute | solution.py:30
  (114 shorter events, 23.2 us)
Async XLA Ops:
  0.0 12.4 %copy-start = (bf16[1,192,1536]{2,1,0:T(8,128)(2,1)S(1)}, bf16[1,192,1536]{2,1,0:T(8,128)(2,1)}, u32[]{:S(2)}) copy-start(bf16[1,192,1536]{2,1,0:T(8,128)(2,1)} %param.4) | copy-start | bytes 1769476
  0.0 12.4 %copy-start.1 = (bf16[1,192,1536]{2,1,0:T(8,128)(2,1)S(1)}, bf16[1,192,1536]{2,1,0:T(8,128)(2,1)}, u32[]{:S(2)}) copy-start(bf16[1,192,1536]{2,1,0:T(8,128)(2,1)} %param.5) | copy-start | bytes 1769476
  1.0 4.2 %collective-permute-start = (bf16[48,256]{1,0:T(8,128)(2,1)S(1)}, bf16[48,256]{1,0:T(8,128)(2,1)S(1)}, u32[]{:S(2)}, u32[]{:S(2)}) collective-permute-start(bf16[48,256]{1,0:T(8,128)(2,1)S(1)} %pad_maximum_fusion.15), channel_id=1, source_target_pairs={{0,1},{1,0},{4,5},{5,4},{8,9},{9,8},{12,13},{13,12},{16,17},{17,16... | collective-permute-start | bytes 73736 | tf_op jit(solution)/shard_map/ppermute | solution.py:30
  6.0 21.6 %all-to-all-start = ((bf16[8,96,256]{2,1,0:T(8,128)(2,1)}), bf16[8,96,256]{2,1,0:T(8,128)(2,1)S(1)}, u32[]{:S(2)}, u32[]{:S(2)}) async-start(bf16[8,96,256]{2,1,0:T(8,128)(2,1)} %broadcast_in_dim.29), calls=%async_computation | async-start | bytes 786432 | tf_op jit(solution)/shard_map/all_to_all | solution.py:285
  13.6 31.6 %copy-start.10 = (f32[2048]{0:T(1024)S(1)}, f32[2048]{0:T(1024)}, u32[]{:S(2)}) copy-start(f32[2048]{0:T(1024)} %param.7) | copy-start | bytes 24580
  13.6 25.2 %collective-permute-start.3 = (bf16[384,1536]{1,0:T(8,128)(2,1)}, bf16[384,1536]{1,0:T(8,128)(2,1)S(1)}, u32[]{:S(2)}, u32[]{:S(2)}) collective-permute-start(bf16[384,1536]{1,0:T(8,128)(2,1)} %pad_maximum_fusion), channel_id=1, source_target_pairs={{0,1},{1,0},{4,5},{5,4},{8,9},{9,8},{12,13},{13,12},{16,17},{17,16... | collective-permute-start | bytes 3538952 | tf_op jit(solution)/shard_map/ppermute | solution.py:30
  27.6 7.4 %collective-permute-start.1 = (bf16[768,128]{1,0:T(8,128)(2,1)S(1)}, bf16[768,128]{1,0:T(8,128)(2,1)S(1)}, u32[]{:S(2)}, u32[]{:S(2)}) collective-permute-start(bf16[768,128]{1,0:T(8,128)(2,1)S(1)} %bitcast.176), channel_id=1, source_target_pairs={{0,130},{1,131},{4,134},{5,135},{8,138},{9,139},{12,142},{13,143},... | collective-permute-start | bytes 589832 | tf_op jit(solution)/shard_map/ppermute | solution.py:30
  30.5 5.8 %collective-permute-start.2 = (bf16[768,128]{1,0:T(8,128)(2,1)S(1)}, bf16[768,128]{1,0:T(8,128)(2,1)}, u32[]{:S(2)}, u32[]{:S(2)}) collective-permute-start(bf16[768,128]{1,0:T(8,128)(2,1)S(1)} %bitcast.174), channel_id=1, source_target_pairs={{0,32},{1,33},{4,36},{5,37},{8,40},{9,41},{12,44},{13,45},{16,48},... | collective-permute-start | bytes 589832 | tf_op jit(solution)/shard_map/ppermute | solution.py:30
  39.9 10.5 %collective-permute-start.4 = (bf16[1536,128]{1,0:T(8,128)(2,1)}, bf16[1536,128]{1,0:T(8,128)(2,1)}, u32[]{:S(2)}, u32[]{:S(2)}) collective-permute-start(bf16[1536,128]{1,0:T(8,128)(2,1)} %bitcast.7.own_ref), channel_id=1, source_target_pairs={{0,32},{1,33},{4,36},{5,37},{8,40},{9,41},{12,44},{13,45},{16,48},... | collective-permute-start | bytes 1179656 | tf_op jit(solution)/shard_map/ppermute | solution.py:30
  41.1 9.3 %collective-permute-start.5 = (bf16[1536,128]{1,0:T(8,128)(2,1)}, bf16[1536,128]{1,0:T(8,128)(2,1)}, u32[]{:S(2)}, u32[]{:S(2)}) collective-permute-start(bf16[1536,128]{1,0:T(8,128)(2,1)} %bitcast.7.own_ref), channel_id=1, source_target_pairs={{0,96},{1,97},{4,100},{5,101},{8,104},{9,105},{12,108},{13,109},{1... | collective-permute-start | bytes 1179656 | tf_op jit(solution)/shard_map/ppermute | solution.py:30
  42.5 9.9 %collective-permute-start.6 = (bf16[768,256]{1,0:T(8,128)(2,1)}, bf16[768,256]{1,0:T(8,128)(2,1)}, u32[]{:S(2)}, u32[]{:S(2)}) collective-permute-start(bf16[768,256]{1,0:T(8,128)(2,1)} %pad_maximum_fusion.8.low_ref), channel_id=1, source_target_pairs={{0,128},{1,129},{4,132},{5,133},{8,136},{9,137},{12,140},{13,141},... | collective-permute-start | bytes 1179656 | tf_op jit(solution)/shard_map/ppermute | solution.py:30
  42.6 9.9 %collective-permute-start.7 = (bf16[768,256]{1,0:T(8,128)(2,1)}, bf16[768,256]{1,0:T(8,128)(2,1)}, u32[]{:S(2)}, u32[]{:S(2)}) collective-permute-start(bf16[768,256]{1,0:T(8,128)(2,1)} %pad_maximum_fusion.8.low_ref), channel_id=1, source_target_pairs={{0,130},{1,131},{4,134},{5,135},{8,138},{9,139},{12,142},{13,143},... | collective-permute-start | bytes 1179656 | tf_op jit(solution)/shard_map/ppermute | solution.py:30
  52.5 8.9 %collective-permute-start.8 = (bf16[1536,128]{1,0:T(8,128)(2,1)}, bf16[1536,128]{1,0:T(8,128)(2,1)S(1)}, u32[]{:S(2)}, u32[]{:S(2)}) collective-permute-start(bf16[1536,128]{1,0:T(8,128)(2,1)} %collective-permute-done.4.left_ref), channel_id=1, source_target_pairs={{0,32},{1,33},{4,36},{5,37},{8,40},{9,41},{12,44},{13,45},{16,48},... | collective-permute-start | bytes 1179656 | tf_op jit(solution)/shard_map/ppermute | solution.py:30
  52.5 8.9 %collective-permute-start.9 = (bf16[768,256]{1,0:T(8,128)(2,1)}, bf16[768,256]{1,0:T(8,128)(2,1)S(1)}, u32[]{:S(2)}, u32[]{:S(2)}) collective-permute-start(bf16[768,256]{1,0:T(8,128)(2,1)} %collective-permute-done.6.low_ref), channel_id=1, source_target_pairs={{0,128},{1,129},{4,132},{5,133},{8,136},{9,137},{12,140},{13,141},... | collective-permute-start | bytes 1179656 | tf_op jit(solution)/shard_map/ppermute | solution.py:30
  66.9 8.9 %collective-permute-start.10 = (f32[1536,384]{1,0:T(8,128)}, f32[1536,384]{1,0:T(8,128)S(1)}, u32[]{:S(2)}, u32[]{:S(2)}) collective-permute-start(f32[1536,384]{1,0:T(8,128)} %get-tuple-element.92.part_ref), channel_id=1, source_target_pairs={{0,1},{1,0},{4,5},{5,4},{8,9},{9,8},{12,13},{13,12},{16,17},{17,16... | collective-permute-start | bytes 7077896 | tf_op jit(solution)/shard_map/ppermute | solution.py:30
  71.0 4.7 %collective-permute-start.11 = (f32[768,128]{1,0:T(8,128)S(1)}, f32[768,128]{1,0:T(8,128)S(1)}, u32[]{:S(2)}, u32[]{:S(2)}) collective-permute-start(f32[768,128]{1,0:T(8,128)S(1)} %get-tuple-element.93.logit_ref), channel_id=1, source_target_pairs={{0,1},{1,0},{4,5},{5,4},{8,9},{9,8},{12,13},{13,12},{16,17},{17,16... | collective-permute-start | bytes 1179656 | tf_op jit(solution)/shard_map/ppermute | solution.py:30
  92.5 1.4 copy-start.8
  92.5 1.6 copy-start.9
  94.3 24.3 %copy-start.6 = (f32[1536,128]{1,0:T(8,128)S(1)}, f32[1536,128]{1,0:T(8,128)}, u32[]{:S(2)}) copy-start(f32[1536,128]{1,0:T(8,128)} %get-tuple-element.104) | copy-start | bytes 2359300
  94.6 12.0 %collective-permute-start.12 = (f16[1552,128]{1,0:T(8,128)(2,1)S(1)}, f16[1552,128]{1,0:T(8,128)(2,1)S(1)}, u32[]{:S(2)}, u32[]{:S(2)}) collective-permute-start(f16[1552,128]{1,0:T(8,128)(2,1)S(1)} %get-tuple-element.113), channel_id=1, source_target_pairs={{0,64},{1,65},{4,68},{5,69},{8,72},{9,73},{12,76},{13,77},{16,80},... | collective-permute-start | bytes 1191944 | tf_op jit(solution)/shard_map/ppermute | solution.py:30
  97.2 19.4 %collective-permute-start.13 = (f16[784,256]{1,0:T(8,128)(2,1)S(1)}, f16[784,256]{1,0:T(8,128)(2,1)S(1)}, u32[]{:S(2)}, u32[]{:S(2)}) collective-permute-start(f16[784,256]{1,0:T(8,128)(2,1)S(1)} %get-tuple-element.114), channel_id=1, source_target_pairs={{0,2},{1,3},{4,6},{5,7},{8,10},{9,11},{12,14},{13,15},{16,18},{17,... | collective-permute-start | bytes 1204232 | tf_op jit(solution)/shard_map/ppermute | solution.py:30
  97.7 20.8 %collective-permute-start.16 = (f16[784,256]{1,0:T(8,128)(2,1)S(1)}, f16[784,256]{1,0:T(8,128)(2,1)S(1)}, u32[]{:S(2)}, u32[]{:S(2)}) collective-permute-start(f16[784,256]{1,0:T(8,128)(2,1)S(1)} %get-tuple-element.117), channel_id=1, source_target_pairs={{0,128},{1,129},{4,132},{5,133},{8,136},{9,137},{12,140},{13,141},... | collective-permute-start | bytes 1204232 | tf_op jit(solution)/shard_map/ppermute | solution.py:30
  98.9 19.6 %collective-permute-start.17 = (f16[784,256]{1,0:T(8,128)(2,1)S(1)}, f16[784,256]{1,0:T(8,128)(2,1)S(1)}, u32[]{:S(2)}, u32[]{:S(2)}) collective-permute-start(f16[784,256]{1,0:T(8,128)(2,1)S(1)} %get-tuple-element.118), channel_id=1, source_target_pairs={{0,130},{1,131},{4,134},{5,135},{8,138},{9,139},{12,142},{13,143},... | collective-permute-start | bytes 1204232 | tf_op jit(solution)/shard_map/ppermute | solution.py:30
  100.3 15.5 %collective-permute-start.14 = (f16[1552,128]{1,0:T(8,128)(2,1)S(1)}, f16[1552,128]{1,0:T(8,128)(2,1)S(1)}, u32[]{:S(2)}, u32[]{:S(2)}) collective-permute-start(f16[1552,128]{1,0:T(8,128)(2,1)S(1)} %get-tuple-element.115), channel_id=1, source_target_pairs={{0,32},{1,33},{4,36},{5,37},{8,40},{9,41},{12,44},{13,45},{16,48},... | collective-permute-start | bytes 1191944 | tf_op jit(solution)/shard_map/ppermute | solution.py:30
  106.7 9.9 %collective-permute-start.15 = (f16[1552,128]{1,0:T(8,128)(2,1)S(1)}, f16[1552,128]{1,0:T(8,128)(2,1)S(1)}, u32[]{:S(2)}, u32[]{:S(2)}) collective-permute-start(f16[1552,128]{1,0:T(8,128)(2,1)S(1)} %get-tuple-element.116), channel_id=1, source_target_pairs={{0,96},{1,97},{4,100},{5,101},{8,104},{9,105},{12,108},{13,109},{1... | collective-permute-start | bytes 1191944 | tf_op jit(solution)/shard_map/ppermute | solution.py:30
  118.6 1.4 copy-start.5
  120.6 7.4 %collective-permute-start.18 = (f16[784,128]{1,0:T(8,128)(2,1)S(1)}, f16[784,128]{1,0:T(8,128)(2,1)S(1)}, u32[]{:S(2)}, u32[]{:S(2)}) collective-permute-start(f16[784,128]{1,0:T(8,128)(2,1)S(1)} %pad_maximum_fusion.11), channel_id=1, source_target_pairs={{0,130},{1,131},{4,134},{5,135},{8,138},{9,139},{12,142},{13,143},... | collective-permute-start | bytes 602120 | tf_op jit(solution)/shard_map/ppermute | solution.py:30
  121.8 6.1 %collective-permute-start.19 = (f16[784,128]{1,0:T(8,128)(2,1)S(1)}, f16[784,128]{1,0:T(8,128)(2,1)S(1)}, u32[]{:S(2)}, u32[]{:S(2)}) collective-permute-start(f16[784,128]{1,0:T(8,128)(2,1)S(1)} %pad_maximum_fusion.12), channel_id=1, source_target_pairs={{0,32},{1,33},{4,36},{5,37},{8,40},{9,41},{12,44},{13,45},{16,48},... | collective-permute-start | bytes 602120 | tf_op jit(solution)/shard_map/ppermute | solution.py:30
  128.2 5.1 %collective-permute-start.20 = (f32[8,48,128]{2,1,0:T(8,128)S(1)}, f32[8,48,128]{2,1,0:T(8,128)S(1)}, u32[]{:S(2)}, u32[]{:S(2)}) collective-permute-start(f32[8,48,128]{2,1,0:T(8,128)S(1)} %select_bitcast_fusion), channel_id=1, source_target_pairs={{0,128},{1,129},{4,132},{5,133},{8,136},{9,137},{12,140},{13,141},... | collective-permute-start | bytes 589832 | tf_op jit(solution)/shard_map/ppermute | solution.py:30
  128.3 6.4 %collective-permute-start.21 = (f32[8,48,128]{2,1,0:T(8,128)S(1)}, f32[8,48,128]{2,1,0:T(8,128)S(1)}, u32[]{:S(2)}, u32[]{:S(2)}) collective-permute-start(f32[8,48,128]{2,1,0:T(8,128)S(1)} %fusion.3), channel_id=1, source_target_pairs={{0,96},{1,97},{4,100},{5,101},{8,104},{9,105},{12,108},{13,109},{1... | collective-permute-start | bytes 589832 | tf_op jit(solution)/shard_map/ppermute | solution.py:30
  149.6 10.2 %all-to-all-start.2 = ((f32[8,48,256]{2,1,0:T(8,128)}), f32[8,48,256]{2,1,0:T(8,128)S(1)}, u32[]{:S(2)}, u32[]{:S(2)}) async-start(f32[8,48,256]{2,1,0:T(8,128)} %broadcast_in_dim.79), calls=%async_computation.2 | async-start | bytes 786432 | tf_op jit(solution)/shard_map/all_to_all | solution.py:405
  160.0 6.3 %collective-permute-start.22 = (f32[48,1024]{1,0:T(8,128)S(1)}, f32[48,1024]{1,0:T(8,128)S(1)}, u32[]{:S(2)}, u32[]{:S(2)}) collective-permute-start(f32[48,1024]{1,0:T(8,128)S(1)} %broadcast_select_fusion.4), channel_id=1, source_target_pairs={{0,1},{1,0},{4,5},{5,4},{8,9},{9,8},{12,13},{13,12},{16,17},{17,16... | collective-permute-start | bytes 589832 | tf_op jit(solution)/shard_map/ppermute | solution.py:30
  (4 other events, 4.6 us)

commit v5 on v4

--- a/solution.py
+++ b/solution.py
@@ -138,11 +138,17 @@
     done(copies)
 
 
-def tokens_kernel(flag_ref, fake_ref, real_ref, other_ref, tokens_ref, tokens_t_hbm, peak_ref, tokens_t_ref, sems):
-    tok = fake_ref.shape[0]
+def tokens_kernel(flag_ref, fake_hbm, real_hbm, other_hbm, tokens_ref, tokens_t_hbm, peak_ref,
+                  own_ref, other_ref, tokens_t_ref, sems):
+    tok = fake_hbm.shape[0]
+    done(
+        fetched(
+            sems, (fake_hbm, own_ref.at[0:tok, :]), (real_hbm, own_ref.at[tok : 2 * tok, :]), (other_hbm, other_ref)
+        )
+    )
     first = flag_ref[0] == 0
-    for kind, own in enumerate((fake_ref, real_ref)):
-        mine, theirs = own[...], other_ref[kind * tok : kind * tok + tok, :]
+    for kind in (0, 1):
+        mine, theirs = (ref[kind * tok : kind * tok + tok, :] for ref in (own_ref, other_ref))
         start = 2 * kind * tok
         tokens_ref[start : start + tok, :] = jnp.where(first, mine, theirs)
         tokens_ref[start + tok : start + 2 * tok, :] = jnp.where(first, theirs, mine)
@@ -180,42 +186,8 @@
         real_ref[:, cols] = (real_gain * slope_ref[n : 2 * n, cols] + back * curve_ref[:, cols]).astype(BF16)
 
 
-def third_kernel(scale, part_ref, part_in_ref, logit_ref, logit_in_ref, peak_ref,
-                 w_2_hbm, slope_2_hbm, curve_2_hbm, lifted_2_hbm, tokens_t_hbm, w_1_hbm, slope_1_hbm, curve_1_hbm, lifted_1_hbm,
-                 across_hbm, far_low_hbm, far_high_hbm, left_hbm, right_hbm, low_hbm, high_hbm, own_hbm, exp_ref,
-                 across_ref, far_low_ref, far_high_ref, left_ref, right_ref, low_ref, high_ref, own_ref,
-                 r1_t_ref, r1_ref, fake_1_ref, real_1_ref, fake_2_ref, real_2_ref,
-                 tokens_t_ref, w_1_ref, slope_1_ref, curve_1_ref, lifted_1_ref,
-                 w_2_ref, slope_2_ref, curve_2_ref, lifted_2_ref, sems, out_sems):
-    copies = fetched(
-        sems,
-        (w_2_hbm, w_2_ref), (slope_2_hbm, slope_2_ref), (curve_2_hbm, curve_2_ref), (lifted_2_hbm, lifted_2_ref),
-        (w_1_hbm, w_1_ref), (slope_1_hbm, slope_1_ref), (curve_1_hbm, curve_1_ref), (lifted_1_hbm, lifted_1_ref),
-        (tokens_t_hbm, tokens_t_ref),
-    )
-    r1_t_ref[...] = (scale * R1_WEIGHT * (part_ref[...] + part_in_ref[...])).astype(BF16)
-    r1_ref[...] = r1_t_ref[...].T
-    logits = jnp.sum(logit_ref[...] + logit_in_ref[...], axis=1, keepdims=True)
-    done(copies[:4])
-    cotangents(scale, logits, r1_ref, w_2_ref, slope_2_ref, curve_2_ref, fake_2_ref, real_2_ref)
-    done(copies[4:])
-    cotangents(scale, logits, r1_ref, w_1_ref, slope_1_ref, curve_1_ref, fake_1_ref, real_1_ref)
-    first, second = (fake_1_ref, real_1_ref, lifted_1_ref), (fake_2_ref, real_2_ref, lifted_2_ref)
-    peaks = [jnp.maximum(peak_of(one[...]), peak_of(two[...])) for one, two in zip(first, second)]
-    n = r1_ref.shape[0]
-    bound = n * (
-        peak_ref[0:1, 0:1] * peaks[0] + peak_ref[8:9, 0:1] * peaks[1] + peak_of(r1_t_ref[...]) * peaks[2]
-    )
-    bound = jnp.broadcast_to(bound, (16, 128))
-    exp_ref[...] = jnp.ceil(jnp.log(jnp.maximum(bound, 1e-30)) * (1.0 / math.log(2.0)) + 0.01) - 15.0
-    outs = [
-        (second, 256, 128, [(0, None, across_ref, across_hbm)]),
-        (second, 0, 256, [(0, 0, far_low_ref, far_low_hbm), (0, 1, far_high_ref, far_high_hbm)]),
-        (first, 128, 256, [(0, None, left_ref, left_hbm), (128, None, right_ref, right_hbm)]),
-        (first, 384, 256, [(0, 0, low_ref, low_hbm), (0, 1, high_ref, high_hbm)]),
-        (first, 0, 128, [(0, None, own_ref, own_hbm)]),
-    ]
-    d_in = tokens_t_ref.shape[0]
+def term_tiles(outs, tokens_t_ref, r1_t_ref, sems):
+    d_in, n = r1_t_ref.shape
     turn = d_in // (2 * NZ)
     height = 4 * turn
     leaving = []
@@ -239,10 +211,68 @@
                         at = row // 2 + k * turn
                         out[at : at + turn, :] = piece[(2 * k + turns) * turn : (2 * k + turns + 1) * turn, :]
                 leaving.append(
-                    pltpu.make_async_copy(out.at[there, :], out_hbm.at[there, :], out_sems.at[len(leaving)])
+                    pltpu.make_async_copy(out.at[there, :], out_hbm.at[there, :], sems.at[len(leaving)])
                 )
                 leaving[-1].start()
     done(leaving)
+
+
+def third_kernel(scale, part_ref, part_in_ref, logit_ref, logit_in_ref, peak_ref,
+                 w_2_hbm, slope_2_hbm, curve_2_hbm, w_1_hbm, slope_1_hbm, curve_1_hbm, lifted_1_hbm, lifted_2_hbm,
+                 tokens_t_hbm,
+                 across_hbm, low_hbm, high_hbm, r1_t_hbm, fake_1_hbm, real_1_hbm, exp_ref,
+                 across_ref, low_ref, high_ref, r1_t_ref, fake_1_ref, real_1_ref, r1_ref, fake_2_ref, real_2_ref,
+                 w_2_ref, slope_2_ref, curve_2_ref, w_1_ref, slope_1_ref, curve_1_ref, lifted_1_ref, lifted_2_ref,
+                 tokens_t_ref, sems, r1_sems, out_sems):
+    copies = fetched(
+        sems,
+        (w_2_hbm, w_2_ref), (slope_2_hbm, slope_2_ref), (curve_2_hbm, curve_2_ref),
+        (w_1_hbm, w_1_ref), (slope_1_hbm, slope_1_ref), (curve_1_hbm, curve_1_ref),
+        (lifted_1_hbm, lifted_1_ref), (lifted_2_hbm, lifted_2_ref), (tokens_t_hbm, tokens_t_ref),
+    )
+    r1_t_ref[...] = (scale * R1_WEIGHT * (part_ref[...] + part_in_ref[...])).astype(BF16)
+    r1_ref[...] = r1_t_ref[...].T
+    logits = jnp.sum(logit_ref[...] + logit_in_ref[...], axis=1, keepdims=True)
+    done(copies[:3])
+    cotangents(scale, logits, r1_ref, w_2_ref, slope_2_ref, curve_2_ref, fake_2_ref, real_2_ref)
+    done(copies[3:6])
+    cotangents(scale, logits, r1_ref, w_1_ref, slope_1_ref, curve_1_ref, fake_1_ref, real_1_ref)
+    passed = fetched(r1_sems, (r1_t_ref, r1_t_hbm), (fake_1_ref, fake_1_hbm), (real_1_ref, real_1_hbm))
+    done(copies[6:])
+    first, second = (fake_1_ref, real_1_ref, lifted_1_ref), (fake_2_ref, real_2_ref, lifted_2_ref)
+    peaks = [jnp.maximum(peak_of(one[...]), peak_of(two[...])) for one, two in zip(first, second)]
+    n = r1_ref.shape[0]
+    bound = n * (
+        peak_ref[0:1, 0:1] * peaks[0] + peak_ref[8:9, 0:1] * peaks[1] + peak_of(r1_t_ref[...]) * peaks[2]
+    )
+    bound = jnp.broadcast_to(bound, (16, 128))
+    exp_ref[...] = jnp.ceil(jnp.log(jnp.maximum(bound, 1e-30)) * (1.0 / math.log(2.0)) + 0.01) - 15.0
+    outs = [
+        (second, 256, 128, [(0, None, across_ref, across_hbm)]),
+        (second, 0, 256, [(0, 0, low_ref, low_hbm), (0, 1, high_ref, high_hbm)]),
+    ]
+    term_tiles(outs, tokens_t_ref, r1_t_ref, out_sems)
+    done(passed)
+
+
+def fourth_kernel(r1_t_hbm, fake_hbm, real_hbm, lifted_hbm, tokens_t_hbm,
+                  left_hbm, right_hbm, low_hbm, high_hbm, own_hbm,
+                  left_ref, right_ref, low_ref, high_ref, own_ref,
+                  r1_t_ref, fake_ref, real_ref, lifted_ref, tokens_t_ref, sems, out_sems):
+    done(
+        fetched(
+            sems,
+            (r1_t_hbm, r1_t_ref), (fake_hbm, fake_ref), (real_hbm, real_ref), (lifted_hbm, lifted_ref),
+            (tokens_t_hbm, tokens_t_ref),
+        )
+    )
+    first = fake_ref, real_ref, lifted_ref
+    outs = [
+        (first, 128, 256, [(0, None, left_ref, left_hbm), (128, None, right_ref, right_hbm)]),
+        (first, 384, 256, [(0, 0, low_ref, low_hbm), (0, 1, high_ref, high_hbm)]),
+        (first, 0, 128, [(0, None, own_ref, own_hbm)]),
+    ]
+    term_tiles(outs, tokens_t_ref, r1_t_ref, out_sems)
 
 
 def call(kernel, flops, outs, scratch, *args, flags=None, there=(), sems=(), vmem_mib=20):
@@ -295,9 +325,9 @@
     def join_tokens(other_tokens):
         return call(
             tokens_kernel, 2 * n * d_in * 128,
-            [((2 * n, d_in), BF16), ((d_in, 2 * n), BF16, True), ((16, 128), F32)], [((d_in, 2 * n), BF16)],
-            fake_tokens[0], real_tokens[0], other_tokens,
-            flags=c[None].astype(jnp.int32), sems=[1],
+            [((2 * n, d_in), BF16), ((d_in, 2 * n), BF16, True), ((16, 128), F32)],
+            [((n, d_in), BF16), ((n, d_in), BF16), ((d_in, 2 * n), BF16)],
+            flags=c[None].astype(jnp.int32), there=(fake_tokens[0], real_tokens[0], other_tokens), sems=[3],
         )
 
     left_a, right_a, left_b, right_b, tokens, tokens_t, peak = together(
@@ -342,34 +372,47 @@
     def works(width):
         return [((n, width), BF16)] * 2
 
+    marked = lambda shapes: [(*shape, True) for shape in shapes]
     strip, side = ((d_in, 128), F32), [((d_in // 2, 256), F32)] * 2
-    results = [strip, *side, strip, strip, *side, strip]
-    across_a, far_low, far_high, left_a, right_a, low_b, high_b, own_a, exponent = call(
-        functools.partial(third_kernel, scale), 8 * n * d_in * half,
-        [*((*shape, True) for shape in results), ((16, 128), F32)],
-        [*results, ((d_in, n), BF16), ((n, d_in), BF16), *works(wide), *works(narrow), ((d_in, 2 * n), BF16),
-         *states(wide)[:4], *states(narrow)[:4]],
+    tall, r1_shape = ((d_in, 2 * n), BF16), ((d_in, n), BF16)
+    results = [strip, *side, r1_shape, *works(wide)]
+    across_a, far_low, far_high, r1_t, fake_1, real_1, exponent = call(
+        functools.partial(third_kernel, scale), 6 * n * d_in * half,
+        [*marked(results), ((16, 128), F32)],
+        [*results, ((n, d_in), BF16), *works(narrow), *states(narrow)[:3], *states(wide)[:4], states(narrow)[3], tall],
         part, part_in, logit, logit_in, peak,
-        there=(w_2, slope_2, curve_2, lifted_2, tokens_t, w_1, slope_1, curve_1, lifted_1), sems=[9, 32], vmem_mib=36,
+        there=(w_2, slope_2, curve_2, w_1, slope_1, curve_1, lifted_1, lifted_2, tokens_t),
+        sems=[9, 3, 12], vmem_mib=36,
     )
     exponent = exponent[:1]
     twice = lambda row: jnp.concatenate([row, row], 1)
 
     own_b = jnp.where(yhi == 0, far_low, far_high)
     across_b = jnp.where(yhi == 0, far_high, far_low)
-    right_b = jnp.where(yhi_right == 0, low_b, high_b)
-    left_b = jnp.where(yhi_left == 0, low_b, high_b)
-    arrived = together(
-        (
-            packed(across_a, exponent),
-            packed(across_b, twice(exponent)),
+
+    def rest_of_term(r1_t):
+        shapes = [strip, strip, *side, strip]
+        left_a, right_a, low_b, high_b, own_a = call(
+            fourth_kernel, 6 * n * d_in * wide, marked(shapes), [*shapes, r1_shape, *works(wide), states(wide)[3], tall],
+            there=(r1_t, fake_1, real_1, lifted_1, tokens_t), sems=[5, 20], vmem_mib=28,
+        )
+        right_b = jnp.where(yhi_right == 0, low_b, high_b)
+        left_b = jnp.where(yhi_left == 0, low_b, high_b)
+        return (
             packed(right_a, exponent),
             packed(left_a, exponent),
             packed(right_b, twice(exponent)),
             packed(left_b, twice(exponent)),
-        ),
-        (lambda x, y, c: (x + 2, y, c), lambda x, y, c: (x, y + 2, c), *RING),
-    )
+            own_a,
+        )
+
+    across_a, across_b, *beside, own_a = together(
+        (packed(across_a, exponent), packed(across_b, twice(exponent))),
+        (lambda x, y, c: (x + 2, y, c), lambda x, y, c: (x, y + 2, c)),
+        rest_of_term,
+        (r1_t,),
+    )
+    arrived = (across_a, across_b, *together(beside, RING))
 
     def summed(own, exponent, *messages):
         for values, theirs in map(unpacked, messages):
@@ -379,27 +422,26 @@
     sum_a, exp_a = summed(own_a, exponent, arrived[2], arrived[3], arrived[0])
     sum_b, exp_b = summed(own_b, twice(exponent), arrived[4], arrived[5], arrived[1])
 
-    turns = sum_a.reshape(NZ, 2, 2 * rows, 128)
-    keep_a = jnp.where(yhi == 0, turns[:, 0], turns[:, 1]).reshape(d_in // 2, 128)
-    give_a = jnp.where(yhi == 0, turns[:, 1], turns[:, 0]).reshape(d_in // 2, 128)
-    keep_b = jnp.where(gray_x, sum_b[:, 128:], sum_b[:, :128])
-    give_b = jnp.where(gray_x, sum_b[:, :128], sum_b[:, 128:])
-    got_a, got_b = together(
-        (packed(give_a, exp_a), packed(give_b, exp_b[:, :128])),
-        (lambda x, y, c: (x, 3 - y, c), lambda x, y, c: (x ^ 1, y, c)),
-    )
-    turns_a = (keep_a + unpacked(got_a)[0]).reshape(NZ, 2, rows, 128)
-    turns_b = (keep_b + unpacked(got_b)[0]).reshape(NZ, 2, rows, 128)
-
-    def split_rows(turns, second):
-        return jnp.where(second, turns[:, 1], turns[:, 0]), jnp.where(second, turns[:, 0], turns[:, 1])
-
-    keep_a, give_a = split_rows(turns_a, gray_y)
-    keep_b, give_b = split_rows(turns_b, x >= 2)
-    got_a, got_b = together(
-        (give_a, give_b), (lambda x, y, c: (x, y ^ 1, c), lambda x, y, c: (3 - x, y, c))
-    )
-    both = jnp.concatenate([keep_a + got_a, keep_b + got_b], 2)
+    quarters_a = sum_a.reshape(NZ, 4, rows, 128)
+    turns_b = sum_b.reshape(NZ, 2, rows, 256)
+    quarters_b = jnp.stack(
+        [turns_b[:, 0, :, :128], turns_b[:, 0, :, 128:], turns_b[:, 1, :, 128:], turns_b[:, 1, :, :128]], 1
+    )
+    gray_order = (0, 1, 3, 2)
+    quarters_a = jnp.stack([quarters_a[:, k] for k in gray_order], 1)
+
+    def quarter(array, k):
+        return lax.dynamic_index_in_dim(array, k % 4, 1, keepdims=False).reshape(NZ * rows, 128)
+
+    away = (1, 3, 2)
+    got = together(
+        [packed(quarter(quarters_a, y + k), exp_a) for k in away]
+        + [packed(quarter(quarters_b, x + k), exp_b[:, :128]) for k in away],
+        [RING[2], RING[3], lambda x, y, c: (x, y + 2, c), RING[0], RING[1], lambda x, y, c: (x + 2, y, c)],
+    )
+    sum_a, _ = summed(quarter(quarters_a, y), exp_a, *got[:3])
+    sum_b, _ = summed(quarter(quarters_b, x), exp_b[:, :128], *got[3:])
+    both = jnp.concatenate([sum_a, sum_b], 1).reshape(NZ, rows, 256)
     both = jnp.sum(lax.all_to_all(both, "z", 0, 0), 0)
 
     spread = lax.all_to_all(jnp.broadcast_to(both[None], (8, *both.shape)), ("ylo", "x"), 0, 0)

time: 168 us -> 161 us (0.958)
  waiting for transfers between devices: 63.1 us -> 47.7 us
  starting transfers between devices: 44.4 us -> 51.4 us
  Pallas kernels: 29 us -> 32.1 us
  other arithmetic: 8.6 us -> 6.32 us
    ppermute x23 -> x25, waiting for transfers between devices: 43 us -> 26.6 us  [send(): return lax.ppermute(array, AXES, pairs)]
    ppermute x23 -> x25, starting transfers between devices: 34.4 us -> 41.5 us  [send(): return lax.ppermute(array, AXES, pairs)]
    pallas_call x4 -> x5, Pallas kernels: 29 us -> 32.1 us  [call(): pl.pallas_call(kernel, out_shape=[(pltpu.HBM if len(out) == 3 else pltpu....]
    convert_element_type x4 -> x6, other arithmetic: 2.26 us -> 3.38 us  [packed(): scaled = (piece * jnp.exp2(-exponent)).astype(F16)]
    unnamed x33 -> x44, local copies, waits for them, and re-layouts: 4.72 us -> 5.72 us
  transfers between devices with their start and end apart: 25 -> 27, of which waited for: 17 -> 14; matrix products, arithmetic and copies ran while one was open for 2% -> 2% of each run, Pallas kernels for 5% -> 11%
where the time goes in v5:
time: 161 us; the launch traced here: 160 us
  starting transfers between devices  51.4 us (32%)
  waiting for transfers between devices  47.7 us (30%)
  Pallas kernels  32.1 us (20%)
  blocking collectives  13.3 us (8%)
  local copies, waits for them, and re-layouts  8.7 us (5%)
  other arithmetic  6.32 us (4%)
    ppermute x25, starting transfers between devices, send(): return lax.ppermute(array, AXES, pairs)  41.5 us
    pallas_call x5, Pallas kernels, call(): pl.pallas_call(kernel, out_shape=[(pltpu.HBM if len(out) == 3 else pltpu....  32.1 us
    ppermute x25, waiting for transfers between devices, send(): return lax.ppermute(array, AXES, pairs)  26.6 us
    all_to_all x1, waiting for transfers between devices, per_device(): lax.all_to_all(jnp.broadcast_to(block[None], (NZ, *block.shape)), 'z', 0, 0)  14.3 us
    all_to_all x1, blocking collectives, per_device(): both = jnp.sum(lax.all_to_all(both, 'z', 0, 0), 0)  13.3 us
    all_to_all x1, waiting for transfers between devices, per_device(): lax.all_to_all(jnp.broadcast_to(both[None], (8, *both.shape)), ('ylo', 'x...  6.77 us
    all_to_all x1, starting transfers between devices, per_device(): lax.all_to_all(jnp.broadcast_to(block[None], (NZ, *block.shape)), 'z', 0, 0)  6.45 us
    unnamed x44, local copies, waits for them, and re-layouts  5.72 us
  transfers between devices with their start and end apart: 27, of which 14 were waited for; matrix products, arithmetic and copies ran while one was open for 2% of the time, Pallas kernels for 11%

profile of v5, /device:TPU:1, one launch (start us, length us, event | category | flops | bytes accessed | tf_op | source)
XLA Modules:
  0.0 160.2 jit_solution(6236185571634742040)
XLA Ops:
  1.0 3.3 %collective-permute-start = (bf16[48,256]{1,0:T(8,128)(2,1)S(1)}, bf16[48,256]{1,0:T(8,128)(2,1)S(1)}, u32[]{:S(2)}, u32[]{:S(2)}) collective-permute-start(bf16[48,256]{1,0:T(8,128)(2,1)S(1)} %pad_maximum_fusion.21), channel_id=1, source_target_pairs={{0,1},{1,0},{4,5},{5,4},{8,9},{9,8},{12,13},{13,12},{16,17},{17,16... | collective-permute-start | bytes 73736 | tf_op jit(solution)/shard_map/ppermute | solution.py:30
  6.0 6.5 %all-to-all-start = ((bf16[8,96,256]{2,1,0:T(8,128)(2,1)}), bf16[8,96,256]{2,1,0:T(8,128)(2,1)S(1)}, u32[]{:S(2)}, u32[]{:S(2)}) async-start(bf16[8,96,256]{2,1,0:T(8,128)(2,1)} %broadcast_in_dim.29), calls=%async_computation | async-start | bytes 786432 | tf_op jit(solution)/shard_map/all_to_all | solution.py:315
  13.2 14.3 %all-to-all-done = bf16[8,96,256]{2,1,0:T(8,128)(2,1)S(1)} async-done(((bf16[8,96,256]{2,1,0:T(8,128)(2,1)}), bf16[8,96,256]{2,1,0:T(8,128)(2,1)S(1)}, u32[]{:S(2)}, u32[]{:S(2)}) %all-to-all-start) | async-done | bytes 393248 | tf_op jit(solution)/shard_map/all_to_all | solution.py:315
  27.6 2.8 %collective-permute-start.1 = (bf16[768,128]{1,0:T(8,128)(2,1)S(1)}, bf16[768,128]{1,0:T(8,128)(2,1)S(1)}, u32[]{:S(2)}, u32[]{:S(2)}) collective-permute-start(bf16[768,128]{1,0:T(8,128)(2,1)S(1)} %bitcast.179), channel_id=1, source_target_pairs={{0,130},{1,131},{4,134},{5,135},{8,138},{9,139},{12,142},{13,143},... | collective-permute-start | bytes 589832 | tf_op jit(solution)/shard_map/ppermute | solution.py:30
  31.7 3.4 %collective-permute-done.1 = bf16[768,128]{1,0:T(8,128)(2,1)S(1)} collective-permute-done((bf16[768,128]{1,0:T(8,128)(2,1)S(1)}, bf16[768,128]{1,0:T(8,128)(2,1)S(1)}, u32[]{:S(2)}, u32[]{:S(2)}) %collective-permute-start.1) | collective-permute-done | bytes 196640 | tf_op jit(solution)/shard_map/ppermute | solution.py:30
  37.6 1.5 collective-permute-start.5
  39.1 2.7 %collective-permute-start.7 = (bf16[768,256]{1,0:T(8,128)(2,1)S(1)}, bf16[768,256]{1,0:T(8,128)(2,1)}, u32[]{:S(2)}, u32[]{:S(2)}) collective-permute-start(bf16[768,256]{1,0:T(8,128)(2,1)S(1)} %pad_maximum_fusion.10.low_ref), channel_id=1, source_target_pairs={{0,130},{1,131},{4,134},{5,135},{8,138},{9,139},{12,142},{13,143},... | collective-permute-start | bytes 1179656 | tf_op jit(solution)/shard_map/ppermute | solution.py:30
  41.9 4.5 %shard_map.46 = (bf16[768,1536]{1,0:T(8,128)(2,1)S(1)}, bf16[1536,768]{1,0:T(8,128)(2,1)}, f32[16,128]{1,0:T(8,128)S(1)}) custom-call(s32[1]{0:T(128)} %bitcast.10.flag_ref, bf16[192,1536]{1,0:T(8,128)(2,1)} %bitcast.167, bf16[192,1536]{1,0:T(8,128)(2,1)} %bitcast.169, bf16[384,1536]{1,0:T(8,128)(2,1)} %copy-done.10), custom_call_target="tpu_custom_call" | custom-call | flops 150994944 | bytes 8000000 | tf_op jit(solution)/shard_map/pallas_call | solution.py:284
  46.7 2.1 %collective-permute-done.6.low_ref = bf16[768,256]{1,0:T(8,128)(2,1)S(1)} collective-permute-done((bf16[768,256]{1,0:T(8,128)(2,1)S(1)}, bf16[768,256]{1,0:T(8,128)(2,1)S(1)}, u32[]{:S(2)}, u32[]{:S(2)}) %collective-permute-start.6) | collective-permute-done | bytes 393248 | tf_op jit(solution)/shard_map/ppermute | solution.py:30
  51.6 5.5 %shard_map.47 = (bf16[1536,640]{1,0:T(8,128)(2,1)}, f32[768,640]{1,0:T(8,128)}, f32[384,640]{1,0:T(8,128)}, bf16[384,640]{1,0:T(8,128)(2,1)}, f32[768,128]{1,0:T(8,128)S(1)}, /*index=5*/f32[1536,384]{1,0:T(8,128)S(1)}) custom-call(s32[1]{0:T(128)} %bitcast.11.flag_ref, bf16[768,1536]{1,0:T(8,128)(2,1)S(1)} %get-tuple-element.94.tokens_ref, ...), custom_call_target="tpu_custom_call" | custom-call | flops 2264924160 | bytes 8000000 | tf_op jit(solution)/shard_map/pallas_call | solution.py:284
  57.1 1.4 collective-permute-done.8.across_ref
  58.5 1.7 %copy-done.1 = bf16[768,1536]{1,0:T(8,128)(2,1)S(1)} copy-done((bf16[768,1536]{1,0:T(8,128)(2,1)S(1)}, bf16[768,1536]{1,0:T(8,128)(2,1)}, u32[]{:S(2)}) %copy-start.1) | copy-done | bytes 2359320
  60.2 4.3 %shard_map.48 = (bf16[1536,384]{1,0:T(8,128)(2,1)}, f32[768,384]{1,0:T(8,128)}, f32[384,384]{1,0:T(8,128)}, bf16[384,384]{1,0:T(8,128)(2,1)}, f32[768,128]{1,0:T(8,128)}, /*index=5*/f32[1536,384]{1,0:T(8,128)S(1)}) custom-call(s32[1]{0:T(128)} %bitcast.flag_ref, bf16[768,1536]{1,0:T(8,128)(2,1)S(1)} %copy-done.1, ...), custom_call_target="tpu_custom_call" | custom-call | flops 1358954496 | bytes 8000000 | tf_op jit(solution)/shard_map/pallas_call | solution.py:284
  64.5 4.0 %collective-permute-start.10 = (f32[1536,384]{1,0:T(8,128)S(1)}, f32[1536,384]{1,0:T(8,128)}, u32[]{:S(2)}, u32[]{:S(2)}) collective-permute-start(f32[1536,384]{1,0:T(8,128)S(1)} %get-tuple-element.105.part_ref), channel_id=1, source_target_pairs={{0,1},{1,0},{4,5},{5,4},{8,9},{9,8},{12,13},{13,12},{16,17},{17,16... | collective-permute-start | bytes 7077896 | tf_op jit(solution)/shard_map/ppermute | solution.py:30
  68.6 4.7 %collective-permute-done.11.logit_in_ref = f32[768,128]{1,0:T(8,128)S(1)} collective-permute-done((f32[768,128]{1,0:T(8,128)}, f32[768,128]{1,0:T(8,128)S(1)}, u32[]{:S(2)}, u32[]{:S(2)}) %collective-permute-start.11) | collective-permute-done | bytes 393248 | tf_op jit(solution)/shard_map/ppermute | solution.py:30
  73.4 10.9 %shard_map.49 = (f32[1536,128]{1,0:T(8,128)}, f32[768,256]{1,0:T(8,128)}, f32[768,256]{1,0:T(8,128)}, bf16[1536,384]{1,0:T(8,128)(2,1)}, bf16[384,640]{1,0:T(8,1...) custom-call(f32[1536,384]{1,0:T(8,128)S(1)} %get-tuple-element.105.part_ref, ...), custom_call_target="tpu_custom_call" | custom-call | flops 3623878656 | bytes 8000000 | tf_op jit(solution)/shard_map/pallas_call | solution.py:284
  84.3 1.3 multiply_convert_fusion.4
  86.0 1.8 %collective-permute-start.13 = (f16[784,256]{1,0:T(8,128)(2,1)S(1)}, f16[784,256]{1,0:T(8,128)(2,1)S(1)}, u32[]{:S(2)}, u32[]{:S(2)}) collective-permute-start(f16[784,256]{1,0:T(8,128)(2,1)S(1)} %pad_maximum_fusion.5), channel_id=1, source_target_pairs={{0,2},{1,3},{4,6},{5,7},{8,10},{9,11},{12,14},{13,15},{16,18},{17,... | collective-permute-start | bytes 1204232 | tf_op jit(solution)/shard_map/ppermute | solution.py:30
  87.7 2.4 %collective-permute-start.12 = (f16[1552,128]{1,0:T(8,128)(2,1)S(1)}, f16[1552,128]{1,0:T(8,128)(2,1)S(1)}, u32[]{:S(2)}, u32[]{:S(2)}) collective-permute-start(f16[1552,128]{1,0:T(8,128)(2,1)S(1)} %pad_maximum_fusion.8), channel_id=1, source_target_pairs={{0,64},{1,65},{4,68},{5,69},{8,72},{9,73},{12,76},{13,77},{16,80},... | collective-permute-start | bytes 1191944 | tf_op jit(solution)/shard_map/ppermute | solution.py:30
  90.2 6.9 %shard_map.50 = (f32[1536,128]{1,0:T(8,128)}, f32[1536,128]{1,0:T(8,128)}, f32[768,256]{1,0:T(8,128)}, f32[768,256]{1,0:T(8,128)}, f32[1536,128]{1,0:T(8,128)}) custom-call(bf16[1536,384]{1,0:T(8,128)(2,1)} %get-tuple-element.124.r1_t_hbm, bf16[384,640]{1,0:T(8,128)(2,1)} %get-tuple-element.125.fake_hbm, bf16[384,640]{1,0:T(8,128)(2,1)} %get-tuple-element.126.real_hbm, ...), custom_call_target="tpu_custom_call" | custom-call | flops 2264924160 | bytes 8000000 | tf_op jit(solution)/shard_map/pallas_call | solution.py:284
  97.1 1.6 %multiply_convert_fusion.2 = (f16[1536,128]{1,0:T(8,128)(2,1)S(1)}, f16[1536,128]{1,0:T(8,128)(2,1)S(1)}) fusion(f32[1536,128]{1,0:T(8,128)} %get-tuple-element.128, f32[128]{0:T(128)S(1)} %get-tuple-element.208, f32[1536,128]{1,0:T(8,128)} %get-tuple-element.127), kind=kLoop, calls=%fused_computation.7 | loop fusion | flops 786432 | bytes 2359808 | tf_op jit(solution)/shard_map/convert_element_type | solution.py:58
  100.1 2.2 %collective-permute-start.17 = (f16[784,256]{1,0:T(8,128)(2,1)S(1)}, f16[784,256]{1,0:T(8,128)(2,1)S(1)}, u32[]{:S(2)}, u32[]{:S(2)}) collective-permute-start(f16[784,256]{1,0:T(8,128)(2,1)S(1)} %get-tuple-element.140), channel_id=1, source_target_pairs={{0,130},{1,131},{4,134},{5,135},{8,138},{9,139},{12,142},{13,143},... | collective-permute-start | bytes 1204232 | tf_op jit(solution)/shard_map/ppermute | solution.py:30
  103.2 1.8 %collective-permute-start.15 = (f16[1552,128]{1,0:T(8,128)(2,1)S(1)}, f16[1552,128]{1,0:T(8,128)(2,1)S(1)}, u32[]{:S(2)}, u32[]{:S(2)}) collective-permute-start(f16[1552,128]{1,0:T(8,128)(2,1)S(1)} %get-tuple-element.138), channel_id=1, source_target_pairs={{0,96},{1,97},{4,100},{5,101},{8,104},{9,105},{12,108},{13,109},{1... | collective-permute-start | bytes 1191944 | tf_op jit(solution)/shard_map/ppermute | solution.py:30
  105.0 7.5 %collective-permute-done.14 = f16[1552,128]{1,0:T(8,128)(2,1)S(1)} collective-permute-done((f16[1552,128]{1,0:T(8,128)(2,1)S(1)}, f16[1552,128]{1,0:T(8,128)(2,1)S(1)}, u32[]{:S(2)}, u32[]{:S(2)}) %collective-permute-start.14) | collective-permute-done | bytes 397344 | tf_op jit(solution)/shard_map/ppermute | solution.py:30
  115.1 2.7 %collective-permute-start.19 = (f16[400,128]{1,0:T(8,128)(2,1)S(1)}, f16[400,128]{1,0:T(8,128)(2,1)S(1)}, u32[]{:S(2)}, u32[]{:S(2)}) collective-permute-start(f16[400,128]{1,0:T(8,128)(2,1)S(1)} %get-tuple-element.148), channel_id=1, source_target_pairs={{0,130},{1,131},{4,134},{5,135},{8,138},{9,139},{12,142},{13,143},... | collective-permute-start | bytes 307208 | tf_op jit(solution)/shard_map/ppermute | solution.py:30
  117.8 2.7 %collective-permute-start.22 = (f16[400,128]{1,0:T(8,128)(2,1)S(1)}, f16[400,128]{1,0:T(8,128)(2,1)S(1)}, u32[]{:S(2)}, u32[]{:S(2)}) collective-permute-start(f16[400,128]{1,0:T(8,128)(2,1)S(1)} %get-tuple-element.151), channel_id=1, source_target_pairs={{0,96},{1,97},{4,100},{5,101},{8,104},{9,105},{12,108},{13,109},{1... | collective-permute-start | bytes 307208 | tf_op jit(solution)/shard_map/ppermute | solution.py:30
  121.5 1.4 collective-permute-done.20
  122.9 2.9 %collective-permute-done.23 = f16[400,128]{1,0:T(8,128)(2,1)S(1)} collective-permute-done((f16[400,128]{1,0:T(8,128)(2,1)S(1)}, f16[400,128]{1,0:T(8,128)(2,1)S(1)}, u32[]{:S(2)}, u32[]{:S(2)}) %collective-permute-start.23) | collective-permute-done | bytes 102432 | tf_op jit(solution)/shard_map/ppermute | solution.py:30
  126.0 13.3 %all_to_all.15 = f32[8,48,256]{2,1,0:T(8,128)S(1)} all-to-all(f32[8,48,256]{2,1,0:T(8,128)S(1)} %bitcast.176), channel_id=1, replica_groups=mesh['ylo'=2,'x'=4,'z'=8,'yhi'=2,'c'=2] {'z'}, dimensions={0} | all-to-all | bytes 786432 | tf_op jit(solution)/shard_map/all_to_all | solution.py:445
  140.2 3.5 %all-to-all-start.2 = ((f32[8,48,256]{2,1,0:T(8,128)}), f32[8,48,256]{2,1,0:T(8,128)S(1)}, u32[]{:S(2)}, u32[]{:S(2)}) async-start(f32[8,48,256]{2,1,0:T(8,128)} %broadcast_in_dim.41), calls=%async_computation.2 | async-start | bytes 786432 | tf_op jit(solution)/shard_map/all_to_all | solution.py:447
  143.6 6.8 %all-to-all-done.2 = f32[8,48,256]{2,1,0:T(8,128)S(1)} async-done(((f32[8,48,256]{2,1,0:T(8,128)}), f32[8,48,256]{2,1,0:T(8,128)S(1)}, u32[]{:S(2)}, u32[]{:S(2)}) %all-to-all-start.2) | async-done | bytes 393248 | tf_op jit(solution)/shard_map/all_to_all | solution.py:447
  150.6 7.7 %collective-permute-start.24 = (f32[48,1024]{1,0:T(8,128)S(1)}, f32[48,1024]{1,0:T(8,128)S(1)}, u32[]{:S(2)}, u32[]{:S(2)}) collective-permute-start(f32[48,1024]{1,0:T(8,128)S(1)} %broadcast_select_fusion.4), channel_id=1, source_target_pairs={{0,1},{1,0},{4,5},{5,4},{8,9},{9,8},{12,13},{13,12},{16,17},{17,16... | collective-permute-start | bytes 589832 | tf_op jit(solution)/shard_map/ppermute | solution.py:30
  (139 shorter events, 19.5 us)
Async XLA Ops:
  0.0 12.4 %copy-start.8 = (bf16[1,192,1536]{2,1,0:T(8,128)(2,1)S(1)}, bf16[1,192,1536]{2,1,0:T(8,128)(2,1)}, u32[]{:S(2)}) copy-start(bf16[1,192,1536]{2,1,0:T(8,128)(2,1)} %param.4) | copy-start | bytes 1769476
  0.0 12.4 %copy-start.9 = (bf16[1,192,1536]{2,1,0:T(8,128)(2,1)S(1)}, bf16[1,192,1536]{2,1,0:T(8,128)(2,1)}, u32[]{:S(2)}) copy-start(bf16[1,192,1536]{2,1,0:T(8,128)(2,1)} %param.5) | copy-start | bytes 1769476
  1.0 4.2 %collective-permute-start = (bf16[48,256]{1,0:T(8,128)(2,1)S(1)}, bf16[48,256]{1,0:T(8,128)(2,1)S(1)}, u32[]{:S(2)}, u32[]{:S(2)}) collective-permute-start(bf16[48,256]{1,0:T(8,128)(2,1)S(1)} %pad_maximum_fusion.21), channel_id=1, source_target_pairs={{0,1},{1,0},{4,5},{5,4},{8,9},{9,8},{12,13},{13,12},{16,17},{17,16... | collective-permute-start | bytes 73736 | tf_op jit(solution)/shard_map/ppermute | solution.py:30
  6.0 21.6 %all-to-all-start = ((bf16[8,96,256]{2,1,0:T(8,128)(2,1)}), bf16[8,96,256]{2,1,0:T(8,128)(2,1)S(1)}, u32[]{:S(2)}, u32[]{:S(2)}) async-start(bf16[8,96,256]{2,1,0:T(8,128)(2,1)} %broadcast_in_dim.29), calls=%async_computation | async-start | bytes 786432 | tf_op jit(solution)/shard_map/all_to_all | solution.py:315
  12.5 29.2 %copy-start.15 = (f32[2048]{0:T(1024)S(1)}, f32[2048]{0:T(1024)}, u32[]{:S(2)}) copy-start(f32[2048]{0:T(1024)} %param.7) | copy-start | bytes 24580
  12.5 23.8 %collective-permute-start.3 = (bf16[384,1536]{1,0:T(8,128)(2,1)S(1)}, bf16[384,1536]{1,0:T(8,128)(2,1)S(1)}, u32[]{:S(2)}, u32[]{:S(2)}) collective-permute-start(bf16[384,1536]{1,0:T(8,128)(2,1)S(1)} %pad_maximum_fusion), channel_id=1, source_target_pairs={{0,1},{1,0},{4,5},{5,4},{8,9},{9,8},{12,13},{13,12},{16,17},{17,16... | collective-permute-start | bytes 3538952 | tf_op jit(solution)/shard_map/ppermute | solution.py:30
  27.6 7.4 %collective-permute-start.1 = (bf16[768,128]{1,0:T(8,128)(2,1)S(1)}, bf16[768,128]{1,0:T(8,128)(2,1)S(1)}, u32[]{:S(2)}, u32[]{:S(2)}) collective-permute-start(bf16[768,128]{1,0:T(8,128)(2,1)S(1)} %bitcast.179), channel_id=1, source_target_pairs={{0,130},{1,131},{4,134},{5,135},{8,138},{9,139},{12,142},{13,143},... | collective-permute-start | bytes 589832 | tf_op jit(solution)/shard_map/ppermute | solution.py:30
  30.5 5.7 %collective-permute-start.2 = (bf16[768,128]{1,0:T(8,128)(2,1)S(1)}, bf16[768,128]{1,0:T(8,128)(2,1)S(1)}, u32[]{:S(2)}, u32[]{:S(2)}) collective-permute-start(bf16[768,128]{1,0:T(8,128)(2,1)S(1)} %bitcast.177), channel_id=1, source_target_pairs={{0,32},{1,33},{4,36},{5,37},{8,40},{9,41},{12,44},{13,45},{16,48},... | collective-permute-start | bytes 589832 | tf_op jit(solution)/shard_map/ppermute | solution.py:30
  36.3 12.5 %copy-start.2 = (bf16[8,2,96,128]{3,2,1,0:T(8,128)(2,1)}, bf16[8,2,96,128]{3,2,1,0:T(8,128)(2,1)S(1)}, u32[]{:S(2)}) copy-start(bf16[8,2,96,128]{3,2,1,0:T(8,128)(2,1)S(1)} %pad_maximum_fusion.9) | copy-start | bytes 1179652
  36.3 10.3 %collective-permute-start.4 = (bf16[1536,128]{1,0:T(8,128)(2,1)S(1)}, bf16[1536,128]{1,0:T(8,128)(2,1)}, u32[]{:S(2)}, u32[]{:S(2)}) collective-permute-start(bf16[1536,128]{1,0:T(8,128)(2,1)S(1)} %bitcast.160), channel_id=1, source_target_pairs={{0,32},{1,33},{4,36},{5,37},{8,40},{9,41},{12,44},{13,45},{16,48},... | collective-permute-start | bytes 1179656 | tf_op jit(solution)/shard_map/ppermute | solution.py:30
  37.6 9.1 %collective-permute-start.5 = (bf16[1536,128]{1,0:T(8,128)(2,1)S(1)}, bf16[1536,128]{1,0:T(8,128)(2,1)}, u32[]{:S(2)}, u32[]{:S(2)}) collective-permute-start(bf16[1536,128]{1,0:T(8,128)(2,1)S(1)} %bitcast.161), channel_id=1, source_target_pairs={{0,96},{1,97},{4,100},{5,101},{8,104},{9,105},{12,108},{13,109},{1... | collective-permute-start | bytes 1179656 | tf_op jit(solution)/shard_map/ppermute | solution.py:30
  39.1 9.7 %collective-permute-start.6 = (bf16[768,256]{1,0:T(8,128)(2,1)S(1)}, bf16[768,256]{1,0:T(8,128)(2,1)S(1)}, u32[]{:S(2)}, u32[]{:S(2)}) collective-permute-start(bf16[768,256]{1,0:T(8,128)(2,1)S(1)} %pad_maximum_fusion.10.low_ref), channel_id=1, source_target_pairs={{0,128},{1,129},{4,132},{5,133},{8,136},{9,137},{12,140},{13,141},... | collective-permute-start | bytes 1179656 | tf_op jit(solution)/shard_map/ppermute | solution.py:30
  39.1 9.7 %collective-permute-start.7 = (bf16[768,256]{1,0:T(8,128)(2,1)S(1)}, bf16[768,256]{1,0:T(8,128)(2,1)}, u32[]{:S(2)}, u32[]{:S(2)}) collective-permute-start(bf16[768,256]{1,0:T(8,128)(2,1)S(1)} %pad_maximum_fusion.10.low_ref), channel_id=1, source_target_pairs={{0,130},{1,131},{4,134},{5,135},{8,138},{9,139},{12,142},{13,143},... | collective-permute-start | bytes 1179656 | tf_op jit(solution)/shard_map/ppermute | solution.py:30
  49.5 9.0 %collective-permute-start.8 = (bf16[1536,128]{1,0:T(8,128)(2,1)}, bf16[1536,128]{1,0:T(8,128)(2,1)S(1)}, u32[]{:S(2)}, u32[]{:S(2)}) collective-permute-start(bf16[1536,128]{1,0:T(8,128)(2,1)} %collective-permute-done.4.left_ref), channel_id=1, source_target_pairs={{0,32},{1,33},{4,36},{5,37},{8,40},{9,41},{12,44},{13,45},{16,48},... | collective-permute-start | bytes 1179656 | tf_op jit(solution)/shard_map/ppermute | solution.py:30
  49.5 9.0 %collective-permute-start.9 = (bf16[768,256]{1,0:T(8,128)(2,1)}, bf16[768,256]{1,0:T(8,128)(2,1)S(1)}, u32[]{:S(2)}, u32[]{:S(2)}) collective-permute-start(bf16[768,256]{1,0:T(8,128)(2,1)} %copy-done.4), channel_id=1, source_target_pairs={{0,128},{1,129},{4,132},{5,133},{8,136},{9,137},{12,140},{13,141},... | collective-permute-start | bytes 1179656 | tf_op jit(solution)/shard_map/ppermute | solution.py:30
  64.5 8.9 %collective-permute-start.10 = (f32[1536,384]{1,0:T(8,128)S(1)}, f32[1536,384]{1,0:T(8,128)}, u32[]{:S(2)}, u32[]{:S(2)}) collective-permute-start(f32[1536,384]{1,0:T(8,128)S(1)} %get-tuple-element.105.part_ref), channel_id=1, source_target_pairs={{0,1},{1,0},{4,5},{5,4},{8,9},{9,8},{12,13},{13,12},{16,17},{17,16... | collective-permute-start | bytes 7077896 | tf_op jit(solution)/shard_map/ppermute | solution.py:30
  68.5 4.8 %collective-permute-start.11 = (f32[768,128]{1,0:T(8,128)}, f32[768,128]{1,0:T(8,128)S(1)}, u32[]{:S(2)}, u32[]{:S(2)}) collective-permute-start(f32[768,128]{1,0:T(8,128)} %get-tuple-element.106.logit_ref), channel_id=1, source_target_pairs={{0,1},{1,0},{4,5},{5,4},{8,9},{9,8},{12,13},{13,12},{16,17},{17,16... | collective-permute-start | bytes 1179656 | tf_op jit(solution)/shard_map/ppermute | solution.py:30
  86.0 13.6 %collective-permute-start.13 = (f16[784,256]{1,0:T(8,128)(2,1)S(1)}, f16[784,256]{1,0:T(8,128)(2,1)S(1)}, u32[]{:S(2)}, u32[]{:S(2)}) collective-permute-start(f16[784,256]{1,0:T(8,128)(2,1)S(1)} %pad_maximum_fusion.5), channel_id=1, source_target_pairs={{0,2},{1,3},{4,6},{5,7},{8,10},{9,11},{12,14},{13,15},{16,18},{17,... | collective-permute-start | bytes 1204232 | tf_op jit(solution)/shard_map/ppermute | solution.py:30
  87.7 11.8 %collective-permute-start.12 = (f16[1552,128]{1,0:T(8,128)(2,1)S(1)}, f16[1552,128]{1,0:T(8,128)(2,1)S(1)}, u32[]{:S(2)}, u32[]{:S(2)}) collective-permute-start(f16[1552,128]{1,0:T(8,128)(2,1)S(1)} %pad_maximum_fusion.8), channel_id=1, source_target_pairs={{0,64},{1,65},{4,68},{5,69},{8,72},{9,73},{12,76},{13,77},{16,80},... | collective-permute-start | bytes 1191944 | tf_op jit(solution)/shard_map/ppermute | solution.py:30
  99.1 13.4 %copy-start.12 = (f32[1536,128]{1,0:T(8,128)S(1)}, f32[1536,128]{1,0:T(8,128)}, u32[]{:S(2)}) copy-start(f32[1536,128]{1,0:T(8,128)} %get-tuple-element.132) | copy-start | bytes 2359300
  99.6 12.9 %collective-permute-start.16 = (f16[784,256]{1,0:T(8,128)(2,1)S(1)}, f16[784,256]{1,0:T(8,128)(2,1)S(1)}, u32[]{:S(2)}, u32[]{:S(2)}) collective-permute-start(f16[784,256]{1,0:T(8,128)(2,1)S(1)} %get-tuple-element.139), channel_id=1, source_target_pairs={{0,128},{1,129},{4,132},{5,133},{8,136},{9,137},{12,140},{13,141},... | collective-permute-start | bytes 1204232 | tf_op jit(solution)/shard_map/ppermute | solution.py:30
  100.1 12.4 %collective-permute-start.17 = (f16[784,256]{1,0:T(8,128)(2,1)S(1)}, f16[784,256]{1,0:T(8,128)(2,1)S(1)}, u32[]{:S(2)}, u32[]{:S(2)}) collective-permute-start(f16[784,256]{1,0:T(8,128)(2,1)S(1)} %get-tuple-element.140), channel_id=1, source_target_pairs={{0,130},{1,131},{4,134},{5,135},{8,138},{9,139},{12,142},{13,143},... | collective-permute-start | bytes 1204232 | tf_op jit(solution)/shard_map/ppermute | solution.py:30
  102.3 10.2 %collective-permute-start.14 = (f16[1552,128]{1,0:T(8,128)(2,1)S(1)}, f16[1552,128]{1,0:T(8,128)(2,1)S(1)}, u32[]{:S(2)}, u32[]{:S(2)}) collective-permute-start(f16[1552,128]{1,0:T(8,128)(2,1)S(1)} %get-tuple-element.137), channel_id=1, source_target_pairs={{0,32},{1,33},{4,36},{5,37},{8,40},{9,41},{12,44},{13,45},{16,48},... | collective-permute-start | bytes 1191944 | tf_op jit(solution)/shard_map/ppermute | solution.py:30
  103.2 9.3 %collective-permute-start.15 = (f16[1552,128]{1,0:T(8,128)(2,1)S(1)}, f16[1552,128]{1,0:T(8,128)(2,1)S(1)}, u32[]{:S(2)}, u32[]{:S(2)}) collective-permute-start(f16[1552,128]{1,0:T(8,128)(2,1)S(1)} %get-tuple-element.138), channel_id=1, source_target_pairs={{0,96},{1,97},{4,100},{5,101},{8,104},{9,105},{12,108},{13,109},{1... | collective-permute-start | bytes 1191944 | tf_op jit(solution)/shard_map/ppermute | solution.py:30
  115.0 5.4 %collective-permute-start.18 = (f16[400,128]{1,0:T(8,128)(2,1)S(1)}, f16[400,128]{1,0:T(8,128)(2,1)S(1)}, u32[]{:S(2)}, u32[]{:S(2)}) collective-permute-start(f16[400,128]{1,0:T(8,128)(2,1)S(1)} %get-tuple-element.147), channel_id=1, source_target_pairs={{0,128},{1,129},{4,132},{5,133},{8,136},{9,137},{12,140},{13,141},... | collective-permute-start | bytes 307208 | tf_op jit(solution)/shard_map/ppermute | solution.py:30
  115.1 6.4 %collective-permute-start.19 = (f16[400,128]{1,0:T(8,128)(2,1)S(1)}, f16[400,128]{1,0:T(8,128)(2,1)S(1)}, u32[]{:S(2)}, u32[]{:S(2)}) collective-permute-start(f16[400,128]{1,0:T(8,128)(2,1)S(1)} %get-tuple-element.148), channel_id=1, source_target_pairs={{0,130},{1,131},{4,134},{5,135},{8,138},{9,139},{12,142},{13,143},... | collective-permute-start | bytes 307208 | tf_op jit(solution)/shard_map/ppermute | solution.py:30
  117.8 5.1 %collective-permute-start.20 = (f16[400,128]{1,0:T(8,128)(2,1)S(1)}, f16[400,128]{1,0:T(8,128)(2,1)S(1)}, u32[]{:S(2)}, u32[]{:S(2)}) collective-permute-start(f16[400,128]{1,0:T(8,128)(2,1)S(1)} %get-tuple-element.149), channel_id=1, source_target_pairs={{0,2},{1,3},{4,6},{5,7},{8,10},{9,11},{12,14},{13,15},{16,18},{17,... | collective-permute-start | bytes 307208 | tf_op jit(solution)/shard_map/ppermute | solution.py:30
  117.8 5.1 %collective-permute-start.21 = (f16[400,128]{1,0:T(8,128)(2,1)S(1)}, f16[400,128]{1,0:T(8,128)(2,1)S(1)}, u32[]{:S(2)}, u32[]{:S(2)}) collective-permute-start(f16[400,128]{1,0:T(8,128)(2,1)S(1)} %get-tuple-element.150), channel_id=1, source_target_pairs={{0,32},{1,33},{4,36},{5,37},{8,40},{9,41},{12,44},{13,45},{16,48},... | collective-permute-start | bytes 307208 | tf_op jit(solution)/shard_map/ppermute | solution.py:30
  117.8 5.1 %collective-permute-start.22 = (f16[400,128]{1,0:T(8,128)(2,1)S(1)}, f16[400,128]{1,0:T(8,128)(2,1)S(1)}, u32[]{:S(2)}, u32[]{:S(2)}) collective-permute-start(f16[400,128]{1,0:T(8,128)(2,1)S(1)} %get-tuple-element.151), channel_id=1, source_target_pairs={{0,96},{1,97},{4,100},{5,101},{8,104},{9,105},{12,108},{13,109},{1... | collective-permute-start | bytes 307208 | tf_op jit(solution)/shard_map/ppermute | solution.py:30
  120.5 5.3 %collective-permute-start.23 = (f16[400,128]{1,0:T(8,128)(2,1)S(1)}, f16[400,128]{1,0:T(8,128)(2,1)S(1)}, u32[]{:S(2)}, u32[]{:S(2)}) collective-permute-start(f16[400,128]{1,0:T(8,128)(2,1)S(1)} %get-tuple-element.152), channel_id=1, source_target_pairs={{0,64},{1,65},{4,68},{5,69},{8,72},{9,73},{12,76},{13,77},{16,80},... | collective-permute-start | bytes 307208 | tf_op jit(solution)/shard_map/ppermute | solution.py:30
  140.2 10.2 %all-to-all-start.2 = ((f32[8,48,256]{2,1,0:T(8,128)}), f32[8,48,256]{2,1,0:T(8,128)S(1)}, u32[]{:S(2)}, u32[]{:S(2)}) async-start(f32[8,48,256]{2,1,0:T(8,128)} %broadcast_in_dim.41), calls=%async_computation.2 | async-start | bytes 786432 | tf_op jit(solution)/shard_map/all_to_all | solution.py:447
  150.6 8.8 %collective-permute-start.24 = (f32[48,1024]{1,0:T(8,128)S(1)}, f32[48,1024]{1,0:T(8,128)S(1)}, u32[]{:S(2)}, u32[]{:S(2)}) collective-permute-start(f32[48,1024]{1,0:T(8,128)S(1)} %broadcast_select_fusion.4), channel_id=1, source_target_pairs={{0,1},{1,0},{4,5},{5,4},{8,9},{9,8},{12,13},{13,12},{16,17},{17,16... | collective-permute-start | bytes 589832 | tf_op jit(solution)/shard_map/ppermute | solution.py:30
  (11 other events, 28.1 us)

commit v6 on v5

v6 whole, which is shorter than its diff:
```python
import functools
import math

import jax
import jax.numpy as jnp
from jax import lax
from jax.experimental import pallas as pl
from jax.experimental.pallas import tpu as pltpu
from jax.sharding import Mesh
from jax.sharding import PartitionSpec as P

R1_WEIGHT = 40.0
NX, NY, NZ = 4, 4, 8
AXES = ("ylo", "x", "z", "yhi", "c")
BF16, F16, F32 = jnp.bfloat16, jnp.float16, jnp.float32


def flat_index(x, y, z, c):
    return ((y % 2) * NX + x) * (NZ * 4) + z * 4 + (y // 2) * 2 + c


def send(array, to):
    pairs = []
    for x in range(NX):
        for y in range(NY):
            for z in range(NZ):
                for c in range(2):
                    tx, ty, tc = to(x, y, c)
                    pairs.append((flat_index(x, y, z, c), flat_index(tx % NX, ty % NY, z, tc)))
    return lax.ppermute(array, AXES, pairs)


def to_core(array):
    return send(array, lambda x, y, c: (x, y, 1 - c))


def together(arrays, routes, beside=None, extra=()):
    arrays = lax.optimization_barrier((*arrays, *extra))
    sent = tuple(send(a, to) for a, to in zip(arrays, routes))
    return lax.optimization_barrier((*sent, *(beside(*arrays[len(sent) :]) if beside else ())))


def ring(step):
    return lambda x, y, c: (x + step, y, c) if c == 0 else (x, y + step, c)


def other_ring(step):
    return lambda x, y, c: (x, y + step, c) if c == 0 else (x + step, y, c)


def pair(x, y, c):
    return (x, 3 - y, c) if c == 0 else (x ^ 1, y, c)


def ordered(first_is_mine, mine, theirs, axis):
    return jnp.concatenate(
        [jnp.where(first_is_mine, mine, theirs), jnp.where(first_is_mine, theirs, mine)], axis
    )


def packed(piece, exponent):
    scaled = (piece * jnp.exp2(-exponent)).astype(F16)
    return jnp.concatenate([scaled, jnp.broadcast_to(exponent.astype(F16), (16, piece.shape[1]))], 0)


def unpacked(message):
    exponent = message[-16:-15].astype(F32)
    return message[:-16].astype(F32) * jnp.exp2(exponent), exponent


def column_tiles(width):
    return [(start, min(256, width - start)) for start in range(0, width, 256)]


def nt(a, b):
    return lax.dot_general(a, b, (((1,), (1,)), ((), ())), preferred_element_type=F32)


def flat(block):
    return block.reshape(block.shape[0] * block.shape[1], block.shape[2])


def forward_tiles(tokens_ref, w_ref, score_ref, slope_ref, curve_ref, lifted_ref, logit_ref, first, arriving):
    n = tokens_ref.shape[0] // 2
    for kind in (0, 1):
        arriving[kind].wait()
        rows = slice(kind * n, kind * n + n)
        total = jnp.zeros((n, 128), F32) if first is None else first[rows, :]
        for start, width in column_tiles(w_ref.shape[2]):
            cols = slice(start, start + width)
            preact = jnp.dot(tokens_ref[rows, :], flat(w_ref[:, :, cols]), preferred_element_type=F32)
            score = score_ref[:, cols]
            squash = jax.nn.sigmoid(preact)
            rest = 1.0 - squash
            act = preact * squash * score
            for lane in range(0, width, 128):
                total = total + act[:, lane : lane + 128]
            slope = squash * (1.0 + preact * rest) * score
            slope_ref[rows, cols] = slope
            if kind == 1:
                lifted_ref[:, cols] = slope.astype(BF16)
                curve_ref[:, cols] = squash * rest * (2.0 + preact * (1.0 - 2.0 * squash)) * score
        logit_ref[rows, :] = total


def pull_back(w_ref, lifted_ref, part_ref, so_far):
    height = 2 * w_ref.shape[1]
    for k in range(w_ref.shape[0] // 2):
        rows = slice(k * height, k * height + height)
        value = nt(flat(w_ref[2 * k : 2 * k + 2]), lifted_ref[...])
        part_ref[rows, :] = value if so_far is None else so_far[rows, :] + value


def place_of(flag_ref, piece, sub):
    return jnp.where(flag_ref[0] == 0, sub, flag_ref[1] ^ piece), jnp.where(flag_ref[0] == 0, piece, sub)


def laid(flag_ref, one_hbm, two_hbm, w_ref):
    height = one_hbm.shape[2]
    pairs = []
    for piece, ref in enumerate((one_hbm, two_hbm)):
        for sub in (0, 1):
            half, block = place_of(flag_ref, piece, sub)
            rows = pl.ds(pl.multiple_of(half * height, 16), height)
            pairs.append((ref.at[sub], w_ref.at[:, rows, pl.ds(pl.multiple_of(block * 256, 128), 256)]))
    return pairs


def fetched(sems, *pairs):
    copies = [pltpu.make_async_copy(source, target, sems.at[k]) for k, (source, target) in enumerate(pairs)]
    for copy in copies:
        copy.start()
    return copies


def done(copies):
    for copy in copies:
        copy.wait()


def forward_kernel(flag_ref, score_ref, *refs, so_far):
    earlier, refs = (refs[:2], refs[2:]) if so_far else ((None, None), refs)
    (tokens_hbm, one_hbm, two_hbm, w_hbm, slope_hbm, curve_hbm, lifted_hbm, logit_ref, part_ref,
     tokens_ref, w_ref, slope_ref, curve_ref, lifted_ref, sems, out_sems) = refs
    n = lifted_ref.shape[0]
    copies = fetched(
        sems,
        *laid(flag_ref, one_hbm, two_hbm, w_ref),
        *((tokens_hbm.at[k * n : k * n + n, :], tokens_ref.at[k * n : k * n + n, :]) for k in (0, 1)),
    )
    done(copies[:4])
    forward_tiles(tokens_ref, w_ref, score_ref, slope_ref, curve_ref, lifted_ref, logit_ref, earlier[0], copies[4:])
    copies = fetched(
        out_sems, (w_ref, w_hbm), (slope_ref, slope_hbm), (curve_ref, curve_hbm), (lifted_ref, lifted_hbm)
    )
    pull_back(w_ref, lifted_ref, part_ref, earlier[1])
    done(copies)


def tokens_kernel(flag_ref, fake_hbm, real_hbm, other_hbm, tokens_ref, tokens_t_hbm, peak_ref,
                  own_ref, other_ref, tokens_t_ref, sems):
    tok = fake_hbm.shape[0]
    done(
        fetched(
            sems, (fake_hbm, own_ref.at[0:tok, :]), (real_hbm, own_ref.at[tok : 2 * tok, :]), (other_hbm, other_ref)
        )
    )
    first = flag_ref[0] == 0
    for kind in (0, 1):
        mine, theirs = (ref[kind * tok : kind * tok + tok, :] for ref in (own_ref, other_ref))
        start = 2 * kind * tok
        tokens_ref[start : start + tok, :] = jnp.where(first, mine, theirs)
        tokens_ref[start + tok : start + 2 * tok, :] = jnp.where(first, theirs, mine)
        peak = peak_of(tokens_ref[start : start + 2 * tok, :])
        peak_ref[8 * kind : 8 * kind + 8, :] = jnp.broadcast_to(peak, (8, 128))
    tokens_t_ref[...] = tokens_ref[...].T
    done(fetched(sems, (tokens_t_ref, tokens_t_hbm)))


def peak_of(array):
    flat = jnp.max(jnp.abs(array).astype(F32), axis=0, keepdims=True)
    return jnp.max(flat, axis=1, keepdims=True)


def cotangents(scale, logits, r1_ref, w_ref, slope_ref, curve_ref, fake_ref, real_ref):
    n = r1_ref.shape[0]
    fake_ref[...] = (scale * jax.nn.sigmoid(logits[:n]) * slope_ref[0:n, :]).astype(BF16)
    real_gain = -scale * jax.nn.sigmoid(-logits[n:])
    for start, width in column_tiles(w_ref.shape[2]):
        cols = slice(start, start + width)
        back = jnp.dot(r1_ref[...], flat(w_ref[:, :, cols]), preferred_element_type=F32)
        real_ref[:, cols] = (real_gain * slope_ref[n : 2 * n, cols] + back * curve_ref[:, cols]).astype(BF16)


def term_tiles(flag_ref, cotangent_refs, tokens_t_ref, r1_t_ref, term_ref, term_hbm, sems):
    fake_ref, real_ref, lifted_ref = cotangent_refs
    d_in, n = r1_t_ref.shape
    turn = d_in // (2 * NZ)
    leaving = []
    for block in (0, 1):
        cols = slice(256 * block, 256 * block + 256)
        for row in range(0, d_in, 4 * turn):
            rows = slice(row, row + 4 * turn)
            value = (
                jnp.dot(tokens_t_ref[rows, 0:n], fake_ref[:, cols], preferred_element_type=F32)
                + jnp.dot(tokens_t_ref[rows, n : 2 * n], real_ref[:, cols], preferred_element_type=F32)
                + jnp.dot(r1_t_ref[rows, :], lifted_ref[:, cols], preferred_element_type=F32)
            )
            there = slice(row // 2, row // 2 + 2 * turn)
            for half in (0, 1):
                for k in range(2):
                    at = row // 2 + k * turn
                    term_ref[half, block, at : at + turn, :] = value[(2 * k + half) * turn : (2 * k + half + 1) * turn, :]
                piece = jnp.where(flag_ref[0] == 0, block, flag_ref[1] ^ half)
                sub = jnp.where(flag_ref[0] == 0, half, block)
                leaving.append(
                    pltpu.make_async_copy(
                        term_ref.at[half, block, there, :], term_hbm.at[piece, sub, there, :], sems.at[len(leaving)]
                    )
                )
                leaving[-1].start()
    done(leaving)


def third_kernel(scale, flag_ref, part_ref, part_in_ref, logit_ref, logit_in_ref, peak_ref,
                 w_2_hbm, slope_2_hbm, curve_2_hbm, w_1_hbm, slope_1_hbm, curve_1_hbm, lifted_1_hbm, lifted_2_hbm,
                 tokens_t_hbm,
                 term_hbm, r1_t_hbm, fake_1_hbm, real_1_hbm, exp_ref,
                 term_ref, r1_t_ref, fake_1_ref, real_1_ref, r1_ref, fake_2_ref, real_2_ref,
                 w_2_ref, slope_2_ref, curve_2_ref, w_1_ref, slope_1_ref, curve_1_ref, lifted_1_ref, lifted_2_ref,
                 tokens_t_ref, sems, r1_sems, out_sems):
    copies = fetched(
        sems,
        (w_2_hbm, w_2_ref), (slope_2_hbm, slope_2_ref), (curve_2_hbm, curve_2_ref),
        (w_1_hbm, w_1_ref), (slope_1_hbm, slope_1_ref), (curve_1_hbm, curve_1_ref),
        (lifted_1_hbm, lifted_1_ref), (lifted_2_hbm, lifted_2_ref), (tokens_t_hbm, tokens_t_ref),
    )
    r1_t_ref[...] = (scale * R1_WEIGHT * (part_ref[...] + part_in_ref[...])).astype(BF16)
    r1_ref[...] = r1_t_ref[...].T
    logits = jnp.sum(logit_ref[...] + logit_in_ref[...], axis=1, keepdims=True)
    done(copies[:3])
    cotangents(scale, logits, r1_ref, w_2_ref, slope_2_ref, curve_2_ref, fake_2_ref, real_2_ref)
    done(copies[3:6])
    cotangents(scale, logits, r1_ref, w_1_ref, slope_1_ref, curve_1_ref, fake_1_ref, real_1_ref)
    passed = fetched(r1_sems, (r1_t_ref, r1_t_hbm), (fake_1_ref, fake_1_hbm), (real_1_ref, real_1_hbm))
    done(copies[6:])
    first, second = (fake_1_ref, real_1_ref, lifted_1_ref), (fake_2_ref, real_2_ref, lifted_2_ref)
    peaks = [jnp.maximum(peak_of(one[...]), peak_of(two[...])) for one, two in zip(first, second)]
    n = r1_ref.shape[0]
    bound = n * (
        peak_ref[0:1, 0:1] * peaks[0] + peak_ref[8:9, 0:1] * peaks[1] + peak_of(r1_t_ref[...]) * peaks[2]
    )
    bound = jnp.broadcast_to(bound, (16, 128))
    exp_ref[...] = jnp.ceil(jnp.log(jnp.maximum(bound, 1e-30)) * (1.0 / math.log(2.0)) + 0.01) - 15.0
    term_tiles(flag_ref, second, tokens_t_ref, r1_t_ref, term_ref, term_hbm, out_sems)
    done(passed)


def fourth_kernel(flag_ref, r1_t_hbm, fake_hbm, real_hbm, lifted_hbm, tokens_t_hbm, term_hbm,
                  term_ref, r1_t_ref, fake_ref, real_ref, lifted_ref, tokens_t_ref, sems, out_sems):
    done(
        fetched(
            sems,
            (r1_t_hbm, r1_t_ref), (fake_hbm, fake_ref), (real_hbm, real_ref), (lifted_hbm, lifted_ref),
            (tokens_t_hbm, tokens_t_ref),
        )
    )
    term_tiles(flag_ref, (fake_ref, real_ref, lifted_ref), tokens_t_ref, r1_t_ref, term_ref, term_hbm, out_sems)


def call(kernel, flops, outs, scratch, *args, flags=None, there=(), sems=(), vmem_mib=20):
    vmem = pl.BlockSpec(memory_space=pltpu.VMEM)
    specs = [vmem] * len(args) + [pl.BlockSpec(memory_space=pltpu.HBM)] * len(there)
    args = (*args, *(pltpu.with_memory_space_constraint(a, pltpu.HBM) for a in there))
    if flags is not None:
        args, specs = (flags, *args), [pl.BlockSpec(memory_space=pltpu.SMEM), *specs]
    return pl.pallas_call(
        kernel,
        out_shape=[(pltpu.HBM if len(out) == 3 else pltpu.VMEM)(*out[:2]) for out in outs],
        in_specs=specs,
        out_specs=[pl.BlockSpec(memory_space=pltpu.HBM) if len(out) == 3 else vmem for out in outs],
        scratch_shapes=[pltpu.VMEM(shape, dtype) for shape, dtype in scratch]
        + [pltpu.SemaphoreType.DMA((k,)) for k in sems],
        compiler_params=pltpu.CompilerParams(vmem_limit_bytes=vmem_mib * 1024 * 1024),
        cost_estimate=pl.CostEstimate(flops=flops, bytes_accessed=8_000_000, transcendentals=0),
    )(*args)


def per_device(fake_tokens, real_tokens, proj_weight, score_vector):
    ylo, x, z, yhi, c = (lax.axis_index(a) for a in AXES)
    y = yhi * 2 + ylo
    gray_x = (x == 1) | (x == 2)
    core0 = c == 0
    tok = fake_tokens.shape[1]
    rows, hid = proj_weight.shape
    half = hid // 2
    d_in = rows * NZ * 4
    n = 2 * tok
    scale = math.sqrt(hid / (8 * 32 * tok))

    def slice_of(side):
        start = jnp.where(side == 0, x * 256, half + ylo * 512 + gray_x * 256)
        return lax.dynamic_slice_in_dim(proj_weight, start, 256, 1)

    block = ordered(core0, slice_of(c), to_core(slice_of(1 - c)), 0)
    over_z = lax.all_to_all(jnp.broadcast_to(block[None], (NZ, *block.shape)), "z", 0, 0)
    sub = over_z.reshape(d_in // 2, 256)
    own = ordered(jnp.where(core0, yhi == 0, ~gray_x), sub, send(sub, pair), 0)

    own_tokens = jnp.concatenate([fake_tokens[0], real_tokens[0]], 0)
    def join_tokens(other_tokens):
        return call(
            tokens_kernel, 2 * n * d_in * 128,
            [((2 * n, d_in), BF16), ((d_in, 2 * n), BF16, True), ((16, 128), F32)],
            [((n, d_in), BF16), ((n, d_in), BF16), ((d_in, 2 * n), BF16)],
            flags=c[None].astype(jnp.int32), there=(fake_tokens[0], real_tokens[0], other_tokens), sems=[3],
        )

    left, right, tokens, tokens_t, peak = together((own, own), (ring(1), ring(-1)), join_tokens, (to_core(own_tokens),))
    across = send(left, ring(1))

    def score_at(start):
        return lax.dynamic_slice_in_dim(score_vector, c * half + start, 256, 0)

    def scores(one, two, group):
        blocks = (jnp.where(core0, one % 4 * 256, group * 512), jnp.where(core0, two % 4 * 256, group * 512 + 256))
        return jnp.concatenate([score_at(b) for b in blocks])[None]

    flags_1, flags_2 = (jnp.stack([c, at]).astype(jnp.int32) for at in ((y + 3) % 4 // 2, yhi))
    turn, wide = d_in // NZ, half // 2
    states = [((NZ, turn, wide), BF16), ((2 * n, wide), F32), ((n, wide), F32), ((n, wide), BF16)]
    sums = [((2 * n, 128), F32), ((d_in, n), F32)]
    marked = lambda shapes: [(*shape, True) for shape in shapes]

    def forward(flags, score, one, two, earlier):
        pieces = [p.reshape(2, NZ, 2 * rows, 256) for p in (one, two)]
        return call(
            functools.partial(forward_kernel, so_far=bool(earlier)), 6 * n * d_in * wide, [*marked(states), *sums],
            [((2 * n, d_in), BF16), *states], score, *earlier,
            flags=flags, there=(tokens, *pieces), sems=[6, 4], vmem_mib=24,
        )

    w_1, slope_1, curve_1, lifted_1, *earlier = forward(flags_1, scores(x + 3, x + 1, 1 - ylo), left, right, ())
    w_2, slope_2, curve_2, lifted_2, logit, part = forward(flags_2, scores(x, x + 2, ylo), own, across, earlier)
    part_in, logit_in = to_core(part), to_core(logit)

    works = [((n, wide), BF16)] * 2
    terms, tall, r1_shape = ((2, 2, d_in // 2, 256), F32), ((d_in, 2 * n), BF16), ((d_in, n), BF16)
    term_2, r1_t, fake_1, real_1, exponent = call(
        functools.partial(third_kernel, scale), 6 * n * d_in * half,
        [*marked([terms, r1_shape, *works]), ((16, 128), F32)],
        [terms, r1_shape, *works, ((n, d_in), BF16), *works, *states[:3], *states, states[3], tall],
        part, part_in, logit, logit_in, peak, flags=flags_2,
        there=(w_2, slope_2, curve_2, w_1, slope_1, curve_1, lifted_1, lifted_2, tokens_t),
        sems=[9, 3, 16], vmem_mib=36,
    )
    exponent = jnp.concatenate([exponent[:1]] * 2, 1)

    def rest_of_term(r1_t):
        (term_1,) = call(
            fourth_kernel, 6 * n * d_in * wide, marked([terms]), [terms, r1_shape, *works, states[3], tall],
            flags=flags_1, there=(r1_t, fake_1, real_1, lifted_1, tokens_t), sems=[5, 16], vmem_mib=28,
        )
        return [packed(term_1[k].reshape(d_in, 256), exponent) for k in (1, 0)]

    across, *beside = together(
        (packed(term_2[1].reshape(d_in, 256), exponent),), (ring(2),), rest_of_term, (r1_t,)
    )
    from_left, from_right = together(beside, (ring(1), ring(-1)))

    def summed(own, exponent, *messages):
        for values, theirs in map(unpacked, messages):
            own, exponent = own + values, jnp.maximum(exponent, theirs)
        return own, exponent + 2.0

    total, exponent = summed(term_2[0].reshape(d_in, 256), exponent, from_left, from_right, across)

    place = jnp.where(core0, y, x)
    total = total.reshape(2, NZ, 2, rows, 256)

    def quarter(k):
        at = (place + k) % 4
        zero = jnp.zeros_like(at)
        return lax.dynamic_slice(total, (at // 2, zero, at % 2, zero, zero), (1, NZ, 1, rows, 256)).reshape(NZ * rows, 256)

    away = (1, 3, 2)
    got = together([packed(quarter(k), exponent) for k in away], [other_ring(k) for k in away])
    both = summed(quarter(0), exponent, *got)[0].reshape(NZ, rows, 256)
    both = jnp.sum(lax.all_to_all(both, "z", 0, 0), 0)

    spread = lax.all_to_all(jnp.broadcast_to(both[None], (8, *both.shape)), ("ylo", "x"), 0, 0)
    spread = spread.reshape(2, 4, rows, 256)

    def row_group(r):
        first = [spread[r, k] for k in range(4)]
        second = [spread[v, 2 * j + r] for v in (0, 1) for j in (0, 1)]
        return jnp.concatenate([jnp.where(core0, f, g) for f, g in zip(first, second)], 1)

    zero, one = row_group(0), row_group(1)
    theirs = to_core(jnp.where(core0, one, zero))
    return ordered(core0, jnp.where(core0, zero, one), theirs, 1)


def solution(mesh):
    split = Mesh(mesh.devices.reshape(2, NX, NZ, 2, 2), AXES)
    tokens = P(("ylo", "x"), ("z", "yhi", "c"), None)
    shard = P(("z", "yhi", "c"), None)
    return jax.shard_map(
        per_device, mesh=split, in_specs=(tokens, tokens, shard, P()), out_specs=shard, check_vma=False
    )
```

time: 161 us -> 172 us (1.068)
  starting transfers between devices: 51.4 us -> 29.2 us
  waiting for transfers between devices: 47.7 us -> 63.7 us
  blocking collectives: 13.3 us -> 29.1 us
    ppermute x25 -> x15, waiting for transfers between devices: 26.6 us -> 49.4 us  [send(): return lax.ppermute(array, AXES, pairs)]
    ppermute x25 -> x15, starting transfers between devices: 41.5 us -> 22.8 us  [send(): return lax.ppermute(array, AXES, pairs)]
    all_to_all x0 -> x1, blocking collectives: none -> 15.4 us  [per_device(): lax.all_to_all(jnp.broadcast_to(both[None], (8, *both.shape)), ('ylo', 'x...]
    all_to_all x1 -> x0, waiting for transfers between devices: 6.77 us -> none  [per_device(): lax.all_to_all(jnp.broadcast_to(both[None], (8, *both.shape)), ('ylo', 'x...]
    slice x3, local copies, waits for them, and re-layouts: 0.12 us -> 4.26 us  [the longest x1 2.17 us: per_device(): term_2[1].reshape(d_in, 256)]
    all_to_all x1 -> x0, starting transfers between devices: 3.45 us -> none  [per_device(): lax.all_to_all(jnp.broadcast_to(both[None], (8, *both.shape)), ('ylo', 'x...]
    convert_element_type x6 -> x3, other arithmetic: 3.38 us -> 0.65 us  [packed(): scaled = (piece * jnp.exp2(-exponent)).astype(F16)]
    unnamed x44 -> x20, local copies, waits for them, and re-layouts: 5.72 us -> 3.29 us
  transfers between devices with their start and end apart: 27 -> 16, of which waited for: 14 -> 13; matrix products, arithmetic and copies ran while one was open for 2% -> 1% of each run, Pallas kernels for 11% -> 6%
where the time goes in v6:
time: 172 us; the launch traced here: 171 us
  waiting for transfers between devices  63.7 us (37%)
  Pallas kernels  32.9 us (19%)
  starting transfers between devices  29.2 us (17%)
  blocking collectives  29.1 us (17%)
  local copies, waits for them, and re-layouts  9.44 us (5%)
  other arithmetic  6.44 us (4%)
    ppermute x15, waiting for transfers between devices, send(): return lax.ppermute(array, AXES, pairs)  49.4 us
    pallas_call x5, Pallas kernels, call(): pl.pallas_call(kernel, out_shape=[(pltpu.HBM if len(out) == 3 else pltpu....  32.9 us
    ppermute x15, starting transfers between devices, send(): return lax.ppermute(array, AXES, pairs)  22.8 us
    all_to_all x1, blocking collectives, per_device(): lax.all_to_all(jnp.broadcast_to(both[None], (8, *both.shape)), ('ylo', 'x...  15.4 us
    all_to_all x1, waiting for transfers between devices, per_device(): lax.all_to_all(jnp.broadcast_to(block[None], (NZ, *block.shape)), 'z', 0, 0)  14.3 us
    all_to_all x1, blocking collectives, per_device(): both = jnp.sum(lax.all_to_all(both, 'z', 0, 0), 0)  13.6 us
    all_to_all x1, starting transfers between devices, per_device(): lax.all_to_all(jnp.broadcast_to(block[None], (NZ, *block.shape)), 'z', 0, 0)  6.45 us
  transfers between devices with their start and end apart: 16, of which 13 were waited for; matrix products, arithmetic and copies ran while one was open for 1% of the time, Pallas kernels for 6%

profile of v6, /device:TPU:1, one launch (start us, length us, event | category | flops | bytes accessed | tf_op | source)
XLA Modules:
  0.0 171.1 jit_solution(10039574029184419222)
XLA Ops:
  0.8 3.2 %collective-permute-start = (bf16[48,256]{1,0:T(8,128)(2,1)S(1)}, bf16[48,256]{1,0:T(8,128)(2,1)S(1)}, u32[]{:S(2)}, u32[]{:S(2)}) collective-permute-start(bf16[48,256]{1,0:T(8,128)(2,1)S(1)} %constant_dynamic-slice_fusion.4), channel_id=1, source_target_pairs={{0,1},{1,0},{4,5},{5,4},{8,9},{9,8},{12,13},{13,12},{16,17},{17,16... | collective-permute-start | bytes 73736 | tf_op jit(solution)/shard_map/ppermute | solution.py:30
  6.5 6.4 %all-to-all-start = ((bf16[8,96,256]{2,1,0:T(8,128)(2,1)}), bf16[8,96,256]{2,1,0:T(8,128)(2,1)S(1)}, u32[]{:S(2)}, u32[]{:S(2)}) async-start(bf16[8,96,256]{2,1,0:T(8,128)(2,1)} %broadcast_in_dim.16), calls=%async_computation | async-start | bytes 786432 | tf_op jit(solution)/shard_map/all_to_all | solution.py:306
  13.7 14.3 %all-to-all-done = bf16[8,96,256]{2,1,0:T(8,128)(2,1)S(1)} async-done(((bf16[8,96,256]{2,1,0:T(8,128)(2,1)}), bf16[8,96,256]{2,1,0:T(8,128)(2,1)S(1)}, u32[]{:S(2)}, u32[]{:S(2)}) %all-to-all-start) | async-done | bytes 393248 | tf_op jit(solution)/shard_map/all_to_all | solution.py:306
  29.3 5.7 %collective-permute-done.1 = bf16[768,256]{1,0:T(8,128)(2,1)S(1)} collective-permute-done((bf16[768,256]{1,0:T(8,128)(2,1)S(1)}, bf16[768,256]{1,0:T(8,128)(2,1)S(1)}, u32[]{:S(2)}, u32[]{:S(2)}) %collective-permute-start.1) | collective-permute-done | bytes 393248 | tf_op jit(solution)/shard_map/ppermute | solution.py:30
  35.2 1.4 collective-permute-start.3
  36.5 1.5 collective-permute-start.4
  38.1 4.6 %shard_map.46 = (bf16[768,1536]{1,0:T(8,128)(2,1)S(1)}, bf16[1536,768]{1,0:T(8,128)(2,1)}, f32[16,128]{1,0:T(8,128)S(1)}) custom-call(s32[1]{0:T(128)} %bitcast.flag_ref, bf16[192,1536]{1,0:T(8,128)(2,1)} %bitcast.89, bf16[192,1536]{1,0:T(8,128)(2,1)} %bitcast.91, bf16[384,1536]{1,0:T(8,128)(2,1)} %copy-done.3), custom_call_target="tpu_custom_call" | custom-call | flops 150994944 | bytes 8000000 | tf_op jit(solution)/shard_map/pallas_call | solution.py:277
  42.7 1.4 copy-done
  44.1 3.6 %collective-permute-done.3 = bf16[1536,256]{1,0:T(8,128)(2,1)S(1)} collective-permute-done((bf16[1536,256]{1,0:T(8,128)(2,1)S(1)}, bf16[1536,256]{1,0:T(8,128)(2,1)S(1)}, u32[]{:S(2)}, u32[]{:S(2)}) %collective-permute-start.3) | collective-permute-done | bytes 786464 | tf_op jit(solution)/shard_map/ppermute | solution.py:30
  48.6 1.3 collective-permute-start.5
  50.1 6.1 %shard_map.47 = (bf16[8,192,512]{2,1,0:T(8,128)(2,1)}, f32[768,512]{1,0:T(8,128)}, f32[384,512]{1,0:T(8,128)}, bf16[384,512]{1,0:T(8,128)(2,1)}, f32[768,128]{1,0:T(8,128)S(1)}, /*index=5*/f32[1536,384]{1,0:T(8,128)S(1)}) custom-call(s32[2]{0:T(128)S(1)} %pad_add_fusion.1.flag_ref, f32[1,512]{1,0:T(1,128)S(1)} %bitcast.87, bf16[768,1536]{1,0:T(8,128)(2,1)} %copy-done, ...), custom_call_target="tpu_custom_call" | custom-call | flops 1811939328 | bytes 8000000 | tf_op jit(solution)/shard_map/pallas_call | solution.py:277
  56.2 4.8 %collective-permute-done.5 = bf16[1536,256]{1,0:T(8,128)(2,1)S(1)} collective-permute-done((bf16[1536,256]{1,0:T(8,128)(2,1)S(1)}, bf16[1536,256]{1,0:T(8,128)(2,1)S(1)}, u32[]{:S(2)}, u32[]{:S(2)}) %collective-permute-start.5) | collective-permute-done | bytes 786464 | tf_op jit(solution)/shard_map/ppermute | solution.py:30
  61.9 6.1 %shard_map.48 = (bf16[8,192,512]{2,1,0:T(8,128)(2,1)}, f32[768,512]{1,0:T(8,128)}, f32[384,512]{1,0:T(8,128)}, bf16[384,512]{1,0:T(8,128)(2,1)}, f32[768,128]{1,0:T(8,128)S(1)}, /*index=5*/f32[1536,384]{1,0:T(8,128)S(1)}) custom-call(s32[2]{0:T(128)S(1)} %pad_add_fusion.flag_ref, f32[1,512]{1,0:T(1,128)S(1)} %bitcast.86, ...), custom_call_target="tpu_custom_call" | custom-call | flops 1811939328 | bytes 8000000 | tf_op jit(solution)/shard_map/pallas_call | solution.py:277
  68.0 4.5 %collective-permute-start.6 = (f32[1536,384]{1,0:T(8,128)S(1)}, f32[1536,384]{1,0:T(8,128)S(1)}, u32[]{:S(2)}, u32[]{:S(2)}) collective-permute-start(f32[1536,384]{1,0:T(8,128)S(1)} %get-tuple-element.59.part_ref), channel_id=1, source_target_pairs={{0,1},{1,0},{4,5},{5,4},{8,9},{9,8},{12,13},{13,12},{16,17},{17,16... | collective-permute-start | bytes 7077896 | tf_op jit(solution)/shard_map/ppermute | solution.py:30
  72.8 4.4 %collective-permute-done.7.logit_in_ref = f32[768,128]{1,0:T(8,128)S(1)} collective-permute-done((f32[768,128]{1,0:T(8,128)S(1)}, f32[768,128]{1,0:T(8,128)S(1)}, u32[]{:S(2)}, u32[]{:S(2)}) %collective-permute-start.7) | collective-permute-done | bytes 393248 | tf_op jit(solution)/shard_map/ppermute | solution.py:30
  77.2 9.6 %shard_map.49 = (f32[2,2,768,256]{3,2,1,0:T(8,128)}, bf16[1536,384]{1,0:T(8,128)(2,1)}, bf16[384,512]{1,0:T(8,128)(2,1)}, bf16[384,512]{1,0:T(8,128)(2,1)}, f32[16,128]{1,0:T(8,128)S(1)}) custom-call(s32[2]{0:T(128)S(1)} %pad_add_fusion.flag_ref, f32[1536,384]{1,0:T(8,128)S(1)} %get-tuple-element.59.part_ref, ...), custom_call_target="tpu_custom_call" | custom-call | flops 3623878656 | bytes 8000000 | tf_op jit(solution)/shard_map/pallas_call | solution.py:277
  86.8 2.2 %fusion.18 = (f32[1,2,768,256]{3,2,1,0:T(8,128)S(1)}, f32[1,2,768,256]{3,2,1,0:T(8,128)S(1)}) fusion(f32[2,2,768,256]{3,2,1,0:T(8,128)} %get-tuple-element.71), kind=kLoop, calls=%fused_computation.72 | loop fusion | bytes 6291456 | tf_op jit(solution)/shard_map/slice | solution.py:367
  89.4 6.6 %shard_map.50 = f32[2,2,768,256]{3,2,1,0:T(8,128)} custom-call(s32[2]{0:T(128)S(1)} %pad_add_fusion.1.flag_ref, bf16[1536,384]{1,0:T(8,128)(2,1)} %get-tuple-element.75.r1_t_hbm, bf16[384,512]{1,0:T(8,128)(2,1)} %get-tuple-element.76.fake_hbm, bf16[384,512]{1,0:T(8,128)(2,1)} %get-tuple-element.77.real_hbm, ...), custom_call_target="tpu_custom_call" | custom-call | flops 1811939328 | bytes 8000000 | tf_op jit(solution)/shard_map/pallas_call | solution.py:277
  96.1 2.1 %fusion.17 = (f32[1,2,768,256]{3,2,1,0:T(8,128)S(1)}, f32[1,2,768,256]{3,2,1,0:T(8,128)S(1)}) fusion(f32[2,2,768,256]{3,2,1,0:T(8,128)} %shard_map.50), kind=kLoop, calls=%fused_computation.71 | loop fusion | bytes 6291456 | tf_op jit(solution)/shard_map/slice | solution.py:364
  98.1 1.8 %collective-permute-start.8 = (f16[1552,256]{1,0:T(8,128)(2,1)S(1)}, f16[1552,256]{1,0:T(8,128)(2,1)S(1)}, u32[]{:S(2)}, u32[]{:S(2)}) collective-permute-start(f16[1552,256]{1,0:T(8,128)(2,1)S(1)} %pad_maximum_fusion.2), channel_id=1, source_target_pairs={{0,64},{1,3},{4,68},{5,7},{8,72},{9,11},{12,76},{13,15},{16,80},{1... | collective-permute-start | bytes 2383880 | tf_op jit(solution)/shard_map/ppermute | solution.py:30
  100.7 10.2 %collective-permute-done.8 = f16[1552,256]{1,0:T(8,128)(2,1)S(1)} collective-permute-done((f16[1552,256]{1,0:T(8,128)(2,1)S(1)}, f16[1552,256]{1,0:T(8,128)(2,1)S(1)}, u32[]{:S(2)}, u32[]{:S(2)}) %collective-permute-start.8) | collective-permute-done | bytes 794656 | tf_op jit(solution)/shard_map/ppermute | solution.py:30
  111.0 2.7 %collective-permute-start.10 = (f16[1552,256]{1,0:T(8,128)(2,1)S(1)}, f16[1552,256]{1,0:T(8,128)(2,1)}, u32[]{:S(2)}, u32[]{:S(2)}) collective-permute-start(f16[1552,256]{1,0:T(8,128)(2,1)S(1)} %get-tuple-element.81), channel_id=1, source_target_pairs={{0,96},{1,131},{4,100},{5,135},{8,104},{9,139},{12,108},{13,143},{... | collective-permute-start | bytes 2383880 | tf_op jit(solution)/shard_map/ppermute | solution.py:30
  113.7 9.0 %collective-permute-done.10 = f16[1552,256]{1,0:T(8,128)(2,1)} collective-permute-done((f16[1552,256]{1,0:T(8,128)(2,1)S(1)}, f16[1552,256]{1,0:T(8,128)(2,1)}, u32[]{:S(2)}, u32[]{:S(2)}) %collective-permute-start.10) | collective-permute-done | bytes 794656 | tf_op jit(solution)/shard_map/ppermute | solution.py:30
  122.7 3.5 %collective-permute-done.9 = f16[1552,256]{1,0:T(8,128)(2,1)} collective-permute-done((f16[1552,256]{1,0:T(8,128)(2,1)S(1)}, f16[1552,256]{1,0:T(8,128)(2,1)}, u32[]{:S(2)}, u32[]{:S(2)}) %collective-permute-start.9) | collective-permute-done | bytes 794656 | tf_op jit(solution)/shard_map/ppermute | solution.py:30
  126.9 2.1 %fusion.4 = f32[1536,256]{1,0:T(8,128)S(1)} fusion(f32[1,2,768,256]{3,2,1,0:T(8,128)S(1)} %get-tuple-element.96, f32[256]{0:T(256)S(1)} %bitcast.103, f16[1552,256]{1,0:T(8,128)(2,1)} %copy-done.5, f32[256]{0:T(256)S(1)} %bitcast.102, f16[1552,256]{1,0:T(8,128)(2,1)} %collective-permute-done.10, f32[256]{0:T(256)S(1)} %bitcast.101, ...), kind=kLoop, calls=%fused_computation.8 | loop fusion | flops 3538944 | bytes 5508096 | tf_op jit(solution)/shard_map/add | solution.py:373
  129.6 2.7 %collective-permute-start.12 = (f16[400,256]{1,0:T(8,128)(2,1)S(1)}, f16[400,256]{1,0:T(8,128)(2,1)S(1)}, u32[]{:S(2)}, u32[]{:S(2)}) collective-permute-start(f16[400,256]{1,0:T(8,128)(2,1)S(1)} %get-tuple-element.86), channel_id=1, source_target_pairs={{0,130},{1,97},{4,134},{5,101},{8,138},{9,105},{12,142},{13,109},{... | collective-permute-start | bytes 614408 | tf_op jit(solution)/shard_map/ppermute | solution.py:30
  132.3 3.4 %collective-permute-done.11 = f16[400,256]{1,0:T(8,128)(2,1)S(1)} collective-permute-done((f16[400,256]{1,0:T(8,128)(2,1)S(1)}, f16[400,256]{1,0:T(8,128)(2,1)S(1)}, u32[]{:S(2)}, u32[]{:S(2)}) %collective-permute-start.11) | collective-permute-done | bytes 204832 | tf_op jit(solution)/shard_map/ppermute | solution.py:30
  135.7 1.5 collective-permute-done.12
  137.2 1.2 collective-permute-done.13
  138.6 13.6 %all_to_all.15 = f32[8,48,256]{2,1,0:T(8,128)S(1)} all-to-all(f32[8,48,256]{2,1,0:T(8,128)S(1)} %bitcast.95), channel_id=1, replica_groups=mesh['ylo'=2,'x'=4,'z'=8,'yhi'=2,'c'=2] {'z'}, dimensions={0} | all-to-all | bytes 786432 | tf_op jit(solution)/shard_map/all_to_all | solution.py:389
  152.3 15.4 %all_to_all.16 = f32[8,48,256]{2,1,0:T(8,128)S(1)} all-to-all(f32[8,48,256]{2,1,0:T(8,128)S(1)} %broadcast_in_dim.20), channel_id=1, replica_groups=mesh['ylo'=2,'x'=4,'z'=8,'yhi'=2,'c'=2] {'ylo','x'}, dimensions={0} | all-to-all | bytes 786432 | tf_op jit(solution)/shard_map/all_to_all | solution.py:391
  167.8 1.4 collective-permute-start.14
  (64 shorter events, 12.3 us)
Async XLA Ops:
  0.0 12.9 %copy-start.1 = (bf16[1,192,1536]{2,1,0:T(8,128)(2,1)S(1)}, bf16[1,192,1536]{2,1,0:T(8,128)(2,1)}, u32[]{:S(2)}) copy-start(bf16[1,192,1536]{2,1,0:T(8,128)(2,1)} %param.4) | copy-start | bytes 1769476
  0.0 12.9 %copy-start.2 = (bf16[1,192,1536]{2,1,0:T(8,128)(2,1)S(1)}, bf16[1,192,1536]{2,1,0:T(8,128)(2,1)}, u32[]{:S(2)}) copy-start(bf16[1,192,1536]{2,1,0:T(8,128)(2,1)} %param.5) | copy-start | bytes 1769476
  0.8 4.1 %collective-permute-start = (bf16[48,256]{1,0:T(8,128)(2,1)S(1)}, bf16[48,256]{1,0:T(8,128)(2,1)S(1)}, u32[]{:S(2)}, u32[]{:S(2)}) collective-permute-start(bf16[48,256]{1,0:T(8,128)(2,1)S(1)} %constant_dynamic-slice_fusion.4), channel_id=1, source_target_pairs={{0,1},{1,0},{4,5},{5,4},{8,9},{9,8},{12,13},{13,12},{16,17},{17,16... | collective-permute-start | bytes 73736 | tf_op jit(solution)/shard_map/ppermute | solution.py:30
  6.5 21.6 %all-to-all-start = ((bf16[8,96,256]{2,1,0:T(8,128)(2,1)}), bf16[8,96,256]{2,1,0:T(8,128)(2,1)S(1)}, u32[]{:S(2)}, u32[]{:S(2)}) async-start(bf16[8,96,256]{2,1,0:T(8,128)(2,1)} %broadcast_in_dim.16), calls=%async_computation | async-start | bytes 786432 | tf_op jit(solution)/shard_map/all_to_all | solution.py:306
  13.0 22.1 %collective-permute-start.2 = (bf16[384,1536]{1,0:T(8,128)(2,1)S(1)}, bf16[384,1536]{1,0:T(8,128)(2,1)S(1)}, u32[]{:S(2)}, u32[]{:S(2)}) collective-permute-start(bf16[384,1536]{1,0:T(8,128)(2,1)S(1)} %pad_maximum_fusion.3), channel_id=1, source_target_pairs={{0,1},{1,0},{4,5},{5,4},{8,9},{9,8},{12,13},{13,12},{16,17},{17,16... | collective-permute-start | bytes 3538952 | tf_op jit(solution)/shard_map/ppermute | solution.py:30
  28.1 6.9 %collective-permute-start.1 = (bf16[768,256]{1,0:T(8,128)(2,1)S(1)}, bf16[768,256]{1,0:T(8,128)(2,1)S(1)}, u32[]{:S(2)}, u32[]{:S(2)}) collective-permute-start(bf16[768,256]{1,0:T(8,128)(2,1)S(1)} %bitcast.93), channel_id=1, source_target_pairs={{0,130},{1,33},{4,134},{5,37},{8,138},{9,41},{12,142},{13,45},{16,... | collective-permute-start | bytes 1179656 | tf_op jit(solution)/shard_map/ppermute | solution.py:30
  35.1 25.9 %copy-start.4 = (bf16[1536,256]{1,0:T(8,128)(2,1)}, bf16[1536,256]{1,0:T(8,128)(2,1)S(1)}, u32[]{:S(2)}) copy-start(bf16[1536,256]{1,0:T(8,128)(2,1)S(1)} %pad_maximum_fusion.4) | copy-start | bytes 2359300
  35.1 14.9 %copy-start.6 = (f32[2048]{0:T(1024)S(1)}, f32[2048]{0:T(1024)}, u32[]{:S(2)}) copy-start(f32[2048]{0:T(1024)} %param.7) | copy-start | bytes 24580
  35.2 2.9 %copy-start.3 = (bf16[384,1536]{1,0:T(8,128)(2,1)}, bf16[384,1536]{1,0:T(8,128)(2,1)S(1)}, u32[]{:S(2)}) copy-start(bf16[384,1536]{1,0:T(8,128)(2,1)S(1)} %collective-permute-done.2.other_hbm) | copy-start | bytes 3538948
  35.2 12.5 %collective-permute-start.3 = (bf16[1536,256]{1,0:T(8,128)(2,1)S(1)}, bf16[1536,256]{1,0:T(8,128)(2,1)S(1)}, u32[]{:S(2)}, u32[]{:S(2)}) collective-permute-start(bf16[1536,256]{1,0:T(8,128)(2,1)S(1)} %pad_maximum_fusion.4), channel_id=1, source_target_pairs={{0,32},{1,129},{4,36},{5,133},{8,40},{9,137},{12,44},{13,141},{16,... | collective-permute-start | bytes 2359304 | tf_op jit(solution)/shard_map/ppermute | solution.py:30
  36.5 11.1 %collective-permute-start.4 = (bf16[1536,256]{1,0:T(8,128)(2,1)S(1)}, bf16[1536,256]{1,0:T(8,128)(2,1)S(1)}, u32[]{:S(2)}, u32[]{:S(2)}) collective-permute-start(bf16[1536,256]{1,0:T(8,128)(2,1)S(1)} %pad_maximum_fusion.4), channel_id=1, source_target_pairs={{0,96},{1,131},{4,100},{5,135},{8,104},{9,139},{12,108},{13,143},{... | collective-permute-start | bytes 2359304 | tf_op jit(solution)/shard_map/ppermute | solution.py:30
  42.7 1.4 copy-start
  47.7 2.5 %copy-start.7 = (bf16[1536,256]{1,0:T(8,128)(2,1)}, bf16[1536,256]{1,0:T(8,128)(2,1)S(1)}, u32[]{:S(2)}) copy-start(bf16[1536,256]{1,0:T(8,128)(2,1)S(1)} %collective-permute-done.3) | copy-start | bytes 2359300
  47.7 0.9 copy-start.8
  48.6 12.4 %collective-permute-start.5 = (bf16[1536,256]{1,0:T(8,128)(2,1)S(1)}, bf16[1536,256]{1,0:T(8,128)(2,1)S(1)}, u32[]{:S(2)}, u32[]{:S(2)}) collective-permute-start(bf16[1536,256]{1,0:T(8,128)(2,1)S(1)} %collective-permute-done.3), channel_id=1, source_target_pairs={{0,32},{1,129},{4,36},{5,133},{8,40},{9,137},{12,44},{13,141},{16,... | collective-permute-start | bytes 2359304 | tf_op jit(solution)/shard_map/ppermute | solution.py:30
  61.0 0.9 copy-start.9
  68.0 9.2 %collective-permute-start.6 = (f32[1536,384]{1,0:T(8,128)S(1)}, f32[1536,384]{1,0:T(8,128)S(1)}, u32[]{:S(2)}, u32[]{:S(2)}) collective-permute-start(f32[1536,384]{1,0:T(8,128)S(1)} %get-tuple-element.59.part_ref), channel_id=1, source_target_pairs={{0,1},{1,0},{4,5},{5,4},{8,9},{9,8},{12,13},{13,12},{16,17},{17,16... | collective-permute-start | bytes 7077896 | tf_op jit(solution)/shard_map/ppermute | solution.py:30
  72.5 4.7 %collective-permute-start.7 = (f32[768,128]{1,0:T(8,128)S(1)}, f32[768,128]{1,0:T(8,128)S(1)}, u32[]{:S(2)}, u32[]{:S(2)}) collective-permute-start(f32[768,128]{1,0:T(8,128)S(1)} %get-tuple-element.60.logit_ref), channel_id=1, source_target_pairs={{0,1},{1,0},{4,5},{5,4},{8,9},{9,8},{12,13},{13,12},{16,17},{17,16... | collective-permute-start | bytes 1179656 | tf_op jit(solution)/shard_map/ppermute | solution.py:30
  98.1 12.8 %collective-permute-start.8 = (f16[1552,256]{1,0:T(8,128)(2,1)S(1)}, f16[1552,256]{1,0:T(8,128)(2,1)S(1)}, u32[]{:S(2)}, u32[]{:S(2)}) collective-permute-start(f16[1552,256]{1,0:T(8,128)(2,1)S(1)} %pad_maximum_fusion.2), channel_id=1, source_target_pairs={{0,64},{1,3},{4,68},{5,7},{8,72},{9,11},{12,76},{13,15},{16,80},{1... | collective-permute-start | bytes 2383880 | tf_op jit(solution)/shard_map/ppermute | solution.py:30
  111.0 2.7 %copy-start.5 = (f16[1552,256]{1,0:T(8,128)(2,1)}, f16[1552,256]{1,0:T(8,128)(2,1)S(1)}, u32[]{:S(2)}) copy-start(f16[1552,256]{1,0:T(8,128)(2,1)S(1)} %collective-permute-done.8) | copy-start | bytes 2383876
  111.0 11.7 %collective-permute-start.10 = (f16[1552,256]{1,0:T(8,128)(2,1)S(1)}, f16[1552,256]{1,0:T(8,128)(2,1)}, u32[]{:S(2)}, u32[]{:S(2)}) collective-permute-start(f16[1552,256]{1,0:T(8,128)(2,1)S(1)} %get-tuple-element.81), channel_id=1, source_target_pairs={{0,96},{1,131},{4,100},{5,135},{8,104},{9,139},{12,108},{13,143},{... | collective-permute-start | bytes 2383880 | tf_op jit(solution)/shard_map/ppermute | solution.py:30
  113.7 12.5 %collective-permute-start.9 = (f16[1552,256]{1,0:T(8,128)(2,1)S(1)}, f16[1552,256]{1,0:T(8,128)(2,1)}, u32[]{:S(2)}, u32[]{:S(2)}) collective-permute-start(f16[1552,256]{1,0:T(8,128)(2,1)S(1)} %get-tuple-element.80), channel_id=1, source_target_pairs={{0,32},{1,129},{4,36},{5,133},{8,40},{9,137},{12,44},{13,141},{16,... | collective-permute-start | bytes 2383880 | tf_op jit(solution)/shard_map/ppermute | solution.py:30
  129.5 6.2 %collective-permute-start.11 = (f16[400,256]{1,0:T(8,128)(2,1)S(1)}, f16[400,256]{1,0:T(8,128)(2,1)S(1)}, u32[]{:S(2)}, u32[]{:S(2)}) collective-permute-start(f16[400,256]{1,0:T(8,128)(2,1)S(1)} %get-tuple-element.85), channel_id=1, source_target_pairs={{0,128},{1,33},{4,132},{5,37},{8,136},{9,41},{12,140},{13,45},{16,... | collective-permute-start | bytes 614408 | tf_op jit(solution)/shard_map/ppermute | solution.py:30
  129.6 7.6 %collective-permute-start.12 = (f16[400,256]{1,0:T(8,128)(2,1)S(1)}, f16[400,256]{1,0:T(8,128)(2,1)S(1)}, u32[]{:S(2)}, u32[]{:S(2)}) collective-permute-start(f16[400,256]{1,0:T(8,128)(2,1)S(1)} %get-tuple-element.86), channel_id=1, source_target_pairs={{0,130},{1,97},{4,134},{5,101},{8,138},{9,105},{12,142},{13,109},{... | collective-permute-start | bytes 614408 | tf_op jit(solution)/shard_map/ppermute | solution.py:30
  132.3 6.1 %collective-permute-start.13 = (f16[400,256]{1,0:T(8,128)(2,1)S(1)}, f16[400,256]{1,0:T(8,128)(2,1)S(1)}, u32[]{:S(2)}, u32[]{:S(2)}) collective-permute-start(f16[400,256]{1,0:T(8,128)(2,1)S(1)} %get-tuple-element.87), channel_id=1, source_target_pairs={{0,2},{1,65},{4,6},{5,69},{8,10},{9,73},{12,14},{13,77},{16,18},{1... | collective-permute-start | bytes 614408 | tf_op jit(solution)/shard_map/ppermute | solution.py:30
  167.8 2.5 %collective-permute-start.14 = (f32[48,1024]{1,0:T(8,128)S(1)}, f32[48,1024]{1,0:T(8,128)S(1)}, u32[]{:S(2)}, u32[]{:S(2)}) collective-permute-start(f32[48,1024]{1,0:T(8,128)S(1)} %fusion.10), channel_id=1, source_target_pairs={{0,1},{1,0},{4,5},{5,4},{8,9},{9,8},{12,13},{13,12},{16,17},{17,16... | collective-permute-start | bytes 589832 | tf_op jit(solution)/shard_map/ppermute | solution.py:30

commit v7 on v6

--- a/solution.py
+++ b/solution.py
@@ -115,14 +115,15 @@
     return jnp.where(flag_ref[0] == 0, sub, flag_ref[1] ^ piece), jnp.where(flag_ref[0] == 0, piece, sub)
 
 
-def laid(flag_ref, one_hbm, two_hbm, w_ref):
-    height = one_hbm.shape[2]
+def laid(flag_ref, subs, w_ref):
     pairs = []
-    for piece, ref in enumerate((one_hbm, two_hbm)):
+    for piece in (0, 1):
         for sub in (0, 1):
             half, block = place_of(flag_ref, piece, sub)
+            ref = subs[2 * piece + sub]
+            height = ref.shape[1]
             rows = pl.ds(pl.multiple_of(half * height, 16), height)
-            pairs.append((ref.at[sub], w_ref.at[:, rows, pl.ds(pl.multiple_of(block * 256, 128), 256)]))
+            pairs.append((ref, w_ref.at[:, rows, pl.ds(pl.multiple_of(block * 256, 128), 256)]))
     return pairs
 
 
@@ -140,12 +141,14 @@
 
 def forward_kernel(flag_ref, score_ref, *refs, so_far):
     earlier, refs = (refs[:2], refs[2:]) if so_far else ((None, None), refs)
-    (tokens_hbm, one_hbm, two_hbm, w_hbm, slope_hbm, curve_hbm, lifted_hbm, logit_ref, part_ref,
+    tokens_hbm, one_hbm, refs = refs[0], refs[1], refs[2:]
+    two, refs = ((refs[0], refs[1]), refs[2:]) if so_far else ((refs[0].at[0], refs[0].at[1]), refs[1:])
+    (w_hbm, slope_hbm, curve_hbm, lifted_hbm, logit_ref, part_ref,
      tokens_ref, w_ref, slope_ref, curve_ref, lifted_ref, sems, out_sems) = refs
     n = lifted_ref.shape[0]
     copies = fetched(
         sems,
-        *laid(flag_ref, one_hbm, two_hbm, w_ref),
+        *laid(flag_ref, (one_hbm.at[0], one_hbm.at[1], *two), w_ref),
         *((tokens_hbm.at[k * n : k * n + n, :], tokens_ref.at[k * n : k * n + n, :]) for k in (0, 1)),
     )
     done(copies[:4])
@@ -268,10 +271,11 @@
     term_tiles(flag_ref, (fake_ref, real_ref, lifted_ref), tokens_t_ref, r1_t_ref, term_ref, term_hbm, out_sems)
 
 
-def call(kernel, flops, outs, scratch, *args, flags=None, there=(), sems=(), vmem_mib=20):
+def call(kernel, flops, outs, scratch, *args, flags=None, there=(), anywhere=(), sems=(), vmem_mib=20):
     vmem = pl.BlockSpec(memory_space=pltpu.VMEM)
     specs = [vmem] * len(args) + [pl.BlockSpec(memory_space=pltpu.HBM)] * len(there)
-    args = (*args, *(pltpu.with_memory_space_constraint(a, pltpu.HBM) for a in there))
+    specs += [pl.BlockSpec(memory_space=pl.ANY)] * len(anywhere)
+    args = (*args, *(pltpu.with_memory_space_constraint(a, pltpu.HBM) for a in there), *anywhere)
     if flags is not None:
         args, specs = (flags, *args), [pl.BlockSpec(memory_space=pltpu.SMEM), *specs]
     return pl.pallas_call(
@@ -317,7 +321,7 @@
         )
 
     left, right, tokens, tokens_t, peak = together((own, own), (ring(1), ring(-1)), join_tokens, (to_core(own_tokens),))
-    across = send(left, ring(1))
+    across = together((left[: d_in // 2], right[d_in // 2 :]), (ring(1), ring(-1)))
 
     def score_at(start):
         return lax.dynamic_slice_in_dim(score_vector, c * half + start, 256, 0)
@@ -332,16 +336,17 @@
     sums = [((2 * n, 128), F32), ((d_in, n), F32)]
     marked = lambda shapes: [(*shape, True) for shape in shapes]
 
-    def forward(flags, score, one, two, earlier):
-        pieces = [p.reshape(2, NZ, 2 * rows, 256) for p in (one, two)]
+    def forward(flags, score, pieces, earlier):
         return call(
             functools.partial(forward_kernel, so_far=bool(earlier)), 6 * n * d_in * wide, [*marked(states), *sums],
             [((2 * n, d_in), BF16), *states], score, *earlier,
-            flags=flags, there=(tokens, *pieces), sems=[6, 4], vmem_mib=24,
+            flags=flags, there=(tokens,), anywhere=pieces, sems=[6, 4], vmem_mib=24,
         )
 
-    w_1, slope_1, curve_1, lifted_1, *earlier = forward(flags_1, scores(x + 3, x + 1, 1 - ylo), left, right, ())
-    w_2, slope_2, curve_2, lifted_2, logit, part = forward(flags_2, scores(x, x + 2, ylo), own, across, earlier)
+    left, right, own = (p.reshape(2, NZ, 2 * rows, 256) for p in (left, right, own))
+    w_1, slope_1, curve_1, lifted_1, *earlier = forward(flags_1, scores(x + 3, x + 1, 1 - ylo), (left, right), ())
+    across = [p.reshape(NZ, 2 * rows, 256) for p in across]
+    w_2, slope_2, curve_2, lifted_2, logit, part = forward(flags_2, scores(x, x + 2, ylo), (own, *across), earlier)
     part_in, logit_in = to_core(part), to_core(logit)
 
     works = [((n, wide), BF16)] * 2
@@ -361,11 +366,12 @@
             fourth_kernel, 6 * n * d_in * wide, marked([terms]), [terms, r1_shape, *works, states[3], tall],
             flags=flags_1, there=(r1_t, fake_1, real_1, lifted_1, tokens_t), sems=[5, 16], vmem_mib=28,
         )
-        return [packed(term_1[k].reshape(d_in, 256), exponent) for k in (1, 0)]
-
-    across, *beside = together(
+        return (term_1,)
+
+    across, term_1 = together(
         (packed(term_2[1].reshape(d_in, 256), exponent),), (ring(2),), rest_of_term, (r1_t,)
     )
+    beside = [packed(term_1[k].reshape(d_in, 256), exponent) for k in (1, 0)]
     from_left, from_right = together(beside, (ring(1), ring(-1)))
 
     def summed(own, exponent, *messages):

time: 172 us -> 158 us (0.919)
  waiting for transfers between devices: 63.7 us -> 49.6 us
  starting transfers between devices: 29.2 us -> 38 us
  blocking collectives: 29.1 us -> 23.4 us
    ppermute x15 -> x16, waiting for transfers between devices: 49.4 us -> 35.3 us  [send(): return lax.ppermute(array, AXES, pairs)]
    ppermute x15 -> x16, starting transfers between devices: 22.8 us -> 31.6 us  [send(): return lax.ppermute(array, AXES, pairs)]
    all_to_all x1, blocking collectives: 15.4 us -> 9.98 us  [per_device(): lax.all_to_all(jnp.broadcast_to(both[None], (8, *both.shape)), ('ylo', 'x...]
    unnamed x20 -> x12, local copies, waits for them, and re-layouts: 3.29 us -> 1.43 us
  transfers between devices with their start and end apart: 16 -> 17, of which waited for: 13 -> 11; matrix products, arithmetic and copies ran while one was open for 1% -> 0% of each run, Pallas kernels for 6% -> 11%
where the time goes in v7:
time: 158 us
  waiting for transfers between devices  49.6 us (31%)
  starting transfers between devices  38 us (24%)
  Pallas kernels  32.2 us (20%)
  blocking collectives  23.4 us (15%)
  local copies, waits for them, and re-layouts  7.92 us (5%)
  other arithmetic  6.36 us (4%)
    ppermute x16, waiting for transfers between devices, send(): return lax.ppermute(array, AXES, pairs)  35.3 us
    pallas_call x5, Pallas kernels, call(): pl.pallas_call(kernel, out_shape=[(pltpu.HBM if len(out) == 3 else pltpu....  32.2 us
    ppermute x16, starting transfers between devices, send(): return lax.ppermute(array, AXES, pairs)  31.6 us
    all_to_all x1, waiting for transfers between devices, per_device(): lax.all_to_all(jnp.broadcast_to(block[None], (NZ, *block.shape)), 'z', 0, 0)  14.3 us
    all_to_all x1, blocking collectives, per_device(): both = jnp.sum(lax.all_to_all(both, 'z', 0, 0), 0)  13.4 us
    all_to_all x1, blocking collectives, per_device(): lax.all_to_all(jnp.broadcast_to(both[None], (8, *both.shape)), ('ylo', 'x...  9.98 us
    all_to_all x1, starting transfers between devices, per_device(): lax.all_to_all(jnp.broadcast_to(block[None], (NZ, *block.shape)), 'z', 0, 0)  6.45 us
  transfers between devices with their start and end apart: 17, of which 11 were waited for; matrix products, arithmetic and copies ran while one was open for 0% of the time, Pallas kernels for 11%

profile of v7, /device:TPU:1, one launch (start us, length us, event | category | flops | bytes accessed | tf_op | source)
XLA Modules:
  0.0 157.8 jit_solution(5639061342823928406)
XLA Ops:
  0.8 3.2 %collective-permute-start = (bf16[48,256]{1,0:T(8,128)(2,1)S(1)}, bf16[48,256]{1,0:T(8,128)(2,1)S(1)}, u32[]{:S(2)}, u32[]{:S(2)}) collective-permute-start(bf16[48,256]{1,0:T(8,128)(2,1)S(1)} %constant_dynamic-slice_fusion.4), channel_id=1, source_target_pairs={{0,1},{1,0},{4,5},{5,4},{8,9},{9,8},{12,13},{13,12},{16,17},{17,16... | collective-permute-start | bytes 73736 | tf_op jit(solution)/shard_map/ppermute | solution.py:30
  6.5 6.4 %all-to-all-start = ((bf16[8,96,256]{2,1,0:T(8,128)(2,1)}), bf16[8,96,256]{2,1,0:T(8,128)(2,1)S(1)}, u32[]{:S(2)}, u32[]{:S(2)}) async-start(bf16[8,96,256]{2,1,0:T(8,128)(2,1)} %broadcast_in_dim.16), calls=%async_computation | async-start | bytes 786432 | tf_op jit(solution)/shard_map/all_to_all | solution.py:310
  13.7 14.3 %all-to-all-done = bf16[8,96,256]{2,1,0:T(8,128)(2,1)S(1)} async-done(((bf16[8,96,256]{2,1,0:T(8,128)(2,1)}), bf16[8,96,256]{2,1,0:T(8,128)(2,1)S(1)}, u32[]{:S(2)}, u32[]{:S(2)}) %all-to-all-start) | async-done | bytes 393248 | tf_op jit(solution)/shard_map/all_to_all | solution.py:310
  28.1 1.2 collective-permute-start.1
  29.3 5.7 %collective-permute-done.1 = bf16[768,256]{1,0:T(8,128)(2,1)S(1)} collective-permute-done((bf16[768,256]{1,0:T(8,128)(2,1)S(1)}, bf16[768,256]{1,0:T(8,128)(2,1)S(1)}, u32[]{:S(2)}, u32[]{:S(2)}) %collective-permute-start.1) | collective-permute-done | bytes 393248 | tf_op jit(solution)/shard_map/ppermute | solution.py:30
  35.2 1.4 collective-permute-start.3
  36.5 1.5 collective-permute-start.4
  38.1 4.6 %shard_map.46 = (bf16[768,1536]{1,0:T(8,128)(2,1)S(1)}, bf16[1536,768]{1,0:T(8,128)(2,1)}, f32[16,128]{1,0:T(8,128)S(1)}) custom-call(s32[1]{0:T(128)} %bitcast.flag_ref, bf16[192,1536]{1,0:T(8,128)(2,1)} %bitcast.95, bf16[192,1536]{1,0:T(8,128)(2,1)} %bitcast.97, bf16[384,1536]{1,0:T(8,128)(2,1)} %copy-done.3), custom_call_target="tpu_custom_call" | custom-call | flops 150994944 | bytes 8000000 | tf_op jit(solution)/shard_map/pallas_call | solution.py:281
  42.8 1.4 copy-done
  44.2 3.5 %collective-permute-done.3 = bf16[1536,256]{1,0:T(8,128)(2,1)S(1)} collective-permute-done((bf16[1536,256]{1,0:T(8,128)(2,1)S(1)}, bf16[1536,256]{1,0:T(8,128)(2,1)S(1)}, u32[]{:S(2)}, u32[]{:S(2)}) %collective-permute-start.3) | collective-permute-done | bytes 786464 | tf_op jit(solution)/shard_map/ppermute | solution.py:30
  47.7 1.4 collective-permute-start.5
  49.1 1.5 collective-permute-start.6
  50.7 5.7 %shard_map.47 = (bf16[8,192,512]{2,1,0:T(8,128)(2,1)}, f32[768,512]{1,0:T(8,128)}, f32[384,512]{1,0:T(8,128)}, bf16[384,512]{1,0:T(8,128)(2,1)}, f32[768,128]{1,0:T(8,128)S(1)}, /*index=5*/f32[1536,384]{1,0:T(8,128)S(1)}) custom-call(s32[2]{0:T(128)S(1)} %get-tuple-element.143.flag_ref, f32[1,512]{1,0:T(1,128)S(1)} %bitcast.91, bf16[768,1536]{1,0:T(8,128)(2,1)} %copy-done, ...), custom_call_target="tpu_custom_call" | custom-call | flops 1811939328 | bytes 8000000 | tf_op jit(solution)/shard_map/pallas_call | solution.py:281
  56.4 5.7 %shard_map.48 = (bf16[8,192,512]{2,1,0:T(8,128)(2,1)}, f32[768,512]{1,0:T(8,128)}, f32[384,512]{1,0:T(8,128)}, bf16[384,512]{1,0:T(8,128)(2,1)}, f32[768,128]{1,0:T(8,128)S(1)}, /*index=5*/f32[1536,384]{1,0:T(8,128)S(1)}) custom-call(s32[2]{0:T(128)S(1)} %get-tuple-element.142.flag_ref, f32[1,512]{1,0:T(1,128)S(1)} %bitcast.90, ...), custom_call_target="tpu_custom_call" | custom-call | flops 1811939328 | bytes 8000000 | tf_op jit(solution)/shard_map/pallas_call | solution.py:281
  62.1 4.5 %collective-permute-start.7 = (f32[1536,384]{1,0:T(8,128)S(1)}, f32[1536,384]{1,0:T(8,128)S(1)}, u32[]{:S(2)}, u32[]{:S(2)}) collective-permute-start(f32[1536,384]{1,0:T(8,128)S(1)} %get-tuple-element.66.part_ref), channel_id=1, source_target_pairs={{0,1},{1,0},{4,5},{5,4},{8,9},{9,8},{12,13},{13,12},{16,17},{17,16... | collective-permute-start | bytes 7077896 | tf_op jit(solution)/shard_map/ppermute | solution.py:30
  66.8 4.6 %collective-permute-done.8.logit_in_ref = f32[768,128]{1,0:T(8,128)S(1)} collective-permute-done((f32[768,128]{1,0:T(8,128)S(1)}, f32[768,128]{1,0:T(8,128)S(1)}, u32[]{:S(2)}, u32[]{:S(2)}) %collective-permute-start.8) | collective-permute-done | bytes 393248 | tf_op jit(solution)/shard_map/ppermute | solution.py:30
  71.4 9.6 %shard_map.49 = (f32[2,2,768,256]{3,2,1,0:T(8,128)}, bf16[1536,384]{1,0:T(8,128)(2,1)}, bf16[384,512]{1,0:T(8,128)(2,1)}, bf16[384,512]{1,0:T(8,128)(2,1)}, f32[16,128]{1,0:T(8,128)S(1)}) custom-call(s32[2]{0:T(128)S(1)} %get-tuple-element.142.flag_ref, f32[1536,384]{1,0:T(8,128)S(1)} %get-tuple-element.66.part_ref, ...), custom_call_target="tpu_custom_call" | custom-call | flops 3623878656 | bytes 8000000 | tf_op jit(solution)/shard_map/pallas_call | solution.py:281
  81.0 2.2 %fusion.18 = (f32[1,2,768,256]{3,2,1,0:T(8,128)S(1)}, f32[1,2,768,256]{3,2,1,0:T(8,128)S(1)}) fusion(f32[2,2,768,256]{3,2,1,0:T(8,128)} %get-tuple-element.78), kind=kLoop, calls=%fused_computation.72 | loop fusion | bytes 6291456 | tf_op jit(solution)/shard_map/slice | solution.py:372
  83.6 1.8 %collective-permute-start.9 = (f16[1552,256]{1,0:T(8,128)(2,1)S(1)}, f16[1552,256]{1,0:T(8,128)(2,1)S(1)}, u32[]{:S(2)}, u32[]{:S(2)}) collective-permute-start(f16[1552,256]{1,0:T(8,128)(2,1)S(1)} %pad_maximum_fusion.2), channel_id=1, source_target_pairs={{0,64},{1,3},{4,68},{5,7},{8,72},{9,11},{12,76},{13,15},{16,80},{1... | collective-permute-start | bytes 2383880 | tf_op jit(solution)/shard_map/ppermute | solution.py:30
  85.3 6.6 %shard_map.50 = f32[2,2,768,256]{3,2,1,0:T(8,128)} custom-call(s32[2]{0:T(128)S(1)} %get-tuple-element.143.flag_ref, bf16[1536,384]{1,0:T(8,128)(2,1)} %get-tuple-element.82.r1_t_hbm, bf16[384,512]{1,0:T(8,128)(2,1)} %get-tuple-element.83.fake_hbm, bf16[384,512]{1,0:T(8,128)(2,1)} %get-tuple-element.84.real_hbm, ...), custom_call_target="tpu_custom_call" | custom-call | flops 1811939328 | bytes 8000000 | tf_op jit(solution)/shard_map/pallas_call | solution.py:281
  92.0 4.4 %collective-permute-done.9 = f16[1552,256]{1,0:T(8,128)(2,1)S(1)} collective-permute-done((f16[1552,256]{1,0:T(8,128)(2,1)S(1)}, f16[1552,256]{1,0:T(8,128)(2,1)S(1)}, u32[]{:S(2)}, u32[]{:S(2)}) %collective-permute-start.9) | collective-permute-done | bytes 794656 | tf_op jit(solution)/shard_map/ppermute | solution.py:30
  96.4 2.4 %fusion.17 = (f32[1,2,768,256]{3,2,1,0:T(8,128)S(1)}, f32[1,2,768,256]{3,2,1,0:T(8,128)S(1)}) fusion(f32[2,2,768,256]{3,2,1,0:T(8,128)} %shard_map.50), kind=kLoop, calls=%fused_computation.71 | loop fusion | bytes 6291456 | tf_op jit(solution)/shard_map/slice | solution.py:374
  100.0 2.5 %collective-permute-start.11 = (f16[1552,256]{1,0:T(8,128)(2,1)S(1)}, f16[1552,256]{1,0:T(8,128)(2,1)}, u32[]{:S(2)}, u32[]{:S(2)}) collective-permute-start(f16[1552,256]{1,0:T(8,128)(2,1)S(1)} %get-tuple-element.87), channel_id=1, source_target_pairs={{0,96},{1,131},{4,100},{5,135},{8,104},{9,139},{12,108},{13,143},{... | collective-permute-start | bytes 2383880 | tf_op jit(solution)/shard_map/ppermute | solution.py:30
  102.4 9.8 %collective-permute-done.10 = f16[1552,256]{1,0:T(8,128)(2,1)} collective-permute-done((f16[1552,256]{1,0:T(8,128)(2,1)S(1)}, f16[1552,256]{1,0:T(8,128)(2,1)}, u32[]{:S(2)}, u32[]{:S(2)}) %collective-permute-start.10) | collective-permute-done | bytes 794656 | tf_op jit(solution)/shard_map/ppermute | solution.py:30
  112.9 2.1 %fusion.4 = f32[1536,256]{1,0:T(8,128)S(1)} fusion(f32[1,2,768,256]{3,2,1,0:T(8,128)S(1)} %get-tuple-element.102, f32[256]{0:T(256)S(1)} %bitcast.108, f16[1552,256]{1,0:T(8,128)(2,1)} %copy-done.4, f32[256]{0:T(256)S(1)} %bitcast.107, f16[1552,256]{1,0:T(8,128)(2,1)} %collective-permute-done.11, f32[256]{0:T(256)S(1)} %bitcast.106, ...), kind=kLoop, calls=%fused_computation.8 | loop fusion | flops 3538944 | bytes 5508096 | tf_op jit(solution)/shard_map/add | solution.py:379
  115.9 2.4 %collective-permute-start.13 = (f16[400,256]{1,0:T(8,128)(2,1)S(1)}, f16[400,256]{1,0:T(8,128)(2,1)S(1)}, u32[]{:S(2)}, u32[]{:S(2)}) collective-permute-start(f16[400,256]{1,0:T(8,128)(2,1)S(1)} %get-tuple-element.92), channel_id=1, source_target_pairs={{0,130},{1,97},{4,134},{5,101},{8,138},{9,105},{12,142},{13,109},{... | collective-permute-start | bytes 614408 | tf_op jit(solution)/shard_map/ppermute | solution.py:30
  119.4 2.0 %collective-permute-done.12 = f16[400,256]{1,0:T(8,128)(2,1)S(1)} collective-permute-done((f16[400,256]{1,0:T(8,128)(2,1)S(1)}, f16[400,256]{1,0:T(8,128)(2,1)S(1)}, u32[]{:S(2)}, u32[]{:S(2)}) %collective-permute-start.12) | collective-permute-done | bytes 204832 | tf_op jit(solution)/shard_map/ppermute | solution.py:30
  121.4 1.8 %collective-permute-done.13 = f16[400,256]{1,0:T(8,128)(2,1)S(1)} collective-permute-done((f16[400,256]{1,0:T(8,128)(2,1)S(1)}, f16[400,256]{1,0:T(8,128)(2,1)S(1)}, u32[]{:S(2)}, u32[]{:S(2)}) %collective-permute-start.13) | collective-permute-done | bytes 204832 | tf_op jit(solution)/shard_map/ppermute | solution.py:30
  123.2 1.5 collective-permute-done.14
  125.0 13.4 %all_to_all.15 = f32[8,48,256]{2,1,0:T(8,128)S(1)} all-to-all(f32[8,48,256]{2,1,0:T(8,128)S(1)} %bitcast.101), channel_id=1, replica_groups=mesh['ylo'=2,'x'=4,'z'=8,'yhi'=2,'c'=2] {'z'}, dimensions={0} | all-to-all | bytes 786432 | tf_op jit(solution)/shard_map/all_to_all | solution.py:395
  138.5 10.0 %all_to_all.16 = f32[8,48,256]{2,1,0:T(8,128)S(1)} all-to-all(f32[8,48,256]{2,1,0:T(8,128)S(1)} %broadcast_in_dim.20), channel_id=1, replica_groups=mesh['ylo'=2,'x'=4,'z'=8,'yhi'=2,'c'=2] {'ylo','x'}, dimensions={0} | all-to-all | bytes 786432 | tf_op jit(solution)/shard_map/all_to_all | solution.py:397
  148.5 7.4 %collective-permute-start.15 = (f32[48,1024]{1,0:T(8,128)S(1)}, f32[48,1024]{1,0:T(8,128)S(1)}, u32[]{:S(2)}, u32[]{:S(2)}) collective-permute-start(f32[48,1024]{1,0:T(8,128)S(1)} %fusion.10), channel_id=1, source_target_pairs={{0,1},{1,0},{4,5},{5,4},{8,9},{9,8},{12,13},{13,12},{16,17},{17,16... | collective-permute-start | bytes 589832 | tf_op jit(solution)/shard_map/ppermute | solution.py:30
  (59 shorter events, 10.9 us)
Async XLA Ops:
  0.0 12.9 %copy-start.1 = (bf16[1,192,1536]{2,1,0:T(8,128)(2,1)S(1)}, bf16[1,192,1536]{2,1,0:T(8,128)(2,1)}, u32[]{:S(2)}) copy-start(bf16[1,192,1536]{2,1,0:T(8,128)(2,1)} %param.4) | copy-start | bytes 1769476
  0.0 12.9 %copy-start.2 = (bf16[1,192,1536]{2,1,0:T(8,128)(2,1)S(1)}, bf16[1,192,1536]{2,1,0:T(8,128)(2,1)}, u32[]{:S(2)}) copy-start(bf16[1,192,1536]{2,1,0:T(8,128)(2,1)} %param.5) | copy-start | bytes 1769476
  0.8 4.1 %collective-permute-start = (bf16[48,256]{1,0:T(8,128)(2,1)S(1)}, bf16[48,256]{1,0:T(8,128)(2,1)S(1)}, u32[]{:S(2)}, u32[]{:S(2)}) collective-permute-start(bf16[48,256]{1,0:T(8,128)(2,1)S(1)} %constant_dynamic-slice_fusion.4), channel_id=1, source_target_pairs={{0,1},{1,0},{4,5},{5,4},{8,9},{9,8},{12,13},{13,12},{16,17},{17,16... | collective-permute-start | bytes 73736 | tf_op jit(solution)/shard_map/ppermute | solution.py:30
  6.5 21.6 %all-to-all-start = ((bf16[8,96,256]{2,1,0:T(8,128)(2,1)}), bf16[8,96,256]{2,1,0:T(8,128)(2,1)S(1)}, u32[]{:S(2)}, u32[]{:S(2)}) async-start(bf16[8,96,256]{2,1,0:T(8,128)(2,1)} %broadcast_in_dim.16), calls=%async_computation | async-start | bytes 786432 | tf_op jit(solution)/shard_map/all_to_all | solution.py:310
  13.0 22.1 %collective-permute-start.2 = (bf16[384,1536]{1,0:T(8,128)(2,1)S(1)}, bf16[384,1536]{1,0:T(8,128)(2,1)S(1)}, u32[]{:S(2)}, u32[]{:S(2)}) collective-permute-start(bf16[384,1536]{1,0:T(8,128)(2,1)S(1)} %pad_maximum_fusion.3), channel_id=1, source_target_pairs={{0,1},{1,0},{4,5},{5,4},{8,9},{9,8},{12,13},{13,12},{16,17},{17,16... | collective-permute-start | bytes 3538952 | tf_op jit(solution)/shard_map/ppermute | solution.py:30
  28.1 6.9 %collective-permute-start.1 = (bf16[768,256]{1,0:T(8,128)(2,1)S(1)}, bf16[768,256]{1,0:T(8,128)(2,1)S(1)}, u32[]{:S(2)}, u32[]{:S(2)}) collective-permute-start(bf16[768,256]{1,0:T(8,128)(2,1)S(1)} %bitcast.99), channel_id=1, source_target_pairs={{0,130},{1,33},{4,134},{5,37},{8,138},{9,41},{12,142},{13,45},{16,... | collective-permute-start | bytes 1179656 | tf_op jit(solution)/shard_map/ppermute | solution.py:30
  29.3 8.8 %copy-start.5 = (f32[2048]{0:T(1024)S(1)}, f32[2048]{0:T(1024)}, u32[]{:S(2)}) copy-start(f32[2048]{0:T(1024)} %param.7) | copy-start | bytes 24580
  35.1 3.0 %copy-start.3 = (bf16[384,1536]{1,0:T(8,128)(2,1)}, bf16[384,1536]{1,0:T(8,128)(2,1)S(1)}, u32[]{:S(2)}) copy-start(bf16[384,1536]{1,0:T(8,128)(2,1)S(1)} %collective-permute-done.2.other_hbm) | copy-start | bytes 3538948
  35.2 12.5 %collective-permute-start.3 = (bf16[1536,256]{1,0:T(8,128)(2,1)S(1)}, bf16[1536,256]{1,0:T(8,128)(2,1)S(1)}, u32[]{:S(2)}, u32[]{:S(2)}) collective-permute-start(bf16[1536,256]{1,0:T(8,128)(2,1)S(1)} %pad_maximum_fusion.4), channel_id=1, source_target_pairs={{0,32},{1,129},{4,36},{5,133},{8,40},{9,137},{12,44},{13,141},{16,... | collective-permute-start | bytes 2359304 | tf_op jit(solution)/shard_map/ppermute | solution.py:30
  36.5 11.1 %collective-permute-start.4 = (bf16[1536,256]{1,0:T(8,128)(2,1)S(1)}, bf16[1536,256]{1,0:T(8,128)(2,1)S(1)}, u32[]{:S(2)}, u32[]{:S(2)}) collective-permute-start(bf16[1536,256]{1,0:T(8,128)(2,1)S(1)} %pad_maximum_fusion.4), channel_id=1, source_target_pairs={{0,96},{1,131},{4,100},{5,135},{8,104},{9,139},{12,108},{13,143},{... | collective-permute-start | bytes 2359304 | tf_op jit(solution)/shard_map/ppermute | solution.py:30
  42.7 1.4 copy-start
  47.7 8.7 %collective-permute-start.5 = (bf16[768,256]{1,0:T(8,128)(2,1)S(1)}, bf16[768,256]{1,0:T(8,128)(2,1)S(1)}, u32[]{:S(2)}, u32[]{:S(2)}) collective-permute-start(bf16[768,256]{1,0:T(8,128)(2,1)S(1)} %slice.89), channel_id=1, source_target_pairs={{0,32},{1,129},{4,36},{5,133},{8,40},{9,137},{12,44},{13,141},{16,... | collective-permute-start | bytes 1179656 | tf_op jit(solution)/shard_map/ppermute | solution.py:30
  49.1 7.3 %collective-permute-start.6 = (bf16[768,256]{1,0:T(8,128)(2,1)S(1)}, bf16[768,256]{1,0:T(8,128)(2,1)S(1)}, u32[]{:S(2)}, u32[]{:S(2)}) collective-permute-start(bf16[768,256]{1,0:T(8,128)(2,1)S(1)} %slice.90), channel_id=1, source_target_pairs={{0,96},{1,131},{4,100},{5,135},{8,104},{9,139},{12,108},{13,143},{... | collective-permute-start | bytes 1179656 | tf_op jit(solution)/shard_map/ppermute | solution.py:30
  62.1 9.2 %collective-permute-start.7 = (f32[1536,384]{1,0:T(8,128)S(1)}, f32[1536,384]{1,0:T(8,128)S(1)}, u32[]{:S(2)}, u32[]{:S(2)}) collective-permute-start(f32[1536,384]{1,0:T(8,128)S(1)} %get-tuple-element.66.part_ref), channel_id=1, source_target_pairs={{0,1},{1,0},{4,5},{5,4},{8,9},{9,8},{12,13},{13,12},{16,17},{17,16... | collective-permute-start | bytes 7077896 | tf_op jit(solution)/shard_map/ppermute | solution.py:30
  66.7 4.7 %collective-permute-start.8 = (f32[768,128]{1,0:T(8,128)S(1)}, f32[768,128]{1,0:T(8,128)S(1)}, u32[]{:S(2)}, u32[]{:S(2)}) collective-permute-start(f32[768,128]{1,0:T(8,128)S(1)} %get-tuple-element.67.logit_ref), channel_id=1, source_target_pairs={{0,1},{1,0},{4,5},{5,4},{8,9},{9,8},{12,13},{13,12},{16,17},{17,16... | collective-permute-start | bytes 1179656 | tf_op jit(solution)/shard_map/ppermute | solution.py:30
  83.6 12.8 %collective-permute-start.9 = (f16[1552,256]{1,0:T(8,128)(2,1)S(1)}, f16[1552,256]{1,0:T(8,128)(2,1)S(1)}, u32[]{:S(2)}, u32[]{:S(2)}) collective-permute-start(f16[1552,256]{1,0:T(8,128)(2,1)S(1)} %pad_maximum_fusion.2), channel_id=1, source_target_pairs={{0,64},{1,3},{4,68},{5,7},{8,72},{9,11},{12,76},{13,15},{16,80},{1... | collective-permute-start | bytes 2383880 | tf_op jit(solution)/shard_map/ppermute | solution.py:30
  96.4 2.7 %copy-start.4 = (f16[1552,256]{1,0:T(8,128)(2,1)}, f16[1552,256]{1,0:T(8,128)(2,1)S(1)}, u32[]{:S(2)}) copy-start(f16[1552,256]{1,0:T(8,128)(2,1)S(1)} %collective-permute-done.9) | copy-start | bytes 2383876
  99.5 12.7 %collective-permute-start.10 = (f16[1552,256]{1,0:T(8,128)(2,1)S(1)}, f16[1552,256]{1,0:T(8,128)(2,1)}, u32[]{:S(2)}, u32[]{:S(2)}) collective-permute-start(f16[1552,256]{1,0:T(8,128)(2,1)S(1)} %get-tuple-element.86), channel_id=1, source_target_pairs={{0,32},{1,129},{4,36},{5,133},{8,40},{9,137},{12,44},{13,141},{16,... | collective-permute-start | bytes 2383880 | tf_op jit(solution)/shard_map/ppermute | solution.py:30
  100.0 12.3 %collective-permute-start.11 = (f16[1552,256]{1,0:T(8,128)(2,1)S(1)}, f16[1552,256]{1,0:T(8,128)(2,1)}, u32[]{:S(2)}, u32[]{:S(2)}) collective-permute-start(f16[1552,256]{1,0:T(8,128)(2,1)S(1)} %get-tuple-element.87), channel_id=1, source_target_pairs={{0,96},{1,131},{4,100},{5,135},{8,104},{9,139},{12,108},{13,143},{... | collective-permute-start | bytes 2383880 | tf_op jit(solution)/shard_map/ppermute | solution.py:30
  115.5 5.9 %collective-permute-start.12 = (f16[400,256]{1,0:T(8,128)(2,1)S(1)}, f16[400,256]{1,0:T(8,128)(2,1)S(1)}, u32[]{:S(2)}, u32[]{:S(2)}) collective-permute-start(f16[400,256]{1,0:T(8,128)(2,1)S(1)} %get-tuple-element.91), channel_id=1, source_target_pairs={{0,128},{1,33},{4,132},{5,37},{8,136},{9,41},{12,140},{13,45},{16,... | collective-permute-start | bytes 614408 | tf_op jit(solution)/shard_map/ppermute | solution.py:30
  115.9 7.3 %collective-permute-start.13 = (f16[400,256]{1,0:T(8,128)(2,1)S(1)}, f16[400,256]{1,0:T(8,128)(2,1)S(1)}, u32[]{:S(2)}, u32[]{:S(2)}) collective-permute-start(f16[400,256]{1,0:T(8,128)(2,1)S(1)} %get-tuple-element.92), channel_id=1, source_target_pairs={{0,130},{1,97},{4,134},{5,101},{8,138},{9,105},{12,142},{13,109},{... | collective-permute-start | bytes 614408 | tf_op jit(solution)/shard_map/ppermute | solution.py:30
  118.3 6.4 %collective-permute-start.14 = (f16[400,256]{1,0:T(8,128)(2,1)S(1)}, f16[400,256]{1,0:T(8,128)(2,1)S(1)}, u32[]{:S(2)}, u32[]{:S(2)}) collective-permute-start(f16[400,256]{1,0:T(8,128)(2,1)S(1)} %get-tuple-element.93), channel_id=1, source_target_pairs={{0,2},{1,65},{4,6},{5,69},{8,10},{9,73},{12,14},{13,77},{16,18},{1... | collective-permute-start | bytes 614408 | tf_op jit(solution)/shard_map/ppermute | solution.py:30
  148.5 8.4 %collective-permute-start.15 = (f32[48,1024]{1,0:T(8,128)S(1)}, f32[48,1024]{1,0:T(8,128)S(1)}, u32[]{:S(2)}, u32[]{:S(2)}) collective-permute-start(f32[48,1024]{1,0:T(8,128)S(1)} %fusion.10), channel_id=1, source_target_pairs={{0,1},{1,0},{4,5},{5,4},{8,9},{9,8},{12,13},{13,12},{16,17},{17,16... | collective-permute-start | bytes 589832 | tf_op jit(solution)/shard_map/ppermute | solution.py:30

commit v8 on v7

--- a/solution.py
+++ b/solution.py
@@ -58,8 +58,12 @@
     )
 
 
+def scaled_down(array, exponent):
+    return (array * jnp.exp2(-exponent)).astype(F16)
+
+
 def packed(piece, exponent):
-    scaled = (piece * jnp.exp2(-exponent)).astype(F16)
+    scaled = piece if piece.dtype == F16 else scaled_down(piece, exponent)
     return jnp.concatenate([scaled, jnp.broadcast_to(exponent.astype(F16), (16, piece.shape[1]))], 0)
 
 
@@ -369,9 +373,11 @@
         return (term_1,)
 
     across, term_1 = together(
-        (packed(term_2[1].reshape(d_in, 256), exponent),), (ring(2),), rest_of_term, (r1_t,)
-    )
-    beside = [packed(term_1[k].reshape(d_in, 256), exponent) for k in (1, 0)]
+        (packed(lax.optimization_barrier(scaled_down(term_2, exponent))[1].reshape(d_in, 256), exponent),),
+        (ring(2),), rest_of_term, (r1_t,),
+    )
+    halves = lax.optimization_barrier(scaled_down(term_1, exponent))
+    beside = [packed(halves[k].reshape(d_in, 256), exponent) for k in (1, 0)]
     from_left, from_right = together(beside, (ring(1), ring(-1)))
 
     def summed(own, exponent, *messages):

time: 158 us -> 160 us (1.013)
  other arithmetic: 6.36 us -> 11.8 us
  local copies, waits for them, and re-layouts: 7.92 us -> 4.05 us
    convert_element_type x3, other arithmetic: 0.65 us -> 4.97 us  [scaled_down(): return (array * jnp.exp2(-exponent)).astype(F16)]
    slice x2 -> x3, local copies, waits for them, and re-layouts: 4.55 us -> 0.67 us  [the longest x1 0.39 us: per_device(): beside = [packed(halves[k].reshape(d_in, 256), exponent) for k in (1, 0)]]
where the time goes in v8:
time: 160 us
  waiting for transfers between devices  49.7 us (31%)
  starting transfers between devices  38.1 us (24%)
  Pallas kernels  32.2 us (20%)
  blocking collectives  23.4 us (15%)
  other arithmetic  11.8 us (7%)
  local copies, waits for them, and re-layouts  4.05 us (3%)
    ppermute x16, waiting for transfers between devices, send(): return lax.ppermute(array, AXES, pairs)  35.4 us
    pallas_call x5, Pallas kernels, call(): pl.pallas_call(kernel, out_shape=[(pltpu.HBM if len(out) == 3 else pltpu....  32.2 us
    ppermute x16, starting transfers between devices, send(): return lax.ppermute(array, AXES, pairs)  31.6 us
    all_to_all x1, waiting for transfers between devices, per_device(): lax.all_to_all(jnp.broadcast_to(block[None], (NZ, *block.shape)), 'z', 0, 0)  14.3 us
    all_to_all x1, blocking collectives, per_device(): both = jnp.sum(lax.all_to_all(both, 'z', 0, 0), 0)  13.4 us
    all_to_all x1, blocking collectives, per_device(): lax.all_to_all(jnp.broadcast_to(both[None], (8, *both.shape)), ('ylo', 'x...  9.99 us
    all_to_all x1, starting transfers between devices, per_device(): lax.all_to_all(jnp.broadcast_to(block[None], (NZ, *block.shape)), 'z', 0, 0)  6.45 us
    convert_element_type x3, other arithmetic, scaled_down(): return (array * jnp.exp2(-exponent)).astype(F16)  4.97 us
  transfers between devices with their start and end apart: 17, of which 11 were waited for; matrix products, arithmetic and copies ran while one was open for 0% of the time, Pallas kernels for 11%

profile of v8, /device:TPU:1, one launch (start us, length us, event | category | flops | bytes accessed | tf_op | source)
XLA Modules:
  0.0 159.6 jit_solution(6890326692115037328)
XLA Ops:
  0.8 3.2 %collective-permute-start = (bf16[48,256]{1,0:T(8,128)(2,1)S(1)}, bf16[48,256]{1,0:T(8,128)(2,1)S(1)}, u32[]{:S(2)}, u32[]{:S(2)}) collective-permute-start(bf16[48,256]{1,0:T(8,128)(2,1)S(1)} %constant_dynamic-slice_fusion.4), channel_id=1, source_target_pairs={{0,1},{1,0},{4,5},{5,4},{8,9},{9,8},{12,13},{13,12},{16,17},{17,16... | collective-permute-start | bytes 73736 | tf_op jit(solution)/shard_map/ppermute | solution.py:30
  6.5 6.4 %all-to-all-start = ((bf16[8,96,256]{2,1,0:T(8,128)(2,1)}), bf16[8,96,256]{2,1,0:T(8,128)(2,1)S(1)}, u32[]{:S(2)}, u32[]{:S(2)}) async-start(bf16[8,96,256]{2,1,0:T(8,128)(2,1)} %broadcast_in_dim.16), calls=%async_computation | async-start | bytes 786432 | tf_op jit(solution)/shard_map/all_to_all | solution.py:314
  13.7 14.3 %all-to-all-done = bf16[8,96,256]{2,1,0:T(8,128)(2,1)S(1)} async-done(((bf16[8,96,256]{2,1,0:T(8,128)(2,1)}), bf16[8,96,256]{2,1,0:T(8,128)(2,1)S(1)}, u32[]{:S(2)}, u32[]{:S(2)}) %all-to-all-start) | async-done | bytes 393248 | tf_op jit(solution)/shard_map/all_to_all | solution.py:314
  29.3 5.7 %collective-permute-done.1 = bf16[768,256]{1,0:T(8,128)(2,1)S(1)} collective-permute-done((bf16[768,256]{1,0:T(8,128)(2,1)S(1)}, bf16[768,256]{1,0:T(8,128)(2,1)S(1)}, u32[]{:S(2)}, u32[]{:S(2)}) %collective-permute-start.1) | collective-permute-done | bytes 393248 | tf_op jit(solution)/shard_map/ppermute | solution.py:30
  35.2 1.4 collective-permute-start.3
  36.5 1.5 collective-permute-start.4
  38.1 4.6 %shard_map.46 = (bf16[768,1536]{1,0:T(8,128)(2,1)S(1)}, bf16[1536,768]{1,0:T(8,128)(2,1)}, f32[16,128]{1,0:T(8,128)S(1)}) custom-call(s32[1]{0:T(128)} %bitcast.flag_ref, bf16[192,1536]{1,0:T(8,128)(2,1)} %bitcast.89, bf16[192,1536]{1,0:T(8,128)(2,1)} %bitcast.91, bf16[384,1536]{1,0:T(8,128)(2,1)} %copy-done.4), custom_call_target="tpu_custom_call" | custom-call | flops 150994944 | bytes 8000000 | tf_op jit(solution)/shard_map/pallas_call | solution.py:285
  42.8 1.4 copy-done
  44.2 3.4 %collective-permute-done.3 = bf16[1536,256]{1,0:T(8,128)(2,1)S(1)} collective-permute-done((bf16[1536,256]{1,0:T(8,128)(2,1)S(1)}, bf16[1536,256]{1,0:T(8,128)(2,1)S(1)}, u32[]{:S(2)}, u32[]{:S(2)}) %collective-permute-start.3) | collective-permute-done | bytes 786464 | tf_op jit(solution)/shard_map/ppermute | solution.py:30
  47.7 1.4 collective-permute-start.5
  49.1 1.5 collective-permute-start.6
  50.7 5.7 %shard_map.47 = (bf16[8,192,512]{2,1,0:T(8,128)(2,1)}, f32[768,512]{1,0:T(8,128)}, f32[384,512]{1,0:T(8,128)}, bf16[384,512]{1,0:T(8,128)(2,1)}, f32[768,128]{1,0:T(8,128)S(1)}, /*index=5*/f32[1536,384]{1,0:T(8,128)S(1)}) custom-call(s32[2]{0:T(128)S(1)} %get-tuple-element.139.flag_ref, f32[1,512]{1,0:T(1,128)S(1)} %bitcast.82, bf16[768,1536]{1,0:T(8,128)(2,1)} %copy-done, ...), custom_call_target="tpu_custom_call" | custom-call | flops 1811939328 | bytes 8000000 | tf_op jit(solution)/shard_map/pallas_call | solution.py:285
  56.4 5.7 %shard_map.48 = (bf16[8,192,512]{2,1,0:T(8,128)(2,1)}, f32[768,512]{1,0:T(8,128)}, f32[384,512]{1,0:T(8,128)}, bf16[384,512]{1,0:T(8,128)(2,1)}, f32[768,128]{1,0:T(8,128)S(1)}, /*index=5*/f32[1536,384]{1,0:T(8,128)S(1)}) custom-call(s32[2]{0:T(128)S(1)} %get-tuple-element.138.flag_ref, f32[1,512]{1,0:T(1,128)S(1)} %bitcast.81, ...), custom_call_target="tpu_custom_call" | custom-call | flops 1811939328 | bytes 8000000 | tf_op jit(solution)/shard_map/pallas_call | solution.py:285
  62.1 4.5 %collective-permute-start.7 = (f32[1536,384]{1,0:T(8,128)S(1)}, f32[1536,384]{1,0:T(8,128)S(1)}, u32[]{:S(2)}, u32[]{:S(2)}) collective-permute-start(f32[1536,384]{1,0:T(8,128)S(1)} %get-tuple-element.66.part_ref), channel_id=1, source_target_pairs={{0,1},{1,0},{4,5},{5,4},{8,9},{9,8},{12,13},{13,12},{16,17},{17,16... | collective-permute-start | bytes 7077896 | tf_op jit(solution)/shard_map/ppermute | solution.py:30
  66.8 4.6 %collective-permute-done.8.logit_in_ref = f32[768,128]{1,0:T(8,128)S(1)} collective-permute-done((f32[768,128]{1,0:T(8,128)S(1)}, f32[768,128]{1,0:T(8,128)S(1)}, u32[]{:S(2)}, u32[]{:S(2)}) %collective-permute-start.8) | collective-permute-done | bytes 393248 | tf_op jit(solution)/shard_map/ppermute | solution.py:30
  71.4 9.6 %shard_map.49 = (f32[2,2,768,256]{3,2,1,0:T(8,128)}, bf16[1536,384]{1,0:T(8,128)(2,1)}, bf16[384,512]{1,0:T(8,128)(2,1)}, bf16[384,512]{1,0:T(8,128)(2,1)}, f32[16,128]{1,0:T(8,128)S(1)}) custom-call(s32[2]{0:T(128)S(1)} %get-tuple-element.138.flag_ref, f32[1536,384]{1,0:T(8,128)S(1)} %get-tuple-element.66.part_ref, ...), custom_call_target="tpu_custom_call" | custom-call | flops 3623878656 | bytes 8000000 | tf_op jit(solution)/shard_map/pallas_call | solution.py:285
  81.0 2.3 %multiply_convert_fusion.1 = f16[2,2,768,256]{3,2,1,0:T(8,128)(2,1)S(1)} fusion(f32[2,2,768,256]{3,2,1,0:T(8,128)} %get-tuple-element.78, f32[256]{0:T(256)S(1)} %get-tuple-element.136), kind=kLoop, calls=%fused_computation.1 | loop fusion | flops 1572864 | bytes 4719616 | tf_op jit(solution)/shard_map/convert_element_type | solution.py:62
  83.7 1.8 %collective-permute-start.9 = (f16[1552,256]{1,0:T(8,128)(2,1)S(1)}, f16[1552,256]{1,0:T(8,128)(2,1)S(1)}, u32[]{:S(2)}, u32[]{:S(2)}) collective-permute-start(f16[1552,256]{1,0:T(8,128)(2,1)S(1)} %pad_maximum_fusion.2), channel_id=1, source_target_pairs={{0,64},{1,3},{4,68},{5,7},{8,72},{9,11},{12,76},{13,15},{16,80},{1... | collective-permute-start | bytes 2383880 | tf_op jit(solution)/shard_map/ppermute | solution.py:30
  85.5 6.7 %shard_map.50 = f32[2,2,768,256]{3,2,1,0:T(8,128)} custom-call(s32[2]{0:T(128)S(1)} %get-tuple-element.139.flag_ref, bf16[1536,384]{1,0:T(8,128)(2,1)} %get-tuple-element.82.r1_t_hbm, bf16[384,512]{1,0:T(8,128)(2,1)} %get-tuple-element.83.fake_hbm, bf16[384,512]{1,0:T(8,128)(2,1)} %get-tuple-element.84.real_hbm, ...), custom_call_target="tpu_custom_call" | custom-call | flops 1811939328 | bytes 8000000 | tf_op jit(solution)/shard_map/pallas_call | solution.py:285
  92.1 4.4 %collective-permute-done.9 = f16[1552,256]{1,0:T(8,128)(2,1)S(1)} collective-permute-done((f16[1552,256]{1,0:T(8,128)(2,1)S(1)}, f16[1552,256]{1,0:T(8,128)(2,1)S(1)}, u32[]{:S(2)}, u32[]{:S(2)}) %collective-permute-start.9) | collective-permute-done | bytes 794656 | tf_op jit(solution)/shard_map/ppermute | solution.py:30
  96.5 2.6 %multiply_convert_fusion = f16[2,2,768,256]{3,2,1,0:T(8,128)(2,1)S(1)} fusion(f32[2,2,768,256]{3,2,1,0:T(8,128)} %shard_map.50, f32[256]{0:T(256)S(1)} %get-tuple-element.136), kind=kLoop, calls=%fused_computation | loop fusion | flops 1572864 | bytes 4719616 | tf_op jit(solution)/shard_map/convert_element_type | solution.py:62
  99.5 1.6 %pad_maximum_fusion = (f16[1552,256]{1,0:T(8,128)(2,1)}, f16[1552,256]{1,0:T(8,128)(2,1)}) fusion(f16[16,256]{1,0:T(8,128)(2,1)S(1)} %broadcast_in_dim.17, f16[1536,256]{1,0:T(8,128)(2,1)S(1)} %bitcast.87, f16[1536,256]{1,0:T(8,128)(2,1)S(1)} %bitcast.88), kind=kLoop, calls=%fused_computation.5 | loop fusion | flops 794624 | bytes 3170304 | tf_op jit(solution)/shard_map/concatenate | solution.py:67
  101.4 2.4 %collective-permute-start.11 = (f16[1552,256]{1,0:T(8,128)(2,1)}, f16[1552,256]{1,0:T(8,128)(2,1)}, u32[]{:S(2)}, u32[]{:S(2)}) collective-permute-start(f16[1552,256]{1,0:T(8,128)(2,1)} %get-tuple-element.87), channel_id=1, source_target_pairs={{0,96},{1,131},{4,100},{5,135},{8,104},{9,139},{12,108},{13,143},{... | collective-permute-start | bytes 2383880 | tf_op jit(solution)/shard_map/ppermute | solution.py:30
  103.9 10.0 %collective-permute-done.10 = f16[1552,256]{1,0:T(8,128)(2,1)} collective-permute-done((f16[1552,256]{1,0:T(8,128)(2,1)}, f16[1552,256]{1,0:T(8,128)(2,1)}, u32[]{:S(2)}, u32[]{:S(2)}) %collective-permute-start.10) | collective-permute-done | bytes 794656 | tf_op jit(solution)/shard_map/ppermute | solution.py:30
  114.6 2.1 %fusion.1 = f32[1536,256]{1,0:T(8,128)S(1)} fusion(f32[1,2,768,256]{3,2,1,0:T(8,128)S(1)} %slice.91, f32[256]{0:T(256)S(1)} %bitcast.102, f16[1552,256]{1,0:T(8,128)(2,1)S(1)} %copy-done.6, f32[256]{0:T(256)S(1)} %bitcast.101, f16[1552,256]{1,0:T(8,128)(2,1)} %collective-permute-done.11, f32[256]{0:T(256)S(1)} %bitcast.100, ...), kind=kLoop, calls=%fused_computation.4 | loop fusion | flops 3538944 | bytes 5508096 | tf_op jit(solution)/shard_map/add | solution.py:385
  117.8 2.4 %collective-permute-start.13 = (f16[400,256]{1,0:T(8,128)(2,1)S(1)}, f16[400,256]{1,0:T(8,128)(2,1)S(1)}, u32[]{:S(2)}, u32[]{:S(2)}) collective-permute-start(f16[400,256]{1,0:T(8,128)(2,1)S(1)} %get-tuple-element.92), channel_id=1, source_target_pairs={{0,130},{1,97},{4,134},{5,101},{8,138},{9,105},{12,142},{13,109},{... | collective-permute-start | bytes 614408 | tf_op jit(solution)/shard_map/ppermute | solution.py:30
  121.3 2.0 %collective-permute-done.12 = f16[400,256]{1,0:T(8,128)(2,1)S(1)} collective-permute-done((f16[400,256]{1,0:T(8,128)(2,1)S(1)}, f16[400,256]{1,0:T(8,128)(2,1)S(1)}, u32[]{:S(2)}, u32[]{:S(2)}) %collective-permute-start.12) | collective-permute-done | bytes 204832 | tf_op jit(solution)/shard_map/ppermute | solution.py:30
  123.3 1.8 %collective-permute-done.13 = f16[400,256]{1,0:T(8,128)(2,1)S(1)} collective-permute-done((f16[400,256]{1,0:T(8,128)(2,1)S(1)}, f16[400,256]{1,0:T(8,128)(2,1)S(1)}, u32[]{:S(2)}, u32[]{:S(2)}) %collective-permute-start.13) | collective-permute-done | bytes 204832 | tf_op jit(solution)/shard_map/ppermute | solution.py:30
  125.1 1.5 collective-permute-done.14
  126.8 13.4 %all_to_all.15 = f32[8,48,256]{2,1,0:T(8,128)S(1)} all-to-all(f32[8,48,256]{2,1,0:T(8,128)S(1)} %bitcast.95), channel_id=1, replica_groups=mesh['ylo'=2,'x'=4,'z'=8,'yhi'=2,'c'=2] {'z'}, dimensions={0} | all-to-all | bytes 786432 | tf_op jit(solution)/shard_map/all_to_all | solution.py:401
  140.3 10.0 %all_to_all.16 = f32[8,48,256]{2,1,0:T(8,128)S(1)} all-to-all(f32[8,48,256]{2,1,0:T(8,128)S(1)} %broadcast_in_dim.20), channel_id=1, replica_groups=mesh['ylo'=2,'x'=4,'z'=8,'yhi'=2,'c'=2] {'ylo','x'}, dimensions={0} | all-to-all | bytes 786432 | tf_op jit(solution)/shard_map/all_to_all | solution.py:403
  150.4 7.4 %collective-permute-start.15 = (f32[48,1024]{1,0:T(8,128)S(1)}, f32[48,1024]{1,0:T(8,128)S(1)}, u32[]{:S(2)}, u32[]{:S(2)}) collective-permute-start(f32[48,1024]{1,0:T(8,128)S(1)} %fusion.7), channel_id=1, source_target_pairs={{0,1},{1,0},{4,5},{5,4},{8,9},{9,8},{12,13},{13,12},{16,17},{17,16... | collective-permute-start | bytes 589832 | tf_op jit(solution)/shard_map/ppermute | solution.py:30
  (64 shorter events, 12.0 us)
Async XLA Ops:
  0.0 12.9 %copy-start.2 = (bf16[1,192,1536]{2,1,0:T(8,128)(2,1)S(1)}, bf16[1,192,1536]{2,1,0:T(8,128)(2,1)}, u32[]{:S(2)}) copy-start(bf16[1,192,1536]{2,1,0:T(8,128)(2,1)} %param.4) | copy-start | bytes 1769476
  0.0 12.9 %copy-start.3 = (bf16[1,192,1536]{2,1,0:T(8,128)(2,1)S(1)}, bf16[1,192,1536]{2,1,0:T(8,128)(2,1)}, u32[]{:S(2)}) copy-start(bf16[1,192,1536]{2,1,0:T(8,128)(2,1)} %param.5) | copy-start | bytes 1769476
  0.8 4.1 %collective-permute-start = (bf16[48,256]{1,0:T(8,128)(2,1)S(1)}, bf16[48,256]{1,0:T(8,128)(2,1)S(1)}, u32[]{:S(2)}, u32[]{:S(2)}) collective-permute-start(bf16[48,256]{1,0:T(8,128)(2,1)S(1)} %constant_dynamic-slice_fusion.4), channel_id=1, source_target_pairs={{0,1},{1,0},{4,5},{5,4},{8,9},{9,8},{12,13},{13,12},{16,17},{17,16... | collective-permute-start | bytes 73736 | tf_op jit(solution)/shard_map/ppermute | solution.py:30
  6.5 21.6 %all-to-all-start = ((bf16[8,96,256]{2,1,0:T(8,128)(2,1)}), bf16[8,96,256]{2,1,0:T(8,128)(2,1)S(1)}, u32[]{:S(2)}, u32[]{:S(2)}) async-start(bf16[8,96,256]{2,1,0:T(8,128)(2,1)} %broadcast_in_dim.16), calls=%async_computation | async-start | bytes 786432 | tf_op jit(solution)/shard_map/all_to_all | solution.py:314
  13.0 22.1 %collective-permute-start.2 = (bf16[384,1536]{1,0:T(8,128)(2,1)S(1)}, bf16[384,1536]{1,0:T(8,128)(2,1)S(1)}, u32[]{:S(2)}, u32[]{:S(2)}) collective-permute-start(bf16[384,1536]{1,0:T(8,128)(2,1)S(1)} %pad_maximum_fusion.3), channel_id=1, source_target_pairs={{0,1},{1,0},{4,5},{5,4},{8,9},{9,8},{12,13},{13,12},{16,17},{17,16... | collective-permute-start | bytes 3538952 | tf_op jit(solution)/shard_map/ppermute | solution.py:30
  28.1 6.9 %collective-permute-start.1 = (bf16[768,256]{1,0:T(8,128)(2,1)S(1)}, bf16[768,256]{1,0:T(8,128)(2,1)S(1)}, u32[]{:S(2)}, u32[]{:S(2)}) collective-permute-start(bf16[768,256]{1,0:T(8,128)(2,1)S(1)} %bitcast.93), channel_id=1, source_target_pairs={{0,130},{1,33},{4,134},{5,37},{8,138},{9,41},{12,142},{13,45},{16,... | collective-permute-start | bytes 1179656 | tf_op jit(solution)/shard_map/ppermute | solution.py:30
  29.3 8.8 %copy-start.7 = (f32[2048]{0:T(1024)S(1)}, f32[2048]{0:T(1024)}, u32[]{:S(2)}) copy-start(f32[2048]{0:T(1024)} %param.7) | copy-start | bytes 24580
  35.1 3.0 %copy-start.4 = (bf16[384,1536]{1,0:T(8,128)(2,1)}, bf16[384,1536]{1,0:T(8,128)(2,1)S(1)}, u32[]{:S(2)}) copy-start(bf16[384,1536]{1,0:T(8,128)(2,1)S(1)} %collective-permute-done.2.other_hbm) | copy-start | bytes 3538948
  35.2 12.5 %collective-permute-start.3 = (bf16[1536,256]{1,0:T(8,128)(2,1)S(1)}, bf16[1536,256]{1,0:T(8,128)(2,1)S(1)}, u32[]{:S(2)}, u32[]{:S(2)}) collective-permute-start(bf16[1536,256]{1,0:T(8,128)(2,1)S(1)} %pad_maximum_fusion.4), channel_id=1, source_target_pairs={{0,32},{1,129},{4,36},{5,133},{8,40},{9,137},{12,44},{13,141},{16,... | collective-permute-start | bytes 2359304 | tf_op jit(solution)/shard_map/ppermute | solution.py:30
  36.5 11.1 %collective-permute-start.4 = (bf16[1536,256]{1,0:T(8,128)(2,1)S(1)}, bf16[1536,256]{1,0:T(8,128)(2,1)S(1)}, u32[]{:S(2)}, u32[]{:S(2)}) collective-permute-start(bf16[1536,256]{1,0:T(8,128)(2,1)S(1)} %pad_maximum_fusion.4), channel_id=1, source_target_pairs={{0,96},{1,131},{4,100},{5,135},{8,104},{9,139},{12,108},{13,143},{... | collective-permute-start | bytes 2359304 | tf_op jit(solution)/shard_map/ppermute | solution.py:30
  42.8 1.4 copy-start
  47.7 8.7 %collective-permute-start.5 = (bf16[768,256]{1,0:T(8,128)(2,1)S(1)}, bf16[768,256]{1,0:T(8,128)(2,1)S(1)}, u32[]{:S(2)}, u32[]{:S(2)}) collective-permute-start(bf16[768,256]{1,0:T(8,128)(2,1)S(1)} %slice.89), channel_id=1, source_target_pairs={{0,32},{1,129},{4,36},{5,133},{8,40},{9,137},{12,44},{13,141},{16,... | collective-permute-start | bytes 1179656 | tf_op jit(solution)/shard_map/ppermute | solution.py:30
  49.1 7.3 %collective-permute-start.6 = (bf16[768,256]{1,0:T(8,128)(2,1)S(1)}, bf16[768,256]{1,0:T(8,128)(2,1)S(1)}, u32[]{:S(2)}, u32[]{:S(2)}) collective-permute-start(bf16[768,256]{1,0:T(8,128)(2,1)S(1)} %slice.90), channel_id=1, source_target_pairs={{0,96},{1,131},{4,100},{5,135},{8,104},{9,139},{12,108},{13,143},{... | collective-permute-start | bytes 1179656 | tf_op jit(solution)/shard_map/ppermute | solution.py:30
  62.1 9.2 %collective-permute-start.7 = (f32[1536,384]{1,0:T(8,128)S(1)}, f32[1536,384]{1,0:T(8,128)S(1)}, u32[]{:S(2)}, u32[]{:S(2)}) collective-permute-start(f32[1536,384]{1,0:T(8,128)S(1)} %get-tuple-element.66.part_ref), channel_id=1, source_target_pairs={{0,1},{1,0},{4,5},{5,4},{8,9},{9,8},{12,13},{13,12},{16,17},{17,16... | collective-permute-start | bytes 7077896 | tf_op jit(solution)/shard_map/ppermute | solution.py:30
  66.7 4.7 %collective-permute-start.8 = (f32[768,128]{1,0:T(8,128)S(1)}, f32[768,128]{1,0:T(8,128)S(1)}, u32[]{:S(2)}, u32[]{:S(2)}) collective-permute-start(f32[768,128]{1,0:T(8,128)S(1)} %get-tuple-element.67.logit_ref), channel_id=1, source_target_pairs={{0,1},{1,0},{4,5},{5,4},{8,9},{9,8},{12,13},{13,12},{16,17},{17,16... | collective-permute-start | bytes 1179656 | tf_op jit(solution)/shard_map/ppermute | solution.py:30
  83.7 12.8 %collective-permute-start.9 = (f16[1552,256]{1,0:T(8,128)(2,1)S(1)}, f16[1552,256]{1,0:T(8,128)(2,1)S(1)}, u32[]{:S(2)}, u32[]{:S(2)}) collective-permute-start(f16[1552,256]{1,0:T(8,128)(2,1)S(1)} %pad_maximum_fusion.2), channel_id=1, source_target_pairs={{0,64},{1,3},{4,68},{5,7},{8,72},{9,11},{12,76},{13,15},{16,80},{1... | collective-permute-start | bytes 2383880 | tf_op jit(solution)/shard_map/ppermute | solution.py:30
  96.5 2.6 %copy-start.5 = (f16[1552,256]{1,0:T(8,128)(2,1)}, f16[1552,256]{1,0:T(8,128)(2,1)S(1)}, u32[]{:S(2)}) copy-start(f16[1552,256]{1,0:T(8,128)(2,1)S(1)} %collective-permute-done.9) | copy-start | bytes 2383876
  99.5 4.4 %copy-start.1 = (f32[2,2,768,256]{3,2,1,0:T(8,128)S(1)}, f32[2,2,768,256]{3,2,1,0:T(8,128)}, u32[]{:S(2)}) copy-start(f32[2,2,768,256]{3,2,1,0:T(8,128)} %get-tuple-element.78) | copy-start | bytes 9437188
  101.1 12.8 %collective-permute-start.10 = (f16[1552,256]{1,0:T(8,128)(2,1)}, f16[1552,256]{1,0:T(8,128)(2,1)}, u32[]{:S(2)}, u32[]{:S(2)}) collective-permute-start(f16[1552,256]{1,0:T(8,128)(2,1)} %get-tuple-element.86), channel_id=1, source_target_pairs={{0,32},{1,129},{4,36},{5,133},{8,40},{9,137},{12,44},{13,141},{16,... | collective-permute-start | bytes 2383880 | tf_op jit(solution)/shard_map/ppermute | solution.py:30
  101.4 12.5 %collective-permute-start.11 = (f16[1552,256]{1,0:T(8,128)(2,1)}, f16[1552,256]{1,0:T(8,128)(2,1)}, u32[]{:S(2)}, u32[]{:S(2)}) collective-permute-start(f16[1552,256]{1,0:T(8,128)(2,1)} %get-tuple-element.87), channel_id=1, source_target_pairs={{0,96},{1,131},{4,100},{5,135},{8,104},{9,139},{12,108},{13,143},{... | collective-permute-start | bytes 2383880 | tf_op jit(solution)/shard_map/ppermute | solution.py:30
  103.8 10.1 %copy-start.6 = (f16[1552,256]{1,0:T(8,128)(2,1)S(1)}, f16[1552,256]{1,0:T(8,128)(2,1)}, u32[]{:S(2)}) copy-start(f16[1552,256]{1,0:T(8,128)(2,1)} %copy-done.5) | copy-start | bytes 2383876
  117.1 6.1 %collective-permute-start.12 = (f16[400,256]{1,0:T(8,128)(2,1)S(1)}, f16[400,256]{1,0:T(8,128)(2,1)S(1)}, u32[]{:S(2)}, u32[]{:S(2)}) collective-permute-start(f16[400,256]{1,0:T(8,128)(2,1)S(1)} %get-tuple-element.91), channel_id=1, source_target_pairs={{0,128},{1,33},{4,132},{5,37},{8,136},{9,41},{12,140},{13,45},{16,... | collective-permute-start | bytes 614408 | tf_op jit(solution)/shard_map/ppermute | solution.py:30
  117.8 7.3 %collective-permute-start.13 = (f16[400,256]{1,0:T(8,128)(2,1)S(1)}, f16[400,256]{1,0:T(8,128)(2,1)S(1)}, u32[]{:S(2)}, u32[]{:S(2)}) collective-permute-start(f16[400,256]{1,0:T(8,128)(2,1)S(1)} %get-tuple-element.92), channel_id=1, source_target_pairs={{0,130},{1,97},{4,134},{5,101},{8,138},{9,105},{12,142},{13,109},{... | collective-permute-start | bytes 614408 | tf_op jit(solution)/shard_map/ppermute | solution.py:30
  120.2 6.4 %collective-permute-start.14 = (f16[400,256]{1,0:T(8,128)(2,1)S(1)}, f16[400,256]{1,0:T(8,128)(2,1)S(1)}, u32[]{:S(2)}, u32[]{:S(2)}) collective-permute-start(f16[400,256]{1,0:T(8,128)(2,1)S(1)} %get-tuple-element.93), channel_id=1, source_target_pairs={{0,2},{1,65},{4,6},{5,69},{8,10},{9,73},{12,14},{13,77},{16,18},{1... | collective-permute-start | bytes 614408 | tf_op jit(solution)/shard_map/ppermute | solution.py:30
  150.4 8.4 %collective-permute-start.15 = (f32[48,1024]{1,0:T(8,128)S(1)}, f32[48,1024]{1,0:T(8,128)S(1)}, u32[]{:S(2)}, u32[]{:S(2)}) collective-permute-start(f32[48,1024]{1,0:T(8,128)S(1)} %fusion.7), channel_id=1, source_target_pairs={{0,1},{1,0},{4,5},{5,4},{8,9},{9,8},{12,13},{13,12},{16,17},{17,16... | collective-permute-start | bytes 589832 | tf_op jit(solution)/shard_map/ppermute | solution.py:30

commit v9 on v7

--- a/solution.py
+++ b/solution.py
@@ -366,13 +366,15 @@
             fourth_kernel, 6 * n * d_in * wide, marked([terms]), [terms, r1_shape, *works, states[3], tall],
             flags=flags_1, there=(r1_t, fake_1, real_1, lifted_1, tokens_t), sems=[5, 16], vmem_mib=28,
         )
+        raw.append(term_1)
         return (term_1,)
 
-    across, term_1 = together(
+    raw = []
+    across, _ = together(
         (packed(term_2[1].reshape(d_in, 256), exponent),), (ring(2),), rest_of_term, (r1_t,)
     )
-    beside = [packed(term_1[k].reshape(d_in, 256), exponent) for k in (1, 0)]
-    from_left, from_right = together(beside, (ring(1), ring(-1)))
+    beside = [packed(raw[0][k].reshape(d_in, 256), exponent) for k in (1, 0)]
+    from_left, from_right, across = together(beside, (ring(1), ring(-1)), lambda a: (a,), (across,))
 
     def summed(own, exponent, *messages):
         for values, theirs in map(unpacked, messages):

time: 158 us -> 155 us (0.981)
  waiting for transfers between devices: 49.6 us -> 46.9 us
    ppermute x16, waiting for transfers between devices: 35.3 us -> 32.6 us  [send(): return lax.ppermute(array, AXES, pairs)]
  transfers between devices with their start and end apart: 17 -> 17, of which waited for: 11 -> 11; matrix products, arithmetic and copies ran while one was open for 0% -> 2% of each run, Pallas kernels for 11% -> 11%
where the time goes in v9:
time: 155 us; the launch traced here: 154 us
  waiting for transfers between devices  46.9 us (30%)
  starting transfers between devices  37.9 us (24%)
  Pallas kernels  32.1 us (21%)
  blocking collectives  23.4 us (15%)
  local copies, waits for them, and re-layouts  7.55 us (5%)
  other arithmetic  6.34 us (4%)
    ppermute x16, waiting for transfers between devices, send(): return lax.ppermute(array, AXES, pairs)  32.6 us
    pallas_call x5, Pallas kernels, call(): pl.pallas_call(kernel, out_shape=[(pltpu.HBM if len(out) == 3 else pltpu....  32.1 us
    ppermute x16, starting transfers between devices, send(): return lax.ppermute(array, AXES, pairs)  31.4 us
    all_to_all x1, waiting for transfers between devices, per_device(): lax.all_to_all(jnp.broadcast_to(block[None], (NZ, *block.shape)), 'z', 0, 0)  14.3 us
    all_to_all x1, blocking collectives, per_device(): both = jnp.sum(lax.all_to_all(both, 'z', 0, 0), 0)  13.4 us
    all_to_all x1, blocking collectives, per_device(): lax.all_to_all(jnp.broadcast_to(both[None], (8, *both.shape)), ('ylo', 'x...  9.99 us
    all_to_all x1, starting transfers between devices, per_device(): lax.all_to_all(jnp.broadcast_to(block[None], (NZ, *block.shape)), 'z', 0, 0)  6.45 us
  transfers between devices with their start and end apart: 17, of which 11 were waited for; matrix products, arithmetic and copies ran while one was open for 2% of the time, Pallas kernels for 11%

profile of v9, /device:TPU:1, one launch (start us, length us, event | category | flops | bytes accessed | tf_op | source)
XLA Modules:
  0.0 154.5 jit_solution(14971935048104410755)
XLA Ops:
  0.8 3.2 %collective-permute-start = (bf16[48,256]{1,0:T(8,128)(2,1)S(1)}, bf16[48,256]{1,0:T(8,128)(2,1)S(1)}, u32[]{:S(2)}, u32[]{:S(2)}) collective-permute-start(bf16[48,256]{1,0:T(8,128)(2,1)S(1)} %constant_dynamic-slice_fusion.4), channel_id=1, source_target_pairs={{0,1},{1,0},{4,5},{5,4},{8,9},{9,8},{12,13},{13,12},{16,17},{17,16... | collective-permute-start | bytes 73736 | tf_op jit(solution)/shard_map/ppermute | solution.py:30
  6.5 6.4 %all-to-all-start = ((bf16[8,96,256]{2,1,0:T(8,128)(2,1)}), bf16[8,96,256]{2,1,0:T(8,128)(2,1)S(1)}, u32[]{:S(2)}, u32[]{:S(2)}) async-start(bf16[8,96,256]{2,1,0:T(8,128)(2,1)} %broadcast_in_dim.16), calls=%async_computation | async-start | bytes 786432 | tf_op jit(solution)/shard_map/all_to_all | solution.py:310
  13.7 14.3 %all-to-all-done = bf16[8,96,256]{2,1,0:T(8,128)(2,1)S(1)} async-done(((bf16[8,96,256]{2,1,0:T(8,128)(2,1)}), bf16[8,96,256]{2,1,0:T(8,128)(2,1)S(1)}, u32[]{:S(2)}, u32[]{:S(2)}) %all-to-all-start) | async-done | bytes 393248 | tf_op jit(solution)/shard_map/all_to_all | solution.py:310
  28.1 1.2 collective-permute-start.1
  29.3 5.7 %collective-permute-done.1 = bf16[768,256]{1,0:T(8,128)(2,1)S(1)} collective-permute-done((bf16[768,256]{1,0:T(8,128)(2,1)S(1)}, bf16[768,256]{1,0:T(8,128)(2,1)S(1)}, u32[]{:S(2)}, u32[]{:S(2)}) %collective-permute-start.1) | collective-permute-done | bytes 393248 | tf_op jit(solution)/shard_map/ppermute | solution.py:30
  35.2 1.4 collective-permute-start.3
  36.5 1.5 collective-permute-start.4
  38.1 4.6 %shard_map.46 = (bf16[768,1536]{1,0:T(8,128)(2,1)S(1)}, bf16[1536,768]{1,0:T(8,128)(2,1)}, f32[16,128]{1,0:T(8,128)S(1)}) custom-call(s32[1]{0:T(128)} %bitcast.flag_ref, bf16[192,1536]{1,0:T(8,128)(2,1)} %bitcast.95, bf16[192,1536]{1,0:T(8,128)(2,1)} %bitcast.97, bf16[384,1536]{1,0:T(8,128)(2,1)} %copy-done.3), custom_call_target="tpu_custom_call" | custom-call | flops 150994944 | bytes 8000000 | tf_op jit(solution)/shard_map/pallas_call | solution.py:281
  42.7 1.4 copy-done
  44.2 3.5 %collective-permute-done.3 = bf16[1536,256]{1,0:T(8,128)(2,1)S(1)} collective-permute-done((bf16[1536,256]{1,0:T(8,128)(2,1)S(1)}, bf16[1536,256]{1,0:T(8,128)(2,1)S(1)}, u32[]{:S(2)}, u32[]{:S(2)}) %collective-permute-start.3) | collective-permute-done | bytes 786464 | tf_op jit(solution)/shard_map/ppermute | solution.py:30
  47.7 1.4 collective-permute-start.5
  49.1 1.5 collective-permute-start.6
  50.7 5.7 %shard_map.47 = (bf16[8,192,512]{2,1,0:T(8,128)(2,1)}, f32[768,512]{1,0:T(8,128)}, f32[384,512]{1,0:T(8,128)}, bf16[384,512]{1,0:T(8,128)(2,1)}, f32[768,128]{1,0:T(8,128)S(1)}, /*index=5*/f32[1536,384]{1,0:T(8,128)S(1)}) custom-call(s32[2]{0:T(128)S(1)} %get-tuple-element.145.flag_ref, f32[1,512]{1,0:T(1,128)S(1)} %bitcast.91, bf16[768,1536]{1,0:T(8,128)(2,1)} %copy-done, ...), custom_call_target="tpu_custom_call" | custom-call | flops 1811939328 | bytes 8000000 | tf_op jit(solution)/shard_map/pallas_call | solution.py:281
  56.4 5.7 %shard_map.48 = (bf16[8,192,512]{2,1,0:T(8,128)(2,1)}, f32[768,512]{1,0:T(8,128)}, f32[384,512]{1,0:T(8,128)}, bf16[384,512]{1,0:T(8,128)(2,1)}, f32[768,128]{1,0:T(8,128)S(1)}, /*index=5*/f32[1536,384]{1,0:T(8,128)S(1)}) custom-call(s32[2]{0:T(128)S(1)} %get-tuple-element.144.flag_ref, f32[1,512]{1,0:T(1,128)S(1)} %bitcast.90, ...), custom_call_target="tpu_custom_call" | custom-call | flops 1811939328 | bytes 8000000 | tf_op jit(solution)/shard_map/pallas_call | solution.py:281
  62.2 4.5 %collective-permute-start.7 = (f32[1536,384]{1,0:T(8,128)S(1)}, f32[1536,384]{1,0:T(8,128)S(1)}, u32[]{:S(2)}, u32[]{:S(2)}) collective-permute-start(f32[1536,384]{1,0:T(8,128)S(1)} %get-tuple-element.67.part_ref), channel_id=1, source_target_pairs={{0,1},{1,0},{4,5},{5,4},{8,9},{9,8},{12,13},{13,12},{16,17},{17,16... | collective-permute-start | bytes 7077896 | tf_op jit(solution)/shard_map/ppermute | solution.py:30
  66.8 4.6 %collective-permute-done.8.logit_in_ref = f32[768,128]{1,0:T(8,128)S(1)} collective-permute-done((f32[768,128]{1,0:T(8,128)S(1)}, f32[768,128]{1,0:T(8,128)S(1)}, u32[]{:S(2)}, u32[]{:S(2)}) %collective-permute-start.8) | collective-permute-done | bytes 393248 | tf_op jit(solution)/shard_map/ppermute | solution.py:30
  71.4 9.5 %shard_map.49 = (f32[2,2,768,256]{3,2,1,0:T(8,128)}, bf16[1536,384]{1,0:T(8,128)(2,1)}, bf16[384,512]{1,0:T(8,128)(2,1)}, bf16[384,512]{1,0:T(8,128)(2,1)}, f32[16,128]{1,0:T(8,128)S(1)}) custom-call(s32[2]{0:T(128)S(1)} %get-tuple-element.144.flag_ref, f32[1536,384]{1,0:T(8,128)S(1)} %get-tuple-element.67.part_ref, ...), custom_call_target="tpu_custom_call" | custom-call | flops 3623878656 | bytes 8000000 | tf_op jit(solution)/shard_map/pallas_call | solution.py:281
  80.9 2.1 %fusion.18 = (f32[1,2,768,256]{3,2,1,0:T(8,128)S(1)}, f32[1,2,768,256]{3,2,1,0:T(8,128)S(1)}) fusion(f32[2,2,768,256]{3,2,1,0:T(8,128)} %get-tuple-element.79), kind=kLoop, calls=%fused_computation.72 | loop fusion | bytes 6291456 | tf_op jit(solution)/shard_map/slice | solution.py:374
  83.4 1.8 %collective-permute-start.9 = (f16[1552,256]{1,0:T(8,128)(2,1)S(1)}, f16[1552,256]{1,0:T(8,128)(2,1)}, u32[]{:S(2)}, u32[]{:S(2)}) collective-permute-start(f16[1552,256]{1,0:T(8,128)(2,1)S(1)} %pad_maximum_fusion.2), channel_id=1, source_target_pairs={{0,64},{1,3},{4,68},{5,7},{8,72},{9,11},{12,76},{13,15},{16,80},{1... | collective-permute-start | bytes 2383880 | tf_op jit(solution)/shard_map/ppermute | solution.py:30
  85.2 6.6 %shard_map.50 = f32[2,2,768,256]{3,2,1,0:T(8,128)} custom-call(s32[2]{0:T(128)S(1)} %get-tuple-element.145.flag_ref, bf16[1536,384]{1,0:T(8,128)(2,1)} %get-tuple-element.82.r1_t_hbm, bf16[384,512]{1,0:T(8,128)(2,1)} %get-tuple-element.83.fake_hbm, bf16[384,512]{1,0:T(8,128)(2,1)} %get-tuple-element.84.real_hbm, ...), custom_call_target="tpu_custom_call" | custom-call | flops 1811939328 | bytes 8000000 | tf_op jit(solution)/shard_map/pallas_call | solution.py:281
  91.8 2.1 %fusion.17 = (f32[1,2,768,256]{3,2,1,0:T(8,128)S(1)}, f32[1,2,768,256]{3,2,1,0:T(8,128)S(1)}) fusion(f32[2,2,768,256]{3,2,1,0:T(8,128)} %shard_map.50), kind=kLoop, calls=%fused_computation.71 | loop fusion | bytes 6291456 | tf_op jit(solution)/shard_map/slice | solution.py:376
  94.7 1.6 %collective-permute-done.9 = f16[1552,256]{1,0:T(8,128)(2,1)} collective-permute-done((f16[1552,256]{1,0:T(8,128)(2,1)S(1)}, f16[1552,256]{1,0:T(8,128)(2,1)}, u32[]{:S(2)}, u32[]{:S(2)}) %collective-permute-start.9) | collective-permute-done | bytes 794656 | tf_op jit(solution)/shard_map/ppermute | solution.py:30
  96.7 2.4 %collective-permute-start.11 = (f16[1552,256]{1,0:T(8,128)(2,1)S(1)}, f16[1552,256]{1,0:T(8,128)(2,1)}, u32[]{:S(2)}, u32[]{:S(2)}) collective-permute-start(f16[1552,256]{1,0:T(8,128)(2,1)S(1)} %get-tuple-element.88), channel_id=1, source_target_pairs={{0,96},{1,131},{4,100},{5,135},{8,104},{9,139},{12,108},{13,143},{... | collective-permute-start | bytes 2383880 | tf_op jit(solution)/shard_map/ppermute | solution.py:30
  99.1 9.9 %collective-permute-done.10 = f16[1552,256]{1,0:T(8,128)(2,1)} collective-permute-done((f16[1552,256]{1,0:T(8,128)(2,1)S(1)}, f16[1552,256]{1,0:T(8,128)(2,1)}, u32[]{:S(2)}, u32[]{:S(2)}) %collective-permute-start.10) | collective-permute-done | bytes 794656 | tf_op jit(solution)/shard_map/ppermute | solution.py:30
  109.7 2.1 %fusion.4 = f32[1536,256]{1,0:T(8,128)S(1)} fusion(f32[1,2,768,256]{3,2,1,0:T(8,128)S(1)} %get-tuple-element.104, f32[256]{0:T(256)S(1)} %bitcast.108, f16[1552,256]{1,0:T(8,128)(2,1)} %collective-permute-done.9, f32[256]{0:T(256)S(1)} %bitcast.107, f16[1552,256]{1,0:T(8,128)(2,1)} %collective-permute-done.11, f32[256]{0:T(256)S(1)} %bitcast.106, ...), kind=kLoop, calls=%fused_computation.8 | loop fusion | flops 3538944 | bytes 5508096 | tf_op jit(solution)/shard_map/add | solution.py:381
  112.6 2.4 %collective-permute-start.13 = (f16[400,256]{1,0:T(8,128)(2,1)S(1)}, f16[400,256]{1,0:T(8,128)(2,1)S(1)}, u32[]{:S(2)}, u32[]{:S(2)}) collective-permute-start(f16[400,256]{1,0:T(8,128)(2,1)S(1)} %get-tuple-element.94), channel_id=1, source_target_pairs={{0,130},{1,97},{4,134},{5,101},{8,138},{9,105},{12,142},{13,109},{... | collective-permute-start | bytes 614408 | tf_op jit(solution)/shard_map/ppermute | solution.py:30
  116.2 2.0 %collective-permute-done.12 = f16[400,256]{1,0:T(8,128)(2,1)S(1)} collective-permute-done((f16[400,256]{1,0:T(8,128)(2,1)S(1)}, f16[400,256]{1,0:T(8,128)(2,1)S(1)}, u32[]{:S(2)}, u32[]{:S(2)}) %collective-permute-start.12) | collective-permute-done | bytes 204832 | tf_op jit(solution)/shard_map/ppermute | solution.py:30
  118.1 1.8 %collective-permute-done.13 = f16[400,256]{1,0:T(8,128)(2,1)S(1)} collective-permute-done((f16[400,256]{1,0:T(8,128)(2,1)S(1)}, f16[400,256]{1,0:T(8,128)(2,1)S(1)}, u32[]{:S(2)}, u32[]{:S(2)}) %collective-permute-start.13) | collective-permute-done | bytes 204832 | tf_op jit(solution)/shard_map/ppermute | solution.py:30
  120.0 1.5 collective-permute-done.14
  121.7 13.4 %all_to_all.15 = f32[8,48,256]{2,1,0:T(8,128)S(1)} all-to-all(f32[8,48,256]{2,1,0:T(8,128)S(1)} %bitcast.101), channel_id=1, replica_groups=mesh['ylo'=2,'x'=4,'z'=8,'yhi'=2,'c'=2] {'z'}, dimensions={0} | all-to-all | bytes 786432 | tf_op jit(solution)/shard_map/all_to_all | solution.py:397
  135.2 10.0 %all_to_all.16 = f32[8,48,256]{2,1,0:T(8,128)S(1)} all-to-all(f32[8,48,256]{2,1,0:T(8,128)S(1)} %broadcast_in_dim.20), channel_id=1, replica_groups=mesh['ylo'=2,'x'=4,'z'=8,'yhi'=2,'c'=2] {'ylo','x'}, dimensions={0} | all-to-all | bytes 786432 | tf_op jit(solution)/shard_map/all_to_all | solution.py:399
  145.2 7.4 %collective-permute-start.15 = (f32[48,1024]{1,0:T(8,128)S(1)}, f32[48,1024]{1,0:T(8,128)S(1)}, u32[]{:S(2)}, u32[]{:S(2)}) collective-permute-start(f32[48,1024]{1,0:T(8,128)S(1)} %fusion.10), channel_id=1, source_target_pairs={{0,1},{1,0},{4,5},{5,4},{8,9},{9,8},{12,13},{13,12},{16,17},{17,16... | collective-permute-start | bytes 589832 | tf_op jit(solution)/shard_map/ppermute | solution.py:30
  (57 shorter events, 10.8 us)
Async XLA Ops:
  0.0 12.9 %copy-start.1 = (bf16[1,192,1536]{2,1,0:T(8,128)(2,1)S(1)}, bf16[1,192,1536]{2,1,0:T(8,128)(2,1)}, u32[]{:S(2)}) copy-start(bf16[1,192,1536]{2,1,0:T(8,128)(2,1)} %param.4) | copy-start | bytes 1769476
  0.0 12.9 %copy-start.2 = (bf16[1,192,1536]{2,1,0:T(8,128)(2,1)S(1)}, bf16[1,192,1536]{2,1,0:T(8,128)(2,1)}, u32[]{:S(2)}) copy-start(bf16[1,192,1536]{2,1,0:T(8,128)(2,1)} %param.5) | copy-start | bytes 1769476
  0.8 4.1 %collective-permute-start = (bf16[48,256]{1,0:T(8,128)(2,1)S(1)}, bf16[48,256]{1,0:T(8,128)(2,1)S(1)}, u32[]{:S(2)}, u32[]{:S(2)}) collective-permute-start(bf16[48,256]{1,0:T(8,128)(2,1)S(1)} %constant_dynamic-slice_fusion.4), channel_id=1, source_target_pairs={{0,1},{1,0},{4,5},{5,4},{8,9},{9,8},{12,13},{13,12},{16,17},{17,16... | collective-permute-start | bytes 73736 | tf_op jit(solution)/shard_map/ppermute | solution.py:30
  6.5 21.6 %all-to-all-start = ((bf16[8,96,256]{2,1,0:T(8,128)(2,1)}), bf16[8,96,256]{2,1,0:T(8,128)(2,1)S(1)}, u32[]{:S(2)}, u32[]{:S(2)}) async-start(bf16[8,96,256]{2,1,0:T(8,128)(2,1)} %broadcast_in_dim.16), calls=%async_computation | async-start | bytes 786432 | tf_op jit(solution)/shard_map/all_to_all | solution.py:310
  13.0 22.1 %collective-permute-start.2 = (bf16[384,1536]{1,0:T(8,128)(2,1)S(1)}, bf16[384,1536]{1,0:T(8,128)(2,1)S(1)}, u32[]{:S(2)}, u32[]{:S(2)}) collective-permute-start(bf16[384,1536]{1,0:T(8,128)(2,1)S(1)} %pad_maximum_fusion.3), channel_id=1, source_target_pairs={{0,1},{1,0},{4,5},{5,4},{8,9},{9,8},{12,13},{13,12},{16,17},{17,16... | collective-permute-start | bytes 3538952 | tf_op jit(solution)/shard_map/ppermute | solution.py:30
  28.1 6.9 %collective-permute-start.1 = (bf16[768,256]{1,0:T(8,128)(2,1)S(1)}, bf16[768,256]{1,0:T(8,128)(2,1)S(1)}, u32[]{:S(2)}, u32[]{:S(2)}) collective-permute-start(bf16[768,256]{1,0:T(8,128)(2,1)S(1)} %bitcast.99), channel_id=1, source_target_pairs={{0,130},{1,33},{4,134},{5,37},{8,138},{9,41},{12,142},{13,45},{16,... | collective-permute-start | bytes 1179656 | tf_op jit(solution)/shard_map/ppermute | solution.py:30
  29.3 8.8 %copy-start.4 = (f32[2048]{0:T(1024)S(1)}, f32[2048]{0:T(1024)}, u32[]{:S(2)}) copy-start(f32[2048]{0:T(1024)} %param.7) | copy-start | bytes 24580
  35.1 3.0 %copy-start.3 = (bf16[384,1536]{1,0:T(8,128)(2,1)}, bf16[384,1536]{1,0:T(8,128)(2,1)S(1)}, u32[]{:S(2)}) copy-start(bf16[384,1536]{1,0:T(8,128)(2,1)S(1)} %collective-permute-done.2.other_hbm) | copy-start | bytes 3538948
  35.2 12.5 %collective-permute-start.3 = (bf16[1536,256]{1,0:T(8,128)(2,1)S(1)}, bf16[1536,256]{1,0:T(8,128)(2,1)S(1)}, u32[]{:S(2)}, u32[]{:S(2)}) collective-permute-start(bf16[1536,256]{1,0:T(8,128)(2,1)S(1)} %pad_maximum_fusion.4), channel_id=1, source_target_pairs={{0,32},{1,129},{4,36},{5,133},{8,40},{9,137},{12,44},{13,141},{16,... | collective-permute-start | bytes 2359304 | tf_op jit(solution)/shard_map/ppermute | solution.py:30
  36.5 11.1 %collective-permute-start.4 = (bf16[1536,256]{1,0:T(8,128)(2,1)S(1)}, bf16[1536,256]{1,0:T(8,128)(2,1)S(1)}, u32[]{:S(2)}, u32[]{:S(2)}) collective-permute-start(bf16[1536,256]{1,0:T(8,128)(2,1)S(1)} %pad_maximum_fusion.4), channel_id=1, source_target_pairs={{0,96},{1,131},{4,100},{5,135},{8,104},{9,139},{12,108},{13,143},{... | collective-permute-start | bytes 2359304 | tf_op jit(solution)/shard_map/ppermute | solution.py:30
  42.7 1.4 copy-start
  47.7 8.7 %collective-permute-start.5 = (bf16[768,256]{1,0:T(8,128)(2,1)S(1)}, bf16[768,256]{1,0:T(8,128)(2,1)S(1)}, u32[]{:S(2)}, u32[]{:S(2)}) collective-permute-start(bf16[768,256]{1,0:T(8,128)(2,1)S(1)} %slice.89), channel_id=1, source_target_pairs={{0,32},{1,129},{4,36},{5,133},{8,40},{9,137},{12,44},{13,141},{16,... | collective-permute-start | bytes 1179656 | tf_op jit(solution)/shard_map/ppermute | solution.py:30
  49.1 7.3 %collective-permute-start.6 = (bf16[768,256]{1,0:T(8,128)(2,1)S(1)}, bf16[768,256]{1,0:T(8,128)(2,1)S(1)}, u32[]{:S(2)}, u32[]{:S(2)}) collective-permute-start(bf16[768,256]{1,0:T(8,128)(2,1)S(1)} %slice.90), channel_id=1, source_target_pairs={{0,96},{1,131},{4,100},{5,135},{8,104},{9,139},{12,108},{13,143},{... | collective-permute-start | bytes 1179656 | tf_op jit(solution)/shard_map/ppermute | solution.py:30
  62.2 9.2 %collective-permute-start.7 = (f32[1536,384]{1,0:T(8,128)S(1)}, f32[1536,384]{1,0:T(8,128)S(1)}, u32[]{:S(2)}, u32[]{:S(2)}) collective-permute-start(f32[1536,384]{1,0:T(8,128)S(1)} %get-tuple-element.67.part_ref), channel_id=1, source_target_pairs={{0,1},{1,0},{4,5},{5,4},{8,9},{9,8},{12,13},{13,12},{16,17},{17,16... | collective-permute-start | bytes 7077896 | tf_op jit(solution)/shard_map/ppermute | solution.py:30
  66.7 4.7 %collective-permute-start.8 = (f32[768,128]{1,0:T(8,128)S(1)}, f32[768,128]{1,0:T(8,128)S(1)}, u32[]{:S(2)}, u32[]{:S(2)}) collective-permute-start(f32[768,128]{1,0:T(8,128)S(1)} %get-tuple-element.68.logit_ref), channel_id=1, source_target_pairs={{0,1},{1,0},{4,5},{5,4},{8,9},{9,8},{12,13},{13,12},{16,17},{17,16... | collective-permute-start | bytes 1179656 | tf_op jit(solution)/shard_map/ppermute | solution.py:30
  83.4 12.9 %collective-permute-start.9 = (f16[1552,256]{1,0:T(8,128)(2,1)S(1)}, f16[1552,256]{1,0:T(8,128)(2,1)}, u32[]{:S(2)}, u32[]{:S(2)}) collective-permute-start(f16[1552,256]{1,0:T(8,128)(2,1)S(1)} %pad_maximum_fusion.2), channel_id=1, source_target_pairs={{0,64},{1,3},{4,68},{5,7},{8,72},{9,11},{12,76},{13,15},{16,80},{1... | collective-permute-start | bytes 2383880 | tf_op jit(solution)/shard_map/ppermute | solution.py:30
  96.3 12.6 %collective-permute-start.10 = (f16[1552,256]{1,0:T(8,128)(2,1)S(1)}, f16[1552,256]{1,0:T(8,128)(2,1)}, u32[]{:S(2)}, u32[]{:S(2)}) collective-permute-start(f16[1552,256]{1,0:T(8,128)(2,1)S(1)} %get-tuple-element.87), channel_id=1, source_target_pairs={{0,32},{1,129},{4,36},{5,133},{8,40},{9,137},{12,44},{13,141},{16,... | collective-permute-start | bytes 2383880 | tf_op jit(solution)/shard_map/ppermute | solution.py:30
  96.7 12.3 %collective-permute-start.11 = (f16[1552,256]{1,0:T(8,128)(2,1)S(1)}, f16[1552,256]{1,0:T(8,128)(2,1)}, u32[]{:S(2)}, u32[]{:S(2)}) collective-permute-start(f16[1552,256]{1,0:T(8,128)(2,1)S(1)} %get-tuple-element.88), channel_id=1, source_target_pairs={{0,96},{1,131},{4,100},{5,135},{8,104},{9,139},{12,108},{13,143},{... | collective-permute-start | bytes 2383880 | tf_op jit(solution)/shard_map/ppermute | solution.py:30
  112.2 5.9 %collective-permute-start.12 = (f16[400,256]{1,0:T(8,128)(2,1)S(1)}, f16[400,256]{1,0:T(8,128)(2,1)S(1)}, u32[]{:S(2)}, u32[]{:S(2)}) collective-permute-start(f16[400,256]{1,0:T(8,128)(2,1)S(1)} %get-tuple-element.93), channel_id=1, source_target_pairs={{0,128},{1,33},{4,132},{5,37},{8,136},{9,41},{12,140},{13,45},{16,... | collective-permute-start | bytes 614408 | tf_op jit(solution)/shard_map/ppermute | solution.py:30
  112.6 7.3 %collective-permute-start.13 = (f16[400,256]{1,0:T(8,128)(2,1)S(1)}, f16[400,256]{1,0:T(8,128)(2,1)S(1)}, u32[]{:S(2)}, u32[]{:S(2)}) collective-permute-start(f16[400,256]{1,0:T(8,128)(2,1)S(1)} %get-tuple-element.94), channel_id=1, source_target_pairs={{0,130},{1,97},{4,134},{5,101},{8,138},{9,105},{12,142},{13,109},{... | collective-permute-start | bytes 614408 | tf_op jit(solution)/shard_map/ppermute | solution.py:30
  115.1 6.4 %collective-permute-start.14 = (f16[400,256]{1,0:T(8,128)(2,1)S(1)}, f16[400,256]{1,0:T(8,128)(2,1)S(1)}, u32[]{:S(2)}, u32[]{:S(2)}) collective-permute-start(f16[400,256]{1,0:T(8,128)(2,1)S(1)} %get-tuple-element.95), channel_id=1, source_target_pairs={{0,2},{1,65},{4,6},{5,69},{8,10},{9,73},{12,14},{13,77},{16,18},{1... | collective-permute-start | bytes 614408 | tf_op jit(solution)/shard_map/ppermute | solution.py:30
  145.2 8.4 %collective-permute-start.15 = (f32[48,1024]{1,0:T(8,128)S(1)}, f32[48,1024]{1,0:T(8,128)S(1)}, u32[]{:S(2)}, u32[]{:S(2)}) collective-permute-start(f32[48,1024]{1,0:T(8,128)S(1)} %fusion.10), channel_id=1, source_target_pairs={{0,1},{1,0},{4,5},{5,4},{8,9},{9,8},{12,13},{13,12},{16,17},{17,16... | collective-permute-start | bytes 589832 | tf_op jit(solution)/shard_map/ppermute | solution.py:30
